TPU v7x, 128 devices: a whole 4x4x4 slice. The times are simulated.
128 devices in a mesh: rep: 8 (over y, x_hi), fsdp: 16 (over z, x_lo, core).
Axes of the slice: x: 4 (x_hi: 2, x_lo: 2; x = x_hi * 2 + x_lo), y: 4, z: 4, core: 2. Of those that a mesh axis runs over, the one named last changes fastest.
Arguments:
- hidden: bfloat16 [8, 4096, 8192], P('rep', 'fsdp'), may hold values from -6 to 6
- replay_buffer: bfloat16 [8, 2048, 8192], P('rep', 'fsdp'), may hold values from -6 to 6
- replay_index: int32 [8, 1024], P('rep', 'fsdp'), may hold values from 0 to 127, as said below
- cotangent: bfloat16 [8, 5120, 1024], P('rep', 'fsdp'), may hold values from -8 to 8
- norm_gain: bfloat16 [8192], replicated, may hold values from 0.3 to 2.4
- value_weight: bfloat16 [8, 8192, 1024], P('rep', 'fsdp'), may hold values from -0.0625 to 0.0625
- adam_first: float32 [8, 8192, 1024], P('rep', 'fsdp'), may hold values from -0.0014648438 to 0.0014648438
- adam_second: float32 [8, 8192, 1024], P('rep', 'fsdp'), may hold values from 1.1920929e-08 to 2.3841858e-07
- anchor: float32 [8192, 1024], P('fsdp', 'rep'), may hold values from -0.0625 to 0.0625
- outer_momentum: float32 [8192, 1024], P('fsdp', 'rep'), may hold values from -0.078125 to 0.078125
Outputs:
- input_grad: bfloat16 [8, 5120, 8192], P('rep', 'fsdp')
- first_moment: float32 [8, 8192, 1024], P('rep', 'fsdp')
- second_moment: float32 [8, 8192, 1024], P('rep', 'fsdp')
- synced_weight: bfloat16 [8192, 1024], P('fsdp')
- new_momentum: float32 [8192, 1024], P('fsdp', 'rep')
- new_anchor: float32 [8192, 1024], P('fsdp', 'rep')
Inputs may be any that keep to these rules, and one draw needn't show every extreme that they name: `replay_index`: each entry names a row of the own block of 128 rows of the device that holds it; both 0 and 127 occur among every device's entries.
All inputs are finite; a program needn't handle non-finite values.
Results may differ from a plain program's by a relative error of at most 0.015.
Values may be sent and summed in bfloat16 or wider, within the bound.
No kernel may reach another device: no remote copies, remote signals or barrier semaphores. Data moves between devices by JAX's collectives and lax.ppermute only.
A program may use at most 128 MiB of HBM per device.

v0:
```python
import jax
import jax.numpy as jnp
from jax import lax
from jax.sharding import PartitionSpec as P

norm_eps = 1e-05
adam_eps = 1e-08
inner_rate = 0.01
first_decay = 0.9
second_decay = 0.95
clip_limit = 1.0
outer_beta = 0.9
outer_rate = 0.7
replay_weight = 0.5


def on_device(
    hidden,
    replay_buffer,
    replay_index,
    cotangent,
    norm_gain,
    value_weight,
    adam_first,
    adam_second,
    anchor,
    outer_momentum,
):
    fresh_count = hidden.shape[1]
    replayed = jnp.take(replay_buffer[0], replay_index[0], axis=0)
    row_data = jnp.concatenate([hidden[0], replayed], axis=0)
    row_float = row_data.astype(jnp.float32)
    inv_rms = lax.rsqrt(jnp.mean(row_float * row_float, axis=-1, keepdims=True) + norm_eps)
    gain_float = norm_gain.astype(jnp.float32)
    row_scale = jnp.where(jnp.arange(row_data.shape[0]) < fresh_count, 1.0, replay_weight).astype(
        jnp.bfloat16
    )
    scaled_cot = cotangent[0] * row_scale[:, None]
    local_weight = value_weight[0]
    normed = row_float * inv_rms
    normed_in = (normed * gain_float).astype(jnp.bfloat16)
    grad = lax.psum_scatter(
        lax.dot_general(
            normed_in, scaled_cot, (((0,), (0,)), ((), ())), preferred_element_type=jnp.float32
        ).astype(jnp.bfloat16),
        "fsdp",
        scatter_dimension=0,
        tiled=True,
    ).astype(jnp.float32)
    product = lax.dot_general(
        scaled_cot,
        lax.all_gather(local_weight, "fsdp", axis=0, tiled=True),
        (((1,), (1,)), ((), ())),
        preferred_element_type=jnp.float32,
    )
    normed_grad = product.astype(jnp.bfloat16)
    grad_float = lax.optimization_barrier(normed_grad).astype(jnp.float32)
    gained = gain_float * grad_float
    inner_mean = jnp.mean(normed * gained, axis=-1, keepdims=True)
    input_grad = (inv_rms * (gained - normed * inner_mean)).astype(jnp.bfloat16)
    square_total = lax.psum(jnp.sum(grad * grad), "fsdp")
    clip_factor = jnp.minimum(1.0, clip_limit / jnp.sqrt(square_total))
    clipped = grad * clip_factor
    first = first_decay * adam_first[0] + (1.0 - first_decay) * clipped
    second = second_decay * adam_second[0] + (1.0 - second_decay) * clipped * clipped
    inner_new = (
        local_weight.astype(jnp.float32) - inner_rate * first / (jnp.sqrt(second) + adam_eps)
    ).astype(jnp.bfloat16)
    inner_total = lax.psum_scatter(
        inner_new.astype(jnp.float32).astype(jnp.bfloat16), "rep", scatter_dimension=1, tiled=True
    ).astype(jnp.float32)
    outer_grad = anchor - inner_total / lax.axis_size("rep")
    new_momentum = outer_beta * outer_momentum + outer_grad
    new_anchor = anchor - outer_rate * (outer_grad + outer_beta * new_momentum)
    synced_weight = lax.all_gather(new_anchor.astype(jnp.bfloat16), "rep", axis=1, tiled=True)
    return (input_grad[None], first[None], second[None], synced_weight, new_momentum, new_anchor)


def solution(mesh):
    return jax.shard_map(
        on_device,
        mesh=mesh,
        in_specs=(
            P("rep", "fsdp", None),
            P("rep", "fsdp", None),
            P("rep", "fsdp"),
            P("rep", "fsdp", None),
            P(),
            P("rep", "fsdp", None),
            P("rep", "fsdp", None),
            P("rep", "fsdp", None),
            P("fsdp", "rep"),
            P("fsdp", "rep"),
        ),
        out_specs=(
            P("rep", "fsdp", None),
            P("rep", "fsdp", None),
            P("rep", "fsdp", None),
            P("fsdp", None),
            P("fsdp", "rep"),
            P("fsdp", "rep"),
        ),
        check_vma=False,
    )
```

profile of v0, /device:TPU:1, one launch (start us, length us, event | category | flops | bytes accessed | tf_op | source)
XLA Modules:
  0.0 438.5 jit_solution(7506786009028793018)
XLA Ops:
  7.2 0.0 copy-start
  7.2 0.0 reduce-scatter.5.cloned.1.call-start
  7.2 0.8 fusion.27
  8.0 0.7 compare_and_fusion
  8.7 0.7 convert_element_type.46
  9.4 0.0 copy-done
  9.4 2.2 gather_fusion
  11.6 0.0 copy-start.2
  11.6 0.0 copy-start.7
  11.6 1.5 broadcast_select_fusion
  13.1 0.0 copy-start.3
  13.2 3.9 fusion.13
  17.1 0.0 copy-done.2
  17.1 0.0 copy-done.7
  17.1 12.7 %convolution_convert_fusion = bf16[8192,1024]{1,0:T(8,128)(2,1)} fusion(f32[8192]{0:T(1024)S(1)} %convert_element_type.46, f32[320]{0:T(512)S(1)} %get-tuple-element.13, bf16[1,320,1024]{2,1,0:T(8,128)(2,1)S(1)} %copy-done.7, bf16[320]{0:T(512)(128)(2,1)S(1)} %get-tuple-element.12, bf16[64,8192]{1,0:T(8,128)(2,1)S(1)} %broadcast_select_fusion, ...), kind=kOutput, calls=%fused_computation.3 | convolution fusion | flops 5395775488 | bytes 22710144 | tf_op jit(solution)/shard_map/dot_general | solution.py:43
  29.8 0.0 copy-start.4
  29.8 0.0 reduce-scatter.5.cloned.1.call-update
  29.8 0.0 all-gather.6.cloned.1.call-start
  29.8 0.7 all-gather.6.cloned.1.call-update
  30.5 0.0 reduce-scatter.7.cloned.1.call-start
  30.6 183.2 %reduce-scatter.5.cloned.1.call-done = bf16[512,1024]{1,0:T(8,128)(2,1)} async-done(((bf16[8192,1024]{1,0:T(8,128)(2,1)}), bf16[512,1024]{1,0:T(8,128)(2,1)}) %reduce-scatter.5.cloned.1.call-update) | async-done | bytes 1048592 | tf_op jit(solution)/shard_map/reduce_scatter | solution.py:42
  213.8 2.4 fusion.20
  216.2 29.9 %psum.7 = f32[]{:T(128)} all-reduce(f32[]{:T(128)} %fusion.20), channel_id=1, replica_groups=mesh['rep'=8,'fsdp'=16] {'fsdp'}, use_global_device_ids=true, to_apply=%region_4.5 | all-reduce | flops 1 | bytes 8 | tf_op jit(solution)/shard_map/psum | solution.py:61
  246.8 0.0 copy-done.4
  246.8 6.2 %fusion.22 = (bf16[512,1024]{1,0:T(8,128)(2,1)S(1)}, f32[1,512,1024]{2,1,0:T(8,128)}, f32[1,512,1024]{2,1,0:T(8,128)}) fusion(bf16[512,1024]{1,0:T(8,128)(2,1)} %reduce-scatter.5.cloned.1.call-done, f32[1,512,1024]{2,1,0:T(8,128)} %param.16, bf16[1,512,1024]{2,1,0:T(8,128)(2,1)S(1)} %copy-done.4, f32[1,512,1024]{2,1,0:T(8,128)} %param.17, f32[]{:T(128)S(6)} %min.3), kind=kLoop, calls=%fused_computation.29 | loop fusion | flops 7864320 | bytes 11534340 | tf_op jit(solution)/shard_map/convert_element_type | solution.py:68
  253.0 1.3 copy.16
  254.3 0.0 reduce-scatter.7.cloned.1.call-update
  254.3 0.2 all-gather.4.cloned.1.call-start
  254.6 53.7 %all-gather.6.cloned.1.call-done = bf16[1,8192,1024]{2,1,0:T(8,128)(2,1)} async-done(((bf16[1,512,1024]{2,1,0:T(8,128)(2,1)}), bf16[1,8192,1024]{2,1,0:T(8,128)(2,1)}) %all-gather.6.cloned.1.call-update) | async-done | bytes 16777232 | tf_op jit(solution)/shard_map/all_gather | solution.py:52
  308.2 18.9 %fusion.5 = bf16[320,8192]{1,0:T(8,128)(2,1)} fusion(bf16[1,8192,1024]{2,1,0:T(8,128)(2,1)} %all-gather.6.cloned.1.call-done, bf16[1,320,1024]{2,1,0:T(8,128)(2,1)} %param.13, bf16[320]{0:T(512)(128)(2,1)S(1)} %get-tuple-element.12), kind=kOutput, calls=%fused_computation.9 | convolution fusion | flops 5371658240 | bytes 22676096 | tf_op jit(solution)/shard_map/dot_general | solution.py:50
  327.1 0.0 copy-done.3
  327.1 0.0 copy-start.5
  327.1 0.0 copy-start.6
  327.1 5.7 %fusion.8 = f32[320]{0:T(512)S(1)} fusion(bf16[320,8192]{1,0:T(8,128)(2,1)} %fusion.5, f32[8192]{0:T(1024)S(1)} %convert_element_type.46, f32[320]{0:T(512)S(1)} %get-tuple-element.13, bf16[64,8192]{1,0:T(8,128)(2,1)S(1)} %broadcast_select_fusion, bf16[256,8192]{1,0:T(8,128)(2,1)} %bitcast.42), kind=kLoop, calls=%fused_computation.10 | loop fusion | flops 23592640 | bytes 10521088 | tf_op jit(solution)/shard_map/reduce_sum | solution.py:59
  332.8 49.4 %reduce-scatter.7.cloned.1.call-done = bf16[128,512]{1,0:T(8,128)(2,1)} async-done(((bf16[1024,512]{1,0:T(8,128)(2,1)}), bf16[128,512]{1,0:T(8,128)(2,1)}) %reduce-scatter.7.cloned.1.call-update) | async-done | bytes 131088
  382.1 1.0 copy.17
  383.2 0.0 copy-done.5
  383.2 0.0 copy-done.6
  383.2 0.9 fusion.28
  384.1 0.0 all-gather.4.cloned.1.call-update
  384.1 0.0 copy-start.1
  384.1 9.1 %fusion.15 = bf16[1,320,8192]{2,1,0:T(8,128)(2,1)} fusion(bf16[320,8192]{1,0:T(8,128)(2,1)} %fusion.5, f32[320]{0:T(512)S(1)} %broadcast_multiply_fusion, f32[8192]{0:T(1024)S(1)} %convert_element_type.46, f32[320]{0:T(512)S(1)} %get-tuple-element.13, bf16[64,8192]{1,0:T(8,128)(2,1)} %copy-done.3, bf16[256,8192]{1,0:T(8,128)(2,1)} %bitcast.43), kind=kLoop, calls=%fused_computation.17 | loop fusion | flops 28835840 | bytes 15763968 | tf_op jit(solution)/shard_map/broadcast_in_dim | solution.py:76
  393.2 36.6 %all-gather.4.cloned.1.call-done = bf16[512,1024]{1,0:T(8,128)(2,1)} async-done(((bf16[512,128]{1,0:T(8,128)(2,1)}), bf16[512,1024]{1,0:T(8,128)(2,1)}) %all-gather.4.cloned.1.call-update) | async-done | bytes 1048592 | tf_op jit(solution)/shard_map/all_gather | solution.py:75
  429.8 2.3 copy.19
  432.0 0.0 copy-done.1
  (3 shorter events, 0.0 us)
Async XLA Ops:
  7.2 2.3 copy-start
  7.2 206.6 %reduce-scatter.5.cloned.1.call-start = ((), (), s32[]{:S(2)}) async-start(), calls=%async_computation.2 | async-start | bytes 17825792 | tf_op jit(solution)/shard_map/reduce_scatter | solution.py:42
  11.6 5.5 %copy-start.2 = (bf16[1,256,8192]{2,1,0:T(8,128)(2,1)S(1)}, bf16[1,256,8192]{2,1,0:T(8,128)(2,1)}, u32[]{:S(2)}) copy-start(bf16[1,256,8192]{2,1,0:T(8,128)(2,1)} %param.10) | copy-start | bytes 12582916
  11.6 5.5 %copy-start.7 = (bf16[1,320,1024]{2,1,0:T(8,128)(2,1)S(1)}, bf16[1,320,1024]{2,1,0:T(8,128)(2,1)}, u32[]{:S(2)}) copy-start(bf16[1,320,1024]{2,1,0:T(8,128)(2,1)} %param.13) | copy-start | bytes 1966084
  13.1 313.9 %copy-start.3 = (bf16[64,8192]{1,0:T(8,128)(2,1)}, bf16[64,8192]{1,0:T(8,128)(2,1)S(1)}, u32[]{:S(2)}) copy-start(bf16[64,8192]{1,0:T(8,128)(2,1)S(1)} %broadcast_select_fusion) | copy-start | bytes 3145732
  29.8 217.0 %copy-start.4 = (bf16[1,512,1024]{2,1,0:T(8,128)(2,1)S(1)}, bf16[1,512,1024]{2,1,0:T(8,128)(2,1)}, u32[]{:S(2)}) copy-start(bf16[1,512,1024]{2,1,0:T(8,128)(2,1)} %param.15) | copy-start | bytes 3145732
  29.8 278.4 %all-gather.6.cloned.1.call-start = ((), (), s32[]{:S(2)}) async-start(), calls=%async_computation.4 | async-start | bytes 17825792 | tf_op jit(solution)/shard_map/all_gather | solution.py:52
  30.5 351.6 %reduce-scatter.7.cloned.1.call-start = ((), (), s32[]{:S(2)}) async-start(), calls=%async_computation.5 | async-start | bytes 1179648
  254.3 175.4 %all-gather.4.cloned.1.call-start = ((), (), s32[]{:S(2)}) async-start(), calls=%async_computation.3 | async-start | bytes 1179648 | tf_op jit(solution)/shard_map/all_gather | solution.py:75
  327.1 56.1 %copy-start.5 = (f32[512,128]{1,0:T(8,128)S(1)}, f32[512,128]{1,0:T(8,128)}, u32[]{:S(2)}) copy-start(f32[512,128]{1,0:T(8,128)} %param.18) | copy-start | bytes 786436
  327.1 56.1 %copy-start.6 = (f32[512,128]{1,0:T(8,128)S(1)}, f32[512,128]{1,0:T(8,128)}, u32[]{:S(2)}) copy-start(f32[512,128]{1,0:T(8,128)} %param.19) | copy-start | bytes 786436
  384.1 47.9 %copy-start.1 = (bf16[1,128,8192]{2,1,0:T(8,128)(2,1)S(1)}, bf16[1,128,8192]{2,1,0:T(8,128)(2,1)}, u32[]{:S(2)}) copy-start(bf16[1,128,8192]{2,1,0:T(8,128)(2,1)} %param.11) | copy-start | bytes 6291460
Sparse Core Ops, SparseCore 0:
  29.9 183.8 reduce-scatter.4
  215.5 92.6 all-gather.5
  311.8 70.2 reduce-scatter.6
  384.4 45.3 all-gather.3
where the time goes:
time: 439 us
  waiting for transfers between devices  324 us (74%)
  other arithmetic  31.9 us (7%)
  matrix products  31.5 us (7%)
  blocking collectives  29.9 us (7%)
  between operations  14.5 us (3%)
  local copies, waits for them, and re-layouts  6.81 us (2%)
    reduce_scatter x1, waiting for transfers between devices, on_device(): lax.psum_scatter(lax.dot_general(normed_in, scaled_cot, (((0,), (0,)), ((...  183 us
    all_gather x1, waiting for transfers between devices, on_device(): lax.all_gather(local_weight, 'fsdp', axis=0, tiled=True)  53.7 us
    unnamed x5, waiting for transfers between devices  50.1 us
    all_gather x1, waiting for transfers between devices, on_device(): lax.all_gather(new_anchor.astype(jnp.bfloat16), 'rep', axis=1, tiled=True)  36.6 us
    psum x1, blocking collectives, on_device(): square_total = lax.psum(jnp.sum(grad * grad), 'fsdp')  29.9 us
    dot_general x1, matrix products, on_device(): lax.dot_general(scaled_cot, lax.all_gather(local_weight, 'fsdp', axis=0,...  18.9 us
    dot_general x1, matrix products, on_device(): lax.dot_general(normed_in, scaled_cot, (((0,), (0,)), ((), ())), preferre...  12.7 us
    broadcast_in_dim x1, other arithmetic, on_device(): input_grad[None]  9.06 us
  transfers between devices with their start and end apart: 4, of which 4 were waited for; matrix products, arithmetic and copies ran while one was open for 10% of the time, Pallas kernels for 0%

commit v1 on v0

v1 whole, which is shorter than its diff:
```python
import functools

import jax
import jax.numpy as jnp
from jax import lax
from jax.experimental import pallas as pl
from jax.experimental.pallas import tpu as pltpu
from jax.sharding import PartitionSpec as P

norm_eps = 1e-05
adam_eps = 1e-08
inner_rate = 0.01
first_decay = 0.9
second_decay = 0.95
clip_limit = 1.0
outer_beta = 0.9
outer_rate = 0.7
replay_weight = 0.5

F32 = jnp.float32
BF16 = jnp.bfloat16
MIB = 1024 * 1024


def sds(shape, dtype):
    return jax.ShapeDtypeStruct(shape, dtype)


def cost(flops, size):
    return pl.CostEstimate(flops=int(flops), bytes_accessed=int(size), transcendentals=0)


def params(mib):
    return pltpu.CompilerParams(vmem_limit_bytes=mib * MIB)


def clip_index(t, start, count):
    return jnp.clip(t - start, 0, count - 1)


def over_core(value):
    return lax.ppermute(value, "fsdp", [(i, i ^ 1) for i in range(16)])


def over_x(value):
    return lax.ppermute(value, "fsdp", [(i, i ^ 2) for i in range(16)])


def over_z(value, step):
    return lax.ppermute(value, "fsdp", [(i, (i + 4 * step) % 16) for i in range(16)])


def over_x_hi(value):
    return lax.ppermute(value, "rep", [(i, i ^ 1) for i in range(8)])


def over_y(value, step):
    return lax.ppermute(value, "rep", [(i, (i + 2 * step) % 8) for i in range(8)])


def lane_sum(value):
    total = value[:, 0:128]
    for at in range(128, value.shape[1], 128):
        total = total + value[:, at : at + 128]
    return total


def prep_kernel(core_ref, index_ref, hk_ref, hs_ref, bk_ref, bs_ref, cot_ref, xk_ref, xs_ref, cp_ref, inv_ref, total_ref):
    step = pl.program_id(0)
    rows = lax.broadcasted_iota(jnp.int32, (128, 64), 0)
    pick = jnp.where(rows == index_ref[...], 1.0, 0.0).astype(BF16)
    squares = jnp.zeros((320, 128), F32)
    for h_ref, b_ref, x_ref in ((hk_ref, bk_ref, xk_ref), (hs_ref, bs_ref, xs_ref)):
        replayed = lax.dot_general(pick, b_ref[...], (((0,), (0,)), ((), ())), preferred_element_type=F32)
        fresh = h_ref[...]
        x_ref[0:256, :] = fresh
        x_ref[256:320, :] = replayed.astype(BF16)
        fresh = fresh.astype(F32)
        squares = squares + jnp.concatenate([lane_sum(fresh * fresh), lane_sum(replayed * replayed)], axis=0)

    @pl.when(step == 0)
    def _():
        total_ref[...] = squares

    @pl.when(step > 0)
    def _():
        total_ref[...] += squares

    @pl.when(step == 7)
    def _():
        mean = jnp.sum(total_ref[...], axis=1, keepdims=True) / 8192.0
        inv = lax.rsqrt(mean + norm_eps)
        inv_ref[...] = jnp.broadcast_to(inv, (320, 128))
        at = lax.broadcasted_iota(jnp.int32, (320, 1), 0)
        scale = inv * jnp.where(at < 256, 1.0, replay_weight)
        cp_ref[...] = (cot_ref[...].astype(F32) * scale).astype(BF16)


def prep(core, hidden, replay_buffer, replay_index, cotangent):
    def block(rows, flip):
        return pl.BlockSpec((None, rows, 512), lambda g, c: (0, 0, 2 * g + ((1 - c[0]) if flip else c[0])))

    return pl.pallas_call(
        prep_kernel,
        grid_spec=pltpu.PrefetchScalarGridSpec(
            num_scalar_prefetch=1,
            grid=(8,),
            in_specs=[
                pl.BlockSpec((1, 64), lambda g, c: (0, 0)),
                block(256, False),
                block(256, True),
                block(128, False),
                block(128, True),
                pl.BlockSpec((None, 320, 1024), lambda g, c: (0, 0, 0)),
            ],
            out_specs=[
                pl.BlockSpec((None, 320, 512), lambda g, c: (g, 0, 0)),
                pl.BlockSpec((None, 320, 512), lambda g, c: (g, 0, 0)),
                pl.BlockSpec((320, 1024), lambda g, c: (0, 0)),
                pl.BlockSpec((320, 128), lambda g, c: (0, 0)),
            ],
            scratch_shapes=[pltpu.VMEM((320, 128), F32)],
        ),
        out_shape=[
            sds((8, 320, 512), BF16),
            sds((8, 320, 512), BF16),
            sds((320, 1024), BF16),
            sds((320, 128), F32),
        ],
        compiler_params=params(32),
        cost_estimate=cost(2e9, 12e6),
        name="prep",
    )(core, replay_index, hidden, hidden, replay_buffer, replay_buffer, cotangent)


def grad_kernel(runs, table_ref, xk_ref, xs_ref, c_ref, cs_ref, *rest):
    outs, (x_all, c_all) = rest[:-2], rest[-2:]
    step = pl.program_id(0)

    @pl.when(step == 0)
    def _():
        c_all[0:320, :] = c_ref[...]
        c_all[320:640, :] = cs_ref[...]

    x_all[0:320, :] = xk_ref[...]
    x_all[320:640, :] = xs_ref[...]
    part = lax.dot_general(x_all[...], c_all[...], (((0,), (0,)), ((), ())), preferred_element_type=F32).astype(BF16)
    for out_ref, (start, count) in zip(outs, runs):

        @pl.when((step >= start) & (step < start + count))
        def _(out_ref=out_ref):
            out_ref[...] = part


def grad_blocks(place, outputs, xk, xs, c, cs, name):
    z, x = place
    blocks = [b for out in outputs for b in out]
    table = jnp.stack([jnp.stack([((z + dz) % 4) * 2 + (x ^ dx), jnp.int32(h)]) for dz, dx, h in blocks])
    runs, start = [], 0
    for out in outputs:
        runs.append((start, len(out)))
        start += len(out)
    x_spec = pl.BlockSpec((None, 320, 256), lambda t, tab: (tab[t, 0], 0, tab[t, 1]))
    c_spec = pl.BlockSpec((320, 1024), lambda t, tab: (0, 0))
    return pl.pallas_call(
        functools.partial(grad_kernel, runs),
        grid_spec=pltpu.PrefetchScalarGridSpec(
            num_scalar_prefetch=1,
            grid=(len(blocks),),
            in_specs=[x_spec, x_spec, c_spec, c_spec],
            out_specs=[
                pl.BlockSpec((None, 256, 1024), lambda t, tab, s=s, n=n: (clip_index(t, s, n), 0, 0)) for s, n in runs
            ],
            scratch_shapes=[pltpu.VMEM((640, 256), BF16), pltpu.VMEM((640, 1024), BF16)],
        ),
        out_shape=[sds((n, 256, 1024), BF16) for _, n in runs],
        compiler_params=params(48),
        cost_estimate=cost(len(blocks) * 2 * 640 * 256 * 1024, len(blocks) * 900e3),
        name=name,
    )(table, xk, xs, c, cs)


def total_kernel(a0, a1, a2, a3, b0, b1, gain_ref, grad_ref, sq_ref):
    step = pl.program_id(0)
    top = (a0[...].astype(F32) + a1[...].astype(F32)) + (a2[...].astype(F32) + a3[...].astype(F32))
    low = b0[...].astype(F32) + b1[...].astype(F32)
    top = top * gain_ref[0:256, :]
    low = low * gain_ref[256:512, :]
    grad_ref[0:256, :] = top
    grad_ref[256:512, :] = low
    both = lane_sum(top * top + low * low)
    square = jnp.sum(both.reshape(32, 8, 128), axis=0)

    @pl.when(step == 0)
    def _():
        sq_ref[...] = square

    @pl.when(step > 0)
    def _():
        sq_ref[...] += square


def total(a0, a1, a2, a3, b0, b1, gain_rows):
    part = pl.BlockSpec((256, 256), lambda t: (0, t))
    return pl.pallas_call(
        total_kernel,
        grid=(4,),
        in_specs=[part] * 6 + [pl.BlockSpec((512, 1), lambda t: (0, 0))],
        out_specs=[pl.BlockSpec((512, 256), lambda t: (0, t)), pl.BlockSpec((8, 128), lambda t: (0, 0))],
        out_shape=[sds((512, 1024), F32), sds((8, 128), F32)],
        compiler_params=params(32),
        cost_estimate=cost(5e6, 5e6),
        name="total",
    )(a0, a1, a2, a3, b0, b1, gain_rows)


def adam_kernel(table_ref, sq_ref, grad_ref, m_ref, v_ref, w_ref, first_ref, second_ref, *outs):
    step = pl.program_id(0)
    squares = jnp.sum(sq_ref[...], axis=1, keepdims=True)
    squares = jnp.sum(squares, axis=0, keepdims=True)
    factor = jnp.minimum(1.0, clip_limit / jnp.sqrt(squares))
    clipped = grad_ref[...] * factor
    first = first_decay * m_ref[...] + (1.0 - first_decay) * clipped
    second = second_decay * v_ref[...] + (1.0 - second_decay) * clipped * clipped
    first_ref[...] = first
    second_ref[...] = second
    new = w_ref[...].astype(F32) - inner_rate * first / (jnp.sqrt(second) + adam_eps)
    new = new.astype(BF16)
    for k, out_ref in enumerate(outs):

        @pl.when((step >= 2 * k) & (step < 2 * k + 2))
        def _(out_ref=out_ref):
            out_ref[...] = new


def adam(table, sq, grad, first_in, second_in, weight):
    column = pl.BlockSpec((512, 128), lambda t, tab: (0, tab[t]))
    lead = pl.BlockSpec((None, 512, 128), lambda t, tab: (0, 0, tab[t]))
    return pl.pallas_call(
        adam_kernel,
        grid_spec=pltpu.PrefetchScalarGridSpec(
            num_scalar_prefetch=1,
            grid=(8,),
            in_specs=[pl.BlockSpec((8, 128), lambda t, tab: (0, 0)), column, lead, lead, lead],
            out_specs=[lead, lead]
            + [pl.BlockSpec((None, 512, 128), lambda t, tab, k=k: (clip_index(t, 2 * k, 2), 0, 0)) for k in range(4)],
        ),
        out_shape=[sds((1, 512, 1024), F32)] * 2 + [sds((2, 512, 128), BF16)] * 4,
        compiler_params=params(32),
        cost_estimate=cost(2e7, 12e6),
        name="adam",
    )(table, sq, grad, first_in, second_in, weight)


def place_kernel(table_ref, *refs):
    step = pl.program_id(0)
    for k, in_ref in enumerate(refs[:-1]):

        @pl.when((step >= 2 * k) & (step < 2 * k + 2))
        def _(in_ref=in_ref):
            refs[-1][...] = in_ref[...]


def place_columns(table, parts):
    return pl.pallas_call(
        place_kernel,
        grid_spec=pltpu.PrefetchScalarGridSpec(
            num_scalar_prefetch=1,
            grid=(8,),
            in_specs=[
                pl.BlockSpec((None, 512, 128), lambda t, tab, k=k: (clip_index(t, 2 * k, 2), 0, 0)) for k in range(4)
            ],
            out_specs=pl.BlockSpec((512, 128), lambda t, tab: (0, tab[t])),
        ),
        out_shape=sds((512, 1024), BF16),
        compiler_params=params(32),
        cost_estimate=cost(1e6, 2e6),
        name="place",
    )(table, *parts)


def input_kernel(groups, table_ref, xk_ref, xs_ref, cp_ref, inv_ref, gain_ref, *rest):
    weights = rest[: len(groups)]
    out_ref, q_ref, m_ref = rest[len(groups) :]
    step = pl.program_id(0)
    n_q = sum(count for _, count, _, _ in groups)

    @pl.when(step == 0)
    def _():
        m_ref[...] = jnp.zeros_like(m_ref)

    for w_ref, (start, count, sibling, half) in zip(weights, groups):

        @pl.when((step >= start) & (step < start + count))
        def _(w_ref=w_ref, sibling=sibling, half=half):
            q = lax.dot_general(cp_ref[...], w_ref[...], (((1,), (1,)), ((), ())), preferred_element_type=F32)
            g = table_ref[step]
            columns = slice(256 * half, 256 * half + 256)
            gain = gain_ref[2 * g + (table_ref[64] ^ sibling)][:, columns].astype(F32)
            gained = q * gain
            x = (xs_ref if sibling else xk_ref)[...]
            m_ref[...] += lane_sum(gained * x[:, columns].astype(F32))
            q_ref[sibling * 8 + g, :, columns] = gained.astype(BF16)

    for sibling in range(2):

        @pl.when((step >= n_q + 8 * sibling) & (step < n_q + 8 * sibling + 8))
        def _(sibling=sibling):
            g = table_ref[step]
            inv = inv_ref[:, 0:1]
            factor = jnp.sum(m_ref[...], axis=1, keepdims=True) * (inv * inv) / 8192.0
            x = (xs_ref if sibling else xk_ref)[...].astype(F32)
            out_ref[...] = (q_ref[sibling * 8 + g].astype(F32) - x * factor).astype(BF16)


def input_gradient(core, place, xk, xs, cp, inv, gain, weights):
    z, x = place
    groups, order, start = [], [], 0
    for array, sibling, half, chunks in weights:
        groups.append((start, len(chunks), sibling, half))
        order += [((z + dz) % 4) * 2 + (x ^ dx) for dz, dx in chunks]
        start += len(chunks)
    n_q, n_mine = start, start // 2
    order += [jnp.int32(g) for g in range(8)] * 2
    order += [jnp.int32(0)] * (64 - len(order)) + [core]
    table = jnp.stack(order)

    def mine(t, tab):
        at = jnp.where(t < n_mine, t, jnp.where(t < n_q, n_mine - 1, jnp.clip(t, n_q, n_q + 7)))
        return (tab[at], 0, 0)

    def theirs(t, tab):
        at = jnp.where(t < n_q, jnp.clip(t, n_mine, n_q - 1), jnp.where(t < n_q + 8, n_q - 1, t))
        return (tab[at], 0, 0)

    def out_at(t, tab):
        g = tab[jnp.maximum(t, n_q)]
        return (0, 0, 2 * g + (tab[64] ^ jnp.where(t < n_q + 8, 0, 1)))

    return pl.pallas_call(
        functools.partial(input_kernel, groups),
        grid_spec=pltpu.PrefetchScalarGridSpec(
            num_scalar_prefetch=1,
            grid=(n_q + 16,),
            in_specs=[
                pl.BlockSpec((None, 320, 512), mine),
                pl.BlockSpec((None, 320, 512), theirs),
                pl.BlockSpec((320, 1024), lambda t, tab: (0, 0)),
                pl.BlockSpec((320, 128), lambda t, tab: (0, 0)),
                pl.BlockSpec((16, 1, 512), lambda t, tab: (0, 0, 0)),
            ]
            + [
                pl.BlockSpec((None, 256, 1024), lambda t, tab, s=s, n=n: (clip_index(t, s, n), 0, 0))
                for s, n, _, _ in groups
            ],
            out_specs=pl.BlockSpec((None, 320, 512), out_at),
            scratch_shapes=[pltpu.VMEM((16, 320, 512), BF16), pltpu.VMEM((320, 128), F32)],
        ),
        out_shape=sds((1, 320, 8192), BF16),
        compiler_params=params(56),
        cost_estimate=cost(6e9, 40e6),
        name="input_gradient",
    )(table, xk, xs, cp, inv, gain, *[w[0] for w in weights])


def add(*values):
    total_value = values[0].astype(F32)
    for value in values[1:]:
        total_value = total_value + value.astype(F32)
    return total_value.astype(BF16)


def on_device(
    hidden,
    replay_buffer,
    replay_index,
    cotangent,
    norm_gain,
    value_weight,
    adam_first,
    adam_second,
    anchor,
    outer_momentum,
):
    fsdp = lax.axis_index("fsdp")
    rep = lax.axis_index("rep")
    core, x, z = fsdp % 2, (fsdp // 2) % 2, fsdp // 4
    x_hi, y = rep % 2, rep // 2
    place = (z, x)
    columns = jnp.stack([((y + dy) % 4) * 2 + (x_hi ^ dx) for dy in range(4) for dx in range(2)])
    gain_float = norm_gain.astype(F32)

    w0, w1 = value_weight[0, 0:256], value_weight[0, 256:512]
    wx = over_x(w0)
    u_m = over_z(w1, 1)
    u_p = over_z(w1, -1)

    xk, xs, cp, inv = prep(core[None], hidden, replay_buffer, replay_index, cotangent)
    x_sib = over_core(xs)
    c_sib = over_core(cp)

    b_up, b_down, a_send, a_last = grad_blocks(
        place,
        [[(2, 0, 1)], [(2, 1, 1)], [(2, 1, 0), (1, 1, 0), (3, 1, 0)], [(0, 1, 0)]],
        xk, x_sib, cp, c_sib, "grad_a",
    )
    r_up = over_z(b_up, 1)
    r_down = over_z(b_down, -1)
    r_a = over_x(a_send)
    b_10, b_11, b_30, b_31, a_own, b_0 = grad_blocks(
        place,
        [[(1, 0, 1)], [(1, 1, 1)], [(3, 0, 1)], [(3, 1, 1)], [(2, 0, 0), (1, 0, 0), (3, 0, 0), (0, 0, 0)], [(0, 0, 1), (0, 1, 1)]],
        xk, x_sib, cp, c_sib, "grad_b",
    )
    e_up = over_z(b_11, 1)
    e_down = over_z(b_30, -1)
    r_a_last = over_x(a_last)
    l_up = over_z(add(b_10, r_up), 1)
    l_down = over_z(add(b_31, r_down), -1)

    s_2 = add(a_own[0], r_a[0])
    s_1 = add(a_own[1], r_a[1])
    s_3 = add(a_own[2], r_a[2])
    p_up = over_z(s_2[0:128], 1)
    p_down = over_z(s_2[128:256], -1)
    b_mine = add(b_0[0], l_up[0], e_down[0])
    b_theirs = add(b_0[1], e_up[0], l_down[0])
    r_b = over_x(b_theirs)
    s_1 = jnp.concatenate([add(s_1[0:128], p_up), s_1[128:256]], axis=0)
    s_3 = jnp.concatenate([s_3[0:128], add(s_3[128:256], p_down)], axis=0)
    f_up = over_z(s_1, 1)
    f_down = over_z(s_3, -1)

    gain_rows = lax.dynamic_slice(gain_float, (fsdp * 512,), (512,))[:, None]
    grad, squares = total(a_own[3], r_a_last[0], f_up, f_down, b_mine, r_b, gain_rows)

    squares = squares + over_core(squares)
    squares = squares + over_x(squares)
    squares = squares + over_z(squares, 1)
    squares = squares + over_z(squares, 2)

    first, second, n_0, n_1, n_2, n_3 = adam(columns, squares, grad, adam_first, adam_second, value_weight)

    v_up = over_z(u_m[0:128], 1)
    v_down = over_z(u_p[128:256], -1)
    zf = jnp.stack([w1, u_p, jnp.concatenate([v_up, v_down], axis=0), u_m])
    zfx = over_x(zf)
    pair = jnp.stack([w0, wx])
    pair_m = over_z(pair, 1)
    pair_p = over_z(pair, -1)
    pair_2a = over_z(pair_m[0:1], 1)
    pair_2b = over_z(pair_p[1:2], -1)
    xf_order = [(0, 0), (0, 1)]
    gathered = [
        (pair, 0, [(0, 0), (0, 1)]),
        (zf, 1, [(dz, 0) for dz in range(4)]),
        (pair_m, 0, [(3, 0), (3, 1)]),
        (pair_p, 0, [(1, 0), (1, 1)]),
        (pair_2a, 0, [(2, 0)]),
        (pair_2b, 0, [(2, 1)]),
        (zfx, 1, [(dz, 1) for dz in range(4)]),
    ]
    weights = [(array, 0, half, chunks) for array, half, chunks in gathered]
    weights += [(over_core(array), 1, half, chunks) for array, half, chunks in gathered]
    input_grad = input_gradient(
        core, place, xk, xs, cp, inv, gain_float.reshape(16, 1, 512), weights
    )

    m_1 = over_y(n_1, 1)
    m_2 = over_y(n_2, 2)
    m_3 = over_y(n_3, 3)
    summed = n_0.astype(F32) + m_1.astype(F32) + m_2.astype(F32) + m_3.astype(F32)
    inner_total = summed[0] + over_x_hi(summed[1].astype(BF16)).astype(F32)
    outer_grad = anchor - inner_total / 8
    new_momentum = outer_beta * outer_momentum + outer_grad
    new_anchor = anchor - outer_rate * (outer_grad + outer_beta * new_momentum)
    sent = new_anchor.astype(BF16)
    sent = jnp.stack([sent, over_x_hi(sent)])
    parts = [sent, over_y(sent, 3), over_y(sent, 2), over_y(sent, 1)]
    synced_weight = place_columns(columns, parts)
    return (input_grad, first, second, synced_weight, new_momentum, new_anchor)


def solution(mesh):
    return jax.shard_map(
        on_device,
        mesh=mesh,
        in_specs=(
            P("rep", "fsdp", None),
            P("rep", "fsdp", None),
            P("rep", "fsdp"),
            P("rep", "fsdp", None),
            P(),
            P("rep", "fsdp", None),
            P("rep", "fsdp", None),
            P("rep", "fsdp", None),
            P("fsdp", "rep"),
            P("fsdp", "rep"),
        ),
        out_specs=(
            P("rep", "fsdp", None),
            P("rep", "fsdp", None),
            P("rep", "fsdp", None),
            P("fsdp", None),
            P("fsdp", "rep"),
            P("fsdp", "rep"),
        ),
        check_vma=False,
    )
```

time: 439 us -> 298 us (0.68)
  waiting for transfers between devices: 324 us -> 100 us
  Pallas kernels: 0 us -> 80.4 us
  starting transfers between devices: 0.34 us -> 71.9 us
  matrix products: 31.5 us -> 0 us
  blocking collectives: 29.9 us -> 0 us
  local copies, waits for them, and re-layouts: 6.81 us -> 30 us
  other arithmetic: 31.9 us -> 12.7 us
  between operations: 14.5 us -> 0.99 us
    reduce_scatter x1 -> x0, waiting for transfers between devices: 183 us -> none  [on_device(): lax.psum_scatter(lax.dot_general(normed_in, scaled_cot, (((0,), (0,)), ((...]
    ppermute x0 -> x44, waiting for transfers between devices: none -> 100 us  [the longest x20 61.6 us: over_z(): lax.ppermute(value, 'fsdp', [(i, (i + 4 * step) % 16) for i in range(16)])]
    all_gather x2 -> x0, waiting for transfers between devices: 90.2 us -> none  [the longest x1 53.7 us: on_device(): lax.all_gather(local_weight, 'fsdp', axis=0, tiled=True)]
    pallas_call x0 -> x7, Pallas kernels: none -> 80.4 us  [the longest x1 44.6 us: input_gradient(): pl.pallas_call(functools.partial(input_kernel, groups), grid_spec=pltpu.P...]
    ppermute x0 -> x44, starting transfers between devices: none -> 71.9 us  [the longest x10 38.3 us: over_core(): return lax.ppermute(value, 'fsdp', [(i, i ^ 1) for i in range(16)])]
    unnamed x5 -> x0, waiting for transfers between devices: 50.1 us -> none
    dot_general x2 -> x0, matrix products: 31.5 us -> none  [the longest x1 18.9 us: on_device(): lax.dot_general(scaled_cot, lax.all_gather(local_weight, 'fsdp', axis=0,...]
    psum x1 -> x0, blocking collectives: 29.9 us -> none  [on_device(): square_total = lax.psum(jnp.sum(grad * grad), 'fsdp')]
  transfers between devices with their start and end apart: 4 -> 44, of which waited for: 4 -> 18; matrix products, arithmetic and copies ran while one was open for 10% -> 7% of each run, Pallas kernels for 0% -> 24%
where the time goes in v1:
time: 298 us; the launch traced here: 296 us
  waiting for transfers between devices  100 us (34%)
  Pallas kernels  80.4 us (27%)
  starting transfers between devices  71.9 us (24%)
  local copies, waits for them, and re-layouts  30 us (10%)
  other arithmetic  12.7 us (4%)
    ppermute x20, waiting for transfers between devices, over_z(): lax.ppermute(value, 'fsdp', [(i, (i + 4 * step) % 16) for i in range(16)])  61.6 us
    pallas_call x1, Pallas kernels, input_gradient(): pl.pallas_call(functools.partial(input_kernel, groups), grid_spec=pltpu.P...  44.6 us
    ppermute x10, starting transfers between devices, over_core(): return lax.ppermute(value, 'fsdp', [(i, i ^ 1) for i in range(16)])  38.3 us
    ppermute x6, waiting for transfers between devices, over_x(): return lax.ppermute(value, 'fsdp', [(i, i ^ 2) for i in range(16)])  23.7 us
    unnamed x62, local copies, waits for them, and re-layouts  22.2 us
    pallas_call x2, Pallas kernels, grad_blocks(): pl.pallas_call(functools.partial(grad_kernel, runs), grid_spec=pltpu.Pref...  18.4 us
    ppermute x20, starting transfers between devices, over_z(): lax.ppermute(value, 'fsdp', [(i, (i + 4 * step) % 16) for i in range(16)])  18.2 us
    ppermute x6, waiting for transfers between devices, over_y(): lax.ppermute(value, 'rep', [(i, (i + 2 * step) % 8) for i in range(8)])  10 us
  transfers between devices with their start and end apart: 44, of which 18 were waited for; matrix products, arithmetic and copies ran while one was open for 7% of the time, Pallas kernels for 24%

profile of v1, /device:TPU:1, one launch (start us, length us, event | category | flops | bytes accessed | tf_op | source)
XLA Modules:
  0.0 296.2 jit_solution(13002451798649147200)
XLA Ops:
  0.7 2.2 copy-done
  2.8 1.6 copy-done.1
  4.4 1.1 copy-done.10
  6.2 4.9 %prep.1 = (bf16[8,320,512]{2,1,0:T(8,128)(2,1)S(1)}, bf16[8,320,512]{2,1,0:T(8,128)(2,1)}, bf16[320,1024]{1,0:T(8,128)(2,1)S(1)}, f32[320,128]{1,0:T(8,128)S(1)}) custom-call(s32[1]{0:T(128)} %bitcast.8.core_ref, s32[1,64]{1,0:T(1,128)S(1)} %copy-done.16, bf16[1,256,8192]{2,1,0:T(8,128)(2,1)S(1)} %copy-done, bf16[1,256,8192]{2,1,0:T(8,128)(2,1)S(1)} %copy-done, ...), custom_call_target="tpu_custom_call" | custom-call | flops 2000000000 | bytes 12000000 | tf_op jit(solution)/shard_map/prep/pallas_call | solution.py:103
  11.1 1.5 copy-done.3
  12.6 1.4 collective-permute-start.17
  14.0 1.5 fusion.25
  15.5 1.7 collective-permute-start.2
  17.2 2.1 collective-permute-start.1
  19.3 1.2 collective-permute-start
  21.8 1.2 collective-permute-done.18.cs_ref
  23.8 1.1 copy-done.18
  24.9 7.3 %grad_a.1 = (bf16[1,256,1024]{2,1,0:T(8,128)(2,1)S(1)}, bf16[1,256,1024]{2,1,0:T(8,128)(2,1)}, bf16[3,256,1024]{2,1,0:T(8,128)(2,1)S(1)}, bf16[1,256,1024]{2,1,0:T(8,128)(2,1)S(1)}) custom-call(s32[6,2]{1,0:T(8,128)S(1)} %stack.284.table_ref, bf16[8,320,512]{2,1,0:T(8,128)(2,1)} %copy-done.3, bf16[8,320,512]{2,1,0:T(8,128)(2,1)} %collective-permute-done.17.xs_ref, ...), custom_call_target="tpu_custom_call" | custom-call | flops 2013265920 | bytes 5400000 | tf_op jit(solution)/shard_map/grad_a/pallas_call | solution.py:165
  33.8 1.7 collective-permute-start.29
  38.2 1.3 collective-permute-start.25
  39.5 1.1 copy-done.19
  40.6 11.1 %grad_b.1 = (bf16[1,256,1024]{2,1,0:T(8,128)(2,1)S(1)}, bf16[1,256,1024]{2,1,0:T(8,128)(2,1)S(1)}, bf16[1,256,1024]{2,1,0:T(8,128)(2,1)S(1)}, bf16[1,256,1024]{2...) custom-call(s32[10,2]{1,0:T(8,128)S(1)} %stack.271.table_ref, ...), custom_call_target="tpu_custom_call" | custom-call | flops 3355443200 | bytes 9000000 | tf_op jit(solution)/shard_map/grad_b/pallas_call | solution.py:165
  51.8 1.3 add_convert_fusion.1
  53.2 2.7 collective-permute-start.27
  55.9 1.4 collective-permute-start.30
  57.5 1.8 collective-permute-done.3
  59.3 2.1 pad_maximum_fusion.1.rest_0_
  61.5 2.9 pad_maximum_fusion.rest_1_
  64.4 6.1 %collective-permute-done.28 = bf16[1,256,1024]{2,1,0:T(8,128)(2,1)S(1)} collective-permute-done((bf16[1,256,1024]{2,1,0:T(8,128)(2,1)S(1)}, bf16[1,256,1024]{2,1,0:T(8,128)(2,1)S(1)}, u32[]{:S(2)}, u32[]{:S(2)}) %collective-permute-start.28) | collective-permute-done | bytes 524320 | tf_op jit(solution)/shard_map/ppermute | solution.py:50
  70.5 1.2 collective-permute-start.9
  71.8 5.0 %collective-permute-done.30 = bf16[1,256,1024]{2,1,0:T(8,128)(2,1)S(1)} collective-permute-done((bf16[1,256,1024]{2,1,0:T(8,128)(2,1)S(1)}, bf16[1,256,1024]{2,1,0:T(8,128)(2,1)S(1)}, u32[]{:S(2)}, u32[]{:S(2)}) %collective-permute-start.30) | collective-permute-done | bytes 524320 | tf_op jit(solution)/shard_map/ppermute | solution.py:50
  76.7 1.2 collective-permute-start.19
  78.0 3.8 %collective-permute-done.26 = bf16[1,256,1024]{2,1,0:T(8,128)(2,1)S(1)} collective-permute-done((bf16[1,256,1024]{2,1,0:T(8,128)(2,1)S(1)}, bf16[1,256,1024]{2,1,0:T(8,128)(2,1)S(1)}, u32[]{:S(2)}, u32[]{:S(2)}) %collective-permute-start.26) | collective-permute-done | bytes 524320 | tf_op jit(solution)/shard_map/ppermute | solution.py:50
  81.8 1.4 fusion.1
  83.2 1.2 collective-permute-start.31
  85.3 24.6 %collective-permute-done.21 = bf16[128,1024]{1,0:T(8,128)(2,1)S(1)} collective-permute-done((bf16[128,1024]{1,0:T(8,128)(2,1)S(1)}, bf16[128,1024]{1,0:T(8,128)(2,1)S(1)}, u32[]{:S(2)}, u32[]{:S(2)}) %collective-permute-start.21) | collective-permute-done | bytes 262176 | tf_op jit(solution)/shard_map/ppermute | solution.py:50
  111.0 15.4 %collective-permute-done.19 = bf16[1,256,1024]{2,1,0:T(8,128)(2,1)S(1)} collective-permute-done((bf16[1,256,1024]{2,1,0:T(8,128)(2,1)S(1)}, bf16[1,256,1024]{2,1,0:T(8,128)(2,1)S(1)}, u32[]{:S(2)}, u32[]{:S(2)}) %collective-permute-start.19) | collective-permute-done | bytes 524320 | tf_op jit(solution)/shard_map/ppermute | solution.py:46
  127.8 3.1 %collective-permute-start.22 = (bf16[256,1024]{1,0:T(8,128)(2,1)}, bf16[256,1024]{1,0:T(8,128)(2,1)}, u32[]{:S(2)}, u32[]{:S(2)}) collective-permute-start(bf16[256,1024]{1,0:T(8,128)(2,1)} %pad_maximum_fusion.2), channel_id=1, source_target_pairs={{0,4},{1,5},{2,6},{3,7},{4,8},{5,9},{6,10},{7,11},{8,12},{9,13},{1... | collective-permute-start | bytes 1572872 | tf_op jit(solution)/shard_map/ppermute | solution.py:50
  131.8 5.9 %collective-permute-done.31.b1 = bf16[256,1024]{1,0:T(8,128)(2,1)S(1)} collective-permute-done((bf16[256,1024]{1,0:T(8,128)(2,1)S(1)}, bf16[256,1024]{1,0:T(8,128)(2,1)S(1)}, u32[]{:S(2)}, u32[]{:S(2)}) %collective-permute-start.31) | collective-permute-done | bytes 524320 | tf_op jit(solution)/shard_map/ppermute | solution.py:46
  139.3 10.5 %collective-permute-start.10 = (bf16[2,256,1024]{2,1,0:T(8,128)(2,1)}, bf16[2,256,1024]{2,1,0:T(8,128)(2,1)}, u32[]{:S(2)}, u32[]{:S(2)}) collective-permute-start(bf16[2,256,1024]{2,1,0:T(8,128)(2,1)} %pad_maximum_fusion.1.rest_0_), channel_id=1, source_target_pairs={{0,1},{1,0},{2,3},{3,2},{4,5},{5,4},{6,7},{7,6},{8,9},{9,8},{10,11... | collective-permute-start | bytes 3145736 | tf_op jit(solution)/shard_map/ppermute | solution.py:42
  149.8 1.1 slice_bitcast_fusion.a0
  150.9 8.3 %collective-permute-done.24.a3 = bf16[256,1024]{1,0:T(8,128)(2,1)} collective-permute-done((bf16[256,1024]{1,0:T(8,128)(2,1)}, bf16[256,1024]{1,0:T(8,128)(2,1)}, u32[]{:S(2)}, u32[]{:S(2)}) %collective-permute-start.24) | collective-permute-done | bytes 524320 | tf_op jit(solution)/shard_map/ppermute | solution.py:50
  162.3 2.8 total.1
  165.1 1.3 copy-done.6
  166.4 7.4 %collective-permute-start.32 = (f32[8,128]{1,0:T(8,128)S(1)}, f32[8,128]{1,0:T(8,128)S(1)}, u32[]{:S(2)}, u32[]{:S(2)}) collective-permute-start(f32[8,128]{1,0:T(8,128)S(1)} %get-tuple-element.42), channel_id=1, source_target_pairs={{0,1},{1,0},{2,3},{3,2},{4,5},{5,4},{6,7},{7,6},{8,9},{9,8},{10,11... | collective-permute-start | bytes 12296 | tf_op jit(solution)/shard_map/ppermute | solution.py:42
  174.6 2.5 collective-permute-done.33
  177.0 1.5 collective-permute-start.34
  178.5 2.2 collective-permute-done.34
  181.4 3.3 %collective-permute-done.35 = f32[8,128]{1,0:T(8,128)S(1)} collective-permute-done((f32[8,128]{1,0:T(8,128)S(1)}, f32[8,128]{1,0:T(8,128)S(1)}, u32[]{:S(2)}, u32[]{:S(2)}) %collective-permute-start.35) | collective-permute-done | bytes 4128 | tf_op jit(solution)/shard_map/ppermute | solution.py:50
  184.7 1.6 copy-done.5
  186.3 1.6 copy-done.7
  187.9 6.3 %adam.1 = (f32[1,512,1024]{2,1,0:T(8,128)}, f32[1,512,1024]{2,1,0:T(8,128)}, bf16[2,512,128]{2,1,0:T(8,128)(2,1)S(1)}, bf16[2,512,128]{2,1,0:T(8,128)(2,1)S(1)},...) custom-call(s32[8]{0:T(128)S(1)} %stack.250.table_ref, f32[8,128]{1,0:T(8,128)S(1)} %add.348.sq_ref, ...), custom_call_target="tpu_custom_call" | custom-call | flops 20000000 | bytes 12000000 | tf_op jit(solution)/shard_map/adam/pallas_call | solution.py:239
  194.2 2.7 collective-permute-start.38
  196.9 4.1 %collective-permute-start.11 = (bf16[4,256,1024]{2,1,0:T(8,128)(2,1)}, bf16[4,256,1024]{2,1,0:T(8,128)(2,1)S(1)}, u32[]{:S(2)}, u32[]{:S(2)}) collective-permute-start(bf16[4,256,1024]{2,1,0:T(8,128)(2,1)} %pad_maximum_fusion.rest_1_), channel_id=1, source_target_pairs={{0,1},{1,0},{2,3},{3,2},{4,5},{5,4},{6,7},{7,6},{8,9},{9,8},{10,11... | collective-permute-start | bytes 6291464 | tf_op jit(solution)/shard_map/ppermute | solution.py:42
  202.1 1.1 slice.113
  203.2 6.9 %collective-permute-done.37 = bf16[2,512,128]{2,1,0:T(8,128)(2,1)S(1)} collective-permute-done((bf16[2,512,128]{2,1,0:T(8,128)(2,1)S(1)}, bf16[2,512,128]{2,1,0:T(8,128)(2,1)S(1)}, u32[]{:S(2)}, u32[]{:S(2)}) %collective-permute-start.37) | collective-permute-done | bytes 262176 | tf_op jit(solution)/shard_map/ppermute | solution.py:58
  210.4 3.1 %collective-permute-done.36 = bf16[2,512,128]{2,1,0:T(8,128)(2,1)S(1)} collective-permute-done((bf16[2,512,128]{2,1,0:T(8,128)(2,1)S(1)}, bf16[2,512,128]{2,1,0:T(8,128)(2,1)S(1)}, u32[]{:S(2)}, u32[]{:S(2)}) %collective-permute-start.36) | collective-permute-done | bytes 262176 | tf_op jit(solution)/shard_map/ppermute | solution.py:58
  213.5 5.1 %collective-permute-start.12 = (bf16[2,256,1024]{2,1,0:T(8,128)(2,1)}, bf16[2,256,1024]{2,1,0:T(8,128)(2,1)}, u32[]{:S(2)}, u32[]{:S(2)}) collective-permute-start(bf16[2,256,1024]{2,1,0:T(8,128)(2,1)} %collective-permute-done.5.rest_2_), channel_id=1, source_target_pairs={{0,1},{1,0},{2,3},{3,2},{4,5},{5,4},{6,7},{7,6},{8,9},{9,8},{10,11... | collective-permute-start | bytes 3145736 | tf_op jit(solution)/shard_map/ppermute | solution.py:42
  218.7 2.2 collective-permute-start.39
  221.0 1.1 slice.114
  222.6 2.8 collective-permute-done.39
  227.1 5.9 %collective-permute-done.8.rest_5_ = bf16[1,256,1024]{2,1,0:T(8,128)(2,1)} collective-permute-done((bf16[1,256,1024]{2,1,0:T(8,128)(2,1)S(1)}, bf16[1,256,1024]{2,1,0:T(8,128)(2,1)}, u32[]{:S(2)}, u32[]{:S(2)}) %collective-permute-start.8) | collective-permute-done | bytes 524320 | tf_op jit(solution)/shard_map/ppermute | solution.py:50
  233.1 2.1 collective-permute-start.40
  235.2 4.3 %collective-permute-start.14 = (bf16[1,256,1024]{2,1,0:T(8,128)(2,1)S(1)}, bf16[1,256,1024]{2,1,0:T(8,128)(2,1)}, u32[]{:S(2)}, u32[]{:S(2)}) collective-permute-start(bf16[1,256,1024]{2,1,0:T(8,128)(2,1)S(1)} %collective-permute-done.7.rest_4_), channel_id=1, source_target_pairs={{0,1},{1,0},{2,3},{3,2},{4,5},{5,4},{6,7},{7,6},{8,9},{9,8},{10,11... | collective-permute-start | bytes 1572872 | tf_op jit(solution)/shard_map/ppermute | solution.py:42
  239.5 4.0 %collective-permute-start.15 = (bf16[1,256,1024]{2,1,0:T(8,128)(2,1)}, bf16[1,256,1024]{2,1,0:T(8,128)(2,1)}, u32[]{:S(2)}, u32[]{:S(2)}) collective-permute-start(bf16[1,256,1024]{2,1,0:T(8,128)(2,1)} %collective-permute-done.8.rest_5_), channel_id=1, source_target_pairs={{0,1},{1,0},{2,3},{3,2},{4,5},{5,4},{6,7},{7,6},{8,9},{9,8},{10,11... | collective-permute-start | bytes 1572872 | tf_op jit(solution)/shard_map/ppermute | solution.py:42
  244.9 1.3 collective-permute-start.41
  246.9 1.3 copy-done.23
  248.2 44.6 %input_gradient.1 = bf16[1,320,8192]{2,1,0:T(8,128)(2,1)} custom-call(s32[65]{0:T(128)} %stack.235.table_ref, bf16[8,320,512]{2,1,0:T(8,128)(2,1)} %copy-done.3, bf16[8,320,512]{2,1,0:T(8,128)(2,1)} %get-tuple-element.29.xs_ref, bf16[320,1024]{1,0:T(8,128)(2,1)} %copy-done.9, f32[320,128]{1,0:T(8,128)} %copy-done.15, f32[16,1,512]{2,1,0:T(1,128)} %bitcast.105, ...), custom_call_target="tpu_custom_call" | custom-call | flops 6000000000 | bytes 40000000 | tf_op jit(solution)/shard_map/input_gradient/pallas_call | solution.py:340
  292.8 3.3 %place.1 = bf16[512,1024]{1,0:T(8,128)(2,1)} custom-call(s32[8]{0:T(128)S(1)} %stack.250.table_ref, bf16[2,512,128]{2,1,0:T(8,128)(2,1)S(1)} %pad_maximum_fusion.4.refs_0_, bf16[2,512,128]{2,1,0:T(8,128)(2,1)S(1)} %collective-permute-done.41.refs_1_, bf16[2,512,128]{2,1,0:T(8,128)(2,1)S(1)} %collective-permute-done.42.refs_2_, ...), custom_call_target="tpu_custom_call" | custom-call | flops 1000000 | bytes 2000000 | tf_op jit(solution)/shard_map/place/pallas_call | solution.py:265
  (137 shorter events, 23.7 us)
Async XLA Ops:
  0.6 2.2 copy-start
  2.8 1.6 copy-start.1
  6.2 7.9 %copy-start.2 = (bf16[1,512,1024]{2,1,0:T(8,128)(2,1)S(1)}, bf16[1,512,1024]{2,1,0:T(8,128)(2,1)}, u32[]{:S(2)}) copy-start(bf16[1,512,1024]{2,1,0:T(8,128)(2,1)} %w_ref.1) | copy-start | bytes 3145732
  11.1 1.5 copy-start.3
  12.6 7.9 %copy-start.15 = (f32[320,128]{1,0:T(8,128)}, f32[320,128]{1,0:T(8,128)S(1)}, u32[]{:S(2)}) copy-start(f32[320,128]{1,0:T(8,128)S(1)} %get-tuple-element.31.inv_ref) | copy-start | bytes 491524
  12.6 26.9 %copy-start.9 = (bf16[320,1024]{1,0:T(8,128)(2,1)}, bf16[320,1024]{1,0:T(8,128)(2,1)S(1)}, u32[]{:S(2)}) copy-start(bf16[320,1024]{1,0:T(8,128)(2,1)S(1)} %get-tuple-element.30.cp_ref.c_ref) | copy-start | bytes 1966084
  12.6 11.2 %collective-permute-start.17 = (bf16[8,320,512]{2,1,0:T(8,128)(2,1)}, bf16[8,320,512]{2,1,0:T(8,128)(2,1)}, u32[]{:S(2)}, u32[]{:S(2)}) collective-permute-start(bf16[8,320,512]{2,1,0:T(8,128)(2,1)} %get-tuple-element.29.xs_ref), channel_id=1, source_target_pairs={{0,1},{1,0},{2,3},{3,2},{4,5},{5,4},{6,7},{7,6},{8,9},{9,8},{10,11... | collective-permute-start | bytes 7864328 | tf_op jit(solution)/shard_map/ppermute | solution.py:42
  15.5 21.4 %collective-permute-start.2 = (bf16[256,1024]{1,0:T(8,128)(2,1)}, bf16[256,1024]{1,0:T(8,128)(2,1)}, u32[]{:S(2)}, u32[]{:S(2)}) collective-permute-start(bf16[256,1024]{1,0:T(8,128)(2,1)} %get-tuple-element.60), channel_id=1, source_target_pairs={{0,4},{1,5},{2,6},{3,7},{4,8},{5,9},{6,10},{7,11},{8,12},{9,13},{1... | collective-permute-start | bytes 1572872 | tf_op jit(solution)/shard_map/ppermute | solution.py:50
  17.2 18.5 %collective-permute-start.1 = (bf16[256,1024]{1,0:T(8,128)(2,1)}, bf16[256,1024]{1,0:T(8,128)(2,1)}, u32[]{:S(2)}, u32[]{:S(2)}) collective-permute-start(bf16[256,1024]{1,0:T(8,128)(2,1)} %get-tuple-element.60), channel_id=1, source_target_pairs={{0,12},{1,13},{2,14},{3,15},{4,0},{5,1},{6,2},{7,3},{8,4},{9,5},{1... | collective-permute-start | bytes 1572872 | tf_op jit(solution)/shard_map/ppermute | solution.py:50
  19.3 33.8 %collective-permute-start = (bf16[256,1024]{1,0:T(8,128)(2,1)}, bf16[256,1024]{1,0:T(8,128)(2,1)}, u32[]{:S(2)}, u32[]{:S(2)}) collective-permute-start(bf16[256,1024]{1,0:T(8,128)(2,1)} %get-tuple-element.59), channel_id=1, source_target_pairs={{0,2},{1,3},{2,0},{3,1},{4,6},{5,7},{6,4},{7,5},{8,10},{9,11},{10,... | collective-permute-start | bytes 1572872 | tf_op jit(solution)/shard_map/ppermute | solution.py:46
  20.6 2.4 collective-permute-start.18
  23.8 1.1 copy-start.18
  33.8 18.0 %collective-permute-start.29 = (bf16[1,256,1024]{2,1,0:T(8,128)(2,1)}, bf16[1,256,1024]{2,1,0:T(8,128)(2,1)}, u32[]{:S(2)}, u32[]{:S(2)}) collective-permute-start(bf16[1,256,1024]{2,1,0:T(8,128)(2,1)} %get-tuple-element.41), channel_id=1, source_target_pairs={{0,12},{1,13},{2,14},{3,15},{4,0},{5,1},{6,2},{7,3},{8,4},{9,5},{1... | collective-permute-start | bytes 1572872 | tf_op jit(solution)/shard_map/ppermute | solution.py:50
  36.7 16.5 %collective-permute-start.4 = (bf16[128,1024]{1,0:T(8,128)(2,1)S(1)}, bf16[128,1024]{1,0:T(8,128)(2,1)S(1)}, u32[]{:S(2)}, u32[]{:S(2)}) collective-permute-start(bf16[128,1024]{1,0:T(8,128)(2,1)S(1)} %slice.112), channel_id=1, source_target_pairs={{0,12},{1,13},{2,14},{3,15},{4,0},{5,1},{6,2},{7,3},{8,4},{9,5},{1... | collective-permute-start | bytes 786440 | tf_op jit(solution)/shard_map/ppermute | solution.py:50
  37.9 46.6 %collective-permute-start.20 = (bf16[3,256,1024]{2,1,0:T(8,128)(2,1)S(1)}, bf16[3,256,1024]{2,1,0:T(8,128)(2,1)S(1)}, u32[]{:S(2)}, u32[]{:S(2)}) collective-permute-start(bf16[3,256,1024]{2,1,0:T(8,128)(2,1)S(1)} %get-tuple-element.34), channel_id=1, source_target_pairs={{0,2},{1,3},{2,0},{3,1},{4,6},{5,7},{6,4},{7,5},{8,10},{9,11},{10,... | collective-permute-start | bytes 4718600 | tf_op jit(solution)/shard_map/ppermute | solution.py:46
  38.2 17.7 %collective-permute-start.25 = (bf16[1,256,1024]{2,1,0:T(8,128)(2,1)}, bf16[1,256,1024]{2,1,0:T(8,128)(2,1)S(1)}, u32[]{:S(2)}, u32[]{:S(2)}) collective-permute-start(bf16[1,256,1024]{2,1,0:T(8,128)(2,1)} %copy-done.22), channel_id=1, source_target_pairs={{0,4},{1,5},{2,6},{3,7},{4,8},{5,9},{6,10},{7,11},{8,12},{9,13},{1... | collective-permute-start | bytes 1572872 | tf_op jit(solution)/shard_map/ppermute | solution.py:50
  51.7 7.6 %copy-start.25 = (bf16[1,256,1024]{2,1,0:T(8,128)(2,1)S(1)}, bf16[1,256,1024]{2,1,0:T(8,128)(2,1)}, u32[]{:S(2)}) copy-start(bf16[1,256,1024]{2,1,0:T(8,128)(2,1)} %get-tuple-element.61) | copy-start | bytes 1572868
  51.7 7.5 %collective-permute-start.3 = (bf16[128,1024]{1,0:T(8,128)(2,1)S(1)}, bf16[128,1024]{1,0:T(8,128)(2,1)S(1)}, u32[]{:S(2)}, u32[]{:S(2)}) collective-permute-start(bf16[128,1024]{1,0:T(8,128)(2,1)S(1)} %slice.111), channel_id=1, source_target_pairs={{0,4},{1,5},{2,6},{3,7},{4,8},{5,9},{6,10},{7,11},{8,12},{9,13},{1... | collective-permute-start | bytes 786440 | tf_op jit(solution)/shard_map/ppermute | solution.py:50
  53.1 17.4 %collective-permute-start.28 = (bf16[1,256,1024]{2,1,0:T(8,128)(2,1)S(1)}, bf16[1,256,1024]{2,1,0:T(8,128)(2,1)S(1)}, u32[]{:S(2)}, u32[]{:S(2)}) collective-permute-start(bf16[1,256,1024]{2,1,0:T(8,128)(2,1)S(1)} %get-tuple-element.39), channel_id=1, source_target_pairs={{0,4},{1,5},{2,6},{3,7},{4,8},{5,9},{6,10},{7,11},{8,12},{9,13},{1... | collective-permute-start | bytes 1572872 | tf_op jit(solution)/shard_map/ppermute | solution.py:50
  53.2 17.3 %collective-permute-start.27 = (bf16[1,256,1024]{2,1,0:T(8,128)(2,1)S(1)}, bf16[1,256,1024]{2,1,0:T(8,128)(2,1)S(1)}, u32[]{:S(2)}, u32[]{:S(2)}) collective-permute-start(bf16[1,256,1024]{2,1,0:T(8,128)(2,1)S(1)} %get-tuple-element.38), channel_id=1, source_target_pairs={{0,12},{1,13},{2,14},{3,15},{4,0},{5,1},{6,2},{7,3},{8,4},{9,5},{1... | collective-permute-start | bytes 1572872 | tf_op jit(solution)/shard_map/ppermute | solution.py:50
  55.9 20.8 %collective-permute-start.30 = (bf16[1,256,1024]{2,1,0:T(8,128)(2,1)S(1)}, bf16[1,256,1024]{2,1,0:T(8,128)(2,1)S(1)}, u32[]{:S(2)}, u32[]{:S(2)}) collective-permute-start(bf16[1,256,1024]{2,1,0:T(8,128)(2,1)S(1)} %add_convert_fusion.1), channel_id=1, source_target_pairs={{0,12},{1,13},{2,14},{3,15},{4,0},{5,1},{6,2},{7,3},{8,4},{9,5},{1... | collective-permute-start | bytes 1572872 | tf_op jit(solution)/shard_map/ppermute | solution.py:50
  57.3 4.2 %copy-start.26 = (bf16[1,256,1024]{2,1,0:T(8,128)(2,1)S(1)}, bf16[1,256,1024]{2,1,0:T(8,128)(2,1)}, u32[]{:S(2)}) copy-start(bf16[1,256,1024]{2,1,0:T(8,128)(2,1)} %get-tuple-element.58) | copy-start | bytes 1572868
  59.3 22.5 %collective-permute-start.26 = (bf16[1,256,1024]{2,1,0:T(8,128)(2,1)S(1)}, bf16[1,256,1024]{2,1,0:T(8,128)(2,1)S(1)}, u32[]{:S(2)}, u32[]{:S(2)}) collective-permute-start(bf16[1,256,1024]{2,1,0:T(8,128)(2,1)S(1)} %add_convert_fusion.3), channel_id=1, source_target_pairs={{0,4},{1,5},{2,6},{3,7},{4,8},{5,9},{6,10},{7,11},{8,12},{9,13},{1... | collective-permute-start | bytes 1572872 | tf_op jit(solution)/shard_map/ppermute | solution.py:50
  61.5 15.3 %copy-start.21 = (bf16[1,256,1024]{2,1,0:T(8,128)(2,1)S(1)}, bf16[1,256,1024]{2,1,0:T(8,128)(2,1)}, u32[]{:S(2)}) copy-start(bf16[1,256,1024]{2,1,0:T(8,128)(2,1)} %copy-done.20) | copy-start | bytes 1572868
  70.5 126.4 %collective-permute-start.5 = (bf16[2,256,1024]{2,1,0:T(8,128)(2,1)}, bf16[2,256,1024]{2,1,0:T(8,128)(2,1)}, u32[]{:S(2)}, u32[]{:S(2)}) collective-permute-start(bf16[2,256,1024]{2,1,0:T(8,128)(2,1)} %pad_maximum_fusion.1.rest_0_), channel_id=1, source_target_pairs={{0,4},{1,5},{2,6},{3,7},{4,8},{5,9},{6,10},{7,11},{8,12},{9,13},{1... | collective-permute-start | bytes 3145736 | tf_op jit(solution)/shard_map/ppermute | solution.py:50
  70.5 130.5 %collective-permute-start.9 = (bf16[4,256,1024]{2,1,0:T(8,128)(2,1)}, bf16[4,256,1024]{2,1,0:T(8,128)(2,1)}, u32[]{:S(2)}, u32[]{:S(2)}) collective-permute-start(bf16[4,256,1024]{2,1,0:T(8,128)(2,1)} %pad_maximum_fusion.rest_1_), channel_id=1, source_target_pairs={{0,2},{1,3},{2,0},{3,1},{4,6},{5,7},{6,4},{7,5},{8,10},{9,11},{10,... | collective-permute-start | bytes 6291464 | tf_op jit(solution)/shard_map/ppermute | solution.py:46
  76.7 49.7 %collective-permute-start.19 = (bf16[1,256,1024]{2,1,0:T(8,128)(2,1)S(1)}, bf16[1,256,1024]{2,1,0:T(8,128)(2,1)S(1)}, u32[]{:S(2)}, u32[]{:S(2)}) collective-permute-start(bf16[1,256,1024]{2,1,0:T(8,128)(2,1)S(1)} %copy-done.21), channel_id=1, source_target_pairs={{0,2},{1,3},{2,0},{3,1},{4,6},{5,7},{6,4},{7,5},{8,10},{9,11},{10,... | collective-permute-start | bytes 1572872 | tf_op jit(solution)/shard_map/ppermute | solution.py:46
  81.8 2.7 copy-start.24
  83.2 54.4 %collective-permute-start.31 = (bf16[256,1024]{1,0:T(8,128)(2,1)S(1)}, bf16[256,1024]{1,0:T(8,128)(2,1)S(1)}, u32[]{:S(2)}, u32[]{:S(2)}) collective-permute-start(bf16[256,1024]{1,0:T(8,128)(2,1)S(1)} %get-tuple-element.56), channel_id=1, source_target_pairs={{0,2},{1,3},{2,0},{3,1},{4,6},{5,7},{6,4},{7,5},{8,10},{9,11},{10,... | collective-permute-start | bytes 1572872 | tf_op jit(solution)/shard_map/ppermute | solution.py:46
  85.1 24.7 %collective-permute-start.21 = (bf16[128,1024]{1,0:T(8,128)(2,1)S(1)}, bf16[128,1024]{1,0:T(8,128)(2,1)S(1)}, u32[]{:S(2)}, u32[]{:S(2)}) collective-permute-start(bf16[128,1024]{1,0:T(8,128)(2,1)S(1)} %get-tuple-element.63), channel_id=1, source_target_pairs={{0,4},{1,5},{2,6},{3,7},{4,8},{5,9},{6,10},{7,11},{8,12},{9,13},{1... | collective-permute-start | bytes 786440 | tf_op jit(solution)/shard_map/ppermute | solution.py:50
  85.2 53.8 %copy-start.30 = (bf16[8192]{0:T(1024)(128)(2,1)S(1)}, bf16[8192]{0:T(1024)(128)(2,1)}, u32[]{:S(2)}) copy-start(bf16[8192]{0:T(1024)(128)(2,1)} %param.14) | copy-start | bytes 49156
  109.9 18.0 %collective-permute-start.23 = (bf16[128,1024]{1,0:T(8,128)(2,1)S(1)}, bf16[128,1024]{1,0:T(8,128)(2,1)S(1)}, u32[]{:S(2)}, u32[]{:S(2)}) collective-permute-start(bf16[128,1024]{1,0:T(8,128)(2,1)S(1)} %get-tuple-element.62), channel_id=1, source_target_pairs={{0,12},{1,13},{2,14},{3,15},{4,0},{5,1},{6,2},{7,3},{8,4},{9,5},{1... | collective-permute-start | bytes 786440 | tf_op jit(solution)/shard_map/ppermute | solution.py:50
  127.2 73.9 %collective-permute-start.6 = (bf16[2,256,1024]{2,1,0:T(8,128)(2,1)}, bf16[2,256,1024]{2,1,0:T(8,128)(2,1)}, u32[]{:S(2)}, u32[]{:S(2)}) collective-permute-start(bf16[2,256,1024]{2,1,0:T(8,128)(2,1)} %pad_maximum_fusion.1.rest_0_), channel_id=1, source_target_pairs={{0,12},{1,13},{2,14},{3,15},{4,0},{5,1},{6,2},{7,3},{8,4},{9,5},{1... | collective-permute-start | bytes 3145736 | tf_op jit(solution)/shard_map/ppermute | solution.py:50
  127.8 11.5 %collective-permute-start.22 = (bf16[256,1024]{1,0:T(8,128)(2,1)}, bf16[256,1024]{1,0:T(8,128)(2,1)}, u32[]{:S(2)}, u32[]{:S(2)}) collective-permute-start(bf16[256,1024]{1,0:T(8,128)(2,1)} %pad_maximum_fusion.2), channel_id=1, source_target_pairs={{0,4},{1,5},{2,6},{3,7},{4,8},{5,9},{6,10},{7,11},{8,12},{9,13},{1... | collective-permute-start | bytes 1572872 | tf_op jit(solution)/shard_map/ppermute | solution.py:50
  138.4 20.7 %collective-permute-start.24 = (bf16[256,1024]{1,0:T(8,128)(2,1)}, bf16[256,1024]{1,0:T(8,128)(2,1)}, u32[]{:S(2)}, u32[]{:S(2)}) collective-permute-start(bf16[256,1024]{1,0:T(8,128)(2,1)} %pad_maximum_fusion.3), channel_id=1, source_target_pairs={{0,12},{1,13},{2,14},{3,15},{4,0},{5,1},{6,2},{7,3},{8,4},{9,5},{1... | collective-permute-start | bytes 1572872 | tf_op jit(solution)/shard_map/ppermute | solution.py:50
  139.3 45.4 %copy-start.4 = (f32[1,512,1024]{2,1,0:T(8,128)S(1)}, f32[1,512,1024]{2,1,0:T(8,128)}, u32[]{:S(2)}) copy-start(f32[1,512,1024]{2,1,0:T(8,128)} %m_ref.1) | copy-start | bytes 6291460
  139.3 79.4 %collective-permute-start.10 = (bf16[2,256,1024]{2,1,0:T(8,128)(2,1)}, bf16[2,256,1024]{2,1,0:T(8,128)(2,1)}, u32[]{:S(2)}, u32[]{:S(2)}) collective-permute-start(bf16[2,256,1024]{2,1,0:T(8,128)(2,1)} %pad_maximum_fusion.1.rest_0_), channel_id=1, source_target_pairs={{0,1},{1,0},{2,3},{3,2},{4,5},{5,4},{6,7},{7,6},{8,9},{9,8},{10,11... | collective-permute-start | bytes 3145736 | tf_op jit(solution)/shard_map/ppermute | solution.py:42
  165.0 1.3 copy-start.6
  166.4 8.2 %collective-permute-start.32 = (f32[8,128]{1,0:T(8,128)S(1)}, f32[8,128]{1,0:T(8,128)S(1)}, u32[]{:S(2)}, u32[]{:S(2)}) collective-permute-start(f32[8,128]{1,0:T(8,128)S(1)} %get-tuple-element.42), channel_id=1, source_target_pairs={{0,1},{1,0},{2,3},{3,2},{4,5},{5,4},{6,7},{7,6},{8,9},{9,8},{10,11... | collective-permute-start | bytes 12296 | tf_op jit(solution)/shard_map/ppermute | solution.py:42
  174.6 2.5 collective-permute-start.33
  177.0 3.7 %collective-permute-start.34 = (f32[8,128]{1,0:T(8,128)S(1)}, f32[8,128]{1,0:T(8,128)S(1)}, u32[]{:S(2)}, u32[]{:S(2)}) collective-permute-start(f32[8,128]{1,0:T(8,128)S(1)} %add.346), channel_id=1, source_target_pairs={{0,4},{1,5},{2,6},{3,7},{4,8},{5,9},{6,10},{7,11},{8,12},{9,13},{1... | collective-permute-start | bytes 12296 | tf_op jit(solution)/shard_map/ppermute | solution.py:50
  180.7 4.0 %collective-permute-start.35 = (f32[8,128]{1,0:T(8,128)S(1)}, f32[8,128]{1,0:T(8,128)S(1)}, u32[]{:S(2)}, u32[]{:S(2)}) collective-permute-start(f32[8,128]{1,0:T(8,128)S(1)} %add.347), channel_id=1, source_target_pairs={{0,8},{1,9},{2,10},{3,11},{4,12},{5,13},{6,14},{7,15},{8,0},{9,1},... | collective-permute-start | bytes 12296 | tf_op jit(solution)/shard_map/ppermute | solution.py:50
  184.7 1.6 copy-start.5
  186.3 1.6 copy-start.7
  194.2 32.0 %copy-start.28 = (f32[512,128]{1,0:T(8,128)S(1)}, f32[512,128]{1,0:T(8,128)}, u32[]{:S(2)}) copy-start(f32[512,128]{1,0:T(8,128)} %param.18) | copy-start | bytes 786436
  194.2 32.0 %copy-start.29 = (f32[512,128]{1,0:T(8,128)S(1)}, f32[512,128]{1,0:T(8,128)}, u32[]{:S(2)}) copy-start(f32[512,128]{1,0:T(8,128)} %param.19) | copy-start | bytes 786436
  194.2 7.3 %collective-permute-start.38 = (bf16[2,512,128]{2,1,0:T(8,128)(2,1)S(1)}, bf16[2,512,128]{2,1,0:T(8,128)(2,1)S(1)}, u32[]{:S(2)}, u32[]{:S(2)}) collective-permute-start(bf16[2,512,128]{2,1,0:T(8,128)(2,1)S(1)} %get-tuple-element.49), channel_id=1, source_target_pairs={{0,96},{16,112},{32,0},{48,16},{64,32},{80,48},{96,64},{112,80},{1... | collective-permute-start | bytes 786440 | tf_op jit(solution)/shard_map/ppermute | solution.py:58
  196.9 49.9 %collective-permute-start.11 = (bf16[4,256,1024]{2,1,0:T(8,128)(2,1)}, bf16[4,256,1024]{2,1,0:T(8,128)(2,1)S(1)}, u32[]{:S(2)}, u32[]{:S(2)}) collective-permute-start(bf16[4,256,1024]{2,1,0:T(8,128)(2,1)} %pad_maximum_fusion.rest_1_), channel_id=1, source_target_pairs={{0,1},{1,0},{2,3},{3,2},{4,5},{5,4},{6,7},{7,6},{8,9},{9,8},{10,11... | collective-permute-start | bytes 6291464 | tf_op jit(solution)/shard_map/ppermute | solution.py:42
  201.0 45.9 %collective-permute-start.16 = (bf16[4,256,1024]{2,1,0:T(8,128)(2,1)}, bf16[4,256,1024]{2,1,0:T(8,128)(2,1)}, u32[]{:S(2)}, u32[]{:S(2)}) collective-permute-start(bf16[4,256,1024]{2,1,0:T(8,128)(2,1)} %collective-permute-done.9.rest_6_), channel_id=1, source_target_pairs={{0,1},{1,0},{2,3},{3,2},{4,5},{5,4},{6,7},{7,6},{8,9},{9,8},{10,11... | collective-permute-start | bytes 6291464 | tf_op jit(solution)/shard_map/ppermute | solution.py:42
  201.1 9.0 %collective-permute-start.37 = (bf16[2,512,128]{2,1,0:T(8,128)(2,1)S(1)}, bf16[2,512,128]{2,1,0:T(8,128)(2,1)S(1)}, u32[]{:S(2)}, u32[]{:S(2)}) collective-permute-start(bf16[2,512,128]{2,1,0:T(8,128)(2,1)S(1)} %get-tuple-element.48), channel_id=1, source_target_pairs={{0,64},{16,80},{32,96},{48,112},{64,0},{80,16},{96,32},{112,48},{1... | collective-permute-start | bytes 786440 | tf_op jit(solution)/shard_map/ppermute | solution.py:58
  201.5 12.0 %collective-permute-start.36 = (bf16[2,512,128]{2,1,0:T(8,128)(2,1)S(1)}, bf16[2,512,128]{2,1,0:T(8,128)(2,1)S(1)}, u32[]{:S(2)}, u32[]{:S(2)}) collective-permute-start(bf16[2,512,128]{2,1,0:T(8,128)(2,1)S(1)} %get-tuple-element.47), channel_id=1, source_target_pairs={{0,32},{16,48},{32,64},{48,80},{64,96},{80,112},{96,0},{112,16},{1... | collective-permute-start | bytes 786440 | tf_op jit(solution)/shard_map/ppermute | solution.py:58
  210.1 12.5 %collective-permute-start.7 = (bf16[1,256,1024]{2,1,0:T(8,128)(2,1)S(1)}, bf16[1,256,1024]{2,1,0:T(8,128)(2,1)S(1)}, u32[]{:S(2)}, u32[]{:S(2)}) collective-permute-start(bf16[1,256,1024]{2,1,0:T(8,128)(2,1)S(1)} %slice.113), channel_id=1, source_target_pairs={{0,4},{1,5},{2,6},{3,7},{4,8},{5,9},{6,10},{7,11},{8,12},{9,13},{1... | collective-permute-start | bytes 1572872 | tf_op jit(solution)/shard_map/ppermute | solution.py:50
  213.5 21.8 %collective-permute-start.12 = (bf16[2,256,1024]{2,1,0:T(8,128)(2,1)}, bf16[2,256,1024]{2,1,0:T(8,128)(2,1)}, u32[]{:S(2)}, u32[]{:S(2)}) collective-permute-start(bf16[2,256,1024]{2,1,0:T(8,128)(2,1)} %collective-permute-done.5.rest_2_), channel_id=1, source_target_pairs={{0,1},{1,0},{2,3},{3,2},{4,5},{5,4},{6,7},{7,6},{8,9},{9,8},{10,11... | collective-permute-start | bytes 3145736 | tf_op jit(solution)/shard_map/ppermute | solution.py:42
  218.7 6.7 %collective-permute-start.39 = (bf16[512,128]{1,0:T(8,128)(2,1)S(1)}, bf16[512,128]{1,0:T(8,128)(2,1)S(1)}, u32[]{:S(2)}, u32[]{:S(2)}) collective-permute-start(bf16[512,128]{1,0:T(8,128)(2,1)S(1)} %fusion.7), channel_id=1, source_target_pairs={{0,16},{16,0},{32,48},{48,32},{64,80},{80,64},{96,112},{112,96},{1... | collective-permute-start | bytes 393224 | tf_op jit(solution)/shard_map/ppermute | solution.py:54
  222.6 23.6 %copy-start.27 = (bf16[1,256,1024]{2,1,0:T(8,128)(2,1)}, bf16[1,256,1024]{2,1,0:T(8,128)(2,1)S(1)}, u32[]{:S(2)}) copy-start(bf16[1,256,1024]{2,1,0:T(8,128)(2,1)S(1)} %collective-permute-done.7.rest_4_) | copy-start | bytes 1572868
  222.6 10.5 %collective-permute-start.8 = (bf16[1,256,1024]{2,1,0:T(8,128)(2,1)S(1)}, bf16[1,256,1024]{2,1,0:T(8,128)(2,1)}, u32[]{:S(2)}, u32[]{:S(2)}) collective-permute-start(bf16[1,256,1024]{2,1,0:T(8,128)(2,1)S(1)} %slice.114), channel_id=1, source_target_pairs={{0,12},{1,13},{2,14},{3,15},{4,0},{5,1},{6,2},{7,3},{8,4},{9,5},{1... | collective-permute-start | bytes 1572872 | tf_op jit(solution)/shard_map/ppermute | solution.py:50
  225.5 19.4 %collective-permute-start.13 = (bf16[2,256,1024]{2,1,0:T(8,128)(2,1)}, bf16[2,256,1024]{2,1,0:T(8,128)(2,1)}, u32[]{:S(2)}, u32[]{:S(2)}) collective-permute-start(bf16[2,256,1024]{2,1,0:T(8,128)(2,1)} %collective-permute-done.6.rest_3_), channel_id=1, source_target_pairs={{0,1},{1,0},{2,3},{3,2},{4,5},{5,4},{6,7},{7,6},{8,9},{9,8},{10,11... | collective-permute-start | bytes 3145736 | tf_op jit(solution)/shard_map/ppermute | solution.py:42
  233.1 6.4 %collective-permute-start.40 = (bf16[512,128]{1,0:T(8,128)(2,1)S(1)}, bf16[512,128]{1,0:T(8,128)(2,1)S(1)}, u32[]{:S(2)}, u32[]{:S(2)}) collective-permute-start(bf16[512,128]{1,0:T(8,128)(2,1)S(1)} %get-tuple-element.50), channel_id=1, source_target_pairs={{0,16},{16,0},{32,48},{48,32},{64,80},{80,64},{96,112},{112,96},{1... | collective-permute-start | bytes 393224 | tf_op jit(solution)/shard_map/ppermute | solution.py:54
  235.2 11.0 %collective-permute-start.14 = (bf16[1,256,1024]{2,1,0:T(8,128)(2,1)S(1)}, bf16[1,256,1024]{2,1,0:T(8,128)(2,1)}, u32[]{:S(2)}, u32[]{:S(2)}) collective-permute-start(bf16[1,256,1024]{2,1,0:T(8,128)(2,1)S(1)} %collective-permute-done.7.rest_4_), channel_id=1, source_target_pairs={{0,1},{1,0},{2,3},{3,2},{4,5},{5,4},{6,7},{7,6},{8,9},{9,8},{10,11... | collective-permute-start | bytes 1572872 | tf_op jit(solution)/shard_map/ppermute | solution.py:42
  239.5 6.7 %collective-permute-start.15 = (bf16[1,256,1024]{2,1,0:T(8,128)(2,1)}, bf16[1,256,1024]{2,1,0:T(8,128)(2,1)}, u32[]{:S(2)}, u32[]{:S(2)}) collective-permute-start(bf16[1,256,1024]{2,1,0:T(8,128)(2,1)} %collective-permute-done.8.rest_5_), channel_id=1, source_target_pairs={{0,1},{1,0},{2,3},{3,2},{4,5},{5,4},{6,7},{7,6},{8,9},{9,8},{10,11... | collective-permute-start | bytes 1572872 | tf_op jit(solution)/shard_map/ppermute | solution.py:42
  244.9 48.0 %collective-permute-start.41 = (bf16[2,512,128]{2,1,0:T(8,128)(2,1)S(1)}, bf16[2,512,128]{2,1,0:T(8,128)(2,1)S(1)}, u32[]{:S(2)}, u32[]{:S(2)}) collective-permute-start(bf16[2,512,128]{2,1,0:T(8,128)(2,1)S(1)} %pad_maximum_fusion.4.refs_0_), channel_id=1, source_target_pairs={{0,96},{16,112},{32,0},{48,16},{64,32},{80,48},{96,64},{112,80},{1... | collective-permute-start | bytes 786440 | tf_op jit(solution)/shard_map/ppermute | solution.py:58
  246.2 46.6 %collective-permute-start.42 = (bf16[2,512,128]{2,1,0:T(8,128)(2,1)S(1)}, bf16[2,512,128]{2,1,0:T(8,128)(2,1)S(1)}, u32[]{:S(2)}, u32[]{:S(2)}) collective-permute-start(bf16[2,512,128]{2,1,0:T(8,128)(2,1)S(1)} %pad_maximum_fusion.4.refs_0_), channel_id=1, source_target_pairs={{0,64},{16,80},{32,96},{48,112},{64,0},{80,16},{96,32},{112,48},{1... | collective-permute-start | bytes 786440 | tf_op jit(solution)/shard_map/ppermute | solution.py:58
  246.2 46.6 %collective-permute-start.43 = (bf16[2,512,128]{2,1,0:T(8,128)(2,1)S(1)}, bf16[2,512,128]{2,1,0:T(8,128)(2,1)S(1)}, u32[]{:S(2)}, u32[]{:S(2)}) collective-permute-start(bf16[2,512,128]{2,1,0:T(8,128)(2,1)S(1)} %pad_maximum_fusion.4.refs_0_), channel_id=1, source_target_pairs={{0,32},{16,48},{32,64},{48,80},{64,96},{80,112},{96,0},{112,16},{1... | collective-permute-start | bytes 786440 | tf_op jit(solution)/shard_map/ppermute | solution.py:58
  246.9 1.3 copy-start.23
  (11 other events, 10.0 us)

commit v2 on v1

v2 whole, which is shorter than its diff:
```python
import functools

import jax
import jax.numpy as jnp
from jax import lax
from jax.experimental import pallas as pl
from jax.experimental.pallas import tpu as pltpu
from jax.sharding import PartitionSpec as P

norm_eps = 1e-05
adam_eps = 1e-08
inner_rate = 0.01
first_decay = 0.9
second_decay = 0.95
clip_limit = 1.0
outer_beta = 0.9
outer_rate = 0.7
replay_weight = 0.5

F32 = jnp.float32
BF16 = jnp.bfloat16
MIB = 1024 * 1024


def sds(shape, dtype):
    return jax.ShapeDtypeStruct(shape, dtype)


def cost(flops, size):
    return pl.CostEstimate(flops=int(flops), bytes_accessed=int(size), transcendentals=0)


def params(mib):
    return pltpu.CompilerParams(vmem_limit_bytes=mib * MIB)


def clip_index(t, start, count):
    return jnp.clip(t - start, 0, count - 1)


def over_core(value):
    return lax.ppermute(value, "fsdp", [(i, i ^ 1) for i in range(16)])


def over_x(value):
    return lax.ppermute(value, "fsdp", [(i, i ^ 2) for i in range(16)])


def over_z(value, step):
    return lax.ppermute(value, "fsdp", [(i, (i + 4 * step) % 16) for i in range(16)])


def over_x_hi(value):
    return lax.ppermute(value, "rep", [(i, i ^ 1) for i in range(8)])


def over_y(value, step):
    return lax.ppermute(value, "rep", [(i, (i + 2 * step) % 8) for i in range(8)])


def lane_sum(value):
    total = value[:, 0:128]
    for at in range(128, value.shape[1], 128):
        total = total + value[:, at : at + 128]
    return total


def prep_kernel(core_ref, index_ref, h_ref, b_ref, cot_ref, xk_ref, xs_ref, cp_ref, inv_ref, total_ref):
    step = pl.program_id(0)
    core = core_ref[0]
    rows = lax.broadcasted_iota(jnp.int32, (128, 64), 0)
    pick = jnp.where(rows == index_ref[...], 1.0, 0.0).astype(BF16)
    squares = jnp.zeros((320, 128), F32)
    for j in range(2):
        for flip, x_ref in ((0, xk_ref), (1, xs_ref)):
            columns = pl.ds(pl.multiple_of(1024 * j + 512 * (core ^ flip), 512), 512)
            replayed = lax.dot_general(pick, b_ref[:, columns], (((0,), (0,)), ((), ())), preferred_element_type=F32)
            fresh = h_ref[:, columns]
            x_ref[j, 0:256, :] = fresh
            x_ref[j, 256:320, :] = replayed.astype(BF16)
            fresh = fresh.astype(F32)
            squares = squares + jnp.concatenate([lane_sum(fresh * fresh), lane_sum(replayed * replayed)], axis=0)

    @pl.when(step == 0)
    def _():
        total_ref[...] = squares

    @pl.when(step > 0)
    def _():
        total_ref[...] += squares

    @pl.when(step == 3)
    def _():
        mean = jnp.sum(total_ref[...], axis=1, keepdims=True) / 8192.0
        inv = lax.rsqrt(mean + norm_eps)
        inv_ref[...] = jnp.broadcast_to(inv, (320, 128))
        at = lax.broadcasted_iota(jnp.int32, (320, 1), 0)
        scale = inv * jnp.where(at < 256, 1.0, replay_weight)
        cp_ref[...] = (cot_ref[...].astype(F32) * scale).astype(BF16)


def prep(core, hidden, replay_buffer, replay_index, cotangent):
    return pl.pallas_call(
        prep_kernel,
        grid_spec=pltpu.PrefetchScalarGridSpec(
            num_scalar_prefetch=1,
            grid=(4,),
            in_specs=[
                pl.BlockSpec((1, 64), lambda t, c: (0, 0)),
                pl.BlockSpec((None, 256, 2048), lambda t, c: (0, 0, t)),
                pl.BlockSpec((None, 128, 2048), lambda t, c: (0, 0, t)),
                pl.BlockSpec((None, 320, 1024), lambda t, c: (0, 0, 0)),
            ],
            out_specs=[
                pl.BlockSpec((2, 320, 512), lambda t, c: (t, 0, 0)),
                pl.BlockSpec((2, 320, 512), lambda t, c: (t, 0, 0)),
                pl.BlockSpec((320, 1024), lambda t, c: (0, 0)),
                pl.BlockSpec((320, 128), lambda t, c: (0, 0)),
            ],
            scratch_shapes=[pltpu.VMEM((320, 128), F32)],
        ),
        out_shape=[
            sds((8, 320, 512), BF16),
            sds((8, 320, 512), BF16),
            sds((320, 1024), BF16),
            sds((320, 128), F32),
        ],
        compiler_params=params(60),
        cost_estimate=cost(2e9, 12e6),
        name="prep",
    )(core, replay_index, hidden, replay_buffer, cotangent)


x_first = 448
z_first = 1024 - x_first


def grad_kernel(plan, table_ref, xk_ref, xs_ref, c_ref, cs_ref, *rest):
    outs, (x_all, c_all) = rest[:-2], rest[-2:]
    step = pl.program_id(0)
    x = table_ref[4]

    @pl.when(step == 0)
    def _():
        c_all[:, 0:320] = c_ref[...].T
        c_all[:, 320:640] = cs_ref[...].T

    for dx in range(2):
        x_all[0:320, 512 * dx : 512 * dx + 512] = xk_ref[x ^ dx]
        x_all[320:640, 512 * dx : 512 * dx + 512] = xs_ref[x ^ dx]
    for at in range(max(start + count for _, _, start, count in plan)):

        @pl.when(step == at)
        def _(at=at):
            for low in range(2):
                rows = c_all[0:x_first, :] if low else c_all[x_first:1024, :]
                part = jnp.dot(rows, x_all[...], preferred_element_type=F32).astype(BF16)
                for out_ref, (out_low, dx, start, count) in zip(outs, plan):
                    if out_low == low and start <= at < start + count:
                        out_ref[...] = part[:, 512 * dx : 512 * dx + 512]


def grad_blocks(place, chunks, outputs, xk, xs, c, cs, name):
    z, x = place
    table = jnp.stack([(z + dz) % 4 for dz in chunks] + [jnp.int32(0)] * (4 - len(chunks)) + [x])
    x_spec = pl.BlockSpec((2, 320, 512), lambda t, tab: (tab[t], 0, 0))
    c_spec = pl.BlockSpec((320, 1024), lambda t, tab: (0, 0))
    return pl.pallas_call(
        functools.partial(grad_kernel, outputs),
        grid_spec=pltpu.PrefetchScalarGridSpec(
            num_scalar_prefetch=1,
            grid=(len(chunks),),
            in_specs=[x_spec, x_spec, c_spec, c_spec],
            out_specs=[
                pl.BlockSpec(
                    (None, x_first if low else z_first, 512), lambda t, tab, s=s, n=n: (clip_index(t, s, n), 0, 0)
                )
                for low, _, s, n in outputs
            ],
            scratch_shapes=[pltpu.VMEM((640, 1024), BF16), pltpu.VMEM((1024, 640), BF16)],
        ),
        out_shape=[sds((n, x_first if low else z_first, 512), BF16) for low, _, _, n in outputs],
        compiler_params=params(60),
        cost_estimate=cost(len(chunks) * 2 * 640 * 1024 * 1024, len(chunks) * 3.4e6),
        name=name,
    )(table, xk, xs, c, cs)


early_rows = 128


def total_kernel(a0, a1, ue, ul, de, dl, b0, b1, gain_ref, w_ref, grad_ref, sq_ref, late_ref):
    step = pl.program_id(0)
    late_ref[...] = w_ref[early_rows:512, :]
    up = jnp.concatenate([ul[...], ue[...]], axis=0).astype(F32)
    down = jnp.concatenate([de[...], dl[...]], axis=0).astype(F32)
    top = (a0[...].astype(F32) + a1[...].astype(F32)) + (up + down)
    low = b0[...].astype(F32) + b1[...].astype(F32)
    both = jnp.concatenate([top, low], axis=0) * gain_ref[...]
    grad_ref[...] = both.T
    square = jnp.sum((both * both).reshape(128, 8, 128), axis=0)

    @pl.when(step == 0)
    def _():
        sq_ref[...] = square

    @pl.when(step > 0)
    def _():
        sq_ref[...] += square


def total(parts, gain_row, weight):
    return pl.pallas_call(
        total_kernel,
        grid=(4,),
        in_specs=[pl.BlockSpec((p.shape[0], 128), lambda t: (0, t)) for p in parts]
        + [pl.BlockSpec((1, 128), lambda t: (0, t)), pl.BlockSpec((None, 512, 256), lambda t: (0, 0, t))],
        out_specs=[
            pl.BlockSpec((128, 1024), lambda t: (t, 0)),
            pl.BlockSpec((8, 128), lambda t: (0, 0)),
            pl.BlockSpec((512 - early_rows, 256), lambda t: (0, t)),
        ],
        out_shape=[sds((512, 1024), F32), sds((8, 128), F32), sds((512 - early_rows, 1024), BF16)],
        compiler_params=params(60),
        cost_estimate=cost(5e6, 5e6),
        name="total",
    )(*parts, gain_row, weight)


def adam_kernel(table_ref, sq_ref, grad_ref, m_ref, v_ref, w_ref, first_ref, second_ref, *rest):
    outs, new_ref = rest[:-1], rest[-1]
    step = pl.program_id(0)
    squares = jnp.sum(sq_ref[...], axis=1, keepdims=True)
    squares = jnp.sum(squares, axis=0, keepdims=True)
    factor = jnp.minimum(1.0, clip_limit / jnp.sqrt(squares))
    clipped = grad_ref[...] * factor
    first = first_decay * m_ref[...] + (1.0 - first_decay) * clipped
    second = second_decay * v_ref[...] + (1.0 - second_decay) * clipped * clipped
    first_ref[...] = first
    second_ref[...] = second
    new = w_ref[...].astype(F32) - inner_rate * first / (jnp.sqrt(second) + adam_eps)
    new_ref[...] = new.astype(BF16)
    for k, out_ref in enumerate(outs):

        @pl.when(step == k)
        def _(out_ref=out_ref):
            for dx in range(2):
                out_ref[dx] = new_ref[:, pl.ds(pl.multiple_of((table_ref[4] ^ dx) * 128, 128), 128)]


def adam(table, sq, grad, first_in, second_in, weight):
    column = pl.BlockSpec((512, 256), lambda t, tab: (0, tab[t]))
    lead = pl.BlockSpec((None, 512, 256), lambda t, tab: (0, 0, tab[t]))
    return pl.pallas_call(
        adam_kernel,
        grid_spec=pltpu.PrefetchScalarGridSpec(
            num_scalar_prefetch=1,
            grid=(4,),
            in_specs=[pl.BlockSpec((8, 128), lambda t, tab: (0, 0)), column, lead, lead, lead],
            out_specs=[lead, lead] + [pl.BlockSpec((2, 512, 128), lambda t, tab: (0, 0, 0)) for k in range(4)],
            scratch_shapes=[pltpu.VMEM((512, 256), BF16)],
        ),
        out_shape=[sds((1, 512, 1024), F32)] * 2 + [sds((2, 512, 128), BF16)] * 4,
        compiler_params=params(60),
        cost_estimate=cost(2e7, 12e6),
        name="adam",
    )(table, sq, grad, first_in, second_in, weight)


def place_kernel(table_ref, *refs):
    step = pl.program_id(0)
    for k, in_ref in enumerate(refs[:-1]):

        @pl.when(step == k)
        def _(in_ref=in_ref):
            for dx in range(2):
                refs[-1][:, pl.ds(pl.multiple_of((table_ref[4] ^ dx) * 128, 128), 128)] = in_ref[dx]


def place_columns(table, parts):
    return pl.pallas_call(
        place_kernel,
        grid_spec=pltpu.PrefetchScalarGridSpec(
            num_scalar_prefetch=1,
            grid=(4,),
            in_specs=[pl.BlockSpec((2, 512, 128), lambda t, tab: (0, 0, 0)) for k in range(4)],
            out_specs=pl.BlockSpec((512, 256), lambda t, tab: (0, tab[t])),
        ),
        out_shape=sds((512, 1024), BF16),
        compiler_params=params(60),
        cost_estimate=cost(1e6, 2e6),
        name="place",
    )(table, *parts)


def input_kernel(core_ref, cp_ref, inv_ref, gain_ref, xk_ref, xs_ref, ek_ref, es_ref, lk_ref, ls_ref, out_ref, q_ref, m_ref):
    step = pl.program_id(0)
    core = core_ref[0]

    @pl.when(step == 0)
    def _():
        m_ref[...] = jnp.zeros_like(m_ref)

    @pl.when(step < 4)
    def _():
        m = m_ref[...]
        for sibling, (x_ref, e_ref, l_ref) in enumerate(((xk_ref, ek_ref, lk_ref), (xs_ref, es_ref, ls_ref))):
            for w_ref, low, high in ((e_ref, 0, early_rows), (l_ref, early_rows, 512)):
                size = high - low
                w = w_ref[...].reshape(2 * size, 1024)
                q = lax.dot_general(cp_ref[...], w, (((1,), (1,)), ((), ())), preferred_element_type=F32)
                for j in range(2):
                    g = 2 * step + j
                    gained = q[:, size * j : size * (j + 1)] * gain_ref[2 * g + (core ^ sibling)][:, low:high]
                    m = m + lane_sum(gained * x_ref[j, :, low:high].astype(F32))
                    q_ref[8 * sibling + g, :, low:high] = gained.astype(BF16)
        m_ref[...] = m

    @pl.when(step >= 4)
    def _():
        inv = inv_ref[:, 0:1]
        factor = jnp.sum(m_ref[...], axis=1, keepdims=True) * (inv * inv) / 8192.0
        for sibling, x_ref in enumerate((xk_ref, xs_ref)):
            for j in range(2):
                value = q_ref[8 * sibling + 2 * (step - 4) + j].astype(F32) - x_ref[j].astype(F32) * factor
                columns = pl.ds(pl.multiple_of(1024 * j + 512 * (core ^ sibling), 512), 512)
                out_ref[:, columns] = value.astype(BF16)


def input_gradient(core, xk, xs, cp, inv, gain, early, late):
    early = early.reshape(8, 2, early_rows, 1024)
    late = late.reshape(8, 2, 512 - early_rows, 1024)

    def weights(rows, flip):
        return pl.BlockSpec((2, None, rows, 1024), lambda t, c: (jnp.minimum(t, 3), c[0] ^ flip, 0, 0))

    x_spec = pl.BlockSpec((2, 320, 512), lambda t, c: (t % 4, 0, 0))
    return pl.pallas_call(
        input_kernel,
        grid_spec=pltpu.PrefetchScalarGridSpec(
            num_scalar_prefetch=1,
            grid=(8,),
            in_specs=[
                pl.BlockSpec((320, 1024), lambda t, c: (0, 0)),
                pl.BlockSpec((320, 128), lambda t, c: (0, 0)),
                pl.BlockSpec((16, 1, 512), lambda t, c: (0, 0, 0)),
                x_spec,
                x_spec,
                weights(early_rows, 0),
                weights(early_rows, 1),
                weights(512 - early_rows, 0),
                weights(512 - early_rows, 1),
            ],
            out_specs=pl.BlockSpec((None, 320, 2048), lambda t, c: (0, 0, jnp.maximum(t - 4, 0))),
            scratch_shapes=[pltpu.VMEM((16, 320, 512), BF16), pltpu.VMEM((320, 128), F32)],
        ),
        out_shape=sds((1, 320, 8192), BF16),
        compiler_params=params(60),
        cost_estimate=cost(6e9, 4e7),
        name="input_gradient",
    )(core, cp, inv, gain, xk, xs, early, early, late, late)


def add(*values):
    total_value = values[0].astype(F32)
    for value in values[1:]:
        total_value = total_value + value.astype(F32)
    return total_value.astype(BF16)


def on_device(
    hidden,
    replay_buffer,
    replay_index,
    cotangent,
    norm_gain,
    value_weight,
    adam_first,
    adam_second,
    anchor,
    outer_momentum,
):
    fsdp = lax.axis_index("fsdp")
    rep = lax.axis_index("rep")
    core, x, z = fsdp % 2, (fsdp // 2) % 2, fsdp // 4
    x_hi, y = rep % 2, rep // 2
    place = (z, x)
    columns = jnp.stack([(y + dy) % 4 for dy in range(4)] + [x_hi])
    gain_float = norm_gain.astype(F32)

    early = lax.all_gather(value_weight[0, :early_rows], "fsdp", axis=0, tiled=True)

    xk, xs, cp, inv = prep(core[None], hidden, replay_buffer, replay_index, cotangent)
    x_sib = over_core(xs)
    c_sib = over_core(cp)

    b_20, b_21, a_21, a_20 = grad_blocks(
        place, [2], [(0, 0, 0, 1), (0, 1, 0, 1), (1, 1, 0, 1), (1, 0, 0, 1)], xk, x_sib, cp, c_sib, "grad_a"
    )
    r_up = over_z(b_20[0], 1)
    r_down = over_z(b_21[0], -1)
    r_a2 = over_x(a_21[0])
    b_10, b_30, b_00, b_11, b_31, b_01, a_send, a_own = grad_blocks(
        place,
        [1, 3, 0],
        [(0, dx, step, 1) for dx in range(2) for step in range(3)] + [(1, 1, 0, 3), (1, 0, 0, 3)],
        xk, x_sib, cp, c_sib, "grad_b",
    )
    r_a = over_x(a_send)
    e_up = over_z(b_11[0], 1)
    e_down = over_z(b_30[0], -1)
    l_up = over_z(add(b_10[0], r_up), 1)
    l_down = over_z(add(b_31[0], r_down), -1)

    half = x_first // 2
    p_up = over_z(add(a_20[0, :half], r_a2[:half]), 1)
    p_down = over_z(add(a_20[0, half:], r_a2[half:]), -1)
    fe_up = over_z(add(a_own[0, half:], r_a[0, half:]), 1)
    fe_down = over_z(add(a_own[1, :half], r_a[1, :half]), -1)
    b_mine = add(b_00[0], l_up, e_down)
    b_theirs = add(b_01[0], e_up, l_down)
    r_b = over_x(b_theirs)
    fl_up = over_z(add(a_own[0, :half], r_a[0, :half], p_up), 1)
    fl_down = over_z(add(a_own[1, half:], r_a[1, half:], p_down), -1)

    gain_row = lax.dynamic_slice(gain_float, (fsdp * 512,), (512,))[None, :]
    grad, squares, late = total(
        [a_own[2], r_a[2], fe_up, fl_up, fe_down, fl_down, b_mine, r_b], gain_row, value_weight
    )
    late = lax.all_gather(late, "fsdp", axis=0, tiled=True)

    squares = squares + over_core(squares)
    squares = squares + over_x(squares)
    squares = squares + over_z(squares, 1) + over_z(squares, 2) + over_z(squares, 3)

    first, second, n_0, n_1, n_2, n_3 = adam(columns, squares, grad, adam_first, adam_second, value_weight)

    input_grad = input_gradient(core[None], xk, xs, cp, inv, gain_float.reshape(16, 1, 512), early, late)

    m_1 = over_y(n_1, 1)
    m_2 = over_y(n_2, 2)
    m_3 = over_y(n_3, 3)
    summed = n_0.astype(F32) + m_1.astype(F32) + m_2.astype(F32) + m_3.astype(F32)
    inner_total = summed[0] + over_x_hi(summed[1].astype(BF16)).astype(F32)
    outer_grad = anchor - inner_total / 8
    new_momentum = outer_beta * outer_momentum + outer_grad
    new_anchor = anchor - outer_rate * (outer_grad + outer_beta * new_momentum)
    sent = new_anchor.astype(BF16)
    sent = jnp.stack([sent, over_x_hi(sent)])
    parts = [sent, over_y(sent, 3), over_y(sent, 2), over_y(sent, 1)]
    synced_weight = place_columns(columns, parts)
    return (input_grad, first, second, synced_weight, new_momentum, new_anchor)


def solution(mesh):
    return jax.shard_map(
        on_device,
        mesh=mesh,
        in_specs=(
            P("rep", "fsdp", None),
            P("rep", "fsdp", None),
            P("rep", "fsdp"),
            P("rep", "fsdp", None),
            P(),
            P("rep", "fsdp", None),
            P("rep", "fsdp", None),
            P("rep", "fsdp", None),
            P("fsdp", "rep"),
            P("fsdp", "rep"),
        ),
        out_specs=(
            P("rep", "fsdp", None),
            P("rep", "fsdp", None),
            P("rep", "fsdp", None),
            P("fsdp", None),
            P("fsdp", "rep"),
            P("fsdp", "rep"),
        ),
        check_vma=False,
    )
```

time: 298 us -> 212 us (0.71)
  starting transfers between devices: 71.9 us -> 43 us
  Pallas kernels: 80.4 us -> 56.6 us
  local copies, waits for them, and re-layouts: 30 us -> 9.26 us
  waiting for transfers between devices: 100 us -> 80.2 us
  between operations: 0.99 us -> 14.3 us
  other arithmetic: 12.7 us -> 7.68 us
    ppermute x10 -> x3, starting transfers between devices: 38.3 us -> 4.18 us  [over_core(): return lax.ppermute(value, 'fsdp', [(i, i ^ 1) for i in range(16)])]
    pallas_call x4, Pallas kernels: 65.8 us -> 37.9 us  [the longest x2 16.7 us: grad_blocks(): pl.pallas_call(functools.partial(grad_kernel, outputs), grid_spec=pltpu.P...]
    ppermute x6 -> x4, waiting for transfers between devices: 23.7 us -> 1 us  [over_x(): return lax.ppermute(value, 'fsdp', [(i, i ^ 2) for i in range(16)])]
    ppermute x20 -> x15, waiting for transfers between devices: 61.6 us -> 39.9 us  [over_z(): lax.ppermute(value, 'fsdp', [(i, (i + 4 * step) % 16) for i in range(16)])]
    unnamed x62 -> x38, local copies, waits for them, and re-layouts: 22.2 us -> 4.05 us
    ppermute x2, waiting for transfers between devices: 2.84 us -> 11.8 us  [over_x_hi(): return lax.ppermute(value, 'rep', [(i, i ^ 1) for i in range(8)])]
    all_gather x0 -> x2, waiting for transfers between devices: none -> 8.41 us  [the longest x1 8.41 us: on_device(): late = lax.all_gather(late, 'fsdp', axis=0, tiled=True)]
    ppermute x6, starting transfers between devices: 5.75 us -> 12.6 us  [over_y(): lax.ppermute(value, 'rep', [(i, (i + 2 * step) % 8) for i in range(8)])]
  transfers between devices with their start and end apart: 44 -> 32, of which waited for: 18 -> 22; matrix products, arithmetic and copies ran while one was open for 7% -> 5% of each run, Pallas kernels for 24% -> 19%
where the time goes in v2:
time: 212 us; the launch traced here: 211 us
  waiting for transfers between devices  80.2 us (38%)
  Pallas kernels  56.6 us (27%)
  starting transfers between devices  43 us (20%)
  between operations  14.3 us (7%)
  local copies, waits for them, and re-layouts  9.26 us (4%)
  other arithmetic  7.68 us (4%)
    ppermute x15, waiting for transfers between devices, over_z(): lax.ppermute(value, 'fsdp', [(i, (i + 4 * step) % 16) for i in range(16)])  39.9 us
    pallas_call x2, Pallas kernels, grad_blocks(): pl.pallas_call(functools.partial(grad_kernel, outputs), grid_spec=pltpu.P...  16.7 us
    ppermute x15, starting transfers between devices, over_z(): lax.ppermute(value, 'fsdp', [(i, (i + 4 * step) % 16) for i in range(16)])  16.5 us
    pallas_call x1, Pallas kernels, input_gradient(): pl.pallas_call(input_kernel, grid_spec=pltpu.PrefetchScalarGridSpec(num_s...  16.3 us
    ppermute x6, waiting for transfers between devices, over_y(): lax.ppermute(value, 'rep', [(i, (i + 2 * step) % 8) for i in range(8)])  13 us
    ppermute x6, starting transfers between devices, over_y(): lax.ppermute(value, 'rep', [(i, (i + 2 * step) % 8) for i in range(8)])  12.6 us
    ppermute x2, waiting for transfers between devices, over_x_hi(): return lax.ppermute(value, 'rep', [(i, i ^ 1) for i in range(8)])  11.8 us
    all_gather x1, waiting for transfers between devices, on_device(): late = lax.all_gather(late, 'fsdp', axis=0, tiled=True)  8.41 us
  transfers between devices with their start and end apart: 32, of which 22 were waited for; matrix products, arithmetic and copies ran while one was open for 5% of the time, Pallas kernels for 19%

profile of v2, /device:TPU:1, one launch (start us, length us, event | category | flops | bytes accessed | tf_op | source)
XLA Modules:
  0.0 211.0 jit_solution(15000422990790297925)
XLA Ops:
  7.2 1.7 slice.52
  9.0 7.3 %prep.1 = (bf16[8,320,512]{2,1,0:T(8,128)(2,1)}, bf16[8,320,512]{2,1,0:T(8,128)(2,1)}, bf16[320,1024]{1,0:T(8,128)(2,1)}, f32[320,128]{1,0:T(8,128)}) custom-call(s32[1]{0:T(128)} %bitcast.core_ref, s32[1,64]{1,0:T(1,128)} %index_ref.1, bf16[1,256,8192]{2,1,0:T(8,128)(2,1)} %h_ref.1, bf16[1,128,8192]{2,1,0:T(8,128)(2,1)} %b_ref.1, bf16[1,320,1024]{2,1,0:T(8,128)(2,1)} %cot_ref.1), custom_call_target="tpu_custom_call" | custom-call | flops 2000000000 | bytes 12000000 | tf_op jit(solution)/shard_map/prep/pallas_call | solution.py:103
  16.3 1.5 collective-permute-start
  18.5 5.0 %collective-permute-done.1.cs_ref = bf16[320,1024]{1,0:T(8,128)(2,1)S(1)} collective-permute-done((bf16[320,1024]{1,0:T(8,128)(2,1)}, bf16[320,1024]{1,0:T(8,128)(2,1)S(1)}, u32[]{:S(2)}, u32[]{:S(2)}) %collective-permute-start.1) | collective-permute-done | bytes 655392 | tf_op jit(solution)/shard_map/ppermute | solution.py:42
  23.5 0.8 copy-done.3
  24.3 0.9 copy-done
  25.2 5.6 %grad_a.1 = (bf16[1,576,512]{2,1,0:T(8,128)(2,1)}, bf16[1,576,512]{2,1,0:T(8,128)(2,1)}, bf16[1,448,512]{2,1,0:T(8,128)(2,1)}, bf16[1,448,512]{2,1,0:T(8,128)(2,1)}) custom-call(s32[5]{0:T(128)} %pad_add_fusion.table_ref, bf16[8,320,512]{2,1,0:T(8,128)(2,1)} %get-tuple-element.33.xk_ref, bf16[8,320,512]{2,1,0:T(8,128)(2,1)} %copy-done, ...), custom_call_target="tpu_custom_call" | custom-call | flops 1342177280 | bytes 3400000 | tf_op jit(solution)/shard_map/grad_a/pallas_call | solution.py:168
  30.8 4.2 %collective-permute-start.14 = (bf16[576,512]{1,0:T(8,128)(2,1)}, bf16[576,512]{1,0:T(8,128)(2,1)S(1)}, u32[]{:S(2)}, u32[]{:S(2)}) collective-permute-start(bf16[576,512]{1,0:T(8,128)(2,1)} %bitcast.81), channel_id=1, source_target_pairs={{0,12},{1,13},{2,14},{3,15},{4,0},{5,1},{6,2},{7,3},{8,4},{9,5},{1... | collective-permute-start | bytes 1769480 | tf_op jit(solution)/shard_map/ppermute | solution.py:50
  35.0 0.6 dynamic_slice.3
  35.6 0.7 stack.53.table_ref
  36.3 1.2 collective-permute-start.4
  37.5 11.1 %grad_b.1 = (bf16[1,576,512]{2,1,0:T(8,128)(2,1)}, bf16[1,576,512]{2,1,0:T(8,128)(2,1)}, bf16[1,576,512]{2,1,0:T(8,128)(2,1)}, bf16[1,576,512]{2,1,0:T(8,128)(2,...) custom-call(s32[5]{0:T(128)} %stack.53.table_ref, ...), custom_call_target="tpu_custom_call" | custom-call | flops 4026531840 | bytes 10200000 | tf_op jit(solution)/shard_map/grad_b/pallas_call | solution.py:168
  48.5 2.7 %collective-permute-start.12 = (bf16[576,512]{1,0:T(8,128)(2,1)}, bf16[576,512]{1,0:T(8,128)(2,1)S(1)}, u32[]{:S(2)}, u32[]{:S(2)}) collective-permute-start(bf16[576,512]{1,0:T(8,128)(2,1)} %bitcast.82), channel_id=1, source_target_pairs={{0,12},{1,13},{2,14},{3,15},{4,0},{5,1},{6,2},{7,3},{8,4},{9,5},{1... | collective-permute-start | bytes 1769480 | tf_op jit(solution)/shard_map/ppermute | solution.py:50
  51.3 6.8 %collective-permute-done.14 = bf16[576,512]{1,0:T(8,128)(2,1)S(1)} collective-permute-done((bf16[576,512]{1,0:T(8,128)(2,1)}, bf16[576,512]{1,0:T(8,128)(2,1)S(1)}, u32[]{:S(2)}, u32[]{:S(2)}) %collective-permute-start.14) | collective-permute-done | bytes 589856 | tf_op jit(solution)/shard_map/ppermute | solution.py:50
  58.1 1.3 collective-permute-start.2
  59.4 1.3 fusion
  61.0 1.5 collective-permute-start.11
  62.6 0.8 slice_bitcast_fusion.1.a0
  63.5 7.4 %collective-permute-done.13 = bf16[576,512]{1,0:T(8,128)(2,1)S(1)} collective-permute-done((bf16[576,512]{1,0:T(8,128)(2,1)}, bf16[576,512]{1,0:T(8,128)(2,1)S(1)}, u32[]{:S(2)}, u32[]{:S(2)}) %collective-permute-start.13) | collective-permute-done | bytes 589856 | tf_op jit(solution)/shard_map/ppermute | solution.py:50
  70.9 1.8 collective-permute-start.8
  72.7 10.7 %collective-permute-done.15 = bf16[576,512]{1,0:T(8,128)(2,1)S(1)} collective-permute-done((bf16[576,512]{1,0:T(8,128)(2,1)S(1)}, bf16[576,512]{1,0:T(8,128)(2,1)S(1)}, u32[]{:S(2)}, u32[]{:S(2)}) %collective-permute-start.15) | collective-permute-done | bytes 589856 | tf_op jit(solution)/shard_map/ppermute | solution.py:50
  83.4 1.2 collective-permute-start.5
  84.8 1.1 collective-permute-start.16
  85.9 1.0 fusion.5.b0
  86.9 1.4 collective-permute-done.8
  88.3 2.6 %collective-permute-done.5 = bf16[224,512]{1,0:T(8,128)(2,1)S(1)} collective-permute-done((bf16[224,512]{1,0:T(8,128)(2,1)S(1)}, bf16[224,512]{1,0:T(8,128)(2,1)S(1)}, u32[]{:S(2)}, u32[]{:S(2)}) %collective-permute-start.5) | collective-permute-done | bytes 229408 | tf_op jit(solution)/shard_map/ppermute | solution.py:50
  91.3 1.3 collective-permute-start.6
  92.7 1.5 collective-permute-start.7
  94.3 0.8 slice_bitcast_fusion.a1
  95.1 1.4 collective-permute-done.9.dl
  96.5 1.5 collective-permute-done.6.ul
  98.0 3.4 %collective-permute-done.7.de = bf16[224,512]{1,0:T(8,128)(2,1)S(1)} collective-permute-done((bf16[224,512]{1,0:T(8,128)(2,1)S(1)}, bf16[224,512]{1,0:T(8,128)(2,1)S(1)}, u32[]{:S(2)}, u32[]{:S(2)}) %collective-permute-start.7) | collective-permute-done | bytes 229408 | tf_op jit(solution)/shard_map/ppermute | solution.py:50
  101.4 1.6 collective-permute-done.3.ue
  103.0 0.7 copy-done.17
  103.9 4.9 %total.1 = (f32[512,1024]{1,0:T(8,128)}, f32[8,128]{1,0:T(8,128)}, bf16[384,1024]{1,0:T(8,128)(2,1)}) custom-call(bf16[448,512]{1,0:T(8,128)(2,1)} %slice_bitcast_fusion.1.a0, bf16[448,512]{1,0:T(8,128)(2,1)} %slice_bitcast_fusion.a1, bf16[224,512]{1,0:T(8,128)(2,1)} %copy-done.17, bf16[224,512]{1,0:T(8,128)(2,1)} %copy-done.15, ...), custom_call_target="tpu_custom_call" | custom-call | flops 5000000 | bytes 5000000 | tf_op jit(solution)/shard_map/total/pallas_call | solution.py:213
  108.8 2.6 %collective-permute-start.17 = (f32[8,128]{1,0:T(8,128)}, f32[8,128]{1,0:T(8,128)S(1)}, u32[]{:S(2)}, u32[]{:S(2)}) collective-permute-start(f32[8,128]{1,0:T(8,128)} %get-tuple-element.48), channel_id=1, source_target_pairs={{0,1},{1,0},{2,3},{3,2},{4,5},{5,4},{6,7},{7,6},{8,9},{9,8},{10,11... | collective-permute-start | bytes 12296 | tf_op jit(solution)/shard_map/ppermute | solution.py:42
  111.4 1.0 collective-permute-done.17
  112.4 0.7 add.175
  113.1 1.6 collective-permute-start.18
  114.7 1.0 collective-permute-done.18
  115.7 2.0 collective-permute-start.20
  117.7 0.6 stack.61.table_ref
  118.3 1.4 collective-permute-done.20
  119.7 1.7 collective-permute-done.19
  121.9 7.9 %adam.1 = (f32[1,512,1024]{2,1,0:T(8,128)}, f32[1,512,1024]{2,1,0:T(8,128)}, bf16[2,512,128]{2,1,0:T(8,128)(2,1)}, bf16[2,512,128]{2,1,0:T(8,128)(2,1)}, bf16[2,...) custom-call(s32[5]{0:T(128)} %stack.61.table_ref, f32[8,128]{1,0:T(8,128)} %add_add_fusion.sq_ref, ...), custom_call_target="tpu_custom_call" | custom-call | flops 20000000 | bytes 12000000 | tf_op jit(solution)/shard_map/adam/pallas_call | solution.py:254
  129.8 1.5 collective-permute-start.22
  131.3 2.3 %collective-permute-start.23 = (bf16[2,512,128]{2,1,0:T(8,128)(2,1)}, bf16[2,512,128]{2,1,0:T(8,128)(2,1)S(1)}, u32[]{:S(2)}, u32[]{:S(2)}) collective-permute-start(bf16[2,512,128]{2,1,0:T(8,128)(2,1)} %get-tuple-element.54), channel_id=1, source_target_pairs={{0,64},{16,80},{32,96},{48,112},{64,0},{80,16},{96,32},{112,48},{1... | collective-permute-start | bytes 786440 | tf_op jit(solution)/shard_map/ppermute | solution.py:58
  133.6 1.0 collective-permute-start.24
  134.6 1.9 collective-permute-done.22
  136.6 5.7 %collective-permute-done.23 = bf16[2,512,128]{2,1,0:T(8,128)(2,1)S(1)} collective-permute-done((bf16[2,512,128]{2,1,0:T(8,128)(2,1)}, bf16[2,512,128]{2,1,0:T(8,128)(2,1)S(1)}, u32[]{:S(2)}, u32[]{:S(2)}) %collective-permute-start.23) | collective-permute-done | bytes 262176 | tf_op jit(solution)/shard_map/ppermute | solution.py:58
  142.7 1.1 convert_add_fusion.4
  143.9 2.2 %collective-permute-start.25 = (bf16[512,128]{1,0:T(8,128)(2,1)S(1)}, bf16[512,128]{1,0:T(8,128)(2,1)S(1)}, u32[]{:S(2)}, u32[]{:S(2)}) collective-permute-start(bf16[512,128]{1,0:T(8,128)(2,1)S(1)} %fusion.15), channel_id=1, source_target_pairs={{0,16},{16,0},{32,48},{48,32},{64,80},{80,64},{96,112},{112,96},{1... | collective-permute-start | bytes 393224 | tf_op jit(solution)/shard_map/ppermute | solution.py:54
  146.1 5.9 %collective-permute-done.25 = bf16[512,128]{1,0:T(8,128)(2,1)S(1)} collective-permute-done((bf16[512,128]{1,0:T(8,128)(2,1)S(1)}, bf16[512,128]{1,0:T(8,128)(2,1)S(1)}, u32[]{:S(2)}, u32[]{:S(2)}) %collective-permute-start.25) | collective-permute-done | bytes 131104 | tf_op jit(solution)/shard_map/ppermute | solution.py:54
  152.0 0.9 fusion.16
  152.9 2.2 %collective-permute-start.26 = (bf16[512,128]{1,0:T(8,128)(2,1)S(1)}, bf16[512,128]{1,0:T(8,128)(2,1)S(1)}, u32[]{:S(2)}, u32[]{:S(2)}) collective-permute-start(bf16[512,128]{1,0:T(8,128)(2,1)S(1)} %get-tuple-element.56), channel_id=1, source_target_pairs={{0,16},{16,0},{32,48},{48,32},{64,80},{80,64},{96,112},{112,96},{1... | collective-permute-start | bytes 393224 | tf_op jit(solution)/shard_map/ppermute | solution.py:54
  155.1 5.9 %collective-permute-done.26 = bf16[512,128]{1,0:T(8,128)(2,1)S(1)} collective-permute-done((bf16[512,128]{1,0:T(8,128)(2,1)S(1)}, bf16[512,128]{1,0:T(8,128)(2,1)S(1)}, u32[]{:S(2)}, u32[]{:S(2)}) %collective-permute-start.26) | collective-permute-done | bytes 131104 | tf_op jit(solution)/shard_map/ppermute | solution.py:54
  161.1 5.4 %collective-permute-start.29 = (bf16[2,512,128]{2,1,0:T(8,128)(2,1)S(1)}, bf16[2,512,128]{2,1,0:T(8,128)(2,1)S(1)}, u32[]{:S(2)}, u32[]{:S(2)}) collective-permute-start(bf16[2,512,128]{2,1,0:T(8,128)(2,1)S(1)} %pad_maximum_fusion.refs_0_), channel_id=1, source_target_pairs={{0,32},{16,48},{32,64},{48,80},{64,96},{80,112},{96,0},{112,16},{1... | collective-permute-start | bytes 786440 | tf_op jit(solution)/shard_map/ppermute | solution.py:58
  166.9 2.0 collective-permute-start.27
  169.7 4.7 %collective-permute-done.28.refs_2_ = bf16[2,512,128]{2,1,0:T(8,128)(2,1)S(1)} collective-permute-done((bf16[2,512,128]{2,1,0:T(8,128)(2,1)S(1)}, bf16[2,512,128]{2,1,0:T(8,128)(2,1)S(1)}, u32[]{:S(2)}, u32[]{:S(2)}) %collective-permute-start.28) | collective-permute-done | bytes 262176 | tf_op jit(solution)/shard_map/ppermute | solution.py:58
  174.5 0.7 copy-done.10
  175.2 0.7 copy-done.11
  175.9 3.5 %place.1 = bf16[512,1024]{1,0:T(8,128)(2,1)} custom-call(s32[5]{0:T(128)} %stack.61.table_ref, bf16[2,512,128]{2,1,0:T(8,128)(2,1)} %copy-done.2, bf16[2,512,128]{2,1,0:T(8,128)(2,1)} %copy-done.11, bf16[2,512,128]{2,1,0:T(8,128)(2,1)} %copy-done.10, bf16[2,512,128]{2,1,0:T(8,128)(2,1)} %copy-done.9), custom_call_target="tpu_custom_call" | custom-call | flops 1000000 | bytes 2000000 | tf_op jit(solution)/shard_map/place/pallas_call | solution.py:281
  179.4 8.4 %all-gather.4.cloned.1.call-done = bf16[6144,1024]{1,0:T(8,128)(2,1)} async-done(((bf16[384,1024]{1,0:T(8,128)(2,1)}), bf16[6144,1024]{1,0:T(8,128)(2,1)}) %all-gather.4.cloned.1.call-update) | async-done | bytes 12582928 | tf_op jit(solution)/shard_map/all_gather | solution.py:430
  187.8 16.3 %input_gradient.1 = bf16[1,320,8192]{2,1,0:T(8,128)(2,1)} custom-call(s32[1]{0:T(128)} %bitcast.core_ref, bf16[320,1024]{1,0:T(8,128)(2,1)} %get-tuple-element.31.c_ref.cp_ref, f32[320,128]{1,0:T(8,128)} %get-tuple-element.32.inv_ref, f32[16,1,512]{2,1,0:T(1,128)} %bitcast.78, bf16[8,320,512]{2,1,0:T(8,128)(2,1)} %get-tuple-element.33.xk_ref, ...), custom_call_target="tpu_custom_call" | custom-call | flops 6000000000 | bytes 40000000 | tf_op jit(solution)/shard_map/input_gradient/pallas_call | solution.py:338
  (70 shorter events, 4.6 us)
Async XLA Ops:
  7.2 172.2 %all-gather.6.cloned.1.call-start = ((), (), s32[]{:S(2)}) async-start(), calls=%async_computation.1 | async-start | bytes 4456448 | tf_op jit(solution)/shard_map/all_gather | solution.py:391
  8.9 178.9 %all-gather.4.cloned.1.call-start = ((), (), s32[]{:S(2)}) async-start(), calls=%async_computation | async-start | bytes 13369344 | tf_op jit(solution)/shard_map/all_gather | solution.py:430
  16.3 7.2 %collective-permute-start = (bf16[8,320,512]{2,1,0:T(8,128)(2,1)}, bf16[8,320,512]{2,1,0:T(8,128)(2,1)S(1)}, u32[]{:S(2)}, u32[]{:S(2)}) collective-permute-start(bf16[8,320,512]{2,1,0:T(8,128)(2,1)} %get-tuple-element.34.xs_ref), channel_id=1, source_target_pairs={{0,1},{1,0},{2,3},{3,2},{4,5},{5,4},{6,7},{7,6},{8,9},{9,8},{10,11... | collective-permute-start | bytes 7864328 | tf_op jit(solution)/shard_map/ppermute | solution.py:42
  17.8 5.7 %collective-permute-start.1 = (bf16[320,1024]{1,0:T(8,128)(2,1)}, bf16[320,1024]{1,0:T(8,128)(2,1)S(1)}, u32[]{:S(2)}, u32[]{:S(2)}) collective-permute-start(bf16[320,1024]{1,0:T(8,128)(2,1)} %get-tuple-element.31.c_ref.cp_ref), channel_id=1, source_target_pairs={{0,1},{1,0},{2,3},{3,2},{4,5},{5,4},{6,7},{7,6},{8,9},{9,8},{10,11... | collective-permute-start | bytes 1966088 | tf_op jit(solution)/shard_map/ppermute | solution.py:42
  23.5 0.8 copy-start.3
  23.5 1.7 copy-start
  25.2 9.8 %copy-start.18 = (bf16[8192]{0:T(1024)(128)(2,1)S(1)}, bf16[8192]{0:T(1024)(128)(2,1)}, u32[]{:S(2)}) copy-start(bf16[8192]{0:T(1024)(128)(2,1)} %param.14) | copy-start | bytes 49156
  30.8 27.3 %collective-permute-start.14 = (bf16[576,512]{1,0:T(8,128)(2,1)}, bf16[576,512]{1,0:T(8,128)(2,1)S(1)}, u32[]{:S(2)}, u32[]{:S(2)}) collective-permute-start(bf16[576,512]{1,0:T(8,128)(2,1)} %bitcast.81), channel_id=1, source_target_pairs={{0,12},{1,13},{2,14},{3,15},{4,0},{5,1},{6,2},{7,3},{8,4},{9,5},{1... | collective-permute-start | bytes 1769480 | tf_op jit(solution)/shard_map/ppermute | solution.py:50
  36.3 24.8 %collective-permute-start.4 = (bf16[448,512]{1,0:T(8,128)(2,1)}, bf16[448,512]{1,0:T(8,128)(2,1)S(1)}, u32[]{:S(2)}, u32[]{:S(2)}) collective-permute-start(bf16[448,512]{1,0:T(8,128)(2,1)} %bitcast.84), channel_id=1, source_target_pairs={{0,2},{1,3},{2,0},{3,1},{4,6},{5,7},{6,4},{7,5},{8,10},{9,11},{10,... | collective-permute-start | bytes 1376264 | tf_op jit(solution)/shard_map/ppermute | solution.py:46
  37.5 23.3 %collective-permute-start.10 = (bf16[576,512]{1,0:T(8,128)(2,1)}, bf16[576,512]{1,0:T(8,128)(2,1)S(1)}, u32[]{:S(2)}, u32[]{:S(2)}) collective-permute-start(bf16[576,512]{1,0:T(8,128)(2,1)} %bitcast.80), channel_id=1, source_target_pairs={{0,4},{1,5},{2,6},{3,7},{4,8},{5,9},{6,10},{7,11},{8,12},{9,13},{1... | collective-permute-start | bytes 1769480 | tf_op jit(solution)/shard_map/ppermute | solution.py:50
  48.5 12.3 %copy-start.5 = (bf16[1,576,512]{2,1,0:T(8,128)(2,1)S(1)}, bf16[1,576,512]{2,1,0:T(8,128)(2,1)}, u32[]{:S(2)}) copy-start(bf16[1,576,512]{2,1,0:T(8,128)(2,1)} %get-tuple-element.40) | copy-start | bytes 1769476
  48.5 36.3 %collective-permute-start.12 = (bf16[576,512]{1,0:T(8,128)(2,1)}, bf16[576,512]{1,0:T(8,128)(2,1)S(1)}, u32[]{:S(2)}, u32[]{:S(2)}) collective-permute-start(bf16[576,512]{1,0:T(8,128)(2,1)} %bitcast.82), channel_id=1, source_target_pairs={{0,12},{1,13},{2,14},{3,15},{4,0},{5,1},{6,2},{7,3},{8,4},{9,5},{1... | collective-permute-start | bytes 1769480 | tf_op jit(solution)/shard_map/ppermute | solution.py:50
  51.3 19.6 %collective-permute-start.13 = (bf16[576,512]{1,0:T(8,128)(2,1)}, bf16[576,512]{1,0:T(8,128)(2,1)S(1)}, u32[]{:S(2)}, u32[]{:S(2)}) collective-permute-start(bf16[576,512]{1,0:T(8,128)(2,1)} %bitcast.83), channel_id=1, source_target_pairs={{0,4},{1,5},{2,6},{3,7},{4,8},{5,9},{6,10},{7,11},{8,12},{9,13},{1... | collective-permute-start | bytes 1769480 | tf_op jit(solution)/shard_map/ppermute | solution.py:50
  58.1 32.8 %collective-permute-start.2 = (bf16[3,448,512]{2,1,0:T(8,128)(2,1)}, bf16[3,448,512]{2,1,0:T(8,128)(2,1)S(1)}, u32[]{:S(2)}, u32[]{:S(2)}) collective-permute-start(bf16[3,448,512]{2,1,0:T(8,128)(2,1)} %get-tuple-element.36), channel_id=1, source_target_pairs={{0,2},{1,3},{2,0},{3,1},{4,6},{5,7},{6,4},{7,5},{8,10},{9,11},{10,... | collective-permute-start | bytes 4128776 | tf_op jit(solution)/shard_map/ppermute | solution.py:46
  59.4 3.1 %copy-start.1 = (bf16[3,448,512]{2,1,0:T(8,128)(2,1)S(1)}, bf16[3,448,512]{2,1,0:T(8,128)(2,1)}, u32[]{:S(2)}) copy-start(bf16[3,448,512]{2,1,0:T(8,128)(2,1)} %get-tuple-element.35) | copy-start | bytes 4128772
  60.7 2.6 %copy-start.8 = (bf16[1,448,512]{2,1,0:T(8,128)(2,1)S(1)}, bf16[1,448,512]{2,1,0:T(8,128)(2,1)}, u32[]{:S(2)}) copy-start(bf16[1,448,512]{2,1,0:T(8,128)(2,1)} %get-tuple-element.37) | copy-start | bytes 1376260
  60.8 22.6 %collective-permute-start.15 = (bf16[576,512]{1,0:T(8,128)(2,1)S(1)}, bf16[576,512]{1,0:T(8,128)(2,1)S(1)}, u32[]{:S(2)}, u32[]{:S(2)}) collective-permute-start(bf16[576,512]{1,0:T(8,128)(2,1)S(1)} %fusion), channel_id=1, source_target_pairs={{0,12},{1,13},{2,14},{3,15},{4,0},{5,1},{6,2},{7,3},{8,4},{9,5},{1... | collective-permute-start | bytes 1769480 | tf_op jit(solution)/shard_map/ppermute | solution.py:50
  61.0 23.6 %copy-start.7 = (bf16[1,576,512]{2,1,0:T(8,128)(2,1)S(1)}, bf16[1,576,512]{2,1,0:T(8,128)(2,1)}, u32[]{:S(2)}) copy-start(bf16[1,576,512]{2,1,0:T(8,128)(2,1)} %get-tuple-element.43) | copy-start | bytes 1769476
  61.0 24.8 %collective-permute-start.11 = (bf16[576,512]{1,0:T(8,128)(2,1)S(1)}, bf16[576,512]{1,0:T(8,128)(2,1)S(1)}, u32[]{:S(2)}, u32[]{:S(2)}) collective-permute-start(bf16[576,512]{1,0:T(8,128)(2,1)S(1)} %fusion.3), channel_id=1, source_target_pairs={{0,4},{1,5},{2,6},{3,7},{4,8},{5,9},{6,10},{7,11},{8,12},{9,13},{1... | collective-permute-start | bytes 1769480 | tf_op jit(solution)/shard_map/ppermute | solution.py:50
  63.5 22.4 %copy-start.6 = (bf16[1,576,512]{2,1,0:T(8,128)(2,1)S(1)}, bf16[1,576,512]{2,1,0:T(8,128)(2,1)}, u32[]{:S(2)}) copy-start(bf16[1,576,512]{2,1,0:T(8,128)(2,1)} %get-tuple-element.39) | copy-start | bytes 1769476
  70.9 17.4 %collective-permute-start.8 = (bf16[224,512]{1,0:T(8,128)(2,1)S(1)}, bf16[224,512]{1,0:T(8,128)(2,1)S(1)}, u32[]{:S(2)}, u32[]{:S(2)}) collective-permute-start(bf16[224,512]{1,0:T(8,128)(2,1)S(1)} %get-tuple-element.63), channel_id=1, source_target_pairs={{0,12},{1,13},{2,14},{3,15},{4,0},{5,1},{6,2},{7,3},{8,4},{9,5},{1... | collective-permute-start | bytes 688136 | tf_op jit(solution)/shard_map/ppermute | solution.py:50
  83.4 7.5 %collective-permute-start.5 = (bf16[224,512]{1,0:T(8,128)(2,1)S(1)}, bf16[224,512]{1,0:T(8,128)(2,1)S(1)}, u32[]{:S(2)}, u32[]{:S(2)}) collective-permute-start(bf16[224,512]{1,0:T(8,128)(2,1)S(1)} %get-tuple-element.64), channel_id=1, source_target_pairs={{0,4},{1,5},{2,6},{3,7},{4,8},{5,9},{6,10},{7,11},{8,12},{9,13},{1... | collective-permute-start | bytes 688136 | tf_op jit(solution)/shard_map/ppermute | solution.py:50
  84.8 18.2 %collective-permute-start.16 = (bf16[576,512]{1,0:T(8,128)(2,1)S(1)}, bf16[576,512]{1,0:T(8,128)(2,1)S(1)}, u32[]{:S(2)}, u32[]{:S(2)}) collective-permute-start(bf16[576,512]{1,0:T(8,128)(2,1)S(1)} %fusion.2), channel_id=1, source_target_pairs={{0,2},{1,3},{2,0},{3,1},{4,6},{5,7},{6,4},{7,5},{8,10},{9,11},{10,... | collective-permute-start | bytes 1769480 | tf_op jit(solution)/shard_map/ppermute | solution.py:46
  91.1 5.4 %collective-permute-start.9 = (bf16[224,512]{1,0:T(8,128)(2,1)S(1)}, bf16[224,512]{1,0:T(8,128)(2,1)S(1)}, u32[]{:S(2)}, u32[]{:S(2)}) collective-permute-start(bf16[224,512]{1,0:T(8,128)(2,1)S(1)} %get-tuple-element.59), channel_id=1, source_target_pairs={{0,12},{1,13},{2,14},{3,15},{4,0},{5,1},{6,2},{7,3},{8,4},{9,5},{1... | collective-permute-start | bytes 688136 | tf_op jit(solution)/shard_map/ppermute | solution.py:50
  91.3 6.6 %collective-permute-start.6 = (bf16[224,512]{1,0:T(8,128)(2,1)S(1)}, bf16[224,512]{1,0:T(8,128)(2,1)S(1)}, u32[]{:S(2)}, u32[]{:S(2)}) collective-permute-start(bf16[224,512]{1,0:T(8,128)(2,1)S(1)} %get-tuple-element.60), channel_id=1, source_target_pairs={{0,4},{1,5},{2,6},{3,7},{4,8},{5,9},{6,10},{7,11},{8,12},{9,13},{1... | collective-permute-start | bytes 688136 | tf_op jit(solution)/shard_map/ppermute | solution.py:50
  92.7 8.7 %collective-permute-start.7 = (bf16[224,512]{1,0:T(8,128)(2,1)S(1)}, bf16[224,512]{1,0:T(8,128)(2,1)S(1)}, u32[]{:S(2)}, u32[]{:S(2)}) collective-permute-start(bf16[224,512]{1,0:T(8,128)(2,1)S(1)} %get-tuple-element.61), channel_id=1, source_target_pairs={{0,12},{1,13},{2,14},{3,15},{4,0},{5,1},{6,2},{7,3},{8,4},{9,5},{1... | collective-permute-start | bytes 688136 | tf_op jit(solution)/shard_map/ppermute | solution.py:50
  94.2 8.8 %collective-permute-start.3 = (bf16[224,512]{1,0:T(8,128)(2,1)S(1)}, bf16[224,512]{1,0:T(8,128)(2,1)S(1)}, u32[]{:S(2)}, u32[]{:S(2)}) collective-permute-start(bf16[224,512]{1,0:T(8,128)(2,1)S(1)} %get-tuple-element.62), channel_id=1, source_target_pairs={{0,4},{1,5},{2,6},{3,7},{4,8},{5,9},{6,10},{7,11},{8,12},{9,13},{1... | collective-permute-start | bytes 688136 | tf_op jit(solution)/shard_map/ppermute | solution.py:50
  96.5 6.5 %copy-start.14 = (bf16[224,512]{1,0:T(8,128)(2,1)}, bf16[224,512]{1,0:T(8,128)(2,1)S(1)}, u32[]{:S(2)}) copy-start(bf16[224,512]{1,0:T(8,128)(2,1)S(1)} %collective-permute-done.9.dl) | copy-start | bytes 688132
  98.0 5.1 %copy-start.15 = (bf16[224,512]{1,0:T(8,128)(2,1)}, bf16[224,512]{1,0:T(8,128)(2,1)S(1)}, u32[]{:S(2)}) copy-start(bf16[224,512]{1,0:T(8,128)(2,1)S(1)} %collective-permute-done.6.ul) | copy-start | bytes 688132
  101.4 1.6 copy-start.16
  103.0 0.7 copy-start.17
  103.0 0.9 copy-start.4
  108.8 3.6 %collective-permute-start.17 = (f32[8,128]{1,0:T(8,128)}, f32[8,128]{1,0:T(8,128)S(1)}, u32[]{:S(2)}, u32[]{:S(2)}) collective-permute-start(f32[8,128]{1,0:T(8,128)} %get-tuple-element.48), channel_id=1, source_target_pairs={{0,1},{1,0},{2,3},{3,2},{4,5},{5,4},{6,7},{7,6},{8,9},{9,8},{10,11... | collective-permute-start | bytes 12296 | tf_op jit(solution)/shard_map/ppermute | solution.py:42
  113.1 2.6 %collective-permute-start.18 = (f32[8,128]{1,0:T(8,128)S(1)}, f32[8,128]{1,0:T(8,128)S(1)}, u32[]{:S(2)}, u32[]{:S(2)}) collective-permute-start(f32[8,128]{1,0:T(8,128)S(1)} %add.175), channel_id=1, source_target_pairs={{0,2},{1,3},{2,0},{3,1},{4,6},{5,7},{6,4},{7,5},{8,10},{9,11},{10,... | collective-permute-start | bytes 12296 | tf_op jit(solution)/shard_map/ppermute | solution.py:46
  115.7 2.6 %collective-permute-start.21 = (f32[8,128]{1,0:T(8,128)S(1)}, f32[8,128]{1,0:T(8,128)S(1)}, u32[]{:S(2)}, u32[]{:S(2)}) collective-permute-start(f32[8,128]{1,0:T(8,128)S(1)} %add.176), channel_id=1, source_target_pairs={{0,12},{1,13},{2,14},{3,15},{4,0},{5,1},{6,2},{7,3},{8,4},{9,5},{1... | collective-permute-start | bytes 12296 | tf_op jit(solution)/shard_map/ppermute | solution.py:50
  115.7 4.0 %collective-permute-start.20 = (f32[8,128]{1,0:T(8,128)S(1)}, f32[8,128]{1,0:T(8,128)S(1)}, u32[]{:S(2)}, u32[]{:S(2)}) collective-permute-start(f32[8,128]{1,0:T(8,128)S(1)} %add.176), channel_id=1, source_target_pairs={{0,8},{1,9},{2,10},{3,11},{4,12},{5,13},{6,14},{7,15},{8,0},{9,1},... | collective-permute-start | bytes 12296 | tf_op jit(solution)/shard_map/ppermute | solution.py:50
  117.7 3.7 %collective-permute-start.19 = (f32[8,128]{1,0:T(8,128)S(1)}, f32[8,128]{1,0:T(8,128)S(1)}, u32[]{:S(2)}, u32[]{:S(2)}) collective-permute-start(f32[8,128]{1,0:T(8,128)S(1)} %add.176), channel_id=1, source_target_pairs={{0,4},{1,5},{2,6},{3,7},{4,8},{5,9},{6,10},{7,11},{8,12},{9,13},{1... | collective-permute-start | bytes 12296 | tf_op jit(solution)/shard_map/ppermute | solution.py:50
  129.8 22.2 %copy-start.12 = (f32[512,128]{1,0:T(8,128)S(1)}, f32[512,128]{1,0:T(8,128)}, u32[]{:S(2)}) copy-start(f32[512,128]{1,0:T(8,128)} %param.18) | copy-start | bytes 786436
  129.8 22.2 %copy-start.13 = (f32[512,128]{1,0:T(8,128)S(1)}, f32[512,128]{1,0:T(8,128)}, u32[]{:S(2)}) copy-start(f32[512,128]{1,0:T(8,128)} %param.19) | copy-start | bytes 786436
  129.8 6.7 %collective-permute-start.22 = (bf16[2,512,128]{2,1,0:T(8,128)(2,1)}, bf16[2,512,128]{2,1,0:T(8,128)(2,1)S(1)}, u32[]{:S(2)}, u32[]{:S(2)}) collective-permute-start(bf16[2,512,128]{2,1,0:T(8,128)(2,1)} %get-tuple-element.53), channel_id=1, source_target_pairs={{0,32},{16,48},{32,64},{48,80},{64,96},{80,112},{96,0},{112,16},{1... | collective-permute-start | bytes 786440 | tf_op jit(solution)/shard_map/ppermute | solution.py:58
  131.3 11.0 %collective-permute-start.23 = (bf16[2,512,128]{2,1,0:T(8,128)(2,1)}, bf16[2,512,128]{2,1,0:T(8,128)(2,1)S(1)}, u32[]{:S(2)}, u32[]{:S(2)}) collective-permute-start(bf16[2,512,128]{2,1,0:T(8,128)(2,1)} %get-tuple-element.54), channel_id=1, source_target_pairs={{0,64},{16,80},{32,96},{48,112},{64,0},{80,16},{96,32},{112,48},{1... | collective-permute-start | bytes 786440 | tf_op jit(solution)/shard_map/ppermute | solution.py:58
  133.6 9.0 %collective-permute-start.24 = (bf16[2,512,128]{2,1,0:T(8,128)(2,1)}, bf16[2,512,128]{2,1,0:T(8,128)(2,1)S(1)}, u32[]{:S(2)}, u32[]{:S(2)}) collective-permute-start(bf16[2,512,128]{2,1,0:T(8,128)(2,1)} %get-tuple-element.55), channel_id=1, source_target_pairs={{0,96},{16,112},{32,0},{48,16},{64,32},{80,48},{96,64},{112,80},{1... | collective-permute-start | bytes 786440 | tf_op jit(solution)/shard_map/ppermute | solution.py:58
  143.9 8.2 %collective-permute-start.25 = (bf16[512,128]{1,0:T(8,128)(2,1)S(1)}, bf16[512,128]{1,0:T(8,128)(2,1)S(1)}, u32[]{:S(2)}, u32[]{:S(2)}) collective-permute-start(bf16[512,128]{1,0:T(8,128)(2,1)S(1)} %fusion.15), channel_id=1, source_target_pairs={{0,16},{16,0},{32,48},{48,32},{64,80},{80,64},{96,112},{112,96},{1... | collective-permute-start | bytes 393224 | tf_op jit(solution)/shard_map/ppermute | solution.py:54
  152.9 8.1 %collective-permute-start.26 = (bf16[512,128]{1,0:T(8,128)(2,1)S(1)}, bf16[512,128]{1,0:T(8,128)(2,1)S(1)}, u32[]{:S(2)}, u32[]{:S(2)}) collective-permute-start(bf16[512,128]{1,0:T(8,128)(2,1)S(1)} %get-tuple-element.56), channel_id=1, source_target_pairs={{0,16},{16,0},{32,48},{48,32},{64,80},{80,64},{96,112},{112,96},{1... | collective-permute-start | bytes 393224 | tf_op jit(solution)/shard_map/ppermute | solution.py:54
  161.1 13.4 %copy-start.2 = (bf16[2,512,128]{2,1,0:T(8,128)(2,1)}, bf16[2,512,128]{2,1,0:T(8,128)(2,1)S(1)}, u32[]{:S(2)}) copy-start(bf16[2,512,128]{2,1,0:T(8,128)(2,1)S(1)} %pad_maximum_fusion.refs_0_) | copy-start | bytes 786436
  161.1 8.7 %collective-permute-start.29 = (bf16[2,512,128]{2,1,0:T(8,128)(2,1)S(1)}, bf16[2,512,128]{2,1,0:T(8,128)(2,1)S(1)}, u32[]{:S(2)}, u32[]{:S(2)}) collective-permute-start(bf16[2,512,128]{2,1,0:T(8,128)(2,1)S(1)} %pad_maximum_fusion.refs_0_), channel_id=1, source_target_pairs={{0,32},{16,48},{32,64},{48,80},{64,96},{80,112},{96,0},{112,16},{1... | collective-permute-start | bytes 786440 | tf_op jit(solution)/shard_map/ppermute | solution.py:58
  166.4 8.0 %collective-permute-start.28 = (bf16[2,512,128]{2,1,0:T(8,128)(2,1)S(1)}, bf16[2,512,128]{2,1,0:T(8,128)(2,1)S(1)}, u32[]{:S(2)}, u32[]{:S(2)}) collective-permute-start(bf16[2,512,128]{2,1,0:T(8,128)(2,1)S(1)} %pad_maximum_fusion.refs_0_), channel_id=1, source_target_pairs={{0,64},{16,80},{32,96},{48,112},{64,0},{80,16},{96,32},{112,48},{1... | collective-permute-start | bytes 786440 | tf_op jit(solution)/shard_map/ppermute | solution.py:58
  166.9 7.6 %collective-permute-start.27 = (bf16[2,512,128]{2,1,0:T(8,128)(2,1)S(1)}, bf16[2,512,128]{2,1,0:T(8,128)(2,1)S(1)}, u32[]{:S(2)}, u32[]{:S(2)}) collective-permute-start(bf16[2,512,128]{2,1,0:T(8,128)(2,1)S(1)} %pad_maximum_fusion.refs_0_), channel_id=1, source_target_pairs={{0,96},{16,112},{32,0},{48,16},{64,32},{80,48},{96,64},{112,80},{1... | collective-permute-start | bytes 786440 | tf_op jit(solution)/shard_map/ppermute | solution.py:58
  169.7 4.7 %copy-start.9 = (bf16[2,512,128]{2,1,0:T(8,128)(2,1)}, bf16[2,512,128]{2,1,0:T(8,128)(2,1)S(1)}, u32[]{:S(2)}) copy-start(bf16[2,512,128]{2,1,0:T(8,128)(2,1)S(1)} %collective-permute-done.29.refs_3_) | copy-start | bytes 786436
  174.4 0.7 copy-start.10
  175.2 0.7 copy-start.11
Sparse Core Ops, SparseCore 0:
  9.7 49.9 all-gather.5
  108.9 78.8 all-gather.3

commit v3 on v2

--- a/solution.py
+++ b/solution.py
@@ -65,7 +65,7 @@
     return total
 
 
-def prep_kernel(core_ref, index_ref, h_ref, b_ref, cot_ref, xk_ref, xs_ref, cp_ref, inv_ref, total_ref):
+def prep_kernel(core_ref, index_ref, h_ref, b_ref, cot_ref, xk_ref, xs_ref, xf_ref, cp_ref, inv_ref, total_ref):
     step = pl.program_id(0)
     core = core_ref[0]
     rows = lax.broadcasted_iota(jnp.int32, (128, 64), 0)
@@ -81,6 +81,10 @@
             fresh = fresh.astype(F32)
             squares = squares + jnp.concatenate([lane_sum(fresh * fresh), lane_sum(replayed * replayed)], axis=0)
 
+    @pl.when(step == core_ref[1])
+    def _():
+        xf_ref[...] = xs_ref[...]
+
     @pl.when(step == 0)
     def _():
         total_ref[...] = squares
@@ -114,6 +118,7 @@
             out_specs=[
                 pl.BlockSpec((2, 320, 512), lambda t, c: (t, 0, 0)),
                 pl.BlockSpec((2, 320, 512), lambda t, c: (t, 0, 0)),
+                pl.BlockSpec((2, 320, 512), lambda t, c: (0, 0, 0)),
                 pl.BlockSpec((320, 1024), lambda t, c: (0, 0)),
                 pl.BlockSpec((320, 128), lambda t, c: (0, 0)),
             ],
@@ -122,6 +127,7 @@
         out_shape=[
             sds((8, 320, 512), BF16),
             sds((8, 320, 512), BF16),
+            sds((2, 320, 512), BF16),
             sds((320, 1024), BF16),
             sds((320, 128), F32),
         ],
@@ -164,13 +170,14 @@
     z, x = place
     table = jnp.stack([(z + dz) % 4 for dz in chunks] + [jnp.int32(0)] * (4 - len(chunks)) + [x])
     x_spec = pl.BlockSpec((2, 320, 512), lambda t, tab: (tab[t], 0, 0))
+    s_spec = x_spec if xs.shape[0] == 8 else pl.BlockSpec((2, 320, 512), lambda t, tab: (0, 0, 0))
     c_spec = pl.BlockSpec((320, 1024), lambda t, tab: (0, 0))
     return pl.pallas_call(
         functools.partial(grad_kernel, outputs),
         grid_spec=pltpu.PrefetchScalarGridSpec(
             num_scalar_prefetch=1,
             grid=(len(chunks),),
-            in_specs=[x_spec, x_spec, c_spec, c_spec],
+            in_specs=[x_spec, s_spec, c_spec, c_spec],
             out_specs=[
                 pl.BlockSpec(
                     (None, x_first if low else z_first, 512), lambda t, tab, s=s, n=n: (clip_index(t, s, n), 0, 0)
@@ -189,9 +196,25 @@
 early_rows = 128
 
 
-def total_kernel(a0, a1, ue, ul, de, dl, b0, b1, gain_ref, w_ref, grad_ref, sq_ref, late_ref):
-    step = pl.program_id(0)
+def late_kernel(w_ref, after_ref, late_ref):
     late_ref[...] = w_ref[early_rows:512, :]
+
+
+def late_weights(weight, after):
+    return pl.pallas_call(
+        late_kernel,
+        grid=(1,),
+        in_specs=[pl.BlockSpec((None, 512, 1024), lambda t: (0, 0, 0)), pl.BlockSpec(memory_space=pl.ANY)],
+        out_specs=pl.BlockSpec((512 - early_rows, 1024), lambda t: (0, 0)),
+        out_shape=sds((512 - early_rows, 1024), BF16),
+        compiler_params=params(60),
+        cost_estimate=cost(0, 2e6),
+        name="late_weights",
+    )(weight, after)
+
+
+def total_kernel(a0, a1, ue, ul, de, dl, b0, b1, gain_ref, grad_ref, sq_ref):
+    step = pl.program_id(0)
     up = jnp.concatenate([ul[...], ue[...]], axis=0).astype(F32)
     down = jnp.concatenate([de[...], dl[...]], axis=0).astype(F32)
     top = (a0[...].astype(F32) + a1[...].astype(F32)) + (up + down)
@@ -209,22 +232,21 @@
         sq_ref[...] += square
 
 
-def total(parts, gain_row, weight):
+def total(parts, gain_row):
     return pl.pallas_call(
         total_kernel,
         grid=(4,),
         in_specs=[pl.BlockSpec((p.shape[0], 128), lambda t: (0, t)) for p in parts]
-        + [pl.BlockSpec((1, 128), lambda t: (0, t)), pl.BlockSpec((None, 512, 256), lambda t: (0, 0, t))],
+        + [pl.BlockSpec((1, 128), lambda t: (0, t))],
         out_specs=[
             pl.BlockSpec((128, 1024), lambda t: (t, 0)),
             pl.BlockSpec((8, 128), lambda t: (0, 0)),
-            pl.BlockSpec((512 - early_rows, 256), lambda t: (0, t)),
         ],
-        out_shape=[sds((512, 1024), F32), sds((8, 128), F32), sds((512 - early_rows, 1024), BF16)],
+        out_shape=[sds((512, 1024), F32), sds((8, 128), F32)],
         compiler_params=params(60),
         cost_estimate=cost(5e6, 5e6),
         name="total",
-    )(*parts, gain_row, weight)
+    )(*parts, gain_row)
 
 
 def adam_kernel(table_ref, sq_ref, grad_ref, m_ref, v_ref, w_ref, first_ref, second_ref, *rest):
@@ -238,7 +260,10 @@
     second = second_decay * v_ref[...] + (1.0 - second_decay) * clipped * clipped
     first_ref[...] = first
     second_ref[...] = second
-    new = w_ref[...].astype(F32) - inner_rate * first / (jnp.sqrt(second) + adam_eps)
+    root = second * lax.rsqrt(second) + adam_eps
+    inverse = pl.reciprocal(root, approx=True)
+    inverse = inverse * (2.0 - root * inverse)
+    new = w_ref[...].astype(F32) - inner_rate * first * inverse
     new_ref[...] = new.astype(BF16)
     for k, out_ref in enumerate(outs):
 
@@ -293,27 +318,81 @@
     )(table, *parts)
 
 
-def input_kernel(core_ref, cp_ref, inv_ref, gain_ref, xk_ref, xs_ref, ek_ref, es_ref, lk_ref, ls_ref, out_ref, q_ref, m_ref):
+def early_kernel(core_ref, cp_ref, gain_ref, xk_ref, xs_ref, ek_ref, es_ref, q_ref, m_ref):
     step = pl.program_id(0)
     core = core_ref[0]
+    m = jnp.zeros((320, 128), F32)
+    for sibling, (x_ref, e_ref) in enumerate(((xk_ref, ek_ref), (xs_ref, es_ref))):
+        w = e_ref[...].reshape(4 * early_rows, 1024)
+        q = lax.dot_general(cp_ref[...], w, (((1,), (1,)), ((), ())), preferred_element_type=F32)
+        for j in range(4):
+            gain = gain_ref[2 * (4 * step + j) + (core ^ sibling)][:, 0:early_rows]
+            gained = q[:, early_rows * j : early_rows * (j + 1)] * gain
+            m = m + lane_sum(gained * x_ref[j].astype(F32))
+            q_ref[sibling, j] = gained.astype(BF16)
 
     @pl.when(step == 0)
     def _():
-        m_ref[...] = jnp.zeros_like(m_ref)
+        m_ref[...] = m
+
+    @pl.when(step > 0)
+    def _():
+        m_ref[...] += m
+
+
+def early_product(core, xk, xs, cp, gain, early):
+    early = early.reshape(8, 2, early_rows, 1024)
+
+    def weights(flip):
+        return pl.BlockSpec((4, None, early_rows, 1024), lambda t, c: (t, c[0] ^ flip, 0, 0))
+
+    x_spec = pl.BlockSpec((4, 320, early_rows), lambda t, c: (t, 0, 0))
+    return pl.pallas_call(
+        early_kernel,
+        grid_spec=pltpu.PrefetchScalarGridSpec(
+            num_scalar_prefetch=1,
+            grid=(2,),
+            in_specs=[
+                pl.BlockSpec((320, 1024), lambda t, c: (0, 0)),
+                pl.BlockSpec((16, 1, 512), lambda t, c: (0, 0, 0)),
+                x_spec,
+                x_spec,
+                weights(0),
+                weights(1),
+            ],
+            out_specs=[
+                pl.BlockSpec((2, 4, 320, early_rows), lambda t, c: (0, t, 0, 0)),
+                pl.BlockSpec((320, 128), lambda t, c: (0, 0)),
+            ],
+        ),
+        out_shape=[sds((2, 8, 320, early_rows), BF16), sds((320, 128), F32)],
+        compiler_params=params(60),
+        cost_estimate=cost(1.4e9, 8e6),
+        name="early_product",
+    )(core, cp, gain, xk, xs, early, early)
+
+
+def input_kernel(core_ref, cp_ref, inv_ref, gain_ref, xk_ref, xs_ref, qe_ref, me_ref, lk_ref, ls_ref, out_ref, q_ref, m_ref):
+    step = pl.program_id(0)
+    core = core_ref[0]
+
+    @pl.when(step == 0)
+    def _():
+        m_ref[...] = me_ref[...]
 
     @pl.when(step < 4)
     def _():
         m = m_ref[...]
-        for sibling, (x_ref, e_ref, l_ref) in enumerate(((xk_ref, ek_ref, lk_ref), (xs_ref, es_ref, ls_ref))):
-            for w_ref, low, high in ((e_ref, 0, early_rows), (l_ref, early_rows, 512)):
-                size = high - low
-                w = w_ref[...].reshape(2 * size, 1024)
-                q = lax.dot_general(cp_ref[...], w, (((1,), (1,)), ((), ())), preferred_element_type=F32)
-                for j in range(2):
-                    g = 2 * step + j
-                    gained = q[:, size * j : size * (j + 1)] * gain_ref[2 * g + (core ^ sibling)][:, low:high]
-                    m = m + lane_sum(gained * x_ref[j, :, low:high].astype(F32))
-                    q_ref[8 * sibling + g, :, low:high] = gained.astype(BF16)
+        for sibling, (x_ref, w_ref) in enumerate(((xk_ref, lk_ref), (xs_ref, ls_ref))):
+            size = 512 - early_rows
+            w = w_ref[...].reshape(2 * size, 1024)
+            q = lax.dot_general(cp_ref[...], w, (((1,), (1,)), ((), ())), preferred_element_type=F32)
+            for j in range(2):
+                g = 2 * step + j
+                gained = q[:, size * j : size * (j + 1)] * gain_ref[2 * g + (core ^ sibling)][:, early_rows:512]
+                m = m + lane_sum(gained * x_ref[j, :, early_rows:512].astype(F32))
+                q_ref[8 * sibling + g, :, 0:early_rows] = qe_ref[sibling, j]
+                q_ref[8 * sibling + g, :, early_rows:512] = gained.astype(BF16)
         m_ref[...] = m
 
     @pl.when(step >= 4)
@@ -327,12 +406,11 @@
                 out_ref[:, columns] = value.astype(BF16)
 
 
-def input_gradient(core, xk, xs, cp, inv, gain, early, late):
-    early = early.reshape(8, 2, early_rows, 1024)
+def input_gradient(core, xk, xs, cp, inv, gain, q_early, m_early, late):
     late = late.reshape(8, 2, 512 - early_rows, 1024)
 
-    def weights(rows, flip):
-        return pl.BlockSpec((2, None, rows, 1024), lambda t, c: (jnp.minimum(t, 3), c[0] ^ flip, 0, 0))
+    def weights(flip):
+        return pl.BlockSpec((2, None, 512 - early_rows, 1024), lambda t, c: (jnp.minimum(t, 3), c[0] ^ flip, 0, 0))
 
     x_spec = pl.BlockSpec((2, 320, 512), lambda t, c: (t % 4, 0, 0))
     return pl.pallas_call(
@@ -346,19 +424,19 @@
                 pl.BlockSpec((16, 1, 512), lambda t, c: (0, 0, 0)),
                 x_spec,
                 x_spec,
-                weights(early_rows, 0),
-                weights(early_rows, 1),
-                weights(512 - early_rows, 0),
-                weights(512 - early_rows, 1),
+                pl.BlockSpec((2, 2, 320, early_rows), lambda t, c: (0, jnp.minimum(t, 3), 0, 0)),
+                pl.BlockSpec((320, 128), lambda t, c: (0, 0)),
+                weights(0),
+                weights(1),
             ],
             out_specs=pl.BlockSpec((None, 320, 2048), lambda t, c: (0, 0, jnp.maximum(t - 4, 0))),
             scratch_shapes=[pltpu.VMEM((16, 320, 512), BF16), pltpu.VMEM((320, 128), F32)],
         ),
         out_shape=sds((1, 320, 8192), BF16),
         compiler_params=params(60),
-        cost_estimate=cost(6e9, 4e7),
+        cost_estimate=cost(5e9, 3e7),
         name="input_gradient",
-    )(core, cp, inv, gain, xk, xs, early, early, late, late)
+    )(core, cp, inv, gain, xk, xs, q_early, m_early, late, late)
 
 
 def add(*values):
@@ -390,12 +468,18 @@
 
     early = lax.all_gather(value_weight[0, :early_rows], "fsdp", axis=0, tiled=True)
 
-    xk, xs, cp, inv = prep(core[None], hidden, replay_buffer, replay_index, cotangent)
+    xk, xs, xs_first, cp, inv = prep(jnp.stack([core, (z + 2) % 4]), hidden, replay_buffer, replay_index, cotangent)
+    x_first_sib = over_core(xs_first)
+    c_sib = over_core(cp)
     x_sib = over_core(xs)
-    c_sib = over_core(cp)
+
+    outer_1 = 1.0 - outer_rate * (1.0 + outer_beta)
+    kept = outer_1 * anchor - (outer_rate * outer_beta * outer_beta) * outer_momentum
+    kept = lax.optimization_barrier(kept)
+    kept = jnp.stack([kept, over_x_hi(kept)])
 
     b_20, b_21, a_21, a_20 = grad_blocks(
-        place, [2], [(0, 0, 0, 1), (0, 1, 0, 1), (1, 1, 0, 1), (1, 0, 0, 1)], xk, x_sib, cp, c_sib, "grad_a"
+        place, [2], [(0, 0, 0, 1), (0, 1, 0, 1), (1, 1, 0, 1), (1, 0, 0, 1)], xk, x_first_sib, cp, c_sib, "grad_a"
     )
     r_up = over_z(b_20[0], 1)
     r_down = over_z(b_21[0], -1)
@@ -424,10 +508,8 @@
     fl_down = over_z(add(a_own[1, half:], r_a[1, half:], p_down), -1)
 
     gain_row = lax.dynamic_slice(gain_float, (fsdp * 512,), (512,))[None, :]
-    grad, squares, late = total(
-        [a_own[2], r_a[2], fe_up, fl_up, fe_down, fl_down, b_mine, r_b], gain_row, value_weight
-    )
-    late = lax.all_gather(late, "fsdp", axis=0, tiled=True)
+    grad, squares = total([a_own[2], r_a[2], fe_up, fl_up, fe_down, fl_down, b_mine, r_b], gain_row)
+    late = lax.all_gather(late_weights(value_weight, l_up), "fsdp", axis=0, tiled=True)
 
     squares = squares + over_core(squares)
     squares = squares + over_x(squares)
@@ -435,18 +517,19 @@
 
     first, second, n_0, n_1, n_2, n_3 = adam(columns, squares, grad, adam_first, adam_second, value_weight)
 
-    input_grad = input_gradient(core[None], xk, xs, cp, inv, gain_float.reshape(16, 1, 512), early, late)
+    gain = gain_float.reshape(16, 1, 512)
+    q_early, m_early = early_product(core[None], xk, xs, cp, gain, early)
+    input_grad = input_gradient(core[None], xk, xs, cp, inv, gain, q_early, m_early, late)
 
     m_1 = over_y(n_1, 1)
     m_2 = over_y(n_2, 2)
     m_3 = over_y(n_3, 3)
-    summed = n_0.astype(F32) + m_1.astype(F32) + m_2.astype(F32) + m_3.astype(F32)
-    inner_total = summed[0] + over_x_hi(summed[1].astype(BF16)).astype(F32)
-    outer_grad = anchor - inner_total / 8
+    summed = add(n_0, m_1, m_2, m_3)
+    inner_total = summed.astype(F32) + over_x_hi(summed[::-1]).astype(F32)
+    sent = (kept + (1.0 - outer_1) / 8 * inner_total).astype(BF16)
+    outer_grad = anchor - inner_total[0] / 8
     new_momentum = outer_beta * outer_momentum + outer_grad
     new_anchor = anchor - outer_rate * (outer_grad + outer_beta * new_momentum)
-    sent = new_anchor.astype(BF16)
-    sent = jnp.stack([sent, over_x_hi(sent)])
     parts = [sent, over_y(sent, 3), over_y(sent, 2), over_y(sent, 1)]
     synced_weight = place_columns(columns, parts)
     return (input_grad, first, second, synced_weight, new_momentum, new_anchor)

time: 212 us -> 285 us (1.34); the launches traced: 211 us -> 280 us
  waiting for transfers between devices: 80.2 us -> 142 us
  Pallas kernels: 56.6 us -> 62.6 us
  other arithmetic: 7.68 us -> 11.7 us
    ppermute x15, waiting for transfers between devices: 39.9 us -> 93.6 us  [over_z(): lax.ppermute(value, 'fsdp', [(i, (i + 4 * step) % 16) for i in range(16)])]
    ppermute x4, waiting for transfers between devices: 1 us -> 15.9 us  [over_x(): return lax.ppermute(value, 'fsdp', [(i, i ^ 2) for i in range(16)])]
    all_gather x1, waiting for transfers between devices: 8.41 us -> 0.01 us  [on_device(): lax.all_gather(late_weights(value_weight, l_up), 'fsdp', axis=0, tiled=True)]
    pallas_call x0 -> x2, Pallas kernels: none -> 6.99 us  [the longest x1 4.83 us: early_product(): pl.pallas_call(early_kernel, grid_spec=pltpu.PrefetchScalarGridSpec(num_s...]
    ppermute x3 -> x4, starting transfers between devices: 4.18 us -> 8.83 us  [over_core(): return lax.ppermute(value, 'fsdp', [(i, i ^ 1) for i in range(16)])]
    convert_element_type x7 -> x8, other arithmetic: 3.16 us -> 7.56 us  [add(): return total_value.astype(BF16)]
    ppermute x4, starting transfers between devices: 5.17 us -> 1.55 us  [over_x(): return lax.ppermute(value, 'fsdp', [(i, i ^ 2) for i in range(16)])]
    ppermute x6, waiting for transfers between devices: 13 us -> 16.1 us  [over_y(): lax.ppermute(value, 'rep', [(i, (i + 2 * step) % 8) for i in range(8)])]
  transfers between devices with their start and end apart: 32 -> 33, of which waited for: 22 -> 21; matrix products, arithmetic and copies ran while one was open for 5% -> 5% of each run, Pallas kernels for 19% -> 17%
where the time goes in v3:
time: 285 us; the launch traced here: 280 us
  waiting for transfers between devices  142 us (50%)
  Pallas kernels  62.6 us (22%)
  starting transfers between devices  40.8 us (14%)
  between operations  14.3 us (5%)
  other arithmetic  11.7 us (4%)
  local copies, waits for them, and re-layouts  9.12 us (3%)
    ppermute x15, waiting for transfers between devices, over_z(): lax.ppermute(value, 'fsdp', [(i, (i + 4 * step) % 16) for i in range(16)])  93.6 us
    pallas_call x2, Pallas kernels, grad_blocks(): pl.pallas_call(functools.partial(grad_kernel, outputs), grid_spec=pltpu.P...  16.6 us
    ppermute x6, waiting for transfers between devices, over_y(): lax.ppermute(value, 'rep', [(i, (i + 2 * step) % 8) for i in range(8)])  16.1 us
    ppermute x4, waiting for transfers between devices, over_x(): return lax.ppermute(value, 'fsdp', [(i, i ^ 2) for i in range(16)])  15.9 us
    ppermute x15, starting transfers between devices, over_z(): lax.ppermute(value, 'fsdp', [(i, (i + 4 * step) % 16) for i in range(16)])  15.3 us
    pallas_call x1, Pallas kernels, input_gradient(): pl.pallas_call(input_kernel, grid_spec=pltpu.PrefetchScalarGridSpec(num_s...  15 us
    ppermute x6, starting transfers between devices, over_y(): lax.ppermute(value, 'rep', [(i, (i + 2 * step) % 8) for i in range(8)])  10.6 us
    ppermute x2, waiting for transfers between devices, over_x_hi(): return lax.ppermute(value, 'rep', [(i, i ^ 1) for i in range(8)])  9.11 us
  transfers between devices with their start and end apart: 33, of which 21 were waited for; matrix products, arithmetic and copies ran while one was open for 5% of the time, Pallas kernels for 17%

profile of v3, /device:TPU:1, one launch (start us, length us, event | category | flops | bytes accessed | tf_op | source)
XLA Modules:
  0.0 280.2 jit_solution(7480407158986794568)
XLA Ops:
  7.2 1.7 slice.48
  9.6 8.1 %prep.1 = (bf16[8,320,512]{2,1,0:T(8,128)(2,1)}, bf16[8,320,512]{2,1,0:T(8,128)(2,1)}, bf16[2,320,512]{2,1,0:T(8,128)(2,1)}, bf16[320,1024]{1,0:T(8,128)(2,1)}, f32[320,128]{1,0:T(8,128)}) custom-call(s32[2]{0:T(128)} %pad_add_fusion.core_ref, s32[1,64]{1,0:T(1,128)} %index_ref.1, bf16[1,256,8192]{2,1,0:T(8,128)(2,1)} %h_ref.1, bf16[1,128,8192]{2,1,0:T(8,128)(2,1)} %b_ref.1, ...), custom_call_target="tpu_custom_call" | custom-call | flops 2000000000 | bytes 12000000 | tf_op jit(solution)/shard_map/prep/pallas_call | solution.py:107
  17.7 1.5 collective-permute-start
  20.3 5.0 %collective-permute-done.1.cs_ref = bf16[320,1024]{1,0:T(8,128)(2,1)} collective-permute-done((bf16[320,1024]{1,0:T(8,128)(2,1)}, bf16[320,1024]{1,0:T(8,128)(2,1)}, u32[]{:S(2)}, u32[]{:S(2)}) %collective-permute-start.1) | collective-permute-done | bytes 655392 | tf_op jit(solution)/shard_map/ppermute | solution.py:42
  25.3 0.9 collective-permute-done.2.xs_ref
  26.2 5.5 %grad_a.1 = (bf16[1,576,512]{2,1,0:T(8,128)(2,1)}, bf16[1,576,512]{2,1,0:T(8,128)(2,1)}, bf16[1,448,512]{2,1,0:T(8,128)(2,1)}, bf16[1,448,512]{2,1,0:T(8,128)(2,1)}) custom-call(s32[5]{0:T(128)} %pad_add_fusion.1.table_ref, bf16[8,320,512]{2,1,0:T(8,128)(2,1)} %get-tuple-element.35.xk_ref, bf16[2,320,512]{2,1,0:T(8,128)(2,1)} %collective-permute-done.2.xs_ref, ...), custom_call_target="tpu_custom_call" | custom-call | flops 1342177280 | bytes 3400000 | tf_op jit(solution)/shard_map/grad_a/pallas_call | solution.py:175
  31.8 1.7 collective-permute-start.3
  33.5 0.7 stack.60.table_ref
  34.2 1.5 copy-done.18
  35.7 11.1 %grad_b.1 = (bf16[1,576,512]{2,1,0:T(8,128)(2,1)}, bf16[1,576,512]{2,1,0:T(8,128)(2,1)}, bf16[1,576,512]{2,1,0:T(8,128)(2,1)}, bf16[1,576,512]{2,1,0:T(8,128)(2,...) custom-call(s32[5]{0:T(128)} %stack.60.table_ref, ...), custom_call_target="tpu_custom_call" | custom-call | flops 4026531840 | bytes 10200000 | tf_op jit(solution)/shard_map/grad_b/pallas_call | solution.py:175
  46.8 10.5 %collective-permute-done.3 = bf16[576,512]{1,0:T(8,128)(2,1)S(1)} collective-permute-done((bf16[576,512]{1,0:T(8,128)(2,1)}, bf16[576,512]{1,0:T(8,128)(2,1)S(1)}, u32[]{:S(2)}, u32[]{:S(2)}) %collective-permute-start.3) | collective-permute-done | bytes 589856 | tf_op jit(solution)/shard_map/ppermute | solution.py:50
  57.3 1.2 fusion.5
  58.5 2.2 collective-permute-start.4
  60.7 13.9 %collective-permute-done.4.after_ref = bf16[576,512]{1,0:T(8,128)(2,1)S(1)} collective-permute-done((bf16[576,512]{1,0:T(8,128)(2,1)S(1)}, bf16[576,512]{1,0:T(8,128)(2,1)S(1)}, u32[]{:S(2)}, u32[]{:S(2)}) %collective-permute-start.4) | collective-permute-done | bytes 589856 | tf_op jit(solution)/shard_map/ppermute | solution.py:50
  74.6 0.8 copy-done
  75.4 2.2 late_weights.1
  77.6 1.3 collective-permute-start.15
  79.0 1.3 collective-permute-start.5
  80.3 12.5 %collective-permute-done.15 = bf16[576,512]{1,0:T(8,128)(2,1)S(1)} collective-permute-done((bf16[576,512]{1,0:T(8,128)(2,1)S(1)}, bf16[576,512]{1,0:T(8,128)(2,1)S(1)}, u32[]{:S(2)}, u32[]{:S(2)}) %collective-permute-start.15) | collective-permute-done | bytes 589856 | tf_op jit(solution)/shard_map/ppermute | solution.py:50
  92.8 1.0 fusion
  93.7 0.7 collective-permute-start.16
  94.4 0.8 collective-permute-start.14
  95.8 1.9 collective-permute-start.13
  97.7 1.4 fusion.7
  99.2 0.8 slice_bitcast_fusion.1.a0
  100.0 20.4 %collective-permute-done.16 = bf16[576,512]{1,0:T(8,128)(2,1)} collective-permute-done((bf16[576,512]{1,0:T(8,128)(2,1)}, bf16[576,512]{1,0:T(8,128)(2,1)}, u32[]{:S(2)}, u32[]{:S(2)}) %collective-permute-start.16) | collective-permute-done | bytes 589856 | tf_op jit(solution)/shard_map/ppermute | solution.py:50
  120.4 1.5 fusion.2
  122.0 23.7 %collective-permute-done.13 = bf16[576,512]{1,0:T(8,128)(2,1)S(1)} collective-permute-done((bf16[576,512]{1,0:T(8,128)(2,1)}, bf16[576,512]{1,0:T(8,128)(2,1)S(1)}, u32[]{:S(2)}, u32[]{:S(2)}) %collective-permute-start.13) | collective-permute-done | bytes 589856 | tf_op jit(solution)/shard_map/ppermute | solution.py:50
  145.7 1.0 fusion.4.b0
  146.8 8.8 %collective-permute-done.11 = bf16[224,512]{1,0:T(8,128)(2,1)S(1)} collective-permute-done((bf16[224,512]{1,0:T(8,128)(2,1)S(1)}, bf16[224,512]{1,0:T(8,128)(2,1)S(1)}, u32[]{:S(2)}, u32[]{:S(2)}) %collective-permute-start.11) | collective-permute-done | bytes 229408 | tf_op jit(solution)/shard_map/ppermute | solution.py:50
  155.8 1.5 collective-permute-start.9
  157.4 1.4 collective-permute-start.10
  158.9 0.9 slice_bitcast_fusion.a1
  159.8 13.4 %collective-permute-done.17.b1 = bf16[576,512]{1,0:T(8,128)(2,1)S(1)} collective-permute-done((bf16[576,512]{1,0:T(8,128)(2,1)S(1)}, bf16[576,512]{1,0:T(8,128)(2,1)S(1)}, u32[]{:S(2)}, u32[]{:S(2)}) %collective-permute-start.17) | collective-permute-done | bytes 589856 | tf_op jit(solution)/shard_map/ppermute | solution.py:46
  173.2 3.8 %collective-permute-done.10.de = bf16[224,512]{1,0:T(8,128)(2,1)S(1)} collective-permute-done((bf16[224,512]{1,0:T(8,128)(2,1)S(1)}, bf16[224,512]{1,0:T(8,128)(2,1)S(1)}, u32[]{:S(2)}, u32[]{:S(2)}) %collective-permute-start.10) | collective-permute-done | bytes 229408 | tf_op jit(solution)/shard_map/ppermute | solution.py:50
  177.7 4.5 %total.1 = (f32[512,1024]{1,0:T(8,128)}, f32[8,128]{1,0:T(8,128)}) custom-call(bf16[448,512]{1,0:T(8,128)(2,1)} %slice_bitcast_fusion.1.a0, bf16[448,512]{1,0:T(8,128)(2,1)} %slice_bitcast_fusion.a1, bf16[224,512]{1,0:T(8,128)(2,1)} %copy-done.16, bf16[224,512]{1,0:T(8,128)(2,1)} %copy-done.14, bf16[224,512]{1,0:T(8,128)(2,1)} %copy-done.15, ...), custom_call_target="tpu_custom_call" | custom-call | flops 5000000 | bytes 5000000 | tf_op jit(solution)/shard_map/total/pallas_call | solution.py:236
  182.2 6.8 %collective-permute-start.18 = (f32[8,128]{1,0:T(8,128)}, f32[8,128]{1,0:T(8,128)S(1)}, u32[]{:S(2)}, u32[]{:S(2)}) collective-permute-start(f32[8,128]{1,0:T(8,128)} %get-tuple-element.52), channel_id=1, source_target_pairs={{0,1},{1,0},{2,3},{3,2},{4,5},{5,4},{6,7},{7,6},{8,9},{9,8},{10,11... | collective-permute-start | bytes 12296 | tf_op jit(solution)/shard_map/ppermute | solution.py:42
  189.0 1.0 collective-permute-done.18
  190.7 2.5 collective-permute-done.19
  193.2 1.6 collective-permute-start.21
  194.8 2.1 collective-permute-start.22
  196.9 0.7 stack.67.table_ref
  198.2 7.9 %adam.1 = (f32[1,512,1024]{2,1,0:T(8,128)}, f32[1,512,1024]{2,1,0:T(8,128)}, bf16[2,512,128]{2,1,0:T(8,128)(2,1)}, bf16[2,512,128]{2,1,0:T(8,128)(2,1)}, bf16[2,...) custom-call(s32[5]{0:T(128)} %stack.67.table_ref, f32[8,128]{1,0:T(8,128)} %add_add_fusion.sq_ref, ...), custom_call_target="tpu_custom_call" | custom-call | flops 20000000 | bytes 12000000 | tf_op jit(solution)/shard_map/adam/pallas_call | solution.py:279
  206.2 1.0 collective-permute-start.24
  207.2 2.3 collective-permute-start.25
  209.5 1.2 collective-permute-start.26
  210.7 2.2 collective-permute-done.24
  212.9 5.6 %collective-permute-done.25 = bf16[2,512,128]{2,1,0:T(8,128)(2,1)S(1)} collective-permute-done((bf16[2,512,128]{2,1,0:T(8,128)(2,1)}, bf16[2,512,128]{2,1,0:T(8,128)(2,1)S(1)}, u32[]{:S(2)}, u32[]{:S(2)}) %collective-permute-start.25) | collective-permute-done | bytes 262176 | tf_op jit(solution)/shard_map/ppermute | solution.py:58
  218.4 0.8 collective-permute-done.26
  219.3 1.2 add_convert_fusion
  220.5 2.2 collective-permute-start.27
  222.7 4.6 %collective-permute-done.27 = bf16[2,512,128]{2,1,0:T(8,128)(2,1)S(1)} collective-permute-done((bf16[2,512,128]{2,1,0:T(8,128)(2,1)S(1)}, bf16[2,512,128]{2,1,0:T(8,128)(2,1)S(1)}, u32[]{:S(2)}, u32[]{:S(2)}) %collective-permute-start.27) | collective-permute-done | bytes 262176 | tf_op jit(solution)/shard_map/ppermute | solution.py:54
  227.4 0.9 multiply_subtract_fusion
  228.3 2.2 collective-permute-start.23
  230.4 4.6 %collective-permute-done.23 = f32[512,128]{1,0:T(8,128)S(1)} collective-permute-done((f32[512,128]{1,0:T(8,128)S(1)}, f32[512,128]{1,0:T(8,128)S(1)}, u32[]{:S(2)}, u32[]{:S(2)}) %collective-permute-start.23) | collective-permute-done | bytes 262176 | tf_op jit(solution)/shard_map/ppermute | solution.py:54
  235.1 3.9 %collective-permute-start.28 = (bf16[2,512,128]{2,1,0:T(8,128)(2,1)S(1)}, bf16[2,512,128]{2,1,0:T(8,128)(2,1)S(1)}, u32[]{:S(2)}, u32[]{:S(2)}) collective-permute-start(bf16[2,512,128]{2,1,0:T(8,128)(2,1)S(1)} %fusion.6.refs_0_), channel_id=1, source_target_pairs={{0,96},{16,112},{32,0},{48,16},{64,32},{80,48},{96,64},{112,80},{1... | collective-permute-start | bytes 786440 | tf_op jit(solution)/shard_map/ppermute | solution.py:58
  239.0 2.2 collective-permute-start.29
  241.7 1.4 collective-permute-done.28.refs_1_
  243.1 2.7 collective-permute-done.29.refs_2_
  245.8 3.5 %collective-permute-done.30.refs_3_ = bf16[2,512,128]{2,1,0:T(8,128)(2,1)S(1)} collective-permute-done((bf16[2,512,128]{2,1,0:T(8,128)(2,1)S(1)}, bf16[2,512,128]{2,1,0:T(8,128)(2,1)S(1)}, u32[]{:S(2)}, u32[]{:S(2)}) %collective-permute-start.30) | collective-permute-done | bytes 262176 | tf_op jit(solution)/shard_map/ppermute | solution.py:58
  249.3 0.7 copy-done.10
  250.0 3.5 %place.1 = bf16[512,1024]{1,0:T(8,128)(2,1)} custom-call(s32[5]{0:T(128)} %stack.67.table_ref, bf16[2,512,128]{2,1,0:T(8,128)(2,1)} %copy-done.3, bf16[2,512,128]{2,1,0:T(8,128)(2,1)} %copy-done.8, bf16[2,512,128]{2,1,0:T(8,128)(2,1)} %copy-done.9, bf16[2,512,128]{2,1,0:T(8,128)(2,1)} %copy-done.10), custom_call_target="tpu_custom_call" | custom-call | flops 1000000 | bytes 2000000 | tf_op jit(solution)/shard_map/place/pallas_call | solution.py:306
  253.5 4.8 %early_product.1 = (bf16[2,8,320,128]{3,2,1,0:T(8,128)(2,1)}, f32[320,128]{1,0:T(8,128)}) custom-call(s32[1]{0:T(128)} %bitcast.core_ref, bf16[320,1024]{1,0:T(8,128)(2,1)} %get-tuple-element.33.cp_ref.c_ref, f32[16,1,512]{2,1,0:T(1,128)} %bitcast.70, bf16[8,320,512]{2,1,0:T(8,128)(2,1)} %get-tuple-element.35.xk_ref, ...), custom_call_target="tpu_custom_call" | custom-call | flops 1400000000 | bytes 8000000 | tf_op jit(solution)/shard_map/early_product/pallas_call | solution.py:350
  258.4 15.0 %input_gradient.1 = bf16[1,320,8192]{2,1,0:T(8,128)(2,1)} custom-call(s32[1]{0:T(128)} %bitcast.core_ref, bf16[320,1024]{1,0:T(8,128)(2,1)} %get-tuple-element.33.cp_ref.c_ref, f32[320,128]{1,0:T(8,128)} %get-tuple-element.34.inv_ref, f32[16,1,512]{2,1,0:T(1,128)} %bitcast.71, bf16[8,320,512]{2,1,0:T(8,128)(2,1)} %get-tuple-element.35.xk_ref, ...), custom_call_target="tpu_custom_call" | custom-call | flops 5000000000 | bytes 30000000 | tf_op jit(solution)/shard_map/input_gradient/pallas_call | solution.py:416
  (78 shorter events, 6.3 us)
Async XLA Ops:
  7.2 246.4 %all-gather.6.cloned.1.call-start = ((), (), s32[]{:S(2)}) async-start(), calls=%async_computation.1 | async-start | bytes 4456448 | tf_op jit(solution)/shard_map/all_gather | solution.py:469
  8.9 249.5 %all-gather.4.cloned.1.call-start = ((), (), s32[]{:S(2)}) async-start(), calls=%async_computation | async-start | bytes 13369344 | tf_op jit(solution)/shard_map/all_gather | solution.py:512
  17.7 16.5 %collective-permute-start = (bf16[8,320,512]{2,1,0:T(8,128)(2,1)}, bf16[8,320,512]{2,1,0:T(8,128)(2,1)S(1)}, u32[]{:S(2)}, u32[]{:S(2)}) collective-permute-start(bf16[8,320,512]{2,1,0:T(8,128)(2,1)} %get-tuple-element.36.xs_ref), channel_id=1, source_target_pairs={{0,1},{1,0},{2,3},{3,2},{4,5},{5,4},{6,7},{7,6},{8,9},{9,8},{10,11... | collective-permute-start | bytes 7864328 | tf_op jit(solution)/shard_map/ppermute | solution.py:42
  19.2 6.1 %collective-permute-start.1 = (bf16[320,1024]{1,0:T(8,128)(2,1)}, bf16[320,1024]{1,0:T(8,128)(2,1)}, u32[]{:S(2)}, u32[]{:S(2)}) collective-permute-start(bf16[320,1024]{1,0:T(8,128)(2,1)} %get-tuple-element.33.cp_ref.c_ref), channel_id=1, source_target_pairs={{0,1},{1,0},{2,3},{3,2},{4,5},{5,4},{6,7},{7,6},{8,9},{9,8},{10,11... | collective-permute-start | bytes 1966088 | tf_op jit(solution)/shard_map/ppermute | solution.py:42
  19.3 6.9 %collective-permute-start.2 = (bf16[2,320,512]{2,1,0:T(8,128)(2,1)}, bf16[2,320,512]{2,1,0:T(8,128)(2,1)}, u32[]{:S(2)}, u32[]{:S(2)}) collective-permute-start(bf16[2,320,512]{2,1,0:T(8,128)(2,1)} %get-tuple-element.40), channel_id=1, source_target_pairs={{0,1},{1,0},{2,3},{3,2},{4,5},{5,4},{6,7},{7,6},{8,9},{9,8},{10,11... | collective-permute-start | bytes 1966088 | tf_op jit(solution)/shard_map/ppermute | solution.py:42
  31.8 25.5 %collective-permute-start.3 = (bf16[576,512]{1,0:T(8,128)(2,1)}, bf16[576,512]{1,0:T(8,128)(2,1)S(1)}, u32[]{:S(2)}, u32[]{:S(2)}) collective-permute-start(bf16[576,512]{1,0:T(8,128)(2,1)} %bitcast.77), channel_id=1, source_target_pairs={{0,4},{1,5},{2,6},{3,7},{4,8},{5,9},{6,10},{7,11},{8,12},{9,13},{1... | collective-permute-start | bytes 1769480 | tf_op jit(solution)/shard_map/ppermute | solution.py:50
  34.2 1.5 copy-start.18
  58.5 19.1 %copy-start.19 = (bf16[1,576,512]{2,1,0:T(8,128)(2,1)S(1)}, bf16[1,576,512]{2,1,0:T(8,128)(2,1)}, u32[]{:S(2)}) copy-start(bf16[1,576,512]{2,1,0:T(8,128)(2,1)} %get-tuple-element.51) | copy-start | bytes 1769476
  58.5 34.3 %copy-start.5 = (bf16[1,576,512]{2,1,0:T(8,128)(2,1)S(1)}, bf16[1,576,512]{2,1,0:T(8,128)(2,1)}, u32[]{:S(2)}) copy-start(bf16[1,576,512]{2,1,0:T(8,128)(2,1)} %get-tuple-element.50) | copy-start | bytes 1769476
  58.5 16.1 %collective-permute-start.4 = (bf16[576,512]{1,0:T(8,128)(2,1)S(1)}, bf16[576,512]{1,0:T(8,128)(2,1)S(1)}, u32[]{:S(2)}, u32[]{:S(2)}) collective-permute-start(bf16[576,512]{1,0:T(8,128)(2,1)S(1)} %fusion.5), channel_id=1, source_target_pairs={{0,4},{1,5},{2,6},{3,7},{4,8},{5,9},{6,10},{7,11},{8,12},{9,13},{1... | collective-permute-start | bytes 1769480 | tf_op jit(solution)/shard_map/ppermute | solution.py:50
  74.6 0.8 copy-start
  77.5 17.7 %copy-start.17 = (bf16[8192]{0:T(1024)(128)(2,1)S(1)}, bf16[8192]{0:T(1024)(128)(2,1)}, u32[]{:S(2)}) copy-start(bf16[8192]{0:T(1024)(128)(2,1)} %param.14) | copy-start | bytes 49156
  77.6 15.2 %collective-permute-start.15 = (bf16[576,512]{1,0:T(8,128)(2,1)S(1)}, bf16[576,512]{1,0:T(8,128)(2,1)S(1)}, u32[]{:S(2)}, u32[]{:S(2)}) collective-permute-start(bf16[576,512]{1,0:T(8,128)(2,1)S(1)} %bitcast.74), channel_id=1, source_target_pairs={{0,12},{1,13},{2,14},{3,15},{4,0},{5,1},{6,2},{7,3},{8,4},{9,5},{1... | collective-permute-start | bytes 1769480 | tf_op jit(solution)/shard_map/ppermute | solution.py:50
  78.8 18.9 %collective-permute-start.7 = (bf16[448,512]{1,0:T(8,128)(2,1)}, bf16[448,512]{1,0:T(8,128)(2,1)}, u32[]{:S(2)}, u32[]{:S(2)}) collective-permute-start(bf16[448,512]{1,0:T(8,128)(2,1)} %bitcast.21), channel_id=1, source_target_pairs={{0,2},{1,3},{2,0},{3,1},{4,6},{5,7},{6,4},{7,5},{8,10},{9,11},{10,... | collective-permute-start | bytes 1376264 | tf_op jit(solution)/shard_map/ppermute | solution.py:46
  79.0 76.5 %collective-permute-start.5 = (bf16[3,448,512]{2,1,0:T(8,128)(2,1)}, bf16[3,448,512]{2,1,0:T(8,128)(2,1)S(1)}, u32[]{:S(2)}, u32[]{:S(2)}) collective-permute-start(bf16[3,448,512]{2,1,0:T(8,128)(2,1)} %get-tuple-element.43), channel_id=1, source_target_pairs={{0,2},{1,3},{2,0},{3,1},{4,6},{5,7},{6,4},{7,5},{8,10},{9,11},{10,... | collective-permute-start | bytes 4128776 | tf_op jit(solution)/shard_map/ppermute | solution.py:46
  92.8 6.4 %copy-start.2 = (bf16[3,448,512]{2,1,0:T(8,128)(2,1)S(1)}, bf16[3,448,512]{2,1,0:T(8,128)(2,1)}, u32[]{:S(2)}) copy-start(bf16[3,448,512]{2,1,0:T(8,128)(2,1)} %get-tuple-element.42) | copy-start | bytes 4128772
  93.7 26.7 %copy-start.7 = (bf16[1,576,512]{2,1,0:T(8,128)(2,1)S(1)}, bf16[1,576,512]{2,1,0:T(8,128)(2,1)}, u32[]{:S(2)}) copy-start(bf16[1,576,512]{2,1,0:T(8,128)(2,1)} %get-tuple-element.48) | copy-start | bytes 1769476
  93.7 26.7 %collective-permute-start.16 = (bf16[576,512]{1,0:T(8,128)(2,1)}, bf16[576,512]{1,0:T(8,128)(2,1)}, u32[]{:S(2)}, u32[]{:S(2)}) collective-permute-start(bf16[576,512]{1,0:T(8,128)(2,1)} %fusion), channel_id=1, source_target_pairs={{0,12},{1,13},{2,14},{3,15},{4,0},{5,1},{6,2},{7,3},{8,4},{9,5},{1... | collective-permute-start | bytes 1769480 | tf_op jit(solution)/shard_map/ppermute | solution.py:50
  94.4 26.0 %collective-permute-start.14 = (bf16[576,512]{1,0:T(8,128)(2,1)}, bf16[576,512]{1,0:T(8,128)(2,1)}, u32[]{:S(2)}, u32[]{:S(2)}) collective-permute-start(bf16[576,512]{1,0:T(8,128)(2,1)} %bitcast.76), channel_id=1, source_target_pairs={{0,4},{1,5},{2,6},{3,7},{4,8},{5,9},{6,10},{7,11},{8,12},{9,13},{1... | collective-permute-start | bytes 1769480 | tf_op jit(solution)/shard_map/ppermute | solution.py:50
  95.8 49.9 %collective-permute-start.13 = (bf16[576,512]{1,0:T(8,128)(2,1)}, bf16[576,512]{1,0:T(8,128)(2,1)S(1)}, u32[]{:S(2)}, u32[]{:S(2)}) collective-permute-start(bf16[576,512]{1,0:T(8,128)(2,1)} %bitcast.75), channel_id=1, source_target_pairs={{0,12},{1,13},{2,14},{3,15},{4,0},{5,1},{6,2},{7,3},{8,4},{9,5},{1... | collective-permute-start | bytes 1769480 | tf_op jit(solution)/shard_map/ppermute | solution.py:50
  99.1 56.4 %collective-permute-start.11 = (bf16[224,512]{1,0:T(8,128)(2,1)S(1)}, bf16[224,512]{1,0:T(8,128)(2,1)S(1)}, u32[]{:S(2)}, u32[]{:S(2)}) collective-permute-start(bf16[224,512]{1,0:T(8,128)(2,1)S(1)} %get-tuple-element.66), channel_id=1, source_target_pairs={{0,12},{1,13},{2,14},{3,15},{4,0},{5,1},{6,2},{7,3},{8,4},{9,5},{1... | collective-permute-start | bytes 688136 | tf_op jit(solution)/shard_map/ppermute | solution.py:50
  100.0 45.7 %copy-start.1 = (bf16[576,512]{1,0:T(8,128)(2,1)S(1)}, bf16[576,512]{1,0:T(8,128)(2,1)}, u32[]{:S(2)}) copy-start(bf16[576,512]{1,0:T(8,128)(2,1)} %copy-done) | copy-start | bytes 1769476
  100.0 45.7 %copy-start.6 = (bf16[1,576,512]{2,1,0:T(8,128)(2,1)S(1)}, bf16[1,576,512]{2,1,0:T(8,128)(2,1)}, u32[]{:S(2)}) copy-start(bf16[1,576,512]{2,1,0:T(8,128)(2,1)} %get-tuple-element.46) | copy-start | bytes 1769476
  120.4 35.1 %collective-permute-start.8 = (bf16[224,512]{1,0:T(8,128)(2,1)S(1)}, bf16[224,512]{1,0:T(8,128)(2,1)S(1)}, u32[]{:S(2)}, u32[]{:S(2)}) collective-permute-start(bf16[224,512]{1,0:T(8,128)(2,1)S(1)} %get-tuple-element.67), channel_id=1, source_target_pairs={{0,4},{1,5},{2,6},{3,7},{4,8},{5,9},{6,10},{7,11},{8,12},{9,13},{1... | collective-permute-start | bytes 688136 | tf_op jit(solution)/shard_map/ppermute | solution.py:50
  121.9 51.3 %collective-permute-start.17 = (bf16[576,512]{1,0:T(8,128)(2,1)S(1)}, bf16[576,512]{1,0:T(8,128)(2,1)S(1)}, u32[]{:S(2)}, u32[]{:S(2)}) collective-permute-start(bf16[576,512]{1,0:T(8,128)(2,1)S(1)} %fusion.2), channel_id=1, source_target_pairs={{0,2},{1,3},{2,0},{3,1},{4,6},{5,7},{6,4},{7,5},{8,10},{9,11},{10,... | collective-permute-start | bytes 1769480 | tf_op jit(solution)/shard_map/ppermute | solution.py:46
  155.7 17.5 %collective-permute-start.12 = (bf16[224,512]{1,0:T(8,128)(2,1)S(1)}, bf16[224,512]{1,0:T(8,128)(2,1)S(1)}, u32[]{:S(2)}, u32[]{:S(2)}) collective-permute-start(bf16[224,512]{1,0:T(8,128)(2,1)S(1)} %get-tuple-element.62), channel_id=1, source_target_pairs={{0,12},{1,13},{2,14},{3,15},{4,0},{5,1},{6,2},{7,3},{8,4},{9,5},{1... | collective-permute-start | bytes 688136 | tf_op jit(solution)/shard_map/ppermute | solution.py:50
  155.8 17.4 %collective-permute-start.9 = (bf16[224,512]{1,0:T(8,128)(2,1)S(1)}, bf16[224,512]{1,0:T(8,128)(2,1)S(1)}, u32[]{:S(2)}, u32[]{:S(2)}) collective-permute-start(bf16[224,512]{1,0:T(8,128)(2,1)S(1)} %get-tuple-element.63), channel_id=1, source_target_pairs={{0,4},{1,5},{2,6},{3,7},{4,8},{5,9},{6,10},{7,11},{8,12},{9,13},{1... | collective-permute-start | bytes 688136 | tf_op jit(solution)/shard_map/ppermute | solution.py:50
  157.4 19.6 %collective-permute-start.10 = (bf16[224,512]{1,0:T(8,128)(2,1)S(1)}, bf16[224,512]{1,0:T(8,128)(2,1)S(1)}, u32[]{:S(2)}, u32[]{:S(2)}) collective-permute-start(bf16[224,512]{1,0:T(8,128)(2,1)S(1)} %get-tuple-element.64), channel_id=1, source_target_pairs={{0,12},{1,13},{2,14},{3,15},{4,0},{5,1},{6,2},{7,3},{8,4},{9,5},{1... | collective-permute-start | bytes 688136 | tf_op jit(solution)/shard_map/ppermute | solution.py:50
  158.7 18.2 %collective-permute-start.6 = (bf16[224,512]{1,0:T(8,128)(2,1)S(1)}, bf16[224,512]{1,0:T(8,128)(2,1)S(1)}, u32[]{:S(2)}, u32[]{:S(2)}) collective-permute-start(bf16[224,512]{1,0:T(8,128)(2,1)S(1)} %get-tuple-element.65), channel_id=1, source_target_pairs={{0,4},{1,5},{2,6},{3,7},{4,8},{5,9},{6,10},{7,11},{8,12},{9,13},{1... | collective-permute-start | bytes 688136 | tf_op jit(solution)/shard_map/ppermute | solution.py:50
  173.2 3.8 %copy-start.4 = (bf16[576,512]{1,0:T(8,128)(2,1)}, bf16[576,512]{1,0:T(8,128)(2,1)S(1)}, u32[]{:S(2)}) copy-start(bf16[576,512]{1,0:T(8,128)(2,1)S(1)} %collective-permute-done.17.b1) | copy-start | bytes 1769476
  173.2 3.8 %copy-start.13 = (bf16[224,512]{1,0:T(8,128)(2,1)}, bf16[224,512]{1,0:T(8,128)(2,1)S(1)}, u32[]{:S(2)}) copy-start(bf16[224,512]{1,0:T(8,128)(2,1)S(1)} %collective-permute-done.12.dl) | copy-start | bytes 688132
  173.2 3.8 %copy-start.14 = (bf16[224,512]{1,0:T(8,128)(2,1)}, bf16[224,512]{1,0:T(8,128)(2,1)S(1)}, u32[]{:S(2)}) copy-start(bf16[224,512]{1,0:T(8,128)(2,1)S(1)} %collective-permute-done.9.ul) | copy-start | bytes 688132
  177.0 0.7 copy-start.15
  177.0 0.8 copy-start.16
  182.2 7.8 %collective-permute-start.18 = (f32[8,128]{1,0:T(8,128)}, f32[8,128]{1,0:T(8,128)S(1)}, u32[]{:S(2)}, u32[]{:S(2)}) collective-permute-start(f32[8,128]{1,0:T(8,128)} %get-tuple-element.52), channel_id=1, source_target_pairs={{0,1},{1,0},{2,3},{3,2},{4,5},{5,4},{6,7},{7,6},{8,9},{9,8},{10,11... | collective-permute-start | bytes 12296 | tf_op jit(solution)/shard_map/ppermute | solution.py:42
  190.7 2.5 collective-permute-start.19
  193.2 4.4 %collective-permute-start.20 = (f32[8,128]{1,0:T(8,128)S(1)}, f32[8,128]{1,0:T(8,128)S(1)}, u32[]{:S(2)}, u32[]{:S(2)}) collective-permute-start(f32[8,128]{1,0:T(8,128)S(1)} %add.181), channel_id=1, source_target_pairs={{0,4},{1,5},{2,6},{3,7},{4,8},{5,9},{6,10},{7,11},{8,12},{9,13},{1... | collective-permute-start | bytes 12296 | tf_op jit(solution)/shard_map/ppermute | solution.py:50
  193.2 4.4 %collective-permute-start.21 = (f32[8,128]{1,0:T(8,128)S(1)}, f32[8,128]{1,0:T(8,128)S(1)}, u32[]{:S(2)}, u32[]{:S(2)}) collective-permute-start(f32[8,128]{1,0:T(8,128)S(1)} %add.181), channel_id=1, source_target_pairs={{0,8},{1,9},{2,10},{3,11},{4,12},{5,13},{6,14},{7,15},{8,0},{9,1},... | collective-permute-start | bytes 12296 | tf_op jit(solution)/shard_map/ppermute | solution.py:50
  194.8 2.8 %collective-permute-start.22 = (f32[8,128]{1,0:T(8,128)S(1)}, f32[8,128]{1,0:T(8,128)S(1)}, u32[]{:S(2)}, u32[]{:S(2)}) collective-permute-start(f32[8,128]{1,0:T(8,128)S(1)} %add.181), channel_id=1, source_target_pairs={{0,12},{1,13},{2,14},{3,15},{4,0},{5,1},{6,2},{7,3},{8,4},{9,5},{1... | collective-permute-start | bytes 12296 | tf_op jit(solution)/shard_map/ppermute | solution.py:50
  206.2 6.7 %collective-permute-start.24 = (bf16[2,512,128]{2,1,0:T(8,128)(2,1)}, bf16[2,512,128]{2,1,0:T(8,128)(2,1)S(1)}, u32[]{:S(2)}, u32[]{:S(2)}) collective-permute-start(bf16[2,512,128]{2,1,0:T(8,128)(2,1)} %get-tuple-element.57), channel_id=1, source_target_pairs={{0,32},{16,48},{32,64},{48,80},{64,96},{80,112},{96,0},{112,16},{1... | collective-permute-start | bytes 786440 | tf_op jit(solution)/shard_map/ppermute | solution.py:58
  207.2 11.2 %collective-permute-start.25 = (bf16[2,512,128]{2,1,0:T(8,128)(2,1)}, bf16[2,512,128]{2,1,0:T(8,128)(2,1)S(1)}, u32[]{:S(2)}, u32[]{:S(2)}) collective-permute-start(bf16[2,512,128]{2,1,0:T(8,128)(2,1)} %get-tuple-element.58), channel_id=1, source_target_pairs={{0,64},{16,80},{32,96},{48,112},{64,0},{80,16},{96,32},{112,48},{1... | collective-permute-start | bytes 786440 | tf_op jit(solution)/shard_map/ppermute | solution.py:58
  209.5 9.8 %collective-permute-start.26 = (bf16[2,512,128]{2,1,0:T(8,128)(2,1)}, bf16[2,512,128]{2,1,0:T(8,128)(2,1)S(1)}, u32[]{:S(2)}, u32[]{:S(2)}) collective-permute-start(bf16[2,512,128]{2,1,0:T(8,128)(2,1)} %get-tuple-element.59), channel_id=1, source_target_pairs={{0,96},{16,112},{32,0},{48,16},{64,32},{80,48},{96,64},{112,80},{1... | collective-permute-start | bytes 786440 | tf_op jit(solution)/shard_map/ppermute | solution.py:58
  219.3 8.1 %copy-start.11 = (f32[512,128]{1,0:T(8,128)S(1)}, f32[512,128]{1,0:T(8,128)}, u32[]{:S(2)}) copy-start(f32[512,128]{1,0:T(8,128)} %param.18) | copy-start | bytes 786436
  219.3 8.1 %copy-start.12 = (f32[512,128]{1,0:T(8,128)S(1)}, f32[512,128]{1,0:T(8,128)}, u32[]{:S(2)}) copy-start(f32[512,128]{1,0:T(8,128)} %param.19) | copy-start | bytes 786436
  220.5 6.8 %collective-permute-start.27 = (bf16[2,512,128]{2,1,0:T(8,128)(2,1)S(1)}, bf16[2,512,128]{2,1,0:T(8,128)(2,1)S(1)}, u32[]{:S(2)}, u32[]{:S(2)}) collective-permute-start(bf16[2,512,128]{2,1,0:T(8,128)(2,1)S(1)} %rev.3), channel_id=1, source_target_pairs={{0,16},{16,0},{32,48},{48,32},{64,80},{80,64},{96,112},{112,96},{1... | collective-permute-start | bytes 786440 | tf_op jit(solution)/shard_map/ppermute | solution.py:54
  228.3 6.7 %collective-permute-start.23 = (f32[512,128]{1,0:T(8,128)S(1)}, f32[512,128]{1,0:T(8,128)S(1)}, u32[]{:S(2)}, u32[]{:S(2)}) collective-permute-start(f32[512,128]{1,0:T(8,128)S(1)} %get-tuple-element.68), channel_id=1, source_target_pairs={{0,16},{16,0},{32,48},{48,32},{64,80},{80,64},{96,112},{112,96},{1... | collective-permute-start | bytes 786440 | tf_op jit(solution)/shard_map/ppermute | solution.py:54
  235.1 14.2 %copy-start.3 = (bf16[2,512,128]{2,1,0:T(8,128)(2,1)}, bf16[2,512,128]{2,1,0:T(8,128)(2,1)S(1)}, u32[]{:S(2)}) copy-start(bf16[2,512,128]{2,1,0:T(8,128)(2,1)S(1)} %fusion.6.refs_0_) | copy-start | bytes 786436
  235.1 8.0 %collective-permute-start.28 = (bf16[2,512,128]{2,1,0:T(8,128)(2,1)S(1)}, bf16[2,512,128]{2,1,0:T(8,128)(2,1)S(1)}, u32[]{:S(2)}, u32[]{:S(2)}) collective-permute-start(bf16[2,512,128]{2,1,0:T(8,128)(2,1)S(1)} %fusion.6.refs_0_), channel_id=1, source_target_pairs={{0,96},{16,112},{32,0},{48,16},{64,32},{80,48},{96,64},{112,80},{1... | collective-permute-start | bytes 786440 | tf_op jit(solution)/shard_map/ppermute | solution.py:58
  239.0 6.8 %collective-permute-start.29 = (bf16[2,512,128]{2,1,0:T(8,128)(2,1)S(1)}, bf16[2,512,128]{2,1,0:T(8,128)(2,1)S(1)}, u32[]{:S(2)}, u32[]{:S(2)}) collective-permute-start(bf16[2,512,128]{2,1,0:T(8,128)(2,1)S(1)} %fusion.6.refs_0_), channel_id=1, source_target_pairs={{0,64},{16,80},{32,96},{48,112},{64,0},{80,16},{96,32},{112,48},{1... | collective-permute-start | bytes 786440 | tf_op jit(solution)/shard_map/ppermute | solution.py:58
  241.1 8.2 %collective-permute-start.30 = (bf16[2,512,128]{2,1,0:T(8,128)(2,1)S(1)}, bf16[2,512,128]{2,1,0:T(8,128)(2,1)S(1)}, u32[]{:S(2)}, u32[]{:S(2)}) collective-permute-start(bf16[2,512,128]{2,1,0:T(8,128)(2,1)S(1)} %fusion.6.refs_0_), channel_id=1, source_target_pairs={{0,32},{16,48},{32,64},{48,80},{64,96},{80,112},{96,0},{112,16},{1... | collective-permute-start | bytes 786440 | tf_op jit(solution)/shard_map/ppermute | solution.py:58
  243.1 6.2 %copy-start.8 = (bf16[2,512,128]{2,1,0:T(8,128)(2,1)}, bf16[2,512,128]{2,1,0:T(8,128)(2,1)S(1)}, u32[]{:S(2)}) copy-start(bf16[2,512,128]{2,1,0:T(8,128)(2,1)S(1)} %collective-permute-done.28.refs_1_) | copy-start | bytes 786436
  245.8 3.5 %copy-start.9 = (bf16[2,512,128]{2,1,0:T(8,128)(2,1)}, bf16[2,512,128]{2,1,0:T(8,128)(2,1)S(1)}, u32[]{:S(2)}) copy-start(bf16[2,512,128]{2,1,0:T(8,128)(2,1)S(1)} %collective-permute-done.29.refs_2_) | copy-start | bytes 786436
  249.3 0.7 copy-start.10
Sparse Core Ops, SparseCore 0:
  9.7 46.5 all-gather.5
  77.7 116.7 all-gather.3

commit v4 on v3

--- a/solution.py
+++ b/solution.py
@@ -141,8 +141,8 @@
 z_first = 1024 - x_first
 
 
-def grad_kernel(plan, table_ref, xk_ref, xs_ref, c_ref, cs_ref, *rest):
-    outs, (x_all, c_all) = rest[:-2], rest[-2:]
+def grad_kernel(plan, n_after, table_ref, xk_ref, xs_ref, c_ref, cs_ref, *rest):
+    outs, (x_all, c_all) = rest[n_after:-2], rest[-2:]
     step = pl.program_id(0)
     x = table_ref[4]
 
@@ -166,18 +166,18 @@
                         out_ref[...] = part[:, 512 * dx : 512 * dx + 512]
 
 
-def grad_blocks(place, chunks, outputs, xk, xs, c, cs, name):
+def grad_blocks(place, chunks, outputs, xk, xs, c, cs, after, name):
     z, x = place
     table = jnp.stack([(z + dz) % 4 for dz in chunks] + [jnp.int32(0)] * (4 - len(chunks)) + [x])
     x_spec = pl.BlockSpec((2, 320, 512), lambda t, tab: (tab[t], 0, 0))
     s_spec = x_spec if xs.shape[0] == 8 else pl.BlockSpec((2, 320, 512), lambda t, tab: (0, 0, 0))
     c_spec = pl.BlockSpec((320, 1024), lambda t, tab: (0, 0))
     return pl.pallas_call(
-        functools.partial(grad_kernel, outputs),
+        functools.partial(grad_kernel, outputs, len(after)),
         grid_spec=pltpu.PrefetchScalarGridSpec(
             num_scalar_prefetch=1,
             grid=(len(chunks),),
-            in_specs=[x_spec, s_spec, c_spec, c_spec],
+            in_specs=[x_spec, s_spec, c_spec, c_spec] + [pl.BlockSpec(memory_space=pl.ANY)] * len(after),
             out_specs=[
                 pl.BlockSpec(
                     (None, x_first if low else z_first, 512), lambda t, tab, s=s, n=n: (clip_index(t, s, n), 0, 0)
@@ -190,38 +190,37 @@
         compiler_params=params(60),
         cost_estimate=cost(len(chunks) * 2 * 640 * 1024 * 1024, len(chunks) * 3.4e6),
         name=name,
-    )(table, xk, xs, c, cs)
+    )(table, xk, xs, c, cs, *after)
 
 
 early_rows = 128
 
 
-def late_kernel(w_ref, after_ref, late_ref):
-    late_ref[...] = w_ref[early_rows:512, :]
+def late_kernel(w_ref, *rest):
+    rest[-1][...] = w_ref[early_rows:512, :]
 
 
 def late_weights(weight, after):
     return pl.pallas_call(
         late_kernel,
         grid=(1,),
-        in_specs=[pl.BlockSpec((None, 512, 1024), lambda t: (0, 0, 0)), pl.BlockSpec(memory_space=pl.ANY)],
+        in_specs=[pl.BlockSpec((None, 512, 1024), lambda t: (0, 0, 0))] + [pl.BlockSpec(memory_space=pl.ANY)] * len(after),
         out_specs=pl.BlockSpec((512 - early_rows, 1024), lambda t: (0, 0)),
         out_shape=sds((512 - early_rows, 1024), BF16),
         compiler_params=params(60),
         cost_estimate=cost(0, 2e6),
         name="late_weights",
-    )(weight, after)
-
-
-def total_kernel(a0, a1, ue, ul, de, dl, b0, b1, gain_ref, grad_ref, sq_ref):
+    )(weight, *after)
+
+
+def total_kernel(a0, a1, t1, t2, t3, b0, b1, gain_ref, after_ref, grad_ref, sq_ref):
     step = pl.program_id(0)
-    up = jnp.concatenate([ul[...], ue[...]], axis=0).astype(F32)
-    down = jnp.concatenate([de[...], dl[...]], axis=0).astype(F32)
-    top = (a0[...].astype(F32) + a1[...].astype(F32)) + (up + down)
+    top = a0[...].astype(F32) + a1[...].astype(F32)
+    top = top + t1[...].astype(F32) + t2[...].astype(F32) + t3[...].astype(F32)
     low = b0[...].astype(F32) + b1[...].astype(F32)
     both = jnp.concatenate([top, low], axis=0) * gain_ref[...]
     grad_ref[...] = both.T
-    square = jnp.sum((both * both).reshape(128, 8, 128), axis=0)
+    square = jnp.sum(lane_sum(both * both).reshape(128, 8, 128), axis=0)
 
     @pl.when(step == 0)
     def _():
@@ -232,26 +231,26 @@
         sq_ref[...] += square
 
 
-def total(parts, gain_row):
+def total(parts, gain_row, after):
     return pl.pallas_call(
         total_kernel,
-        grid=(4,),
-        in_specs=[pl.BlockSpec((p.shape[0], 128), lambda t: (0, t)) for p in parts]
-        + [pl.BlockSpec((1, 128), lambda t: (0, t))],
+        grid=(2,),
+        in_specs=[pl.BlockSpec((p.shape[0], 256), lambda t: (0, t)) for p in parts]
+        + [pl.BlockSpec((1, 256), lambda t: (0, t))]
+        + [pl.BlockSpec(memory_space=pl.ANY)] * len(after),
         out_specs=[
-            pl.BlockSpec((128, 1024), lambda t: (t, 0)),
+            pl.BlockSpec((256, 1024), lambda t: (t, 0)),
             pl.BlockSpec((8, 128), lambda t: (0, 0)),
         ],
         out_shape=[sds((512, 1024), F32), sds((8, 128), F32)],
         compiler_params=params(60),
         cost_estimate=cost(5e6, 5e6),
         name="total",
-    )(*parts, gain_row)
+    )(*parts, gain_row, *after)
 
 
 def adam_kernel(table_ref, sq_ref, grad_ref, m_ref, v_ref, w_ref, first_ref, second_ref, *rest):
     outs, new_ref = rest[:-1], rest[-1]
-    step = pl.program_id(0)
     squares = jnp.sum(sq_ref[...], axis=1, keepdims=True)
     squares = jnp.sum(squares, axis=0, keepdims=True)
     factor = jnp.minimum(1.0, clip_limit / jnp.sqrt(squares))
@@ -263,27 +262,24 @@
     root = second * lax.rsqrt(second) + adam_eps
     inverse = pl.reciprocal(root, approx=True)
     inverse = inverse * (2.0 - root * inverse)
-    new = w_ref[...].astype(F32) - inner_rate * first * inverse
-    new_ref[...] = new.astype(BF16)
+    new_ref[...] = (w_ref[...].astype(F32) - inner_rate * first * inverse).astype(BF16)
     for k, out_ref in enumerate(outs):
-
-        @pl.when(step == k)
-        def _(out_ref=out_ref):
-            for dx in range(2):
-                out_ref[dx] = new_ref[:, pl.ds(pl.multiple_of((table_ref[4] ^ dx) * 128, 128), 128)]
+        for dx in range(2):
+            column = pl.multiple_of((2 * table_ref[k] + (table_ref[4] ^ dx)) * 128, 128)
+            out_ref[dx] = new_ref[:, pl.ds(column, 128)]
 
 
 def adam(table, sq, grad, first_in, second_in, weight):
-    column = pl.BlockSpec((512, 256), lambda t, tab: (0, tab[t]))
-    lead = pl.BlockSpec((None, 512, 256), lambda t, tab: (0, 0, tab[t]))
+    rows = pl.BlockSpec((128, 1024), lambda t, tab: (t, 0))
+    lead = pl.BlockSpec((None, 128, 1024), lambda t, tab: (0, t, 0))
     return pl.pallas_call(
         adam_kernel,
         grid_spec=pltpu.PrefetchScalarGridSpec(
             num_scalar_prefetch=1,
             grid=(4,),
-            in_specs=[pl.BlockSpec((8, 128), lambda t, tab: (0, 0)), column, lead, lead, lead],
-            out_specs=[lead, lead] + [pl.BlockSpec((2, 512, 128), lambda t, tab: (0, 0, 0)) for k in range(4)],
-            scratch_shapes=[pltpu.VMEM((512, 256), BF16)],
+            in_specs=[pl.BlockSpec((8, 128), lambda t, tab: (0, 0)), rows, lead, lead, lead],
+            out_specs=[lead, lead] + [pl.BlockSpec((2, 128, 128), lambda t, tab: (0, t, 0)) for k in range(4)],
+            scratch_shapes=[pltpu.VMEM((128, 1024), BF16)],
         ),
         out_shape=[sds((1, 512, 1024), F32)] * 2 + [sds((2, 512, 128), BF16)] * 4,
         compiler_params=params(60),
@@ -293,13 +289,10 @@
 
 
 def place_kernel(table_ref, *refs):
-    step = pl.program_id(0)
     for k, in_ref in enumerate(refs[:-1]):
-
-        @pl.when(step == k)
-        def _(in_ref=in_ref):
-            for dx in range(2):
-                refs[-1][:, pl.ds(pl.multiple_of((table_ref[4] ^ dx) * 128, 128), 128)] = in_ref[dx]
+        for dx in range(2):
+            column = pl.multiple_of((2 * table_ref[k] + (table_ref[4] ^ dx)) * 128, 128)
+            refs[-1][:, pl.ds(column, 128)] = in_ref[dx]
 
 
 def place_columns(table, parts):
@@ -307,9 +300,9 @@
         place_kernel,
         grid_spec=pltpu.PrefetchScalarGridSpec(
             num_scalar_prefetch=1,
-            grid=(4,),
-            in_specs=[pl.BlockSpec((2, 512, 128), lambda t, tab: (0, 0, 0)) for k in range(4)],
-            out_specs=pl.BlockSpec((512, 256), lambda t, tab: (0, tab[t])),
+            grid=(2,),
+            in_specs=[pl.BlockSpec((2, 256, 128), lambda t, tab: (0, t, 0)) for k in range(4)],
+            out_specs=pl.BlockSpec((256, 1024), lambda t, tab: (t, 0)),
         ),
         out_shape=sds((512, 1024), BF16),
         compiler_params=params(60),
@@ -479,7 +472,7 @@
     kept = jnp.stack([kept, over_x_hi(kept)])
 
     b_20, b_21, a_21, a_20 = grad_blocks(
-        place, [2], [(0, 0, 0, 1), (0, 1, 0, 1), (1, 1, 0, 1), (1, 0, 0, 1)], xk, x_first_sib, cp, c_sib, "grad_a"
+        place, [2], [(0, 0, 0, 1), (0, 1, 0, 1), (1, 1, 0, 1), (1, 0, 0, 1)], xk, x_first_sib, cp, c_sib, [], "grad_a"
     )
     r_up = over_z(b_20[0], 1)
     r_down = over_z(b_21[0], -1)
@@ -488,7 +481,7 @@
         place,
         [1, 3, 0],
         [(0, dx, step, 1) for dx in range(2) for step in range(3)] + [(1, 1, 0, 3), (1, 0, 0, 3)],
-        xk, x_sib, cp, c_sib, "grad_b",
+        xk, x_sib, cp, c_sib, [kept, b_20], "grad_b",
     )
     r_a = over_x(a_send)
     e_up = over_z(b_11[0], 1)
@@ -496,20 +489,21 @@
     l_up = over_z(add(b_10[0], r_up), 1)
     l_down = over_z(add(b_31[0], r_down), -1)
 
-    half = x_first // 2
-    p_up = over_z(add(a_20[0, :half], r_a2[:half]), 1)
-    p_down = over_z(add(a_20[0, half:], r_a2[half:]), -1)
-    fe_up = over_z(add(a_own[0, half:], r_a[0, half:]), 1)
-    fe_down = over_z(add(a_own[1, :half], r_a[1, :half]), -1)
+    s_2 = add(a_20[0], r_a2)
+    t_2 = over_z(s_2, 2)
+    s_1 = add(a_own[0], r_a[0])
+    s_3 = add(a_own[1], r_a[1])
+    t_1 = over_z(s_1, 1)
+    t_3 = over_z(s_3, -1)
     b_mine = add(b_00[0], l_up, e_down)
     b_theirs = add(b_01[0], e_up, l_down)
     r_b = over_x(b_theirs)
-    fl_up = over_z(add(a_own[0, :half], r_a[0, :half], p_up), 1)
-    fl_down = over_z(add(a_own[1, half:], r_a[1, half:], p_down), -1)
 
     gain_row = lax.dynamic_slice(gain_float, (fsdp * 512,), (512,))[None, :]
-    grad, squares = total([a_own[2], r_a[2], fe_up, fl_up, fe_down, fl_down, b_mine, r_b], gain_row)
-    late = lax.all_gather(late_weights(value_weight, l_up), "fsdp", axis=0, tiled=True)
+    gain = gain_float.reshape(16, 1, 512)
+    q_early, m_early = early_product(core[None], xk, xs, cp, gain, early)
+    grad, squares = total([a_own[2], r_a[2], t_1, t_2, t_3, b_mine, r_b], gain_row, [q_early])
+    late = lax.all_gather(late_weights(value_weight, [b_theirs, b_mine, s_1, s_2, s_3]), "fsdp", axis=0, tiled=True)
 
     squares = squares + over_core(squares)
     squares = squares + over_x(squares)
@@ -517,8 +511,6 @@
 
     first, second, n_0, n_1, n_2, n_3 = adam(columns, squares, grad, adam_first, adam_second, value_weight)
 
-    gain = gain_float.reshape(16, 1, 512)
-    q_early, m_early = early_product(core[None], xk, xs, cp, gain, early)
     input_grad = input_gradient(core[None], xk, xs, cp, inv, gain, q_early, m_early, late)
 
     m_1 = over_y(n_1, 1)

time: 285 us -> 223 us (0.78)
  waiting for transfers between devices: 142 us -> 73.5 us
  starting transfers between devices: 40.8 us -> 49.8 us
    ppermute x15 -> x12, waiting for transfers between devices: 93.6 us -> 43.4 us  [over_z(): lax.ppermute(value, 'fsdp', [(i, (i + 4 * step) % 16) for i in range(16)])]
    ppermute x4, waiting for transfers between devices: 15.9 us -> 8.26 us  [over_x(): return lax.ppermute(value, 'fsdp', [(i, i ^ 2) for i in range(16)])]
    ppermute x2, waiting for transfers between devices: 9.11 us -> 3.76 us  [over_x_hi(): return lax.ppermute(value, 'rep', [(i, i ^ 1) for i in range(8)])]
    ppermute x15 -> x12, starting transfers between devices: 15.3 us -> 19.4 us  [over_z(): lax.ppermute(value, 'fsdp', [(i, (i + 4 * step) % 16) for i in range(16)])]
    ppermute x4, waiting for transfers between devices: 6.93 us -> 3.82 us  [over_core(): return lax.ppermute(value, 'fsdp', [(i, i ^ 1) for i in range(16)])]
    convert_element_type x8 -> x7, other arithmetic: 7.56 us -> 6.97 us  [add(): return total_value.astype(BF16)]
  transfers between devices with their start and end apart: 33 -> 30, of which waited for: 21 -> 21; matrix products, arithmetic and copies ran while one was open for 5% -> 8% of each run, Pallas kernels for 17% -> 21%
where the time goes in v4:
time: 223 us; the launch traced here: 219 us
  waiting for transfers between devices  73.5 us (33%)
  Pallas kernels  60.7 us (27%)
  starting transfers between devices  49.8 us (22%)
  between operations  14.3 us (6%)
  other arithmetic  11.9 us (5%)
  local copies, waits for them, and re-layouts  9.34 us (4%)
    ppermute x12, waiting for transfers between devices, over_z(): lax.ppermute(value, 'fsdp', [(i, (i + 4 * step) % 16) for i in range(16)])  43.4 us
    ppermute x12, starting transfers between devices, over_z(): lax.ppermute(value, 'fsdp', [(i, (i + 4 * step) % 16) for i in range(16)])  19.4 us
    pallas_call x2, Pallas kernels, grad_blocks(): pl.pallas_call(functools.partial(grad_kernel, outputs, len(after)), grid_...  16.6 us
    pallas_call x1, Pallas kernels, input_gradient(): pl.pallas_call(input_kernel, grid_spec=pltpu.PrefetchScalarGridSpec(num_s...  15 us
    ppermute x6, waiting for transfers between devices, over_y(): lax.ppermute(value, 'rep', [(i, (i + 2 * step) % 8) for i in range(8)])  14.1 us
    ppermute x6, starting transfers between devices, over_y(): lax.ppermute(value, 'rep', [(i, (i + 2 * step) % 8) for i in range(8)])  12.5 us
    ppermute x4, starting transfers between devices, over_core(): return lax.ppermute(value, 'fsdp', [(i, i ^ 1) for i in range(16)])  9.37 us
    pallas_call x1, Pallas kernels, prep(): pl.pallas_call(prep_kernel, grid_spec=pltpu.PrefetchScalarGridSpec(num_sc...  8.27 us
  transfers between devices with their start and end apart: 30, of which 21 were waited for; matrix products, arithmetic and copies ran while one was open for 8% of the time, Pallas kernels for 21%

profile of v4, /device:TPU:1, one launch (start us, length us, event | category | flops | bytes accessed | tf_op | source)
XLA Modules:
  0.0 219.5 jit_solution(8309809171075822730)
XLA Ops:
  7.2 1.7 slice.24
  9.0 0.6 pad_add_fusion.core_ref
  9.6 8.3 %prep.1 = (bf16[8,320,512]{2,1,0:T(8,128)(2,1)}, bf16[8,320,512]{2,1,0:T(8,128)(2,1)}, bf16[2,320,512]{2,1,0:T(8,128)(2,1)}, bf16[320,1024]{1,0:T(8,128)(2,1)}, f32[320,128]{1,0:T(8,128)}) custom-call(s32[2]{0:T(128)} %pad_add_fusion.core_ref, s32[1,64]{1,0:T(1,128)} %index_ref.1, bf16[1,256,8192]{2,1,0:T(8,128)(2,1)} %h_ref.1, bf16[1,128,8192]{2,1,0:T(8,128)(2,1)} %b_ref.1, ...), custom_call_target="tpu_custom_call" | custom-call | flops 2000000000 | bytes 12000000 | tf_op jit(solution)/shard_map/prep/pallas_call | solution.py:107
  17.9 1.5 collective-permute-start
  19.9 2.9 %collective-permute-start.2 = (f32[512,128]{1,0:T(8,128)S(1)}, f32[512,128]{1,0:T(8,128)S(1)}, u32[]{:S(2)}, u32[]{:S(2)}) collective-permute-start(f32[512,128]{1,0:T(8,128)S(1)} %multiply_subtract_fusion.1), channel_id=1, source_target_pairs={{0,16},{16,0},{32,48},{48,32},{64,80},{80,64},{96,112},{112,96},{1... | collective-permute-start | bytes 786440 | tf_op jit(solution)/shard_map/ppermute | solution.py:54
  22.9 0.6 pad_add_fusion.1.table_ref
  23.5 1.8 collective-permute-done.3.xs_ref
  25.3 0.9 collective-permute-done.1.cs_ref
  26.3 0.8 copy-done.18
  27.1 5.5 %grad_a.1 = (bf16[1,576,512]{2,1,0:T(8,128)(2,1)}, bf16[1,576,512]{2,1,0:T(8,128)(2,1)}, bf16[1,448,512]{2,1,0:T(8,128)(2,1)}, bf16[1,448,512]{2,1,0:T(8,128)(2,1)}) custom-call(s32[5]{0:T(128)} %pad_add_fusion.1.table_ref, bf16[8,320,512]{2,1,0:T(8,128)(2,1)} %get-tuple-element.35.xk_ref, bf16[2,320,512]{2,1,0:T(8,128)(2,1)} %copy-done.19, ...), custom_call_target="tpu_custom_call" | custom-call | flops 1342177280 | bytes 3400000 | tf_op jit(solution)/shard_map/grad_a/pallas_call | solution.py:175
  32.5 3.8 %collective-permute-start.5 = (bf16[576,512]{1,0:T(8,128)(2,1)}, bf16[576,512]{1,0:T(8,128)(2,1)S(1)}, u32[]{:S(2)}, u32[]{:S(2)}) collective-permute-start(bf16[576,512]{1,0:T(8,128)(2,1)} %bitcast.66), channel_id=1, source_target_pairs={{0,12},{1,13},{2,14},{3,15},{4,0},{5,1},{6,2},{7,3},{8,4},{9,5},{1... | collective-permute-start | bytes 1769480 | tf_op jit(solution)/shard_map/ppermute | solution.py:50
  36.3 0.6 stack.60.table_ref
  36.9 0.8 pad_maximum_fusion.rest_0_
  37.7 1.3 collective-permute-start.11
  39.0 11.1 %grad_b.1 = (bf16[1,576,512]{2,1,0:T(8,128)(2,1)}, bf16[1,576,512]{2,1,0:T(8,128)(2,1)}, bf16[1,576,512]{2,1,0:T(8,128)(2,1)}, bf16[1,576,512]{2,1,0:T(8,128)(2,...) custom-call(s32[5]{0:T(128)} %stack.60.table_ref, ...), custom_call_target="tpu_custom_call" | custom-call | flops 4026531840 | bytes 10200000 | tf_op jit(solution)/shard_map/grad_b/pallas_call | solution.py:175
  50.5 7.8 %collective-permute-done.5 = bf16[576,512]{1,0:T(8,128)(2,1)S(1)} collective-permute-done((bf16[576,512]{1,0:T(8,128)(2,1)}, bf16[576,512]{1,0:T(8,128)(2,1)S(1)}, u32[]{:S(2)}, u32[]{:S(2)}) %collective-permute-start.5) | collective-permute-done | bytes 589856 | tf_op jit(solution)/shard_map/ppermute | solution.py:50
  58.3 1.3 fusion.3
  59.6 3.8 %collective-permute-start.6 = (bf16[576,512]{1,0:T(8,128)(2,1)S(1)}, bf16[576,512]{1,0:T(8,128)(2,1)S(1)}, u32[]{:S(2)}, u32[]{:S(2)}) collective-permute-start(bf16[576,512]{1,0:T(8,128)(2,1)S(1)} %fusion.3), channel_id=1, source_target_pairs={{0,12},{1,13},{2,14},{3,15},{4,0},{5,1},{6,2},{7,3},{8,4},{9,5},{1... | collective-permute-start | bytes 1769480 | tf_op jit(solution)/shard_map/ppermute | solution.py:50
  63.7 2.6 %collective-permute-start.9 = (bf16[576,512]{1,0:T(8,128)(2,1)S(1)}, bf16[576,512]{1,0:T(8,128)(2,1)S(1)}, u32[]{:S(2)}, u32[]{:S(2)}) collective-permute-start(bf16[576,512]{1,0:T(8,128)(2,1)S(1)} %bitcast.67), channel_id=1, source_target_pairs={{0,12},{1,13},{2,14},{3,15},{4,0},{5,1},{6,2},{7,3},{8,4},{9,5},{1... | collective-permute-start | bytes 1769480 | tf_op jit(solution)/shard_map/ppermute | solution.py:50
  66.4 0.9 fusion.6.rest_3_
  67.3 6.3 %collective-permute-done.4 = bf16[576,512]{1,0:T(8,128)(2,1)S(1)} collective-permute-done((bf16[576,512]{1,0:T(8,128)(2,1)}, bf16[576,512]{1,0:T(8,128)(2,1)S(1)}, u32[]{:S(2)}, u32[]{:S(2)}) %collective-permute-start.4) | collective-permute-done | bytes 589856 | tf_op jit(solution)/shard_map/ppermute | solution.py:50
  73.6 2.3 %collective-permute-done.6 = bf16[576,512]{1,0:T(8,128)(2,1)S(1)} collective-permute-done((bf16[576,512]{1,0:T(8,128)(2,1)S(1)}, bf16[576,512]{1,0:T(8,128)(2,1)S(1)}, u32[]{:S(2)}, u32[]{:S(2)}) %collective-permute-start.6) | collective-permute-done | bytes 589856 | tf_op jit(solution)/shard_map/ppermute | solution.py:50
  75.9 1.0 fusion.5.rest_0_
  77.0 9.1 %collective-permute-done.8 = bf16[576,512]{1,0:T(8,128)(2,1)S(1)} collective-permute-done((bf16[576,512]{1,0:T(8,128)(2,1)S(1)}, bf16[576,512]{1,0:T(8,128)(2,1)S(1)}, u32[]{:S(2)}, u32[]{:S(2)}) %collective-permute-start.8) | collective-permute-done | bytes 589856 | tf_op jit(solution)/shard_map/ppermute | solution.py:50
  86.1 2.4 %collective-permute-done.9 = bf16[576,512]{1,0:T(8,128)(2,1)S(1)} collective-permute-done((bf16[576,512]{1,0:T(8,128)(2,1)S(1)}, bf16[576,512]{1,0:T(8,128)(2,1)S(1)}, u32[]{:S(2)}, u32[]{:S(2)}) %collective-permute-start.9) | collective-permute-done | bytes 589856 | tf_op jit(solution)/shard_map/ppermute | solution.py:50
  88.6 1.1 fusion.2.rest_1_.b0
  89.7 1.4 fusion.8
  91.1 2.3 %late_weights.1 = bf16[384,1024]{1,0:T(8,128)(2,1)} custom-call(bf16[1,512,1024]{2,1,0:T(8,128)(2,1)} %w_ref.3, bf16[576,512]{1,0:T(8,128)(2,1)} %fusion.5.rest_0_, bf16[576,512]{1,0:T(8,128)(2,1)} %fusion.2.rest_1_.b0, bf16[448,512]{1,0:T(8,128)(2,1)} %get-tuple-element.63.rest_2_, bf16[448,512]{1,0:T(8,128)(2,1)} %fusion.6.rest_3_, ...), custom_call_target="tpu_custom_call" | custom-call | bytes 2000000 | tf_op jit(solution)/shard_map/late_weights/pallas_call | solution.py:204
  93.4 0.6 convert_element_type.119
  94.0 0.7 dynamic_slice.3
  94.7 3.5 %collective-permute-start.13 = (bf16[448,512]{1,0:T(8,128)(2,1)S(1)}, bf16[448,512]{1,0:T(8,128)(2,1)S(1)}, u32[]{:S(2)}, u32[]{:S(2)}) collective-permute-start(bf16[448,512]{1,0:T(8,128)(2,1)S(1)} %copy-done.1), channel_id=1, source_target_pairs={{0,8},{1,9},{2,10},{3,11},{4,12},{5,13},{6,14},{7,15},{8,0},{9,1},... | collective-permute-start | bytes 1376264 | tf_op jit(solution)/shard_map/ppermute | solution.py:50
  98.4 0.9 collective-permute-start.14
  99.9 1.8 slice_bitcast_fusion.1.a0
  101.7 1.8 slice_bitcast_fusion.a1
  103.5 4.9 %early_product.1 = (bf16[2,8,320,128]{3,2,1,0:T(8,128)(2,1)}, f32[320,128]{1,0:T(8,128)}) custom-call(s32[1]{0:T(128)} %bitcast.core_ref, bf16[320,1024]{1,0:T(8,128)(2,1)} %get-tuple-element.33.cp_ref.c_ref, f32[16,1,512]{2,1,0:T(1,128)} %bitcast.62, bf16[8,320,512]{2,1,0:T(8,128)(2,1)} %get-tuple-element.35.xk_ref, ...), custom_call_target="tpu_custom_call" | custom-call | flops 1400000000 | bytes 8000000 | tf_op jit(solution)/shard_map/early_product/pallas_call | solution.py:343
  108.4 5.4 %collective-permute-done.15.b1 = bf16[576,512]{1,0:T(8,128)(2,1)} collective-permute-done((bf16[576,512]{1,0:T(8,128)(2,1)S(1)}, bf16[576,512]{1,0:T(8,128)(2,1)}, u32[]{:S(2)}, u32[]{:S(2)}) %collective-permute-start.15) | collective-permute-done | bytes 589856 | tf_op jit(solution)/shard_map/ppermute | solution.py:46
  113.8 11.0 %collective-permute-done.14.t3 = bf16[448,512]{1,0:T(8,128)(2,1)} collective-permute-done((bf16[448,512]{1,0:T(8,128)(2,1)S(1)}, bf16[448,512]{1,0:T(8,128)(2,1)}, u32[]{:S(2)}, u32[]{:S(2)}) %collective-permute-start.14) | collective-permute-done | bytes 458784 | tf_op jit(solution)/shard_map/ppermute | solution.py:50
  124.8 1.4 collective-permute-done.12.t1
  126.2 3.4 %total.1 = (f32[512,1024]{1,0:T(8,128)}, f32[8,128]{1,0:T(8,128)}) custom-call(bf16[448,512]{1,0:T(8,128)(2,1)} %slice_bitcast_fusion.1.a0, bf16[448,512]{1,0:T(8,128)(2,1)} %slice_bitcast_fusion.a1, bf16[448,512]{1,0:T(8,128)(2,1)} %collective-permute-done.12.t1, bf16[448,512]{1,0:T(8,128)(2,1)} %copy-done.12, bf16[448,512]{1,0:T(8,128)(2,1)} %collective-permute-done.14.t3, ...), custom_call_target="tpu_custom_call" | custom-call | flops 5000000 | bytes 5000000 | tf_op jit(solution)/shard_map/total/pallas_call | solution.py:235
  129.6 7.3 %collective-permute-start.16 = (f32[8,128]{1,0:T(8,128)}, f32[8,128]{1,0:T(8,128)S(1)}, u32[]{:S(2)}, u32[]{:S(2)}) collective-permute-start(f32[8,128]{1,0:T(8,128)} %get-tuple-element.52), channel_id=1, source_target_pairs={{0,1},{1,0},{2,3},{3,2},{4,5},{5,4},{6,7},{7,6},{8,9},{9,8},{10,11... | collective-permute-start | bytes 12296 | tf_op jit(solution)/shard_map/ppermute | solution.py:42
  136.9 1.0 collective-permute-done.16
  138.0 0.7 add.152
  138.7 2.9 %collective-permute-done.17 = f32[8,128]{1,0:T(8,128)S(1)} collective-permute-done((f32[8,128]{1,0:T(8,128)S(1)}, f32[8,128]{1,0:T(8,128)S(1)}, u32[]{:S(2)}, u32[]{:S(2)}) %collective-permute-start.17) | collective-permute-done | bytes 4128 | tf_op jit(solution)/shard_map/ppermute | solution.py:46
  141.5 4.1 %collective-permute-start.19 = (f32[8,128]{1,0:T(8,128)S(1)}, f32[8,128]{1,0:T(8,128)S(1)}, u32[]{:S(2)}, u32[]{:S(2)}) collective-permute-start(f32[8,128]{1,0:T(8,128)S(1)} %add.153), channel_id=1, source_target_pairs={{0,8},{1,9},{2,10},{3,11},{4,12},{5,13},{6,14},{7,15},{8,0},{9,1},... | collective-permute-start | bytes 12296 | tf_op jit(solution)/shard_map/ppermute | solution.py:50
  145.7 0.7 stack.70.table_ref
  146.7 2.6 %collective-permute-done.18 = f32[8,128]{1,0:T(8,128)S(1)} collective-permute-done((f32[8,128]{1,0:T(8,128)S(1)}, f32[8,128]{1,0:T(8,128)S(1)}, u32[]{:S(2)}, u32[]{:S(2)}) %collective-permute-start.18) | collective-permute-done | bytes 4128 | tf_op jit(solution)/shard_map/ppermute | solution.py:50
  149.3 0.6 add_add_fusion.sq_ref
  149.9 7.4 %adam.1 = (f32[1,512,1024]{2,1,0:T(8,128)}, f32[1,512,1024]{2,1,0:T(8,128)}, bf16[2,512,128]{2,1,0:T(8,128)(2,1)}, bf16[2,512,128]{2,1,0:T(8,128)(2,1)}, bf16[2,...) custom-call(s32[5]{0:T(128)} %stack.70.table_ref, f32[8,128]{1,0:T(8,128)} %add_add_fusion.sq_ref, ...), custom_call_target="tpu_custom_call" | custom-call | flops 20000000 | bytes 12000000 | tf_op jit(solution)/shard_map/adam/pallas_call | solution.py:275
  157.3 2.4 %collective-permute-start.21 = (bf16[2,512,128]{2,1,0:T(8,128)(2,1)}, bf16[2,512,128]{2,1,0:T(8,128)(2,1)S(1)}, u32[]{:S(2)}, u32[]{:S(2)}) collective-permute-start(bf16[2,512,128]{2,1,0:T(8,128)(2,1)} %get-tuple-element.57), channel_id=1, source_target_pairs={{0,32},{16,48},{32,64},{48,80},{64,96},{80,112},{96,0},{112,16},{1... | collective-permute-start | bytes 786440 | tf_op jit(solution)/shard_map/ppermute | solution.py:58
  159.7 0.8 collective-permute-start.22
  160.5 2.0 collective-permute-start.23
  162.5 1.6 collective-permute-done.21
  164.0 5.7 %collective-permute-done.22 = bf16[2,512,128]{2,1,0:T(8,128)(2,1)S(1)} collective-permute-done((bf16[2,512,128]{2,1,0:T(8,128)(2,1)}, bf16[2,512,128]{2,1,0:T(8,128)(2,1)S(1)}, u32[]{:S(2)}, u32[]{:S(2)}) %collective-permute-start.22) | collective-permute-done | bytes 262176 | tf_op jit(solution)/shard_map/ppermute | solution.py:58
  169.7 0.6 collective-permute-done.23
  170.3 1.1 add_convert_fusion.3
  171.4 3.6 %collective-permute-start.24 = (bf16[2,512,128]{2,1,0:T(8,128)(2,1)S(1)}, bf16[2,512,128]{2,1,0:T(8,128)(2,1)S(1)}, u32[]{:S(2)}, u32[]{:S(2)}) collective-permute-start(bf16[2,512,128]{2,1,0:T(8,128)(2,1)S(1)} %rev.3), channel_id=1, source_target_pairs={{0,16},{16,0},{32,48},{48,32},{64,80},{80,64},{96,112},{112,96},{1... | collective-permute-start | bytes 786440 | tf_op jit(solution)/shard_map/ppermute | solution.py:54
  175.1 3.8 %collective-permute-done.24 = bf16[2,512,128]{2,1,0:T(8,128)(2,1)S(1)} collective-permute-done((bf16[2,512,128]{2,1,0:T(8,128)(2,1)S(1)}, bf16[2,512,128]{2,1,0:T(8,128)(2,1)S(1)}, u32[]{:S(2)}, u32[]{:S(2)}) %collective-permute-start.24) | collective-permute-done | bytes 262176 | tf_op jit(solution)/shard_map/ppermute | solution.py:54
  178.9 4.9 %collective-permute-start.27 = (bf16[2,512,128]{2,1,0:T(8,128)(2,1)S(1)}, bf16[2,512,128]{2,1,0:T(8,128)(2,1)S(1)}, u32[]{:S(2)}, u32[]{:S(2)}) collective-permute-start(bf16[2,512,128]{2,1,0:T(8,128)(2,1)S(1)} %get-tuple-element.65.refs_0_), channel_id=1, source_target_pairs={{0,32},{16,48},{32,64},{48,80},{64,96},{80,112},{96,0},{112,16},{1... | collective-permute-start | bytes 786440 | tf_op jit(solution)/shard_map/ppermute | solution.py:58
  184.4 1.9 collective-permute-start.25
  186.4 0.9 multiply_subtract_fusion
  187.4 5.9 %collective-permute-done.26.refs_2_ = bf16[2,512,128]{2,1,0:T(8,128)(2,1)S(1)} collective-permute-done((bf16[2,512,128]{2,1,0:T(8,128)(2,1)S(1)}, bf16[2,512,128]{2,1,0:T(8,128)(2,1)S(1)}, u32[]{:S(2)}, u32[]{:S(2)}) %collective-permute-start.26) | collective-permute-done | bytes 262176 | tf_op jit(solution)/shard_map/ppermute | solution.py:58
  194.1 0.7 copy-done.16
  194.8 2.9 %place.1 = bf16[512,1024]{1,0:T(8,128)(2,1)} custom-call(s32[5]{0:T(128)} %stack.70.table_ref, bf16[2,512,128]{2,1,0:T(8,128)(2,1)} %copy-done.8, bf16[2,512,128]{2,1,0:T(8,128)(2,1)} %copy-done.16, bf16[2,512,128]{2,1,0:T(8,128)(2,1)} %copy-done.15, bf16[2,512,128]{2,1,0:T(8,128)(2,1)} %copy-done.14), custom_call_target="tpu_custom_call" | custom-call | flops 1000000 | bytes 2000000 | tf_op jit(solution)/shard_map/place/pallas_call | solution.py:299
  197.7 15.0 %input_gradient.1 = bf16[1,320,8192]{2,1,0:T(8,128)(2,1)} custom-call(s32[1]{0:T(128)} %bitcast.core_ref, bf16[320,1024]{1,0:T(8,128)(2,1)} %get-tuple-element.33.cp_ref.c_ref, f32[320,128]{1,0:T(8,128)} %get-tuple-element.34.inv_ref, f32[16,1,512]{2,1,0:T(1,128)} %bitcast.63, bf16[8,320,512]{2,1,0:T(8,128)(2,1)} %get-tuple-element.35.xk_ref, ...), custom_call_target="tpu_custom_call" | custom-call | flops 5000000000 | bytes 30000000 | tf_op jit(solution)/shard_map/input_gradient/pallas_call | solution.py:409
  (74 shorter events, 4.1 us)
Async XLA Ops:
  7.2 96.3 %all-gather.6.cloned.1.call-start = ((), (), s32[]{:S(2)}) async-start(), calls=%async_computation.1 | async-start | bytes 4456448 | tf_op jit(solution)/shard_map/all_gather | solution.py:462
  8.9 188.8 %all-gather.4.cloned.1.call-start = ((), (), s32[]{:S(2)}) async-start(), calls=%async_computation | async-start | bytes 13369344 | tf_op jit(solution)/shard_map/all_gather | solution.py:506
  9.6 10.3 %copy-start.6 = (f32[512,128]{1,0:T(8,128)S(1)}, f32[512,128]{1,0:T(8,128)}, u32[]{:S(2)}) copy-start(f32[512,128]{1,0:T(8,128)} %param.19) | copy-start | bytes 786436
  9.6 10.3 %copy-start.7 = (f32[512,128]{1,0:T(8,128)S(1)}, f32[512,128]{1,0:T(8,128)}, u32[]{:S(2)}) copy-start(f32[512,128]{1,0:T(8,128)} %param.18) | copy-start | bytes 786436
  17.9 21.1 %collective-permute-start = (bf16[8,320,512]{2,1,0:T(8,128)(2,1)}, bf16[8,320,512]{2,1,0:T(8,128)(2,1)}, u32[]{:S(2)}, u32[]{:S(2)}) collective-permute-start(bf16[8,320,512]{2,1,0:T(8,128)(2,1)} %get-tuple-element.36.xs_ref), channel_id=1, source_target_pairs={{0,1},{1,0},{2,3},{3,2},{4,5},{5,4},{6,7},{7,6},{8,9},{9,8},{10,11... | collective-permute-start | bytes 7864328 | tf_op jit(solution)/shard_map/ppermute | solution.py:42
  19.4 5.9 %collective-permute-start.3 = (bf16[2,320,512]{2,1,0:T(8,128)(2,1)}, bf16[2,320,512]{2,1,0:T(8,128)(2,1)S(1)}, u32[]{:S(2)}, u32[]{:S(2)}) collective-permute-start(bf16[2,320,512]{2,1,0:T(8,128)(2,1)} %get-tuple-element.39), channel_id=1, source_target_pairs={{0,1},{1,0},{2,3},{3,2},{4,5},{5,4},{6,7},{7,6},{8,9},{9,8},{10,11... | collective-permute-start | bytes 1966088 | tf_op jit(solution)/shard_map/ppermute | solution.py:42
  19.5 6.8 %collective-permute-start.1 = (bf16[320,1024]{1,0:T(8,128)(2,1)}, bf16[320,1024]{1,0:T(8,128)(2,1)S(1)}, u32[]{:S(2)}, u32[]{:S(2)}) collective-permute-start(bf16[320,1024]{1,0:T(8,128)(2,1)} %get-tuple-element.33.cp_ref.c_ref), channel_id=1, source_target_pairs={{0,1},{1,0},{2,3},{3,2},{4,5},{5,4},{6,7},{7,6},{8,9},{9,8},{10,11... | collective-permute-start | bytes 1966088 | tf_op jit(solution)/shard_map/ppermute | solution.py:42
  19.9 17.0 %collective-permute-start.2 = (f32[512,128]{1,0:T(8,128)S(1)}, f32[512,128]{1,0:T(8,128)S(1)}, u32[]{:S(2)}, u32[]{:S(2)}) collective-permute-start(f32[512,128]{1,0:T(8,128)S(1)} %multiply_subtract_fusion.1), channel_id=1, source_target_pairs={{0,16},{16,0},{32,48},{48,32},{64,80},{80,64},{96,112},{112,96},{1... | collective-permute-start | bytes 786440 | tf_op jit(solution)/shard_map/ppermute | solution.py:54
  25.3 0.9 copy-start.19
  26.3 0.8 copy-start.18
  32.5 25.8 %collective-permute-start.5 = (bf16[576,512]{1,0:T(8,128)(2,1)}, bf16[576,512]{1,0:T(8,128)(2,1)S(1)}, u32[]{:S(2)}, u32[]{:S(2)}) collective-permute-start(bf16[576,512]{1,0:T(8,128)(2,1)} %bitcast.66), channel_id=1, source_target_pairs={{0,12},{1,13},{2,14},{3,15},{4,0},{5,1},{6,2},{7,3},{8,4},{9,5},{1... | collective-permute-start | bytes 1769480 | tf_op jit(solution)/shard_map/ppermute | solution.py:50
  37.7 26.0 %collective-permute-start.11 = (bf16[448,512]{1,0:T(8,128)(2,1)}, bf16[448,512]{1,0:T(8,128)(2,1)S(1)}, u32[]{:S(2)}, u32[]{:S(2)}) collective-permute-start(bf16[448,512]{1,0:T(8,128)(2,1)} %bitcast.69), channel_id=1, source_target_pairs={{0,2},{1,3},{2,0},{3,1},{4,6},{5,7},{6,4},{7,5},{8,10},{9,11},{10,... | collective-permute-start | bytes 1376264 | tf_op jit(solution)/shard_map/ppermute | solution.py:46
  39.0 24.5 %collective-permute-start.7 = (bf16[576,512]{1,0:T(8,128)(2,1)}, bf16[576,512]{1,0:T(8,128)(2,1)S(1)}, u32[]{:S(2)}, u32[]{:S(2)}) collective-permute-start(bf16[576,512]{1,0:T(8,128)(2,1)} %bitcast.65), channel_id=1, source_target_pairs={{0,4},{1,5},{2,6},{3,7},{4,8},{5,9},{6,10},{7,11},{8,12},{9,13},{1... | collective-permute-start | bytes 1769480 | tf_op jit(solution)/shard_map/ppermute | solution.py:50
  50.1 13.3 %copy-start.9 = (bf16[1,576,512]{2,1,0:T(8,128)(2,1)S(1)}, bf16[1,576,512]{2,1,0:T(8,128)(2,1)}, u32[]{:S(2)}) copy-start(bf16[1,576,512]{2,1,0:T(8,128)(2,1)} %get-tuple-element.46) | copy-start | bytes 1769476
  50.1 23.5 %collective-permute-start.4 = (bf16[576,512]{1,0:T(8,128)(2,1)}, bf16[576,512]{1,0:T(8,128)(2,1)S(1)}, u32[]{:S(2)}, u32[]{:S(2)}) collective-permute-start(bf16[576,512]{1,0:T(8,128)(2,1)} %bitcast.68), channel_id=1, source_target_pairs={{0,4},{1,5},{2,6},{3,7},{4,8},{5,9},{6,10},{7,11},{8,12},{9,13},{1... | collective-permute-start | bytes 1769480 | tf_op jit(solution)/shard_map/ppermute | solution.py:50
  50.2 39.5 %collective-permute-start.10 = (bf16[3,448,512]{2,1,0:T(8,128)(2,1)}, bf16[3,448,512]{2,1,0:T(8,128)(2,1)S(1)}, u32[]{:S(2)}, u32[]{:S(2)}) collective-permute-start(bf16[3,448,512]{2,1,0:T(8,128)(2,1)} %get-tuple-element.49), channel_id=1, source_target_pairs={{0,2},{1,3},{2,0},{3,1},{4,6},{5,7},{6,4},{7,5},{8,10},{9,11},{10,... | collective-permute-start | bytes 4128776 | tf_op jit(solution)/shard_map/ppermute | solution.py:46
  58.3 5.4 %copy-start.20 = (bf16[1,576,512]{2,1,0:T(8,128)(2,1)S(1)}, bf16[1,576,512]{2,1,0:T(8,128)(2,1)}, u32[]{:S(2)}) copy-start(bf16[1,576,512]{2,1,0:T(8,128)(2,1)} %get-tuple-element.47) | copy-start | bytes 1769476
  58.3 8.0 %copy-start.13 = (bf16[1,448,512]{2,1,0:T(8,128)(2,1)S(1)}, bf16[1,448,512]{2,1,0:T(8,128)(2,1)}, u32[]{:S(2)}) copy-start(bf16[1,448,512]{2,1,0:T(8,128)(2,1)} %get-tuple-element.50) | copy-start | bytes 1376260
  59.6 16.3 %collective-permute-start.6 = (bf16[576,512]{1,0:T(8,128)(2,1)S(1)}, bf16[576,512]{1,0:T(8,128)(2,1)S(1)}, u32[]{:S(2)}, u32[]{:S(2)}) collective-permute-start(bf16[576,512]{1,0:T(8,128)(2,1)S(1)} %fusion.3), channel_id=1, source_target_pairs={{0,12},{1,13},{2,14},{3,15},{4,0},{5,1},{6,2},{7,3},{8,4},{9,5},{1... | collective-permute-start | bytes 1769480 | tf_op jit(solution)/shard_map/ppermute | solution.py:50
  63.5 12.5 %copy-start.11 = (bf16[1,576,512]{2,1,0:T(8,128)(2,1)S(1)}, bf16[1,576,512]{2,1,0:T(8,128)(2,1)}, u32[]{:S(2)}) copy-start(bf16[1,576,512]{2,1,0:T(8,128)(2,1)} %get-tuple-element.41) | copy-start | bytes 1769476
  63.6 22.5 %collective-permute-start.8 = (bf16[576,512]{1,0:T(8,128)(2,1)S(1)}, bf16[576,512]{1,0:T(8,128)(2,1)S(1)}, u32[]{:S(2)}, u32[]{:S(2)}) collective-permute-start(bf16[576,512]{1,0:T(8,128)(2,1)S(1)} %fusion), channel_id=1, source_target_pairs={{0,4},{1,5},{2,6},{3,7},{4,8},{5,9},{6,10},{7,11},{8,12},{9,13},{1... | collective-permute-start | bytes 1769480 | tf_op jit(solution)/shard_map/ppermute | solution.py:50
  63.7 24.8 %collective-permute-start.9 = (bf16[576,512]{1,0:T(8,128)(2,1)S(1)}, bf16[576,512]{1,0:T(8,128)(2,1)S(1)}, u32[]{:S(2)}, u32[]{:S(2)}) collective-permute-start(bf16[576,512]{1,0:T(8,128)(2,1)S(1)} %bitcast.67), channel_id=1, source_target_pairs={{0,12},{1,13},{2,14},{3,15},{4,0},{5,1},{6,2},{7,3},{8,4},{9,5},{1... | collective-permute-start | bytes 1769480 | tf_op jit(solution)/shard_map/ppermute | solution.py:50
  67.3 21.3 %copy-start.10 = (bf16[1,576,512]{2,1,0:T(8,128)(2,1)S(1)}, bf16[1,576,512]{2,1,0:T(8,128)(2,1)}, u32[]{:S(2)}) copy-start(bf16[1,576,512]{2,1,0:T(8,128)(2,1)} %get-tuple-element.45) | copy-start | bytes 1769476
  77.0 12.7 %copy-start.4 = (bf16[3,448,512]{2,1,0:T(8,128)(2,1)S(1)}, bf16[3,448,512]{2,1,0:T(8,128)(2,1)}, u32[]{:S(2)}) copy-start(bf16[3,448,512]{2,1,0:T(8,128)(2,1)} %get-tuple-element.48) | copy-start | bytes 4128772
  89.7 1.4 copy-start.5
  91.1 2.4 %copy-start.17 = (bf16[8192]{0:T(1024)(128)(2,1)S(1)}, bf16[8192]{0:T(1024)(128)(2,1)}, u32[]{:S(2)}) copy-start(bf16[8192]{0:T(1024)(128)(2,1)} %param.14) | copy-start | bytes 49156
  91.1 3.6 %copy-start.1 = (bf16[448,512]{1,0:T(8,128)(2,1)S(1)}, bf16[448,512]{1,0:T(8,128)(2,1)}, u32[]{:S(2)}) copy-start(bf16[448,512]{1,0:T(8,128)(2,1)} %fusion.6.rest_3_) | copy-start | bytes 1376260
  91.1 7.1 %copy-start = (bf16[576,512]{1,0:T(8,128)(2,1)S(1)}, bf16[576,512]{1,0:T(8,128)(2,1)}, u32[]{:S(2)}) copy-start(bf16[576,512]{1,0:T(8,128)(2,1)} %fusion.5.rest_0_) | copy-start | bytes 1769476
  91.1 7.3 %copy-start.3 = (bf16[448,512]{1,0:T(8,128)(2,1)S(1)}, bf16[448,512]{1,0:T(8,128)(2,1)}, u32[]{:S(2)}) copy-start(bf16[448,512]{1,0:T(8,128)(2,1)} %get-tuple-element.62.rest_4_) | copy-start | bytes 1376260
  91.1 8.3 %copy-start.2 = (bf16[448,512]{1,0:T(8,128)(2,1)S(1)}, bf16[448,512]{1,0:T(8,128)(2,1)}, u32[]{:S(2)}) copy-start(bf16[448,512]{1,0:T(8,128)(2,1)} %get-tuple-element.63.rest_2_) | copy-start | bytes 1376260
  94.7 13.7 %collective-permute-start.13 = (bf16[448,512]{1,0:T(8,128)(2,1)S(1)}, bf16[448,512]{1,0:T(8,128)(2,1)S(1)}, u32[]{:S(2)}, u32[]{:S(2)}) collective-permute-start(bf16[448,512]{1,0:T(8,128)(2,1)S(1)} %copy-done.1), channel_id=1, source_target_pairs={{0,8},{1,9},{2,10},{3,11},{4,12},{5,13},{6,14},{7,15},{8,0},{9,1},... | collective-permute-start | bytes 1376264 | tf_op jit(solution)/shard_map/ppermute | solution.py:50
  98.1 15.6 %collective-permute-start.15 = (bf16[576,512]{1,0:T(8,128)(2,1)S(1)}, bf16[576,512]{1,0:T(8,128)(2,1)}, u32[]{:S(2)}, u32[]{:S(2)}) collective-permute-start(bf16[576,512]{1,0:T(8,128)(2,1)S(1)} %copy-done), channel_id=1, source_target_pairs={{0,2},{1,3},{2,0},{3,1},{4,6},{5,7},{6,4},{7,5},{8,10},{9,11},{10,... | collective-permute-start | bytes 1769480 | tf_op jit(solution)/shard_map/ppermute | solution.py:46
  98.4 26.4 %collective-permute-start.14 = (bf16[448,512]{1,0:T(8,128)(2,1)S(1)}, bf16[448,512]{1,0:T(8,128)(2,1)}, u32[]{:S(2)}, u32[]{:S(2)}) collective-permute-start(bf16[448,512]{1,0:T(8,128)(2,1)S(1)} %copy-done.3), channel_id=1, source_target_pairs={{0,12},{1,13},{2,14},{3,15},{4,0},{5,1},{6,2},{7,3},{8,4},{9,5},{1... | collective-permute-start | bytes 1376264 | tf_op jit(solution)/shard_map/ppermute | solution.py:50
  99.3 26.8 %collective-permute-start.12 = (bf16[448,512]{1,0:T(8,128)(2,1)S(1)}, bf16[448,512]{1,0:T(8,128)(2,1)}, u32[]{:S(2)}, u32[]{:S(2)}) collective-permute-start(bf16[448,512]{1,0:T(8,128)(2,1)S(1)} %copy-done.2), channel_id=1, source_target_pairs={{0,4},{1,5},{2,6},{3,7},{4,8},{5,9},{6,10},{7,11},{8,12},{9,13},{1... | collective-permute-start | bytes 1376264 | tf_op jit(solution)/shard_map/ppermute | solution.py:50
  108.4 17.8 %copy-start.12 = (bf16[448,512]{1,0:T(8,128)(2,1)}, bf16[448,512]{1,0:T(8,128)(2,1)S(1)}, u32[]{:S(2)}) copy-start(bf16[448,512]{1,0:T(8,128)(2,1)S(1)} %collective-permute-done.13.t2) | copy-start | bytes 1376260
  129.6 8.4 %collective-permute-start.16 = (f32[8,128]{1,0:T(8,128)}, f32[8,128]{1,0:T(8,128)S(1)}, u32[]{:S(2)}, u32[]{:S(2)}) collective-permute-start(f32[8,128]{1,0:T(8,128)} %get-tuple-element.52), channel_id=1, source_target_pairs={{0,1},{1,0},{2,3},{3,2},{4,5},{5,4},{6,7},{7,6},{8,9},{9,8},{10,11... | collective-permute-start | bytes 12296 | tf_op jit(solution)/shard_map/ppermute | solution.py:42
  138.7 2.9 %collective-permute-start.17 = (f32[8,128]{1,0:T(8,128)S(1)}, f32[8,128]{1,0:T(8,128)S(1)}, u32[]{:S(2)}, u32[]{:S(2)}) collective-permute-start(f32[8,128]{1,0:T(8,128)S(1)} %add.152), channel_id=1, source_target_pairs={{0,2},{1,3},{2,0},{3,1},{4,6},{5,7},{6,4},{7,5},{8,10},{9,11},{10,... | collective-permute-start | bytes 12296 | tf_op jit(solution)/shard_map/ppermute | solution.py:46
  141.5 4.8 %collective-permute-start.20 = (f32[8,128]{1,0:T(8,128)S(1)}, f32[8,128]{1,0:T(8,128)S(1)}, u32[]{:S(2)}, u32[]{:S(2)}) collective-permute-start(f32[8,128]{1,0:T(8,128)S(1)} %add.153), channel_id=1, source_target_pairs={{0,12},{1,13},{2,14},{3,15},{4,0},{5,1},{6,2},{7,3},{8,4},{9,5},{1... | collective-permute-start | bytes 12296 | tf_op jit(solution)/shard_map/ppermute | solution.py:50
  141.5 5.2 %collective-permute-start.19 = (f32[8,128]{1,0:T(8,128)S(1)}, f32[8,128]{1,0:T(8,128)S(1)}, u32[]{:S(2)}, u32[]{:S(2)}) collective-permute-start(f32[8,128]{1,0:T(8,128)S(1)} %add.153), channel_id=1, source_target_pairs={{0,8},{1,9},{2,10},{3,11},{4,12},{5,13},{6,14},{7,15},{8,0},{9,1},... | collective-permute-start | bytes 12296 | tf_op jit(solution)/shard_map/ppermute | solution.py:50
  145.7 3.7 %collective-permute-start.18 = (f32[8,128]{1,0:T(8,128)S(1)}, f32[8,128]{1,0:T(8,128)S(1)}, u32[]{:S(2)}, u32[]{:S(2)}) collective-permute-start(f32[8,128]{1,0:T(8,128)S(1)} %add.153), channel_id=1, source_target_pairs={{0,4},{1,5},{2,6},{3,7},{4,8},{5,9},{6,10},{7,11},{8,12},{9,13},{1... | collective-permute-start | bytes 12296 | tf_op jit(solution)/shard_map/ppermute | solution.py:50
  157.3 6.7 %collective-permute-start.21 = (bf16[2,512,128]{2,1,0:T(8,128)(2,1)}, bf16[2,512,128]{2,1,0:T(8,128)(2,1)S(1)}, u32[]{:S(2)}, u32[]{:S(2)}) collective-permute-start(bf16[2,512,128]{2,1,0:T(8,128)(2,1)} %get-tuple-element.57), channel_id=1, source_target_pairs={{0,32},{16,48},{32,64},{48,80},{64,96},{80,112},{96,0},{112,16},{1... | collective-permute-start | bytes 786440 | tf_op jit(solution)/shard_map/ppermute | solution.py:58
  159.7 10.0 %collective-permute-start.22 = (bf16[2,512,128]{2,1,0:T(8,128)(2,1)}, bf16[2,512,128]{2,1,0:T(8,128)(2,1)S(1)}, u32[]{:S(2)}, u32[]{:S(2)}) collective-permute-start(bf16[2,512,128]{2,1,0:T(8,128)(2,1)} %get-tuple-element.58), channel_id=1, source_target_pairs={{0,64},{16,80},{32,96},{48,112},{64,0},{80,16},{96,32},{112,48},{1... | collective-permute-start | bytes 786440 | tf_op jit(solution)/shard_map/ppermute | solution.py:58
  160.5 9.8 %collective-permute-start.23 = (bf16[2,512,128]{2,1,0:T(8,128)(2,1)}, bf16[2,512,128]{2,1,0:T(8,128)(2,1)S(1)}, u32[]{:S(2)}, u32[]{:S(2)}) collective-permute-start(bf16[2,512,128]{2,1,0:T(8,128)(2,1)} %get-tuple-element.59), channel_id=1, source_target_pairs={{0,96},{16,112},{32,0},{48,16},{64,32},{80,48},{96,64},{112,80},{1... | collective-permute-start | bytes 786440 | tf_op jit(solution)/shard_map/ppermute | solution.py:58
  171.4 7.4 %collective-permute-start.24 = (bf16[2,512,128]{2,1,0:T(8,128)(2,1)S(1)}, bf16[2,512,128]{2,1,0:T(8,128)(2,1)S(1)}, u32[]{:S(2)}, u32[]{:S(2)}) collective-permute-start(bf16[2,512,128]{2,1,0:T(8,128)(2,1)S(1)} %rev.3), channel_id=1, source_target_pairs={{0,16},{16,0},{32,48},{48,32},{64,80},{80,64},{96,112},{112,96},{1... | collective-permute-start | bytes 786440 | tf_op jit(solution)/shard_map/ppermute | solution.py:54
  178.9 14.6 %copy-start.8 = (bf16[2,512,128]{2,1,0:T(8,128)(2,1)}, bf16[2,512,128]{2,1,0:T(8,128)(2,1)S(1)}, u32[]{:S(2)}) copy-start(bf16[2,512,128]{2,1,0:T(8,128)(2,1)S(1)} %get-tuple-element.65.refs_0_) | copy-start | bytes 786436
  178.9 8.5 %collective-permute-start.27 = (bf16[2,512,128]{2,1,0:T(8,128)(2,1)S(1)}, bf16[2,512,128]{2,1,0:T(8,128)(2,1)S(1)}, u32[]{:S(2)}, u32[]{:S(2)}) collective-permute-start(bf16[2,512,128]{2,1,0:T(8,128)(2,1)S(1)} %get-tuple-element.65.refs_0_), channel_id=1, source_target_pairs={{0,32},{16,48},{32,64},{48,80},{64,96},{80,112},{96,0},{112,16},{1... | collective-permute-start | bytes 786440 | tf_op jit(solution)/shard_map/ppermute | solution.py:58
  183.9 9.5 %collective-permute-start.26 = (bf16[2,512,128]{2,1,0:T(8,128)(2,1)S(1)}, bf16[2,512,128]{2,1,0:T(8,128)(2,1)S(1)}, u32[]{:S(2)}, u32[]{:S(2)}) collective-permute-start(bf16[2,512,128]{2,1,0:T(8,128)(2,1)S(1)} %get-tuple-element.65.refs_0_), channel_id=1, source_target_pairs={{0,64},{16,80},{32,96},{48,112},{64,0},{80,16},{96,32},{112,48},{1... | collective-permute-start | bytes 786440 | tf_op jit(solution)/shard_map/ppermute | solution.py:58
  184.4 9.1 %collective-permute-start.25 = (bf16[2,512,128]{2,1,0:T(8,128)(2,1)S(1)}, bf16[2,512,128]{2,1,0:T(8,128)(2,1)S(1)}, u32[]{:S(2)}, u32[]{:S(2)}) collective-permute-start(bf16[2,512,128]{2,1,0:T(8,128)(2,1)S(1)} %get-tuple-element.65.refs_0_), channel_id=1, source_target_pairs={{0,96},{16,112},{32,0},{48,16},{64,32},{80,48},{96,64},{112,80},{1... | collective-permute-start | bytes 786440 | tf_op jit(solution)/shard_map/ppermute | solution.py:58
  187.4 6.1 %copy-start.14 = (bf16[2,512,128]{2,1,0:T(8,128)(2,1)}, bf16[2,512,128]{2,1,0:T(8,128)(2,1)S(1)}, u32[]{:S(2)}) copy-start(bf16[2,512,128]{2,1,0:T(8,128)(2,1)S(1)} %collective-permute-done.27.refs_3_) | copy-start | bytes 786436
  193.4 0.7 copy-start.15
  194.1 0.7 copy-start.16
Sparse Core Ops, SparseCore 0:
  10.3 51.8 all-gather.5
  93.5 86.3 all-gather.3

commit v5 on v4

--- a/solution.py
+++ b/solution.py
@@ -193,30 +193,15 @@
     )(table, xk, xs, c, cs, *after)
 
 
-early_rows = 128
-
-
-def late_kernel(w_ref, *rest):
-    rest[-1][...] = w_ref[early_rows:512, :]
-
-
-def late_weights(weight, after):
-    return pl.pallas_call(
-        late_kernel,
-        grid=(1,),
-        in_specs=[pl.BlockSpec((None, 512, 1024), lambda t: (0, 0, 0))] + [pl.BlockSpec(memory_space=pl.ANY)] * len(after),
-        out_specs=pl.BlockSpec((512 - early_rows, 1024), lambda t: (0, 0)),
-        out_shape=sds((512 - early_rows, 1024), BF16),
-        compiler_params=params(60),
-        cost_estimate=cost(0, 2e6),
-        name="late_weights",
-    )(weight, *after)
-
-
-def total_kernel(a0, a1, t1, t2, t3, b0, b1, gain_ref, after_ref, grad_ref, sq_ref):
+early_rows = 256
+
+
+def total_kernel(a0, a1, ue, ul, de, dl, b0, b1, gain_ref, w_ref, after_ref, grad_ref, sq_ref, late_ref):
     step = pl.program_id(0)
-    top = a0[...].astype(F32) + a1[...].astype(F32)
-    top = top + t1[...].astype(F32) + t2[...].astype(F32) + t3[...].astype(F32)
+    late_ref[...] = w_ref[early_rows:512, :]
+    up = jnp.concatenate([ul[...], ue[...]], axis=0).astype(F32)
+    down = jnp.concatenate([de[...], dl[...]], axis=0).astype(F32)
+    top = (a0[...].astype(F32) + a1[...].astype(F32)) + (up + down)
     low = b0[...].astype(F32) + b1[...].astype(F32)
     both = jnp.concatenate([top, low], axis=0) * gain_ref[...]
     grad_ref[...] = both.T
@@ -231,22 +216,23 @@
         sq_ref[...] += square
 
 
-def total(parts, gain_row, after):
+def total(parts, gain_row, weight, after):
     return pl.pallas_call(
         total_kernel,
         grid=(2,),
         in_specs=[pl.BlockSpec((p.shape[0], 256), lambda t: (0, t)) for p in parts]
-        + [pl.BlockSpec((1, 256), lambda t: (0, t))]
+        + [pl.BlockSpec((1, 256), lambda t: (0, t)), pl.BlockSpec((None, 512, 512), lambda t: (0, 0, t))]
         + [pl.BlockSpec(memory_space=pl.ANY)] * len(after),
         out_specs=[
             pl.BlockSpec((256, 1024), lambda t: (t, 0)),
             pl.BlockSpec((8, 128), lambda t: (0, 0)),
+            pl.BlockSpec((512 - early_rows, 512), lambda t: (0, t)),
         ],
-        out_shape=[sds((512, 1024), F32), sds((8, 128), F32)],
+        out_shape=[sds((512, 1024), F32), sds((8, 128), F32), sds((512 - early_rows, 1024), BF16)],
         compiler_params=params(60),
         cost_estimate=cost(5e6, 5e6),
         name="total",
-    )(*parts, gain_row, *after)
+    )(*parts, gain_row, weight, *after)
 
 
 def adam_kernel(table_ref, sq_ref, grad_ref, m_ref, v_ref, w_ref, first_ref, second_ref, *rest):
@@ -289,26 +275,27 @@
 
 
 def place_kernel(table_ref, *refs):
-    for k, in_ref in enumerate(refs[:-1]):
+    for k, in_ref in enumerate(refs[:4]):
         for dx in range(2):
             column = pl.multiple_of((2 * table_ref[k] + (table_ref[4] ^ dx)) * 128, 128)
             refs[-1][:, pl.ds(column, 128)] = in_ref[dx]
 
 
-def place_columns(table, parts):
+def place_columns(table, parts, after):
     return pl.pallas_call(
         place_kernel,
         grid_spec=pltpu.PrefetchScalarGridSpec(
             num_scalar_prefetch=1,
             grid=(2,),
-            in_specs=[pl.BlockSpec((2, 256, 128), lambda t, tab: (0, t, 0)) for k in range(4)],
+            in_specs=[pl.BlockSpec((2, 256, 128), lambda t, tab: (0, t, 0)) for k in range(4)]
+            + [pl.BlockSpec(memory_space=pl.ANY)],
             out_specs=pl.BlockSpec((256, 1024), lambda t, tab: (t, 0)),
         ),
         out_shape=sds((512, 1024), BF16),
         compiler_params=params(60),
         cost_estimate=cost(1e6, 2e6),
         name="place",
-    )(table, *parts)
+    )(table, *parts, after)
 
 
 def early_kernel(core_ref, cp_ref, gain_ref, xk_ref, xs_ref, ek_ref, es_ref, q_ref, m_ref):
@@ -365,13 +352,14 @@
     )(core, cp, gain, xk, xs, early, early)
 
 
-def input_kernel(core_ref, cp_ref, inv_ref, gain_ref, xk_ref, xs_ref, qe_ref, me_ref, lk_ref, ls_ref, out_ref, q_ref, m_ref):
+def input_kernel(core_ref, cp_ref, inv_ref, gain_ref, xk_ref, xs_ref, qe_ref, me_ref, lk_ref, ls_ref, out_ref, end_ref, q_ref, m_ref):
     step = pl.program_id(0)
     core = core_ref[0]
 
     @pl.when(step == 0)
     def _():
         m_ref[...] = me_ref[...]
+        end_ref[...] = me_ref[0:8, :]
 
     @pl.when(step < 4)
     def _():
@@ -422,10 +410,13 @@
                 weights(0),
                 weights(1),
             ],
-            out_specs=pl.BlockSpec((None, 320, 2048), lambda t, c: (0, 0, jnp.maximum(t - 4, 0))),
+            out_specs=[
+                pl.BlockSpec((None, 320, 2048), lambda t, c: (0, 0, jnp.maximum(t - 4, 0))),
+                pl.BlockSpec((8, 128), lambda t, c: (0, 0)),
+            ],
             scratch_shapes=[pltpu.VMEM((16, 320, 512), BF16), pltpu.VMEM((320, 128), F32)],
         ),
-        out_shape=sds((1, 320, 8192), BF16),
+        out_shape=[sds((1, 320, 8192), BF16), sds((8, 128), F32)],
         compiler_params=params(60),
         cost_estimate=cost(5e9, 3e7),
         name="input_gradient",
@@ -489,21 +480,24 @@
     l_up = over_z(add(b_10[0], r_up), 1)
     l_down = over_z(add(b_31[0], r_down), -1)
 
-    s_2 = add(a_20[0], r_a2)
-    t_2 = over_z(s_2, 2)
-    s_1 = add(a_own[0], r_a[0])
-    s_3 = add(a_own[1], r_a[1])
-    t_1 = over_z(s_1, 1)
-    t_3 = over_z(s_3, -1)
+    half = x_first // 2
+    p_up = over_z(add(a_20[0, :half], r_a2[:half]), 1)
+    p_down = over_z(add(a_20[0, half:], r_a2[half:]), -1)
+    fe_up = over_z(add(a_own[0, half:], r_a[0, half:]), 1)
+    fe_down = over_z(add(a_own[1, :half], r_a[1, :half]), -1)
     b_mine = add(b_00[0], l_up, e_down)
     b_theirs = add(b_01[0], e_up, l_down)
     r_b = over_x(b_theirs)
+    fl_up = over_z(add(a_own[0, :half], r_a[0, :half], p_up), 1)
+    fl_down = over_z(add(a_own[1, half:], r_a[1, half:], p_down), -1)
 
     gain_row = lax.dynamic_slice(gain_float, (fsdp * 512,), (512,))[None, :]
     gain = gain_float.reshape(16, 1, 512)
     q_early, m_early = early_product(core[None], xk, xs, cp, gain, early)
-    grad, squares = total([a_own[2], r_a[2], t_1, t_2, t_3, b_mine, r_b], gain_row, [q_early])
-    late = lax.all_gather(late_weights(value_weight, [b_theirs, b_mine, s_1, s_2, s_3]), "fsdp", axis=0, tiled=True)
+    grad, squares, late = total(
+        [a_own[2], r_a[2], fe_up, fl_up, fe_down, fl_down, b_mine, r_b], gain_row, value_weight, [m_early]
+    )
+    late = lax.all_gather(late, "fsdp", axis=0, tiled=True)
 
     squares = squares + over_core(squares)
     squares = squares + over_x(squares)
@@ -511,7 +505,7 @@
 
     first, second, n_0, n_1, n_2, n_3 = adam(columns, squares, grad, adam_first, adam_second, value_weight)
 
-    input_grad = input_gradient(core[None], xk, xs, cp, inv, gain, q_early, m_early, late)
+    input_grad, input_end = input_gradient(core[None], xk, xs, cp, inv, gain, q_early, m_early, late)
 
     m_1 = over_y(n_1, 1)
     m_2 = over_y(n_2, 2)
@@ -523,7 +517,7 @@
     new_momentum = outer_beta * outer_momentum + outer_grad
     new_anchor = anchor - outer_rate * (outer_grad + outer_beta * new_momentum)
     parts = [sent, over_y(sent, 3), over_y(sent, 2), over_y(sent, 1)]
-    synced_weight = place_columns(columns, parts)
+    synced_weight = place_columns(columns, parts, input_end)
     return (input_grad, first, second, synced_weight, new_momentum, new_anchor)
 
 

time: 223 us -> 212 us (0.951); the launches traced: 219 us -> 211 us
  starting transfers between devices: 49.8 us -> 40.8 us
  waiting for transfers between devices: 73.5 us -> 80.2 us
  other arithmetic: 11.9 us -> 9.16 us
    ppermute x2, waiting for transfers between devices: 3.76 us -> 11.5 us  [over_x_hi(): return lax.ppermute(value, 'rep', [(i, i ^ 1) for i in range(8)])]
    ppermute x12 -> x15, waiting for transfers between devices: 43.4 us -> 50.7 us  [over_z(): lax.ppermute(value, 'fsdp', [(i, (i + 4 * step) % 16) for i in range(16)])]
    ppermute x4, waiting for transfers between devices: 8.26 us -> 2.15 us  [over_x(): return lax.ppermute(value, 'fsdp', [(i, i ^ 2) for i in range(16)])]
    ppermute x6, waiting for transfers between devices: 14.1 us -> 8.03 us  [over_y(): lax.ppermute(value, 'rep', [(i, (i + 2 * step) % 8) for i in range(8)])]
    ppermute x4, starting transfers between devices: 9.37 us -> 4.46 us  [over_core(): return lax.ppermute(value, 'fsdp', [(i, i ^ 1) for i in range(16)])]
    all_gather x1, waiting for transfers between devices: 0.01 us -> 3.65 us  [on_device(): late = lax.all_gather(late, 'fsdp', axis=0, tiled=True)]
    convert_element_type x7 -> x8, other arithmetic: 6.97 us -> 4.26 us  [add(): return total_value.astype(BF16)]
    pallas_call x1, Pallas kernels: 4.86 us -> 7.27 us  [early_product(): pl.pallas_call(early_kernel, grid_spec=pltpu.PrefetchScalarGridSpec(num_s...]
  transfers between devices with their start and end apart: 30 -> 33, of which waited for: 21 -> 17; matrix products, arithmetic and copies ran while one was open for 8% -> 6% of each run, Pallas kernels for 21% -> 25%
where the time goes in v5:
time: 212 us; the launch traced here: 211 us
  waiting for transfers between devices  80.2 us (38%)
  Pallas kernels  59.6 us (28%)
  starting transfers between devices  40.8 us (19%)
  between operations  14.3 us (7%)
  other arithmetic  9.16 us (4%)
  local copies, waits for them, and re-layouts  7.22 us (3%)
    ppermute x15, waiting for transfers between devices, over_z(): lax.ppermute(value, 'fsdp', [(i, (i + 4 * step) % 16) for i in range(16)])  50.7 us
    ppermute x15, starting transfers between devices, over_z(): lax.ppermute(value, 'fsdp', [(i, (i + 4 * step) % 16) for i in range(16)])  17.1 us
    pallas_call x2, Pallas kernels, grad_blocks(): pl.pallas_call(functools.partial(grad_kernel, outputs, len(after)), grid_...  16.6 us
    pallas_call x1, Pallas kernels, input_gradient(): pl.pallas_call(input_kernel, grid_spec=pltpu.PrefetchScalarGridSpec(num_s...  13.4 us
    ppermute x6, starting transfers between devices, over_y(): lax.ppermute(value, 'rep', [(i, (i + 2 * step) % 8) for i in range(8)])  11.7 us
    ppermute x2, waiting for transfers between devices, over_x_hi(): return lax.ppermute(value, 'rep', [(i, i ^ 1) for i in range(8)])  11.5 us
    pallas_call x1, Pallas kernels, prep(): pl.pallas_call(prep_kernel, grid_spec=pltpu.PrefetchScalarGridSpec(num_sc...  8.27 us
    ppermute x6, waiting for transfers between devices, over_y(): lax.ppermute(value, 'rep', [(i, (i + 2 * step) % 8) for i in range(8)])  8.03 us
  transfers between devices with their start and end apart: 33, of which 17 were waited for; matrix products, arithmetic and copies ran while one was open for 6% of the time, Pallas kernels for 25%

profile of v5, /device:TPU:1, one launch (start us, length us, event | category | flops | bytes accessed | tf_op | source)
XLA Modules:
  0.0 211.4 jit_solution(14128498378524981853)
XLA Ops:
  7.2 1.9 slice.48
  9.2 0.6 pad_add_fusion.core_ref
  9.8 8.3 %prep.1 = (bf16[8,320,512]{2,1,0:T(8,128)(2,1)}, bf16[8,320,512]{2,1,0:T(8,128)(2,1)}, bf16[2,320,512]{2,1,0:T(8,128)(2,1)}, bf16[320,1024]{1,0:T(8,128)(2,1)}, f32[320,128]{1,0:T(8,128)}) custom-call(s32[2]{0:T(128)} %pad_add_fusion.core_ref, s32[1,64]{1,0:T(1,128)} %index_ref.1, bf16[1,256,8192]{2,1,0:T(8,128)(2,1)} %h_ref.1, bf16[1,128,8192]{2,1,0:T(8,128)(2,1)} %b_ref.1, ...), custom_call_target="tpu_custom_call" | custom-call | flops 2000000000 | bytes 12000000 | tf_op jit(solution)/shard_map/prep/pallas_call | solution.py:107
  18.1 1.5 collective-permute-start
  19.7 0.4 collective-permute-start.1
  20.2 2.9 %collective-permute-start.2 = (f32[512,128]{1,0:T(8,128)S(1)}, f32[512,128]{1,0:T(8,128)S(1)}, u32[]{:S(2)}, u32[]{:S(2)}) collective-permute-start(f32[512,128]{1,0:T(8,128)S(1)} %multiply_subtract_fusion.1), channel_id=1, source_target_pairs={{0,16},{16,0},{32,48},{48,32},{64,80},{80,64},{96,112},{112,96},{1... | collective-permute-start | bytes 786440 | tf_op jit(solution)/shard_map/ppermute | solution.py:54
  23.1 0.6 pad_add_fusion.1.table_ref
  23.7 2.2 %collective-permute-done.3.xs_ref = bf16[2,320,512]{2,1,0:T(8,128)(2,1)S(1)} collective-permute-done((bf16[2,320,512]{2,1,0:T(8,128)(2,1)}, bf16[2,320,512]{2,1,0:T(8,128)(2,1)S(1)}, u32[]{:S(2)}, u32[]{:S(2)}) %collective-permute-start.3) | collective-permute-done | bytes 655392 | tf_op jit(solution)/shard_map/ppermute | solution.py:42
  25.9 0.9 collective-permute-done.1.cs_ref
  26.8 0.8 copy-done.14
  27.7 5.6 %grad_a.1 = (bf16[1,576,512]{2,1,0:T(8,128)(2,1)}, bf16[1,576,512]{2,1,0:T(8,128)(2,1)}, bf16[1,448,512]{2,1,0:T(8,128)(2,1)}, bf16[1,448,512]{2,1,0:T(8,128)(2,1)}) custom-call(s32[5]{0:T(128)} %pad_add_fusion.1.table_ref, bf16[8,320,512]{2,1,0:T(8,128)(2,1)} %get-tuple-element.38.xk_ref, bf16[2,320,512]{2,1,0:T(8,128)(2,1)} %copy-done.15, ...), custom_call_target="tpu_custom_call" | custom-call | flops 1342177280 | bytes 3400000 | tf_op jit(solution)/shard_map/grad_a/pallas_call | solution.py:175
  33.2 3.8 %collective-permute-start.16 = (bf16[576,512]{1,0:T(8,128)(2,1)}, bf16[576,512]{1,0:T(8,128)(2,1)S(1)}, u32[]{:S(2)}, u32[]{:S(2)}) collective-permute-start(bf16[576,512]{1,0:T(8,128)(2,1)} %bitcast.77), channel_id=1, source_target_pairs={{0,12},{1,13},{2,14},{3,15},{4,0},{5,1},{6,2},{7,3},{8,4},{9,5},{1... | collective-permute-start | bytes 1769480 | tf_op jit(solution)/shard_map/ppermute | solution.py:50
  37.0 0.6 convert_element_type.161
  37.6 0.7 dynamic_slice.3
  38.3 0.7 stack.60.table_ref
  39.0 0.8 pad_maximum_fusion.rest_0_
  39.8 1.4 collective-permute-start.6
  41.2 11.1 %grad_b.1 = (bf16[1,576,512]{2,1,0:T(8,128)(2,1)}, bf16[1,576,512]{2,1,0:T(8,128)(2,1)}, bf16[1,576,512]{2,1,0:T(8,128)(2,1)}, bf16[1,576,512]{2,1,0:T(8,128)(2,...) custom-call(s32[5]{0:T(128)} %stack.60.table_ref, ...), custom_call_target="tpu_custom_call" | custom-call | flops 4026531840 | bytes 10200000 | tf_op jit(solution)/shard_map/grad_b/pallas_call | solution.py:175
  52.6 9.1 %collective-permute-done.16 = bf16[576,512]{1,0:T(8,128)(2,1)S(1)} collective-permute-done((bf16[576,512]{1,0:T(8,128)(2,1)}, bf16[576,512]{1,0:T(8,128)(2,1)S(1)}, u32[]{:S(2)}, u32[]{:S(2)}) %collective-permute-start.16) | collective-permute-done | bytes 589856 | tf_op jit(solution)/shard_map/ppermute | solution.py:50
  61.7 1.3 fusion
  63.1 3.6 %collective-permute-done.12 = bf16[576,512]{1,0:T(8,128)(2,1)S(1)} collective-permute-done((bf16[576,512]{1,0:T(8,128)(2,1)}, bf16[576,512]{1,0:T(8,128)(2,1)S(1)}, u32[]{:S(2)}, u32[]{:S(2)}) %collective-permute-start.12) | collective-permute-done | bytes 589856 | tf_op jit(solution)/shard_map/ppermute | solution.py:50
  66.9 2.3 %collective-permute-start.13 = (bf16[576,512]{1,0:T(8,128)(2,1)S(1)}, bf16[576,512]{1,0:T(8,128)(2,1)S(1)}, u32[]{:S(2)}, u32[]{:S(2)}) collective-permute-start(bf16[576,512]{1,0:T(8,128)(2,1)S(1)} %fusion.3), channel_id=1, source_target_pairs={{0,4},{1,5},{2,6},{3,7},{4,8},{5,9},{6,10},{7,11},{8,12},{9,13},{1... | collective-permute-start | bytes 1769480 | tf_op jit(solution)/shard_map/ppermute | solution.py:50
  69.2 0.5 collective-permute-start.14
  69.8 0.8 slice_bitcast_fusion.1.a0
  70.6 20.4 %collective-permute-done.15 = bf16[576,512]{1,0:T(8,128)(2,1)S(1)} collective-permute-done((bf16[576,512]{1,0:T(8,128)(2,1)}, bf16[576,512]{1,0:T(8,128)(2,1)S(1)}, u32[]{:S(2)}, u32[]{:S(2)}) %collective-permute-start.15) | collective-permute-done | bytes 589856 | tf_op jit(solution)/shard_map/ppermute | solution.py:50
  91.3 1.8 collective-permute-start.7
  93.3 10.2 %collective-permute-done.13 = bf16[576,512]{1,0:T(8,128)(2,1)S(1)} collective-permute-done((bf16[576,512]{1,0:T(8,128)(2,1)S(1)}, bf16[576,512]{1,0:T(8,128)(2,1)S(1)}, u32[]{:S(2)}, u32[]{:S(2)}) %collective-permute-start.13) | collective-permute-done | bytes 589856 | tf_op jit(solution)/shard_map/ppermute | solution.py:50
  103.7 1.0 fusion.5.b0
  104.7 1.4 collective-permute-done.10
  106.2 2.3 %collective-permute-done.7 = bf16[224,512]{1,0:T(8,128)(2,1)S(1)} collective-permute-done((bf16[224,512]{1,0:T(8,128)(2,1)S(1)}, bf16[224,512]{1,0:T(8,128)(2,1)S(1)}, u32[]{:S(2)}, u32[]{:S(2)}) %collective-permute-start.7) | collective-permute-done | bytes 229408 | tf_op jit(solution)/shard_map/ppermute | solution.py:50
  108.6 2.4 %collective-permute-start.11 = (bf16[224,512]{1,0:T(8,128)(2,1)S(1)}, bf16[224,512]{1,0:T(8,128)(2,1)S(1)}, u32[]{:S(2)}, u32[]{:S(2)}) collective-permute-start(bf16[224,512]{1,0:T(8,128)(2,1)S(1)} %get-tuple-element.68), channel_id=1, source_target_pairs={{0,12},{1,13},{2,14},{3,15},{4,0},{5,1},{6,2},{7,3},{8,4},{9,5},{1... | collective-permute-start | bytes 688136 | tf_op jit(solution)/shard_map/ppermute | solution.py:50
  111.2 2.7 %collective-permute-start.9 = (bf16[224,512]{1,0:T(8,128)(2,1)S(1)}, bf16[224,512]{1,0:T(8,128)(2,1)}, u32[]{:S(2)}, u32[]{:S(2)}) collective-permute-start(bf16[224,512]{1,0:T(8,128)(2,1)S(1)} %get-tuple-element.70), channel_id=1, source_target_pairs={{0,12},{1,13},{2,14},{3,15},{4,0},{5,1},{6,2},{7,3},{8,4},{9,5},{1... | collective-permute-start | bytes 688136 | tf_op jit(solution)/shard_map/ppermute | solution.py:50
  113.9 0.8 slice_bitcast_fusion.a1
  114.7 7.3 %early_product.1 = (bf16[2,8,320,256]{3,2,1,0:T(8,128)(2,1)}, f32[320,128]{1,0:T(8,128)}) custom-call(s32[1]{0:T(128)} %bitcast.core_ref, bf16[320,1024]{1,0:T(8,128)(2,1)} %get-tuple-element.36.cp_ref.c_ref, f32[16,1,512]{2,1,0:T(1,128)} %bitcast.73, bf16[8,320,512]{2,1,0:T(8,128)(2,1)} %get-tuple-element.38.xk_ref, ...), custom_call_target="tpu_custom_call" | custom-call | flops 1400000000 | bytes 8000000 | tf_op jit(solution)/shard_map/early_product/pallas_call | solution.py:330
  122.1 0.9 collective-permute-done.5.ue
  123.0 3.7 %total.1 = (f32[512,1024]{1,0:T(8,128)}, f32[8,128]{1,0:T(8,128)}, bf16[256,1024]{1,0:T(8,128)(2,1)}) custom-call(bf16[448,512]{1,0:T(8,128)(2,1)} %slice_bitcast_fusion.1.a0, bf16[448,512]{1,0:T(8,128)(2,1)} %slice_bitcast_fusion.a1, bf16[224,512]{1,0:T(8,128)(2,1)} %collective-permute-done.5.ue, bf16[224,512]{1,0:T(8,128)(2,1)} %collective-permute-done.8.ul, ...), custom_call_target="tpu_custom_call" | custom-call | flops 5000000 | bytes 5000000 | tf_op jit(solution)/shard_map/total/pallas_call | solution.py:220
  126.7 2.4 %collective-permute-start.19 = (f32[8,128]{1,0:T(8,128)}, f32[8,128]{1,0:T(8,128)S(1)}, u32[]{:S(2)}, u32[]{:S(2)}) collective-permute-start(f32[8,128]{1,0:T(8,128)} %get-tuple-element.57), channel_id=1, source_target_pairs={{0,1},{1,0},{2,3},{3,2},{4,5},{5,4},{6,7},{7,6},{8,9},{9,8},{10,11... | collective-permute-start | bytes 12296 | tf_op jit(solution)/shard_map/ppermute | solution.py:42
  129.1 1.0 collective-permute-done.19
  130.2 0.7 add.180
  130.9 0.3 collective-permute-start.20
  131.2 2.1 %collective-permute-done.20 = f32[8,128]{1,0:T(8,128)S(1)} collective-permute-done((f32[8,128]{1,0:T(8,128)S(1)}, f32[8,128]{1,0:T(8,128)S(1)}, u32[]{:S(2)}, u32[]{:S(2)}) %collective-permute-start.20) | collective-permute-done | bytes 4128 | tf_op jit(solution)/shard_map/ppermute | solution.py:46
  133.3 2.5 %collective-permute-start.23 = (f32[8,128]{1,0:T(8,128)S(1)}, f32[8,128]{1,0:T(8,128)S(1)}, u32[]{:S(2)}, u32[]{:S(2)}) collective-permute-start(f32[8,128]{1,0:T(8,128)S(1)} %add.181), channel_id=1, source_target_pairs={{0,12},{1,13},{2,14},{3,15},{4,0},{5,1},{6,2},{7,3},{8,4},{9,5},{1... | collective-permute-start | bytes 12296 | tf_op jit(solution)/shard_map/ppermute | solution.py:50
  135.8 0.6 collective-permute-start.21
  136.4 0.6 stack.70.table_ref
  137.0 2.7 %collective-permute-done.22 = f32[8,128]{1,0:T(8,128)S(1)} collective-permute-done((f32[8,128]{1,0:T(8,128)S(1)}, f32[8,128]{1,0:T(8,128)S(1)}, u32[]{:S(2)}, u32[]{:S(2)}) %collective-permute-start.22) | collective-permute-done | bytes 4128 | tf_op jit(solution)/shard_map/ppermute | solution.py:50
  139.8 0.6 add_add_fusion.sq_ref
  140.4 7.3 %adam.1 = (f32[1,512,1024]{2,1,0:T(8,128)}, f32[1,512,1024]{2,1,0:T(8,128)}, bf16[2,512,128]{2,1,0:T(8,128)(2,1)}, bf16[2,512,128]{2,1,0:T(8,128)(2,1)}, bf16[2,...) custom-call(s32[5]{0:T(128)} %stack.70.table_ref, f32[8,128]{1,0:T(8,128)} %add_add_fusion.sq_ref, ...), custom_call_target="tpu_custom_call" | custom-call | flops 20000000 | bytes 12000000 | tf_op jit(solution)/shard_map/adam/pallas_call | solution.py:261
  147.7 1.3 collective-permute-start.24
  149.0 2.3 %collective-permute-start.25 = (bf16[2,512,128]{2,1,0:T(8,128)(2,1)}, bf16[2,512,128]{2,1,0:T(8,128)(2,1)S(1)}, u32[]{:S(2)}, u32[]{:S(2)}) collective-permute-start(bf16[2,512,128]{2,1,0:T(8,128)(2,1)} %get-tuple-element.63), channel_id=1, source_target_pairs={{0,64},{16,80},{32,96},{48,112},{64,0},{80,16},{96,32},{112,48},{1... | collective-permute-start | bytes 786440 | tf_op jit(solution)/shard_map/ppermute | solution.py:58
  151.4 1.3 collective-permute-start.26
  152.6 1.8 collective-permute-done.24
  154.4 5.8 %collective-permute-done.25 = bf16[2,512,128]{2,1,0:T(8,128)(2,1)S(1)} collective-permute-done((bf16[2,512,128]{2,1,0:T(8,128)(2,1)}, bf16[2,512,128]{2,1,0:T(8,128)(2,1)S(1)}, u32[]{:S(2)}, u32[]{:S(2)}) %collective-permute-start.25) | collective-permute-done | bytes 262176 | tf_op jit(solution)/shard_map/ppermute | solution.py:58
  160.3 0.4 collective-permute-done.26
  160.7 1.1 add_convert_fusion.1
  161.8 2.6 %collective-permute-start.27 = (bf16[2,512,128]{2,1,0:T(8,128)(2,1)S(1)}, bf16[2,512,128]{2,1,0:T(8,128)(2,1)S(1)}, u32[]{:S(2)}, u32[]{:S(2)}) collective-permute-start(bf16[2,512,128]{2,1,0:T(8,128)(2,1)S(1)} %rev.3), channel_id=1, source_target_pairs={{0,16},{16,0},{32,48},{48,32},{64,80},{80,64},{96,112},{112,96},{1... | collective-permute-start | bytes 786440 | tf_op jit(solution)/shard_map/ppermute | solution.py:54
  164.3 11.5 %collective-permute-done.27 = bf16[2,512,128]{2,1,0:T(8,128)(2,1)S(1)} collective-permute-done((bf16[2,512,128]{2,1,0:T(8,128)(2,1)S(1)}, bf16[2,512,128]{2,1,0:T(8,128)(2,1)S(1)}, u32[]{:S(2)}, u32[]{:S(2)}) %collective-permute-start.27) | collective-permute-done | bytes 262176 | tf_op jit(solution)/shard_map/ppermute | solution.py:54
  176.0 4.3 %collective-permute-start.30 = (bf16[2,512,128]{2,1,0:T(8,128)(2,1)S(1)}, bf16[2,512,128]{2,1,0:T(8,128)(2,1)S(1)}, u32[]{:S(2)}, u32[]{:S(2)}) collective-permute-start(bf16[2,512,128]{2,1,0:T(8,128)(2,1)S(1)} %get-tuple-element.75.refs_0_), channel_id=1, source_target_pairs={{0,32},{16,48},{32,64},{48,80},{64,96},{80,112},{96,0},{112,16},{1... | collective-permute-start | bytes 786440 | tf_op jit(solution)/shard_map/ppermute | solution.py:58
  180.2 0.9 collective-permute-start.29
  181.1 1.6 collective-permute-start.28
  182.7 0.9 multiply_subtract_fusion
  183.6 3.7 %all-gather.4.cloned.1.call-done = bf16[4096,1024]{1,0:T(8,128)(2,1)} async-done(((bf16[256,1024]{1,0:T(8,128)(2,1)}), bf16[4096,1024]{1,0:T(8,128)(2,1)}) %all-gather.4.cloned.1.call-update) | async-done | bytes 8388624 | tf_op jit(solution)/shard_map/all_gather | solution.py:500
  187.2 13.4 %input_gradient.1 = (bf16[1,320,8192]{2,1,0:T(8,128)(2,1)}, f32[8,128]{1,0:T(8,128)}) custom-call(s32[1]{0:T(128)} %bitcast.core_ref, bf16[320,1024]{1,0:T(8,128)(2,1)} %get-tuple-element.36.cp_ref.c_ref, f32[320,128]{1,0:T(8,128)} %get-tuple-element.37.inv_ref, f32[16,1,512]{2,1,0:T(1,128)} %bitcast.74, bf16[8,320,512]{2,1,0:T(8,128)(2,1)} %get-tuple-element.38.xk_ref, ...), custom_call_target="tpu_custom_call" | custom-call | flops 5000000000 | bytes 30000000 | tf_op jit(solution)/shard_map/input_gradient/pallas_call | solution.py:397
  200.8 0.6 copy-done.9
  201.6 2.9 %place.1 = bf16[512,1024]{1,0:T(8,128)(2,1)} custom-call(s32[5]{0:T(128)} %stack.70.table_ref, bf16[2,512,128]{2,1,0:T(8,128)(2,1)} %copy-done.3, bf16[2,512,128]{2,1,0:T(8,128)(2,1)} %copy-done.11, bf16[2,512,128]{2,1,0:T(8,128)(2,1)} %copy-done.10, bf16[2,512,128]{2,1,0:T(8,128)(2,1)} %copy-done.9, f32[8,128]{1,0:T(8,128)} %get-tuple-element.65.refs_4_), custom_call_target="tpu_custom_call" | custom-call | flops 1000000 | bytes 2000000 | tf_op jit(solution)/shard_map/place/pallas_call | solution.py:285
  (72 shorter events, 2.3 us)
Async XLA Ops:
  7.2 107.6 %all-gather.6.cloned.1.call-start = ((), (), s32[]{:S(2)}) async-start(), calls=%async_computation.1 | async-start | bytes 8912896 | tf_op jit(solution)/shard_map/all_gather | solution.py:453
  9.1 178.1 %all-gather.4.cloned.1.call-start = ((), (), s32[]{:S(2)}) async-start(), calls=%async_computation | async-start | bytes 8912896 | tf_op jit(solution)/shard_map/all_gather | solution.py:500
  9.8 10.3 %copy-start.1 = (f32[512,128]{1,0:T(8,128)S(1)}, f32[512,128]{1,0:T(8,128)}, u32[]{:S(2)}) copy-start(f32[512,128]{1,0:T(8,128)} %param.19) | copy-start | bytes 786436
  9.8 10.3 %copy-start.2 = (f32[512,128]{1,0:T(8,128)S(1)}, f32[512,128]{1,0:T(8,128)}, u32[]{:S(2)}) copy-start(f32[512,128]{1,0:T(8,128)} %param.18) | copy-start | bytes 786436
  18.1 23.1 %collective-permute-start = (bf16[8,320,512]{2,1,0:T(8,128)(2,1)}, bf16[8,320,512]{2,1,0:T(8,128)(2,1)}, u32[]{:S(2)}, u32[]{:S(2)}) collective-permute-start(bf16[8,320,512]{2,1,0:T(8,128)(2,1)} %get-tuple-element.39.xs_ref), channel_id=1, source_target_pairs={{0,1},{1,0},{2,3},{3,2},{4,5},{5,4},{6,7},{7,6},{8,9},{9,8},{10,11... | collective-permute-start | bytes 7864328 | tf_op jit(solution)/shard_map/ppermute | solution.py:42
  19.6 6.3 %collective-permute-start.3 = (bf16[2,320,512]{2,1,0:T(8,128)(2,1)}, bf16[2,320,512]{2,1,0:T(8,128)(2,1)S(1)}, u32[]{:S(2)}, u32[]{:S(2)}) collective-permute-start(bf16[2,320,512]{2,1,0:T(8,128)(2,1)} %get-tuple-element.42), channel_id=1, source_target_pairs={{0,1},{1,0},{2,3},{3,2},{4,5},{5,4},{6,7},{7,6},{8,9},{9,8},{10,11... | collective-permute-start | bytes 1966088 | tf_op jit(solution)/shard_map/ppermute | solution.py:42
  19.7 7.1 %collective-permute-start.1 = (bf16[320,1024]{1,0:T(8,128)(2,1)}, bf16[320,1024]{1,0:T(8,128)(2,1)S(1)}, u32[]{:S(2)}, u32[]{:S(2)}) collective-permute-start(bf16[320,1024]{1,0:T(8,128)(2,1)} %get-tuple-element.36.cp_ref.c_ref), channel_id=1, source_target_pairs={{0,1},{1,0},{2,3},{3,2},{4,5},{5,4},{6,7},{7,6},{8,9},{9,8},{10,11... | collective-permute-start | bytes 1966088 | tf_op jit(solution)/shard_map/ppermute | solution.py:42
  20.2 18.8 %collective-permute-start.2 = (f32[512,128]{1,0:T(8,128)S(1)}, f32[512,128]{1,0:T(8,128)S(1)}, u32[]{:S(2)}, u32[]{:S(2)}) collective-permute-start(f32[512,128]{1,0:T(8,128)S(1)} %multiply_subtract_fusion.1), channel_id=1, source_target_pairs={{0,16},{16,0},{32,48},{48,32},{64,80},{80,64},{96,112},{112,96},{1... | collective-permute-start | bytes 786440 | tf_op jit(solution)/shard_map/ppermute | solution.py:54
  25.9 0.9 copy-start.15
  26.8 0.8 copy-start.14
  27.7 9.4 %copy-start.13 = (bf16[8192]{0:T(1024)(128)(2,1)S(1)}, bf16[8192]{0:T(1024)(128)(2,1)}, u32[]{:S(2)}) copy-start(bf16[8192]{0:T(1024)(128)(2,1)} %param.14) | copy-start | bytes 49156
  33.2 28.4 %collective-permute-start.16 = (bf16[576,512]{1,0:T(8,128)(2,1)}, bf16[576,512]{1,0:T(8,128)(2,1)S(1)}, u32[]{:S(2)}, u32[]{:S(2)}) collective-permute-start(bf16[576,512]{1,0:T(8,128)(2,1)} %bitcast.77), channel_id=1, source_target_pairs={{0,12},{1,13},{2,14},{3,15},{4,0},{5,1},{6,2},{7,3},{8,4},{9,5},{1... | collective-permute-start | bytes 1769480 | tf_op jit(solution)/shard_map/ppermute | solution.py:50
  39.8 29.3 %collective-permute-start.6 = (bf16[448,512]{1,0:T(8,128)(2,1)}, bf16[448,512]{1,0:T(8,128)(2,1)S(1)}, u32[]{:S(2)}, u32[]{:S(2)}) collective-permute-start(bf16[448,512]{1,0:T(8,128)(2,1)} %bitcast.80), channel_id=1, source_target_pairs={{0,2},{1,3},{2,0},{3,1},{4,6},{5,7},{6,4},{7,5},{8,10},{9,11},{10,... | collective-permute-start | bytes 1376264 | tf_op jit(solution)/shard_map/ppermute | solution.py:46
  41.2 25.5 %collective-permute-start.12 = (bf16[576,512]{1,0:T(8,128)(2,1)}, bf16[576,512]{1,0:T(8,128)(2,1)S(1)}, u32[]{:S(2)}, u32[]{:S(2)}) collective-permute-start(bf16[576,512]{1,0:T(8,128)(2,1)} %bitcast.76), channel_id=1, source_target_pairs={{0,4},{1,5},{2,6},{3,7},{4,8},{5,9},{6,10},{7,11},{8,12},{9,13},{1... | collective-permute-start | bytes 1769480 | tf_op jit(solution)/shard_map/ppermute | solution.py:50
  52.3 14.4 %copy-start.4 = (bf16[1,576,512]{2,1,0:T(8,128)(2,1)S(1)}, bf16[1,576,512]{2,1,0:T(8,128)(2,1)}, u32[]{:S(2)}) copy-start(bf16[1,576,512]{2,1,0:T(8,128)(2,1)} %get-tuple-element.49) | copy-start | bytes 1769476
  52.3 38.7 %collective-permute-start.15 = (bf16[576,512]{1,0:T(8,128)(2,1)}, bf16[576,512]{1,0:T(8,128)(2,1)S(1)}, u32[]{:S(2)}, u32[]{:S(2)}) collective-permute-start(bf16[576,512]{1,0:T(8,128)(2,1)} %bitcast.79), channel_id=1, source_target_pairs={{0,4},{1,5},{2,6},{3,7},{4,8},{5,9},{6,10},{7,11},{8,12},{9,13},{1... | collective-permute-start | bytes 1769480 | tf_op jit(solution)/shard_map/ppermute | solution.py:50
  52.4 56.0 %collective-permute-start.4 = (bf16[3,448,512]{2,1,0:T(8,128)(2,1)}, bf16[3,448,512]{2,1,0:T(8,128)(2,1)S(1)}, u32[]{:S(2)}, u32[]{:S(2)}) collective-permute-start(bf16[3,448,512]{2,1,0:T(8,128)(2,1)} %get-tuple-element.45), channel_id=1, source_target_pairs={{0,2},{1,3},{2,0},{3,1},{4,6},{5,7},{6,4},{7,5},{8,10},{9,11},{10,... | collective-permute-start | bytes 4128776 | tf_op jit(solution)/shard_map/ppermute | solution.py:46
  61.7 7.5 %copy-start.16 = (bf16[1,576,512]{2,1,0:T(8,128)(2,1)S(1)}, bf16[1,576,512]{2,1,0:T(8,128)(2,1)}, u32[]{:S(2)}) copy-start(bf16[1,576,512]{2,1,0:T(8,128)(2,1)} %get-tuple-element.50) | copy-start | bytes 1769476
  61.7 8.0 %copy-start.8 = (bf16[1,448,512]{2,1,0:T(8,128)(2,1)S(1)}, bf16[1,448,512]{2,1,0:T(8,128)(2,1)}, u32[]{:S(2)}) copy-start(bf16[1,448,512]{2,1,0:T(8,128)(2,1)} %get-tuple-element.46) | copy-start | bytes 1376260
  63.0 28.3 %collective-permute-start.17 = (bf16[576,512]{1,0:T(8,128)(2,1)S(1)}, bf16[576,512]{1,0:T(8,128)(2,1)S(1)}, u32[]{:S(2)}, u32[]{:S(2)}) collective-permute-start(bf16[576,512]{1,0:T(8,128)(2,1)S(1)} %fusion), channel_id=1, source_target_pairs={{0,12},{1,13},{2,14},{3,15},{4,0},{5,1},{6,2},{7,3},{8,4},{9,5},{1... | collective-permute-start | bytes 1769480 | tf_op jit(solution)/shard_map/ppermute | solution.py:50
  66.7 3.0 %copy-start = (bf16[3,448,512]{2,1,0:T(8,128)(2,1)S(1)}, bf16[3,448,512]{2,1,0:T(8,128)(2,1)}, u32[]{:S(2)}) copy-start(bf16[3,448,512]{2,1,0:T(8,128)(2,1)} %get-tuple-element.44) | copy-start | bytes 4128772
  66.9 26.2 %copy-start.7 = (bf16[1,576,512]{2,1,0:T(8,128)(2,1)S(1)}, bf16[1,576,512]{2,1,0:T(8,128)(2,1)}, u32[]{:S(2)}) copy-start(bf16[1,576,512]{2,1,0:T(8,128)(2,1)} %get-tuple-element.51) | copy-start | bytes 1769476
  66.9 36.6 %collective-permute-start.13 = (bf16[576,512]{1,0:T(8,128)(2,1)S(1)}, bf16[576,512]{1,0:T(8,128)(2,1)S(1)}, u32[]{:S(2)}, u32[]{:S(2)}) collective-permute-start(bf16[576,512]{1,0:T(8,128)(2,1)S(1)} %fusion.3), channel_id=1, source_target_pairs={{0,4},{1,5},{2,6},{3,7},{4,8},{5,9},{6,10},{7,11},{8,12},{9,13},{1... | collective-permute-start | bytes 1769480 | tf_op jit(solution)/shard_map/ppermute | solution.py:50
  69.2 34.5 %collective-permute-start.14 = (bf16[576,512]{1,0:T(8,128)(2,1)S(1)}, bf16[576,512]{1,0:T(8,128)(2,1)S(1)}, u32[]{:S(2)}, u32[]{:S(2)}) collective-permute-start(bf16[576,512]{1,0:T(8,128)(2,1)S(1)} %bitcast.78), channel_id=1, source_target_pairs={{0,12},{1,13},{2,14},{3,15},{4,0},{5,1},{6,2},{7,3},{8,4},{9,5},{1... | collective-permute-start | bytes 1769480 | tf_op jit(solution)/shard_map/ppermute | solution.py:50
  70.6 33.1 %copy-start.5 = (bf16[1,576,512]{2,1,0:T(8,128)(2,1)S(1)}, bf16[1,576,512]{2,1,0:T(8,128)(2,1)}, u32[]{:S(2)}) copy-start(bf16[1,576,512]{2,1,0:T(8,128)(2,1)} %get-tuple-element.48) | copy-start | bytes 1769476
  91.0 15.2 %collective-permute-start.10 = (bf16[224,512]{1,0:T(8,128)(2,1)S(1)}, bf16[224,512]{1,0:T(8,128)(2,1)S(1)}, u32[]{:S(2)}, u32[]{:S(2)}) collective-permute-start(bf16[224,512]{1,0:T(8,128)(2,1)S(1)} %get-tuple-element.72), channel_id=1, source_target_pairs={{0,12},{1,13},{2,14},{3,15},{4,0},{5,1},{6,2},{7,3},{8,4},{9,5},{1... | collective-permute-start | bytes 688136 | tf_op jit(solution)/shard_map/ppermute | solution.py:50
  91.3 17.2 %collective-permute-start.7 = (bf16[224,512]{1,0:T(8,128)(2,1)S(1)}, bf16[224,512]{1,0:T(8,128)(2,1)S(1)}, u32[]{:S(2)}, u32[]{:S(2)}) collective-permute-start(bf16[224,512]{1,0:T(8,128)(2,1)S(1)} %get-tuple-element.73), channel_id=1, source_target_pairs={{0,4},{1,5},{2,6},{3,7},{4,8},{5,9},{6,10},{7,11},{8,12},{9,13},{1... | collective-permute-start | bytes 688136 | tf_op jit(solution)/shard_map/ppermute | solution.py:50
  103.5 18.5 %collective-permute-start.18 = (bf16[576,512]{1,0:T(8,128)(2,1)S(1)}, bf16[576,512]{1,0:T(8,128)(2,1)S(1)}, u32[]{:S(2)}, u32[]{:S(2)}) collective-permute-start(bf16[576,512]{1,0:T(8,128)(2,1)S(1)} %fusion.2), channel_id=1, source_target_pairs={{0,2},{1,3},{2,0},{3,1},{4,6},{5,7},{6,4},{7,5},{8,10},{9,11},{10,... | collective-permute-start | bytes 1769480 | tf_op jit(solution)/shard_map/ppermute | solution.py:46
  108.6 13.4 %collective-permute-start.11 = (bf16[224,512]{1,0:T(8,128)(2,1)S(1)}, bf16[224,512]{1,0:T(8,128)(2,1)S(1)}, u32[]{:S(2)}, u32[]{:S(2)}) collective-permute-start(bf16[224,512]{1,0:T(8,128)(2,1)S(1)} %get-tuple-element.68), channel_id=1, source_target_pairs={{0,12},{1,13},{2,14},{3,15},{4,0},{5,1},{6,2},{7,3},{8,4},{9,5},{1... | collective-permute-start | bytes 688136 | tf_op jit(solution)/shard_map/ppermute | solution.py:50
  111.1 11.0 %collective-permute-start.8 = (bf16[224,512]{1,0:T(8,128)(2,1)S(1)}, bf16[224,512]{1,0:T(8,128)(2,1)}, u32[]{:S(2)}, u32[]{:S(2)}) collective-permute-start(bf16[224,512]{1,0:T(8,128)(2,1)S(1)} %get-tuple-element.69), channel_id=1, source_target_pairs={{0,4},{1,5},{2,6},{3,7},{4,8},{5,9},{6,10},{7,11},{8,12},{9,13},{1... | collective-permute-start | bytes 688136 | tf_op jit(solution)/shard_map/ppermute | solution.py:50
  111.2 10.9 %collective-permute-start.9 = (bf16[224,512]{1,0:T(8,128)(2,1)S(1)}, bf16[224,512]{1,0:T(8,128)(2,1)}, u32[]{:S(2)}, u32[]{:S(2)}) collective-permute-start(bf16[224,512]{1,0:T(8,128)(2,1)S(1)} %get-tuple-element.70), channel_id=1, source_target_pairs={{0,12},{1,13},{2,14},{3,15},{4,0},{5,1},{6,2},{7,3},{8,4},{9,5},{1... | collective-permute-start | bytes 688136 | tf_op jit(solution)/shard_map/ppermute | solution.py:50
  113.9 9.0 %collective-permute-start.5 = (bf16[224,512]{1,0:T(8,128)(2,1)S(1)}, bf16[224,512]{1,0:T(8,128)(2,1)}, u32[]{:S(2)}, u32[]{:S(2)}) collective-permute-start(bf16[224,512]{1,0:T(8,128)(2,1)S(1)} %get-tuple-element.71), channel_id=1, source_target_pairs={{0,4},{1,5},{2,6},{3,7},{4,8},{5,9},{6,10},{7,11},{8,12},{9,13},{1... | collective-permute-start | bytes 688136 | tf_op jit(solution)/shard_map/ppermute | solution.py:50
  122.0 1.0 copy-start.6
  122.0 0.9 copy-start.12
  126.7 3.5 %collective-permute-start.19 = (f32[8,128]{1,0:T(8,128)}, f32[8,128]{1,0:T(8,128)S(1)}, u32[]{:S(2)}, u32[]{:S(2)}) collective-permute-start(f32[8,128]{1,0:T(8,128)} %get-tuple-element.57), channel_id=1, source_target_pairs={{0,1},{1,0},{2,3},{3,2},{4,5},{5,4},{6,7},{7,6},{8,9},{9,8},{10,11... | collective-permute-start | bytes 12296 | tf_op jit(solution)/shard_map/ppermute | solution.py:42
  130.9 2.5 %collective-permute-start.20 = (f32[8,128]{1,0:T(8,128)S(1)}, f32[8,128]{1,0:T(8,128)S(1)}, u32[]{:S(2)}, u32[]{:S(2)}) collective-permute-start(f32[8,128]{1,0:T(8,128)S(1)} %add.180), channel_id=1, source_target_pairs={{0,2},{1,3},{2,0},{3,1},{4,6},{5,7},{6,4},{7,5},{8,10},{9,11},{10,... | collective-permute-start | bytes 12296 | tf_op jit(solution)/shard_map/ppermute | solution.py:46
  133.3 3.7 %collective-permute-start.23 = (f32[8,128]{1,0:T(8,128)S(1)}, f32[8,128]{1,0:T(8,128)S(1)}, u32[]{:S(2)}, u32[]{:S(2)}) collective-permute-start(f32[8,128]{1,0:T(8,128)S(1)} %add.181), channel_id=1, source_target_pairs={{0,12},{1,13},{2,14},{3,15},{4,0},{5,1},{6,2},{7,3},{8,4},{9,5},{1... | collective-permute-start | bytes 12296 | tf_op jit(solution)/shard_map/ppermute | solution.py:50
  135.8 4.0 %collective-permute-start.22 = (f32[8,128]{1,0:T(8,128)S(1)}, f32[8,128]{1,0:T(8,128)S(1)}, u32[]{:S(2)}, u32[]{:S(2)}) collective-permute-start(f32[8,128]{1,0:T(8,128)S(1)} %add.181), channel_id=1, source_target_pairs={{0,8},{1,9},{2,10},{3,11},{4,12},{5,13},{6,14},{7,15},{8,0},{9,1},... | collective-permute-start | bytes 12296 | tf_op jit(solution)/shard_map/ppermute | solution.py:50
  135.8 4.0 %collective-permute-start.21 = (f32[8,128]{1,0:T(8,128)S(1)}, f32[8,128]{1,0:T(8,128)S(1)}, u32[]{:S(2)}, u32[]{:S(2)}) collective-permute-start(f32[8,128]{1,0:T(8,128)S(1)} %add.181), channel_id=1, source_target_pairs={{0,4},{1,5},{2,6},{3,7},{4,8},{5,9},{6,10},{7,11},{8,12},{9,13},{1... | collective-permute-start | bytes 12296 | tf_op jit(solution)/shard_map/ppermute | solution.py:50
  147.7 6.7 %collective-permute-start.24 = (bf16[2,512,128]{2,1,0:T(8,128)(2,1)}, bf16[2,512,128]{2,1,0:T(8,128)(2,1)S(1)}, u32[]{:S(2)}, u32[]{:S(2)}) collective-permute-start(bf16[2,512,128]{2,1,0:T(8,128)(2,1)} %get-tuple-element.62), channel_id=1, source_target_pairs={{0,32},{16,48},{32,64},{48,80},{64,96},{80,112},{96,0},{112,16},{1... | collective-permute-start | bytes 786440 | tf_op jit(solution)/shard_map/ppermute | solution.py:58
  149.0 11.2 %collective-permute-start.25 = (bf16[2,512,128]{2,1,0:T(8,128)(2,1)}, bf16[2,512,128]{2,1,0:T(8,128)(2,1)S(1)}, u32[]{:S(2)}, u32[]{:S(2)}) collective-permute-start(bf16[2,512,128]{2,1,0:T(8,128)(2,1)} %get-tuple-element.63), channel_id=1, source_target_pairs={{0,64},{16,80},{32,96},{48,112},{64,0},{80,16},{96,32},{112,48},{1... | collective-permute-start | bytes 786440 | tf_op jit(solution)/shard_map/ppermute | solution.py:58
  151.4 9.3 %collective-permute-start.26 = (bf16[2,512,128]{2,1,0:T(8,128)(2,1)}, bf16[2,512,128]{2,1,0:T(8,128)(2,1)S(1)}, u32[]{:S(2)}, u32[]{:S(2)}) collective-permute-start(bf16[2,512,128]{2,1,0:T(8,128)(2,1)} %get-tuple-element.64), channel_id=1, source_target_pairs={{0,96},{16,112},{32,0},{48,16},{64,32},{80,48},{96,64},{112,80},{1... | collective-permute-start | bytes 786440 | tf_op jit(solution)/shard_map/ppermute | solution.py:58
  161.8 14.1 %collective-permute-start.27 = (bf16[2,512,128]{2,1,0:T(8,128)(2,1)S(1)}, bf16[2,512,128]{2,1,0:T(8,128)(2,1)S(1)}, u32[]{:S(2)}, u32[]{:S(2)}) collective-permute-start(bf16[2,512,128]{2,1,0:T(8,128)(2,1)S(1)} %rev.3), channel_id=1, source_target_pairs={{0,16},{16,0},{32,48},{48,32},{64,80},{80,64},{96,112},{112,96},{1... | collective-permute-start | bytes 786440 | tf_op jit(solution)/shard_map/ppermute | solution.py:54
  176.0 24.7 %copy-start.3 = (bf16[2,512,128]{2,1,0:T(8,128)(2,1)}, bf16[2,512,128]{2,1,0:T(8,128)(2,1)S(1)}, u32[]{:S(2)}) copy-start(bf16[2,512,128]{2,1,0:T(8,128)(2,1)S(1)} %get-tuple-element.75.refs_0_) | copy-start | bytes 786436
  176.0 24.7 %collective-permute-start.30 = (bf16[2,512,128]{2,1,0:T(8,128)(2,1)S(1)}, bf16[2,512,128]{2,1,0:T(8,128)(2,1)S(1)}, u32[]{:S(2)}, u32[]{:S(2)}) collective-permute-start(bf16[2,512,128]{2,1,0:T(8,128)(2,1)S(1)} %get-tuple-element.75.refs_0_), channel_id=1, source_target_pairs={{0,32},{16,48},{32,64},{48,80},{64,96},{80,112},{96,0},{112,16},{1... | collective-permute-start | bytes 786440 | tf_op jit(solution)/shard_map/ppermute | solution.py:58
  180.2 20.5 %collective-permute-start.29 = (bf16[2,512,128]{2,1,0:T(8,128)(2,1)S(1)}, bf16[2,512,128]{2,1,0:T(8,128)(2,1)S(1)}, u32[]{:S(2)}, u32[]{:S(2)}) collective-permute-start(bf16[2,512,128]{2,1,0:T(8,128)(2,1)S(1)} %get-tuple-element.75.refs_0_), channel_id=1, source_target_pairs={{0,64},{16,80},{32,96},{48,112},{64,0},{80,16},{96,32},{112,48},{1... | collective-permute-start | bytes 786440 | tf_op jit(solution)/shard_map/ppermute | solution.py:58
  181.1 19.6 %collective-permute-start.28 = (bf16[2,512,128]{2,1,0:T(8,128)(2,1)S(1)}, bf16[2,512,128]{2,1,0:T(8,128)(2,1)S(1)}, u32[]{:S(2)}, u32[]{:S(2)}) collective-permute-start(bf16[2,512,128]{2,1,0:T(8,128)(2,1)S(1)} %get-tuple-element.75.refs_0_), channel_id=1, source_target_pairs={{0,96},{16,112},{32,0},{48,16},{64,32},{80,48},{96,64},{112,80},{1... | collective-permute-start | bytes 786440 | tf_op jit(solution)/shard_map/ppermute | solution.py:58
  200.7 0.7 copy-start.9
  200.7 0.8 copy-start.10
  200.7 0.9 copy-start.11
Sparse Core Ops, SparseCore 0:
  9.7 87.5 all-gather.5
  126.8 60.3 all-gather.3

commit v6 on v5

--- a/solution.py
+++ b/solution.py
@@ -16,6 +16,7 @@
 outer_beta = 0.9
 outer_rate = 0.7
 replay_weight = 0.5
+outer_kept = 1.0 - outer_rate * (1.0 + outer_beta)
 
 F32 = jnp.float32
 BF16 = jnp.bfloat16
@@ -28,6 +29,9 @@
 
 def cost(flops, size):
     return pl.CostEstimate(flops=int(flops), bytes_accessed=int(size), transcendentals=0)
+
+
+anywhere = pl.BlockSpec(memory_space=pl.ANY)
 
 
 def params(mib):
@@ -81,7 +85,7 @@
             fresh = fresh.astype(F32)
             squares = squares + jnp.concatenate([lane_sum(fresh * fresh), lane_sum(replayed * replayed)], axis=0)
 
-    @pl.when(step == core_ref[1])
+    @pl.when(step == core_ref[6])
     def _():
         xf_ref[...] = xs_ref[...]
 
@@ -137,6 +141,22 @@
     )(core, replay_index, hidden, replay_buffer, cotangent)
 
 
+def after_kernel(*refs):
+    pass
+
+
+def after(value, *tokens):
+    return pl.pallas_call(
+        after_kernel,
+        in_specs=[anywhere] * (1 + len(tokens)),
+        out_specs=anywhere,
+        out_shape=sds(value.shape, value.dtype),
+        input_output_aliases={0: 0},
+        cost_estimate=cost(0, 0),
+        name="after",
+    )(value, *tokens)
+
+
 x_first = 448
 z_first = 1024 - x_first
 
@@ -144,7 +164,7 @@
 def grad_kernel(plan, n_after, table_ref, xk_ref, xs_ref, c_ref, cs_ref, *rest):
     outs, (x_all, c_all) = rest[n_after:-2], rest[-2:]
     step = pl.program_id(0)
-    x = table_ref[4]
+    x = table_ref[2]
 
     @pl.when(step == 0)
     def _():
@@ -166,10 +186,14 @@
                         out_ref[...] = part[:, 512 * dx : 512 * dx + 512]
 
 
-def grad_blocks(place, chunks, outputs, xk, xs, c, cs, after, name):
-    z, x = place
-    table = jnp.stack([(z + dz) % 4 for dz in chunks] + [jnp.int32(0)] * (4 - len(chunks)) + [x])
-    x_spec = pl.BlockSpec((2, 320, 512), lambda t, tab: (tab[t], 0, 0))
+def grad_blocks(table, chunks, outputs, xk, xs, c, cs, after, name):
+    order = chunks + [0] * (3 - len(chunks))
+
+    def at_z(t, tab):
+        dz = jnp.where(t == 0, order[0], jnp.where(t == 1, order[1], order[2]))
+        return (tab[4 + dz], 0, 0)
+
+    x_spec = pl.BlockSpec((2, 320, 512), at_z)
     s_spec = x_spec if xs.shape[0] == 8 else pl.BlockSpec((2, 320, 512), lambda t, tab: (0, 0, 0))
     c_spec = pl.BlockSpec((320, 1024), lambda t, tab: (0, 0))
     return pl.pallas_call(
@@ -193,17 +217,16 @@
     )(table, xk, xs, c, cs, *after)
 
 
-early_rows = 256
-
-
-def total_kernel(a0, a1, ue, ul, de, dl, b0, b1, gain_ref, w_ref, after_ref, grad_ref, sq_ref, late_ref):
+early_rows = 128
+
+
+def total_kernel(table_ref, a0, a1, ue, ul, de, dl, b0, b1, gain_ref, after_ref, grad_ref, sq_ref):
     step = pl.program_id(0)
-    late_ref[...] = w_ref[early_rows:512, :]
     up = jnp.concatenate([ul[...], ue[...]], axis=0).astype(F32)
     down = jnp.concatenate([de[...], dl[...]], axis=0).astype(F32)
     top = (a0[...].astype(F32) + a1[...].astype(F32)) + (up + down)
     low = b0[...].astype(F32) + b1[...].astype(F32)
-    both = jnp.concatenate([top, low], axis=0) * gain_ref[...]
+    both = jnp.concatenate([top, low], axis=0) * gain_ref[...].astype(F32)
     grad_ref[...] = both.T
     square = jnp.sum(lane_sum(both * both).reshape(128, 8, 128), axis=0)
 
@@ -216,23 +239,35 @@
         sq_ref[...] += square
 
 
-def total(parts, gain_row, weight, after):
+def total(table, parts, gain, after):
+    specs, arrays = [], []
+    for part in parts:
+        if isinstance(part, tuple):
+            specs.append(pl.BlockSpec((None, part[0].shape[1], 256), lambda t, tab, k=part[1]: (k, 0, t)))
+            arrays.append(part[0])
+        else:
+            specs.append(pl.BlockSpec((part.shape[0], 256), lambda t, tab: (0, t)))
+            arrays.append(part)
     return pl.pallas_call(
         total_kernel,
-        grid=(2,),
-        in_specs=[pl.BlockSpec((p.shape[0], 256), lambda t: (0, t)) for p in parts]
-        + [pl.BlockSpec((1, 256), lambda t: (0, t)), pl.BlockSpec((None, 512, 512), lambda t: (0, 0, t))]
-        + [pl.BlockSpec(memory_space=pl.ANY)] * len(after),
-        out_specs=[
-            pl.BlockSpec((256, 1024), lambda t: (t, 0)),
-            pl.BlockSpec((8, 128), lambda t: (0, 0)),
-            pl.BlockSpec((512 - early_rows, 512), lambda t: (0, t)),
-        ],
-        out_shape=[sds((512, 1024), F32), sds((8, 128), F32), sds((512 - early_rows, 1024), BF16)],
+        grid_spec=pltpu.PrefetchScalarGridSpec(
+            num_scalar_prefetch=1,
+            grid=(2,),
+            in_specs=specs
+            + [
+                pl.BlockSpec((1, 256), lambda t, tab: (0, 2 * tab[12] + t)),
+                pl.BlockSpec(memory_space=pl.ANY),
+            ],
+            out_specs=[
+                pl.BlockSpec((256, 1024), lambda t, tab: (t, 0)),
+                pl.BlockSpec((8, 128), lambda t, tab: (0, 0)),
+            ],
+        ),
+        out_shape=[sds((512, 1024), F32), sds((8, 128), F32)],
         compiler_params=params(60),
         cost_estimate=cost(5e6, 5e6),
         name="total",
-    )(*parts, gain_row, weight, *after)
+    )(table, *arrays, gain, after)
 
 
 def adam_kernel(table_ref, sq_ref, grad_ref, m_ref, v_ref, w_ref, first_ref, second_ref, *rest):
@@ -251,7 +286,7 @@
     new_ref[...] = (w_ref[...].astype(F32) - inner_rate * first * inverse).astype(BF16)
     for k, out_ref in enumerate(outs):
         for dx in range(2):
-            column = pl.multiple_of((2 * table_ref[k] + (table_ref[4] ^ dx)) * 128, 128)
+            column = pl.multiple_of((2 * table_ref[8 + k] + (table_ref[3] ^ dx)) * 128, 128)
             out_ref[dx] = new_ref[:, pl.ds(column, 128)]
 
 
@@ -277,7 +312,7 @@
 def place_kernel(table_ref, *refs):
     for k, in_ref in enumerate(refs[:4]):
         for dx in range(2):
-            column = pl.multiple_of((2 * table_ref[k] + (table_ref[4] ^ dx)) * 128, 128)
+            column = pl.multiple_of((2 * table_ref[8 + k] + (table_ref[3] ^ dx)) * 128, 128)
             refs[-1][:, pl.ds(column, 128)] = in_ref[dx]
 
 
@@ -306,7 +341,8 @@
         w = e_ref[...].reshape(4 * early_rows, 1024)
         q = lax.dot_general(cp_ref[...], w, (((1,), (1,)), ((), ())), preferred_element_type=F32)
         for j in range(4):
-            gain = gain_ref[2 * (4 * step + j) + (core ^ sibling)][:, 0:early_rows]
+            column = pl.multiple_of((2 * (4 * step + j) + (core ^ sibling)) * 512, 512)
+            gain = gain_ref[:, pl.ds(column, 512)][:, 0:early_rows].astype(F32)
             gained = q[:, early_rows * j : early_rows * (j + 1)] * gain
             m = m + lane_sum(gained * x_ref[j].astype(F32))
             q_ref[sibling, j] = gained.astype(BF16)
@@ -334,7 +370,7 @@
             grid=(2,),
             in_specs=[
                 pl.BlockSpec((320, 1024), lambda t, c: (0, 0)),
-                pl.BlockSpec((16, 1, 512), lambda t, c: (0, 0, 0)),
+                pl.BlockSpec((1, 8192), lambda t, c: (0, 0)),
                 x_spec,
                 x_spec,
                 weights(0),
@@ -370,7 +406,9 @@
             q = lax.dot_general(cp_ref[...], w, (((1,), (1,)), ((), ())), preferred_element_type=F32)
             for j in range(2):
                 g = 2 * step + j
-                gained = q[:, size * j : size * (j + 1)] * gain_ref[2 * g + (core ^ sibling)][:, early_rows:512]
+                column = pl.multiple_of((2 * g + (core ^ sibling)) * 512, 512)
+                gain = gain_ref[:, pl.ds(column, 512)][:, early_rows:512].astype(F32)
+                gained = q[:, size * j : size * (j + 1)] * gain
                 m = m + lane_sum(gained * x_ref[j, :, early_rows:512].astype(F32))
                 q_ref[8 * sibling + g, :, 0:early_rows] = qe_ref[sibling, j]
                 q_ref[8 * sibling + g, :, early_rows:512] = gained.astype(BF16)
@@ -402,7 +440,7 @@
             in_specs=[
                 pl.BlockSpec((320, 1024), lambda t, c: (0, 0)),
                 pl.BlockSpec((320, 128), lambda t, c: (0, 0)),
-                pl.BlockSpec((16, 1, 512), lambda t, c: (0, 0, 0)),
+                pl.BlockSpec((1, 8192), lambda t, c: (0, 0)),
                 x_spec,
                 x_spec,
                 pl.BlockSpec((2, 2, 320, early_rows), lambda t, c: (0, jnp.minimum(t, 3), 0, 0)),
@@ -421,6 +459,54 @@
         cost_estimate=cost(5e9, 3e7),
         name="input_gradient",
     )(core, cp, inv, gain, xk, xs, q_early, m_early, late, late)
+
+
+def sum_kernel(a, b, c, d, *rest):
+    total_value = (a[...].astype(F32) + b[...].astype(F32)) + (c[...].astype(F32) + d[...].astype(F32))
+    total_value = total_value.astype(BF16)
+    sum_ref, flip_ref = rest[-2:]
+    sum_ref[...] = total_value
+    flip_ref[0] = total_value[1]
+    flip_ref[1] = total_value[0]
+
+
+def sum_over_y(parts, after):
+    block = pl.BlockSpec((2, 512, 128), lambda t: (0, 0, 0))
+    return pl.pallas_call(
+        sum_kernel,
+        grid=(1,),
+        in_specs=[block] * 4 + [anywhere] * len(after),
+        out_specs=[block] * 2,
+        out_shape=[sds((2, 512, 128), BF16)] * 2,
+        compiler_params=params(60),
+        cost_estimate=cost(1e6, 2e6),
+        name="sum_over_y",
+    )(*parts, *after)
+
+
+def outer_kernel(mine, theirs, kept_ref, kept_theirs_ref, anchor_ref, momentum_ref, sent_ref, new_momentum_ref, new_anchor_ref):
+    inner_total = mine[...].astype(F32) + theirs[...].astype(F32)
+    sent_ref[0] = (kept_ref[...] + (1.0 - outer_kept) / 8 * inner_total[0]).astype(BF16)
+    sent_ref[1] = (kept_theirs_ref[...] + (1.0 - outer_kept) / 8 * inner_total[1]).astype(BF16)
+    outer_grad = anchor_ref[...] - inner_total[0] / 8
+    new_momentum = outer_beta * momentum_ref[...] + outer_grad
+    new_momentum_ref[...] = new_momentum
+    new_anchor_ref[...] = anchor_ref[...] - outer_rate * (outer_grad + outer_beta * new_momentum)
+
+
+def outer_step(mine, theirs, kept, kept_theirs, anchor, momentum):
+    pair = pl.BlockSpec((2, 512, 128), lambda t: (0, 0, 0))
+    one = pl.BlockSpec((512, 128), lambda t: (0, 0))
+    return pl.pallas_call(
+        outer_kernel,
+        grid=(1,),
+        in_specs=[pair, pair, one, one, one, one],
+        out_specs=[pair, one, one],
+        out_shape=[sds((2, 512, 128), BF16), sds((512, 128), F32), sds((512, 128), F32)],
+        compiler_params=params(60),
+        cost_estimate=cost(1e6, 3e6),
+        name="outer_step",
+    )(mine, theirs, kept, kept_theirs, anchor, momentum)
 
 
 def add(*values):
@@ -446,37 +532,34 @@
     rep = lax.axis_index("rep")
     core, x, z = fsdp % 2, (fsdp // 2) % 2, fsdp // 4
     x_hi, y = rep % 2, rep // 2
-    place = (z, x)
-    columns = jnp.stack([(y + dy) % 4 for dy in range(4)] + [x_hi])
-    gain_float = norm_gain.astype(F32)
+    table = jnp.stack(
+        [core, z, x, x_hi] + [(z + k) % 4 for k in range(4)] + [(y + k) % 4 for k in range(4)] + [fsdp]
+    )
+    gain = norm_gain[None]
 
     early = lax.all_gather(value_weight[0, :early_rows], "fsdp", axis=0, tiled=True)
 
-    xk, xs, xs_first, cp, inv = prep(jnp.stack([core, (z + 2) % 4]), hidden, replay_buffer, replay_index, cotangent)
+    xk, xs, xs_first, cp, inv = prep(table, hidden, replay_buffer, replay_index, cotangent)
     x_first_sib = over_core(xs_first)
     c_sib = over_core(cp)
+    xs = after(xs, x_first_sib, c_sib)
     x_sib = over_core(xs)
 
-    outer_1 = 1.0 - outer_rate * (1.0 + outer_beta)
-    kept = outer_1 * anchor - (outer_rate * outer_beta * outer_beta) * outer_momentum
-    kept = lax.optimization_barrier(kept)
-    kept = jnp.stack([kept, over_x_hi(kept)])
-
     b_20, b_21, a_21, a_20 = grad_blocks(
-        place, [2], [(0, 0, 0, 1), (0, 1, 0, 1), (1, 1, 0, 1), (1, 0, 0, 1)], xk, x_first_sib, cp, c_sib, [], "grad_a"
+        table, [2], [(0, 0, 0, 1), (0, 1, 0, 1), (1, 1, 0, 1), (1, 0, 0, 1)], xk, x_first_sib, cp, c_sib, [], "grad_a"
     )
     r_up = over_z(b_20[0], 1)
     r_down = over_z(b_21[0], -1)
     r_a2 = over_x(a_21[0])
     b_10, b_30, b_00, b_11, b_31, b_01, a_send, a_own = grad_blocks(
-        place,
+        table,
         [1, 3, 0],
         [(0, dx, step, 1) for dx in range(2) for step in range(3)] + [(1, 1, 0, 3), (1, 0, 0, 3)],
-        xk, x_sib, cp, c_sib, [kept, b_20], "grad_b",
+        xk, x_sib, cp, c_sib, [b_20], "grad_b",
     )
-    r_a = over_x(a_send)
-    e_up = over_z(b_11[0], 1)
-    e_down = over_z(b_30[0], -1)
+    r_a = over_x(after(a_send, r_a2))
+    e_up = over_z(after(b_11[0], r_up), 1)
+    e_down = over_z(after(b_30[0], r_down), -1)
     l_up = over_z(add(b_10[0], r_up), 1)
     l_down = over_z(add(b_31[0], r_down), -1)
 
@@ -488,36 +571,40 @@
     b_mine = add(b_00[0], l_up, e_down)
     b_theirs = add(b_01[0], e_up, l_down)
     r_b = over_x(b_theirs)
-    fl_up = over_z(add(a_own[0, :half], r_a[0, :half], p_up), 1)
-    fl_down = over_z(add(a_own[1, half:], r_a[1, half:], p_down), -1)
-
-    gain_row = lax.dynamic_slice(gain_float, (fsdp * 512,), (512,))[None, :]
-    gain = gain_float.reshape(16, 1, 512)
-    q_early, m_early = early_product(core[None], xk, xs, cp, gain, early)
-    grad, squares, late = total(
-        [a_own[2], r_a[2], fe_up, fl_up, fe_down, fl_down, b_mine, r_b], gain_row, value_weight, [m_early]
+    l_1 = add(a_own[0, :half], r_a[0, :half], p_up)
+    l_3 = add(a_own[1, half:], r_a[1, half:], p_down)
+    fl_up = over_z(l_1, 1)
+    fl_down = over_z(l_3, -1)
+    late = after(value_weight[0, early_rows:], b_mine, r_b, fe_up, fe_down, l_1, l_3)
+    late = lax.all_gather(late, "fsdp", axis=0, tiled=True)
+
+    q_early, m_early = early_product(table, xk, xs, cp, gain, early)
+    grad, squares = total(
+        table,
+        [(a_own, 2), (r_a, 2), fe_up, fl_up, fe_down, fl_down, b_mine, r_b],
+        gain,
+        m_early,
     )
-    late = lax.all_gather(late, "fsdp", axis=0, tiled=True)
-
     squares = squares + over_core(squares)
     squares = squares + over_x(squares)
     squares = squares + over_z(squares, 1) + over_z(squares, 2) + over_z(squares, 3)
 
-    first, second, n_0, n_1, n_2, n_3 = adam(columns, squares, grad, adam_first, adam_second, value_weight)
-
-    input_grad, input_end = input_gradient(core[None], xk, xs, cp, inv, gain, q_early, m_early, late)
+    first, second, n_0, n_1, n_2, n_3 = adam(table, squares, grad, adam_first, adam_second, value_weight)
+
+    input_grad, input_end = input_gradient(table, xk, xs, cp, inv, gain, q_early, m_early, late)
 
     m_1 = over_y(n_1, 1)
     m_2 = over_y(n_2, 2)
     m_3 = over_y(n_3, 3)
-    summed = add(n_0, m_1, m_2, m_3)
-    inner_total = summed.astype(F32) + over_x_hi(summed[::-1]).astype(F32)
-    sent = (kept + (1.0 - outer_1) / 8 * inner_total).astype(BF16)
-    outer_grad = anchor - inner_total[0] / 8
-    new_momentum = outer_beta * outer_momentum + outer_grad
-    new_anchor = anchor - outer_rate * (outer_grad + outer_beta * new_momentum)
+    kept = outer_kept * anchor - (outer_rate * outer_beta * outer_beta) * outer_momentum
+    kept = lax.optimization_barrier(kept)
+    kept_theirs = over_x_hi(kept)
+    summed, flipped = sum_over_y([n_0, m_1, m_2, m_3], [kept_theirs])
+    sent, new_momentum, new_anchor = outer_step(
+        summed, over_x_hi(flipped), kept, kept_theirs, anchor, outer_momentum
+    )
     parts = [sent, over_y(sent, 3), over_y(sent, 2), over_y(sent, 1)]
-    synced_weight = place_columns(columns, parts, input_end)
+    synced_weight = place_columns(table, parts, input_end)
     return (input_grad, first, second, synced_weight, new_momentum, new_anchor)
 
 

time: 212 us -> 215 us (1.014)
  waiting for transfers between devices: 80.2 us -> 70.1 us
  Pallas kernels: 59.6 us -> 64.4 us
  local copies, waits for them, and re-layouts: 7.22 us -> 10.9 us
  starting transfers between devices: 40.8 us -> 44.4 us
    ppermute x15, waiting for transfers between devices: 50.7 us -> 23.9 us  [over_z(): lax.ppermute(value, 'fsdp', [(i, (i + 4 * step) % 16) for i in range(16)])]
    ppermute x4, waiting for transfers between devices: 2.15 us -> 12.4 us  [over_x(): return lax.ppermute(value, 'fsdp', [(i, i ^ 2) for i in range(16)])]
    all_gather x1, waiting for transfers between devices: 3.65 us -> 9.65 us  [on_device(): late = lax.all_gather(late, 'fsdp', axis=0, tiled=True)]
    unnamed x34 -> x62, local copies, waits for them, and re-layouts: 1.74 us -> 7.1 us
    pallas_call x1 -> x8, Pallas kernels: 3.7 us -> 8.53 us  [the longest x1 4.09 us: total(): pl.pallas_call(total_kernel, grid_spec=pltpu.PrefetchScalarGridSpec(num_s...]
    convert_element_type x8 -> x7, other arithmetic: 4.26 us -> 8.39 us  [add(): return total_value.astype(BF16)]
    ppermute x4, starting transfers between devices: 2.08 us -> 5.27 us  [over_x(): return lax.ppermute(value, 'fsdp', [(i, i ^ 2) for i in range(16)])]
    pallas_call x1, Pallas kernels: 13.4 us -> 15.6 us  [input_gradient(): pl.pallas_call(input_kernel, grid_spec=pltpu.PrefetchScalarGridSpec(num_s...]
  transfers between devices with their start and end apart: 33 -> 33, of which waited for: 17 -> 19; matrix products, arithmetic and copies ran while one was open for 6% -> 6% of each run, Pallas kernels for 25% -> 29%
where the time goes in v6:
time: 215 us; the launch traced here: 214 us
  waiting for transfers between devices  70.1 us (33%)
  Pallas kernels  64.4 us (30%)
  starting transfers between devices  44.4 us (21%)
  between operations  14.5 us (7%)
  local copies, waits for them, and re-layouts  10.9 us (5%)
  other arithmetic  9.71 us (5%)
    ppermute x15, waiting for transfers between devices, over_z(): lax.ppermute(value, 'fsdp', [(i, (i + 4 * step) % 16) for i in range(16)])  23.9 us
    ppermute x15, starting transfers between devices, over_z(): lax.ppermute(value, 'fsdp', [(i, (i + 4 * step) % 16) for i in range(16)])  16.5 us
    pallas_call x2, Pallas kernels, grad_blocks(): pl.pallas_call(functools.partial(grad_kernel, outputs, len(after)), grid_...  16.5 us
    pallas_call x1, Pallas kernels, input_gradient(): pl.pallas_call(input_kernel, grid_spec=pltpu.PrefetchScalarGridSpec(num_s...  15.6 us
    ppermute x4, waiting for transfers between devices, over_x(): return lax.ppermute(value, 'fsdp', [(i, i ^ 2) for i in range(16)])  12.4 us
    ppermute x2, waiting for transfers between devices, over_x_hi(): return lax.ppermute(value, 'rep', [(i, i ^ 1) for i in range(8)])  11.9 us
    ppermute x6, starting transfers between devices, over_y(): lax.ppermute(value, 'rep', [(i, (i + 2 * step) % 8) for i in range(8)])  11.5 us
    all_gather x1, waiting for transfers between devices, on_device(): late = lax.all_gather(late, 'fsdp', axis=0, tiled=True)  9.65 us
  transfers between devices with their start and end apart: 33, of which 19 were waited for; matrix products, arithmetic and copies ran while one was open for 6% of the time, Pallas kernels for 29%

profile of v6, /device:TPU:1, one launch (start us, length us, event | category | flops | bytes accessed | tf_op | source)
XLA Modules:
  0.0 214.0 jit_solution(8945379386493279015)
XLA Ops:
  7.2 1.7 slice.42
  9.8 8.1 %prep.1 = (bf16[8,320,512]{2,1,0:T(8,128)(2,1)}, bf16[8,320,512]{2,1,0:T(8,128)(2,1)}, bf16[2,320,512]{2,1,0:T(8,128)(2,1)}, bf16[320,1024]{1,0:T(8,128)(2,1)}, f32[320,128]{1,0:T(8,128)}) custom-call(s32[13]{0:T(128)} %stack.55.core_ref.table_ref, s32[1,64]{1,0:T(1,128)} %index_ref.1, bf16[1,256,8192]{2,1,0:T(8,128)(2,1)} %h_ref.1, ...), custom_call_target="tpu_custom_call" | custom-call | flops 2000000000 | bytes 12000000 | tf_op jit(solution)/shard_map/prep/pallas_call | solution.py:111
  17.9 1.5 collective-permute-start
  19.5 1.8 collective-permute-done.refs_1_.xs_ref
  21.4 0.9 collective-permute-done.1.refs_2_.cs_ref
  22.3 0.8 copy-done.16
  23.5 5.4 %grad_a.1 = (bf16[1,576,512]{2,1,0:T(8,128)(2,1)}, bf16[1,576,512]{2,1,0:T(8,128)(2,1)}, bf16[1,448,512]{2,1,0:T(8,128)(2,1)}, bf16[1,448,512]{2,1,0:T(8,128)(2,1)}) custom-call(s32[13]{0:T(128)} %stack.55.core_ref.table_ref, bf16[8,320,512]{2,1,0:T(8,128)(2,1)} %get-tuple-element.42.xk_ref, bf16[2,320,512]{2,1,0:T(8,128)(2,1)} %copy-done.17, ...), custom_call_target="tpu_custom_call" | custom-call | flops 1342177280 | bytes 3400000 | tf_op jit(solution)/shard_map/grad_a/pallas_call | solution.py:199
  28.9 3.9 %collective-permute-start.5 = (bf16[576,512]{1,0:T(8,128)(2,1)}, bf16[576,512]{1,0:T(8,128)(2,1)S(1)}, u32[]{:S(2)}, u32[]{:S(2)}) collective-permute-start(bf16[576,512]{1,0:T(8,128)(2,1)} %bitcast.59), channel_id=1, source_target_pairs={{0,12},{1,13},{2,14},{3,15},{4,0},{5,1},{6,2},{7,3},{8,4},{9,5},{1... | collective-permute-start | bytes 1769480 | tf_op jit(solution)/shard_map/ppermute | solution.py:54
  32.8 1.2 collective-permute-start.10
  34.0 11.1 %grad_b.1 = (bf16[1,576,512]{2,1,0:T(8,128)(2,1)}, bf16[1,576,512]{2,1,0:T(8,128)(2,1)}, bf16[1,576,512]{2,1,0:T(8,128)(2,1)}, bf16[1,576,512]{2,1,0:T(8,128)(2,...) custom-call(s32[13]{0:T(128)} %stack.55.core_ref.table_ref, ...), custom_call_target="tpu_custom_call" | custom-call | flops 4026531840 | bytes 10200000 | tf_op jit(solution)/shard_map/grad_b/pallas_call | solution.py:199
  45.0 8.5 %collective-permute-done.10.refs_1_ = bf16[448,512]{1,0:T(8,128)(2,1)S(1)} collective-permute-done((bf16[448,512]{1,0:T(8,128)(2,1)}, bf16[448,512]{1,0:T(8,128)(2,1)S(1)}, u32[]{:S(2)}, u32[]{:S(2)}) %collective-permute-start.10) | collective-permute-done | bytes 458784 | tf_op jit(solution)/shard_map/ppermute | solution.py:50
  53.6 0.8 copy-done.6
  54.3 2.2 %collective-permute-start.11 = (bf16[3,448,512]{2,1,0:T(8,128)(2,1)}, bf16[3,448,512]{2,1,0:T(8,128)(2,1)S(1)}, u32[]{:S(2)}, u32[]{:S(2)}) collective-permute-start(bf16[3,448,512]{2,1,0:T(8,128)(2,1)} %after.8), channel_id=1, source_target_pairs={{0,2},{1,3},{2,0},{3,1},{4,6},{5,7},{6,4},{7,5},{8,10},{9,11},{10,... | collective-permute-start | bytes 4128776 | tf_op jit(solution)/shard_map/ppermute | solution.py:50
  56.9 2.2 %fusion = bf16[576,512]{1,0:T(8,128)(2,1)} fusion(bf16[576,512]{1,0:T(8,128)(2,1)S(1)} %collective-permute-done.5.refs_1_, bf16[1,576,512]{2,1,0:T(8,128)(2,1)} %get-tuple-element.54), kind=kLoop, calls=%fused_computation.1 | loop fusion | flops 1179648 | bytes 1769472 | tf_op jit(solution)/shard_map/convert_element_type | solution.py:516
  59.1 1.8 collective-permute-start.8
  60.9 2.2 %collective-permute-start.6 = (bf16[576,512]{1,0:T(8,128)(2,1)}, bf16[576,512]{1,0:T(8,128)(2,1)}, u32[]{:S(2)}, u32[]{:S(2)}) collective-permute-start(bf16[576,512]{1,0:T(8,128)(2,1)} %after.6), channel_id=1, source_target_pairs={{0,12},{1,13},{2,14},{3,15},{4,0},{5,1},{6,2},{7,3},{8,4},{9,5},{1... | collective-permute-start | bytes 1769480 | tf_op jit(solution)/shard_map/ppermute | solution.py:54
  63.1 0.8 copy-done.3
  64.0 1.5 fusion.3
  65.6 0.9 slice_bitcast_fusion.refs_0_
  66.7 7.8 %collective-permute-done.8 = bf16[576,512]{1,0:T(8,128)(2,1)} collective-permute-done((bf16[576,512]{1,0:T(8,128)(2,1)}, bf16[576,512]{1,0:T(8,128)(2,1)}, u32[]{:S(2)}, u32[]{:S(2)}) %collective-permute-start.8) | collective-permute-done | bytes 589856 | tf_op jit(solution)/shard_map/ppermute | solution.py:54
  74.4 2.5 %collective-permute-start.15 = (bf16[224,512]{1,0:T(8,128)(2,1)S(1)}, bf16[224,512]{1,0:T(8,128)(2,1)S(1)}, u32[]{:S(2)}, u32[]{:S(2)}) collective-permute-start(bf16[224,512]{1,0:T(8,128)(2,1)S(1)} %get-tuple-element.78), channel_id=1, source_target_pairs={{0,12},{1,13},{2,14},{3,15},{4,0},{5,1},{6,2},{7,3},{8,4},{9,5},{1... | collective-permute-start | bytes 688136 | tf_op jit(solution)/shard_map/ppermute | solution.py:54
  76.9 2.4 %collective-permute-done.7 = bf16[576,512]{1,0:T(8,128)(2,1)S(1)} collective-permute-done((bf16[576,512]{1,0:T(8,128)(2,1)}, bf16[576,512]{1,0:T(8,128)(2,1)S(1)}, u32[]{:S(2)}, u32[]{:S(2)}) %collective-permute-start.7) | collective-permute-done | bytes 589856 | tf_op jit(solution)/shard_map/ppermute | solution.py:54
  79.4 1.3 fusion.2
  80.7 6.4 %collective-permute-done.6 = bf16[576,512]{1,0:T(8,128)(2,1)} collective-permute-done((bf16[576,512]{1,0:T(8,128)(2,1)}, bf16[576,512]{1,0:T(8,128)(2,1)}, u32[]{:S(2)}, u32[]{:S(2)}) %collective-permute-start.6) | collective-permute-done | bytes 589856 | tf_op jit(solution)/shard_map/ppermute | solution.py:54
  87.1 0.8 collective-permute-start.9
  87.9 4.1 %collective-permute-done.4 = bf16[576,512]{1,0:T(8,128)(2,1)S(1)} collective-permute-done((bf16[576,512]{1,0:T(8,128)(2,1)S(1)}, bf16[576,512]{1,0:T(8,128)(2,1)S(1)}, u32[]{:S(2)}, u32[]{:S(2)}) %collective-permute-start.4) | collective-permute-done | bytes 589856 | tf_op jit(solution)/shard_map/ppermute | solution.py:54
  92.0 2.1 %fusion.5.refs_1_.b0 = bf16[576,512]{1,0:T(8,128)(2,1)} fusion(bf16[576,512]{1,0:T(8,128)(2,1)} %collective-permute-done.6, bf16[576,512]{1,0:T(8,128)(2,1)S(1)} %collective-permute-done.4, bf16[1,576,512]{2,1,0:T(8,128)(2,1)S(1)} %copy-done.18), kind=kLoop, calls=%fused_computation.9 | loop fusion | flops 1769472 | bytes 2359296 | tf_op jit(solution)/shard_map/convert_element_type | solution.py:516
  94.4 1.5 collective-permute-start.12
  95.8 1.1 collective-permute-done.14
  96.9 0.9 fusion.8
  97.8 2.0 collective-permute-done.9.refs_2_.b1
  99.8 0.7 collective-permute-done.12.refs_3_.ue
  101.2 0.9 copy-done.13
  102.1 2.1 collective-permute-start.17
  104.2 0.6 broadcast_in_dim.3.gain_ref
  104.9 5.4 %early_product.1 = (bf16[2,8,320,128]{3,2,1,0:T(8,128)(2,1)}, f32[320,128]{1,0:T(8,128)}) custom-call(s32[13]{0:T(128)} %stack.55.core_ref.table_ref, bf16[320,1024]{1,0:T(8,128)(2,1)} %get-tuple-element.40.cp_ref.c_ref, bf16[1,8192]{1,0:T(2,128)(2,1)} %broadcast_in_dim.3.gain_ref, bf16[8,320,512]{2,1,0:T(8,128)(2,1)} %get-tuple-element.42.xk_ref, ...), custom_call_target="tpu_custom_call" | custom-call | flops 1400000000 | bytes 8000000 | tf_op jit(solution)/shard_map/early_product/pallas_call | solution.py:366
  110.4 0.6 copy-done.28
  111.1 4.1 %total.1 = (f32[512,1024]{1,0:T(8,128)}, f32[8,128]{1,0:T(8,128)}) custom-call(s32[13]{0:T(128)} %stack.55.core_ref.table_ref, bf16[3,448,512]{2,1,0:T(8,128)(2,1)} %get-tuple-element.55.a0, bf16[3,448,512]{2,1,0:T(8,128)(2,1)} %copy-done.2, bf16[224,512]{1,0:T(8,128)(2,1)} %copy-done.15, bf16[224,512]{1,0:T(8,128)(2,1)} %copy-done.29, ...), custom_call_target="tpu_custom_call" | custom-call | flops 5000000 | bytes 5000000 | tf_op jit(solution)/shard_map/total/pallas_call | solution.py:251
  115.2 4.3 %collective-permute-start.18 = (f32[8,128]{1,0:T(8,128)}, f32[8,128]{1,0:T(8,128)S(1)}, u32[]{:S(2)}, u32[]{:S(2)}) collective-permute-start(f32[8,128]{1,0:T(8,128)} %get-tuple-element.60), channel_id=1, source_target_pairs={{0,1},{1,0},{2,3},{3,2},{4,5},{5,4},{6,7},{7,6},{8,9},{9,8},{10,11... | collective-permute-start | bytes 12296 | tf_op jit(solution)/shard_map/ppermute | solution.py:46
  119.5 1.0 collective-permute-done.18
  120.6 0.7 add.153
  121.2 1.0 collective-permute-start.19
  122.3 1.9 collective-permute-done.19
  124.2 1.9 collective-permute-start.22
  126.7 2.2 %collective-permute-start.26 = (f32[512,128]{1,0:T(8,128)S(1)}, f32[512,128]{1,0:T(8,128)S(1)}, u32[]{:S(2)}, u32[]{:S(2)}) collective-permute-start(f32[512,128]{1,0:T(8,128)S(1)} %multiply_subtract_fusion.kept_ref), channel_id=1, source_target_pairs={{0,16},{16,0},{32,48},{48,32},{64,80},{80,64},{96,112},{112,96},{1... | collective-permute-start | bytes 786440 | tf_op jit(solution)/shard_map/ppermute | solution.py:58
  128.9 1.1 collective-permute-done.21
  130.7 7.2 %adam.1 = (f32[1,512,1024]{2,1,0:T(8,128)}, f32[1,512,1024]{2,1,0:T(8,128)}, bf16[2,512,128]{2,1,0:T(8,128)(2,1)}, bf16[2,512,128]{2,1,0:T(8,128)(2,1)}, bf16[2,...) custom-call(s32[13]{0:T(128)} %stack.55.core_ref.table_ref, f32[8,128]{1,0:T(8,128)} %add_add_fusion.sq_ref, ...), custom_call_target="tpu_custom_call" | custom-call | flops 20000000 | bytes 12000000 | tf_op jit(solution)/shard_map/adam/pallas_call | solution.py:296
  137.9 1.2 collective-permute-start.23
  139.1 2.5 %collective-permute-start.24 = (bf16[2,512,128]{2,1,0:T(8,128)(2,1)}, bf16[2,512,128]{2,1,0:T(8,128)(2,1)S(1)}, u32[]{:S(2)}, u32[]{:S(2)}) collective-permute-start(bf16[2,512,128]{2,1,0:T(8,128)(2,1)} %get-tuple-element.66), channel_id=1, source_target_pairs={{0,64},{16,80},{32,96},{48,112},{64,0},{80,16},{96,32},{112,48},{1... | collective-permute-start | bytes 786440 | tf_op jit(solution)/shard_map/ppermute | solution.py:62
  141.6 1.1 collective-permute-start.25
  142.7 1.9 collective-permute-done.23.b
  144.6 6.0 %collective-permute-done.24.c = bf16[2,512,128]{2,1,0:T(8,128)(2,1)S(1)} collective-permute-done((bf16[2,512,128]{2,1,0:T(8,128)(2,1)}, bf16[2,512,128]{2,1,0:T(8,128)(2,1)S(1)}, u32[]{:S(2)}, u32[]{:S(2)}) %collective-permute-start.24) | collective-permute-done | bytes 262176 | tf_op jit(solution)/shard_map/ppermute | solution.py:62
  151.8 2.1 sum_over_y.1
  154.0 2.4 %collective-permute-start.27 = (bf16[2,512,128]{2,1,0:T(8,128)(2,1)}, bf16[2,512,128]{2,1,0:T(8,128)(2,1)S(1)}, u32[]{:S(2)}, u32[]{:S(2)}) collective-permute-start(bf16[2,512,128]{2,1,0:T(8,128)(2,1)} %get-tuple-element.69), channel_id=1, source_target_pairs={{0,16},{16,0},{32,48},{48,32},{64,80},{80,64},{96,112},{112,96},{1... | collective-permute-start | bytes 786440 | tf_op jit(solution)/shard_map/ppermute | solution.py:58
  156.3 11.9 %collective-permute-done.27.theirs = bf16[2,512,128]{2,1,0:T(8,128)(2,1)S(1)} collective-permute-done((bf16[2,512,128]{2,1,0:T(8,128)(2,1)}, bf16[2,512,128]{2,1,0:T(8,128)(2,1)S(1)}, u32[]{:S(2)}, u32[]{:S(2)}) %collective-permute-start.27) | collective-permute-done | bytes 262176 | tf_op jit(solution)/shard_map/ppermute | solution.py:58
  168.2 0.7 copy-done.27
  168.9 2.3 %outer_step.1 = (bf16[2,512,128]{2,1,0:T(8,128)(2,1)}, f32[512,128]{1,0:T(8,128)}, f32[512,128]{1,0:T(8,128)}) custom-call(bf16[2,512,128]{2,1,0:T(8,128)(2,1)} %get-tuple-element.68.mine, bf16[2,512,128]{2,1,0:T(8,128)(2,1)} %copy-done.27, f32[512,128]{1,0:T(8,128)} %copy-done.10, f32[512,128]{1,0:T(8,128)} %copy-done.11, f32[512,128]{1,0:T(8,128)} %anchor_ref.1, ...), custom_call_target="tpu_custom_call" | custom-call | flops 1000000 | bytes 3000000 | tf_op jit(solution)/shard_map/outer_step/pallas_call | solution.py:500
  171.2 4.3 %collective-permute-start.30 = (bf16[2,512,128]{2,1,0:T(8,128)(2,1)}, bf16[2,512,128]{2,1,0:T(8,128)(2,1)S(1)}, u32[]{:S(2)}, u32[]{:S(2)}) collective-permute-start(bf16[2,512,128]{2,1,0:T(8,128)(2,1)} %get-tuple-element.70.refs_0_), channel_id=1, source_target_pairs={{0,32},{16,48},{32,64},{48,80},{64,96},{80,112},{96,0},{112,16},{1... | collective-permute-start | bytes 786440 | tf_op jit(solution)/shard_map/ppermute | solution.py:62
  175.6 1.0 collective-permute-start.29
  176.6 1.4 collective-permute-start.28
  178.0 9.6 %all-gather.4.cloned.1.call-done = bf16[6144,1024]{1,0:T(8,128)(2,1)} async-done(((bf16[384,1024]{1,0:T(8,128)(2,1)}), bf16[6144,1024]{1,0:T(8,128)(2,1)}) %all-gather.4.cloned.1.call-update) | async-done | bytes 12582928 | tf_op jit(solution)/shard_map/all_gather | solution.py:579
  187.6 15.6 %input_gradient.1 = (bf16[1,320,8192]{2,1,0:T(8,128)(2,1)}, f32[8,128]{1,0:T(8,128)}) custom-call(s32[13]{0:T(128)} %stack.55.core_ref.table_ref, bf16[320,1024]{1,0:T(8,128)(2,1)} %get-tuple-element.40.cp_ref.c_ref, f32[320,128]{1,0:T(8,128)} %get-tuple-element.41.inv_ref, bf16[1,8192]{1,0:T(2,128)(2,1)} %broadcast_in_dim.3.gain_ref, ...), custom_call_target="tpu_custom_call" | custom-call | flops 5000000000 | bytes 30000000 | tf_op jit(solution)/shard_map/input_gradient/pallas_call | solution.py:435
  203.3 0.7 copy-done.21
  204.2 2.9 %place.1 = bf16[512,1024]{1,0:T(8,128)(2,1)} custom-call(s32[13]{0:T(128)} %stack.55.core_ref.table_ref, bf16[2,512,128]{2,1,0:T(8,128)(2,1)} %get-tuple-element.70.refs_0_, bf16[2,512,128]{2,1,0:T(8,128)(2,1)} %copy-done.23, bf16[2,512,128]{2,1,0:T(8,128)(2,1)} %copy-done.22, bf16[2,512,128]{2,1,0:T(8,128)(2,1)} %copy-done.21, ...), custom_call_target="tpu_custom_call" | custom-call | flops 1000000 | bytes 2000000 | tf_op jit(solution)/shard_map/place/pallas_call | solution.py:320
  (96 shorter events, 5.5 us)
Async XLA Ops:
  7.2 97.7 %all-gather.6.cloned.1.call-start = ((), (), s32[]{:S(2)}) async-start(), calls=%async_computation.1 | async-start | bytes 4456448 | tf_op jit(solution)/shard_map/all_gather | solution.py:540
  8.9 178.7 %all-gather.4.cloned.1.call-start = ((), (), s32[]{:S(2)}) async-start(), calls=%async_computation | async-start | bytes 13369344 | tf_op jit(solution)/shard_map/all_gather | solution.py:579
  17.9 3.5 %collective-permute-start = (bf16[2,320,512]{2,1,0:T(8,128)(2,1)}, bf16[2,320,512]{2,1,0:T(8,128)(2,1)S(1)}, u32[]{:S(2)}, u32[]{:S(2)}) collective-permute-start(bf16[2,320,512]{2,1,0:T(8,128)(2,1)} %get-tuple-element.44), channel_id=1, source_target_pairs={{0,1},{1,0},{2,3},{3,2},{4,5},{5,4},{6,7},{7,6},{8,9},{9,8},{10,11... | collective-permute-start | bytes 1966088 | tf_op jit(solution)/shard_map/ppermute | solution.py:46
  19.4 2.9 %collective-permute-start.1 = (bf16[320,1024]{1,0:T(8,128)(2,1)}, bf16[320,1024]{1,0:T(8,128)(2,1)S(1)}, u32[]{:S(2)}, u32[]{:S(2)}) collective-permute-start(bf16[320,1024]{1,0:T(8,128)(2,1)} %get-tuple-element.40.cp_ref.c_ref), channel_id=1, source_target_pairs={{0,1},{1,0},{2,3},{3,2},{4,5},{5,4},{6,7},{7,6},{8,9},{9,8},{10,11... | collective-permute-start | bytes 1966088 | tf_op jit(solution)/shard_map/ppermute | solution.py:46
  21.4 0.9 copy-start.17
  22.3 0.8 copy-start.16
  23.1 10.8 %collective-permute-start.2 = (bf16[8,320,512]{2,1,0:T(8,128)(2,1)}, bf16[8,320,512]{2,1,0:T(8,128)(2,1)}, u32[]{:S(2)}, u32[]{:S(2)}) collective-permute-start(bf16[8,320,512]{2,1,0:T(8,128)(2,1)} %after.5.xs_ref), channel_id=1, source_target_pairs={{0,1},{1,0},{2,3},{3,2},{4,5},{5,4},{6,7},{7,6},{8,9},{9,8},{10,11... | collective-permute-start | bytes 7864328 | tf_op jit(solution)/shard_map/ppermute | solution.py:46
  28.9 28.0 %collective-permute-start.5 = (bf16[576,512]{1,0:T(8,128)(2,1)}, bf16[576,512]{1,0:T(8,128)(2,1)S(1)}, u32[]{:S(2)}, u32[]{:S(2)}) collective-permute-start(bf16[576,512]{1,0:T(8,128)(2,1)} %bitcast.59), channel_id=1, source_target_pairs={{0,12},{1,13},{2,14},{3,15},{4,0},{5,1},{6,2},{7,3},{8,4},{9,5},{1... | collective-permute-start | bytes 1769480 | tf_op jit(solution)/shard_map/ppermute | solution.py:54
  32.8 20.8 %collective-permute-start.10 = (bf16[448,512]{1,0:T(8,128)(2,1)}, bf16[448,512]{1,0:T(8,128)(2,1)S(1)}, u32[]{:S(2)}, u32[]{:S(2)}) collective-permute-start(bf16[448,512]{1,0:T(8,128)(2,1)} %bitcast.60), channel_id=1, source_target_pairs={{0,2},{1,3},{2,0},{3,1},{4,6},{5,7},{6,4},{7,5},{8,10},{9,11},{10,... | collective-permute-start | bytes 1376264 | tf_op jit(solution)/shard_map/ppermute | solution.py:50
  34.0 29.2 %collective-permute-start.3 = (bf16[576,512]{1,0:T(8,128)(2,1)}, bf16[576,512]{1,0:T(8,128)(2,1)S(1)}, u32[]{:S(2)}, u32[]{:S(2)}) collective-permute-start(bf16[576,512]{1,0:T(8,128)(2,1)} %bitcast.58), channel_id=1, source_target_pairs={{0,4},{1,5},{2,6},{3,7},{4,8},{5,9},{6,10},{7,11},{8,12},{9,13},{1... | collective-permute-start | bytes 1769480 | tf_op jit(solution)/shard_map/ppermute | solution.py:54
  53.6 0.8 copy-start.6
  54.3 39.8 %collective-permute-start.11 = (bf16[3,448,512]{2,1,0:T(8,128)(2,1)}, bf16[3,448,512]{2,1,0:T(8,128)(2,1)S(1)}, u32[]{:S(2)}, u32[]{:S(2)}) collective-permute-start(bf16[3,448,512]{2,1,0:T(8,128)(2,1)} %after.8), channel_id=1, source_target_pairs={{0,2},{1,3},{2,0},{3,1},{4,6},{5,7},{6,4},{7,5},{8,10},{9,11},{10,... | collective-permute-start | bytes 4128776 | tf_op jit(solution)/shard_map/ppermute | solution.py:50
  56.9 4.0 %copy-start.4 = (bf16[576,512]{1,0:T(8,128)(2,1)}, bf16[576,512]{1,0:T(8,128)(2,1)S(1)}, u32[]{:S(2)}) copy-start(bf16[576,512]{1,0:T(8,128)(2,1)S(1)} %collective-permute-done.5.refs_1_) | copy-start | bytes 1769476
  59.1 15.3 %collective-permute-start.8 = (bf16[576,512]{1,0:T(8,128)(2,1)}, bf16[576,512]{1,0:T(8,128)(2,1)}, u32[]{:S(2)}, u32[]{:S(2)}) collective-permute-start(bf16[576,512]{1,0:T(8,128)(2,1)} %fusion), channel_id=1, source_target_pairs={{0,12},{1,13},{2,14},{3,15},{4,0},{5,1},{6,2},{7,3},{8,4},{9,5},{1... | collective-permute-start | bytes 1769480 | tf_op jit(solution)/shard_map/ppermute | solution.py:54
  60.9 26.1 %collective-permute-start.6 = (bf16[576,512]{1,0:T(8,128)(2,1)}, bf16[576,512]{1,0:T(8,128)(2,1)}, u32[]{:S(2)}, u32[]{:S(2)}) collective-permute-start(bf16[576,512]{1,0:T(8,128)(2,1)} %after.6), channel_id=1, source_target_pairs={{0,12},{1,13},{2,14},{3,15},{4,0},{5,1},{6,2},{7,3},{8,4},{9,5},{1... | collective-permute-start | bytes 1769480 | tf_op jit(solution)/shard_map/ppermute | solution.py:54
  63.1 0.8 copy-start.3
  63.9 1.7 copy-start
  63.9 15.4 %collective-permute-start.7 = (bf16[576,512]{1,0:T(8,128)(2,1)}, bf16[576,512]{1,0:T(8,128)(2,1)S(1)}, u32[]{:S(2)}, u32[]{:S(2)}) collective-permute-start(bf16[576,512]{1,0:T(8,128)(2,1)} %after.7), channel_id=1, source_target_pairs={{0,4},{1,5},{2,6},{3,7},{4,8},{5,9},{6,10},{7,11},{8,12},{9,13},{1... | collective-permute-start | bytes 1769480 | tf_op jit(solution)/shard_map/ppermute | solution.py:54
  63.9 2.6 %copy-start.7 = (bf16[448,512]{1,0:T(8,128)(2,1)S(1)}, bf16[448,512]{1,0:T(8,128)(2,1)}, u32[]{:S(2)}) copy-start(bf16[448,512]{1,0:T(8,128)(2,1)} %copy-done.6) | copy-start | bytes 1376260
  63.9 2.6 %copy-start.20 = (bf16[1,448,512]{2,1,0:T(8,128)(2,1)S(1)}, bf16[1,448,512]{2,1,0:T(8,128)(2,1)}, u32[]{:S(2)}) copy-start(bf16[1,448,512]{2,1,0:T(8,128)(2,1)} %get-tuple-element.58) | copy-start | bytes 1376260
  65.5 13.9 %copy-start.19 = (bf16[1,576,512]{2,1,0:T(8,128)(2,1)S(1)}, bf16[1,576,512]{2,1,0:T(8,128)(2,1)}, u32[]{:S(2)}) copy-start(bf16[1,576,512]{2,1,0:T(8,128)(2,1)} %get-tuple-element.52) | copy-start | bytes 1769476
  65.5 26.5 %collective-permute-start.4 = (bf16[576,512]{1,0:T(8,128)(2,1)S(1)}, bf16[576,512]{1,0:T(8,128)(2,1)S(1)}, u32[]{:S(2)}, u32[]{:S(2)}) collective-permute-start(bf16[576,512]{1,0:T(8,128)(2,1)S(1)} %fusion.3), channel_id=1, source_target_pairs={{0,4},{1,5},{2,6},{3,7},{4,8},{5,9},{6,10},{7,11},{8,12},{9,13},{1... | collective-permute-start | bytes 1769480 | tf_op jit(solution)/shard_map/ppermute | solution.py:54
  66.7 25.3 %copy-start.18 = (bf16[1,576,512]{2,1,0:T(8,128)(2,1)S(1)}, bf16[1,576,512]{2,1,0:T(8,128)(2,1)}, u32[]{:S(2)}) copy-start(bf16[1,576,512]{2,1,0:T(8,128)(2,1)} %get-tuple-element.48) | copy-start | bytes 1769476
  74.4 21.4 %collective-permute-start.15 = (bf16[224,512]{1,0:T(8,128)(2,1)S(1)}, bf16[224,512]{1,0:T(8,128)(2,1)S(1)}, u32[]{:S(2)}, u32[]{:S(2)}) collective-permute-start(bf16[224,512]{1,0:T(8,128)(2,1)S(1)} %get-tuple-element.78), channel_id=1, source_target_pairs={{0,12},{1,13},{2,14},{3,15},{4,0},{5,1},{6,2},{7,3},{8,4},{9,5},{1... | collective-permute-start | bytes 688136 | tf_op jit(solution)/shard_map/ppermute | solution.py:54
  79.3 17.6 %collective-permute-start.14 = (bf16[224,512]{1,0:T(8,128)(2,1)S(1)}, bf16[224,512]{1,0:T(8,128)(2,1)S(1)}, u32[]{:S(2)}, u32[]{:S(2)}) collective-permute-start(bf16[224,512]{1,0:T(8,128)(2,1)S(1)} %get-tuple-element.79), channel_id=1, source_target_pairs={{0,4},{1,5},{2,6},{3,7},{4,8},{5,9},{6,10},{7,11},{8,12},{9,13},{1... | collective-permute-start | bytes 688136 | tf_op jit(solution)/shard_map/ppermute | solution.py:54
  80.6 13.5 %copy-start.1 = (bf16[3,448,512]{2,1,0:T(8,128)(2,1)S(1)}, bf16[3,448,512]{2,1,0:T(8,128)(2,1)}, u32[]{:S(2)}) copy-start(bf16[3,448,512]{2,1,0:T(8,128)(2,1)} %get-tuple-element.55.a0) | copy-start | bytes 4128772
  87.1 12.7 %collective-permute-start.9 = (bf16[576,512]{1,0:T(8,128)(2,1)S(1)}, bf16[576,512]{1,0:T(8,128)(2,1)S(1)}, u32[]{:S(2)}, u32[]{:S(2)}) collective-permute-start(bf16[576,512]{1,0:T(8,128)(2,1)S(1)} %fusion.2), channel_id=1, source_target_pairs={{0,2},{1,3},{2,0},{3,1},{4,6},{5,7},{6,4},{7,5},{8,10},{9,11},{10,... | collective-permute-start | bytes 1769480 | tf_op jit(solution)/shard_map/ppermute | solution.py:50
  94.1 3.7 %copy-start.2 = (bf16[3,448,512]{2,1,0:T(8,128)(2,1)}, bf16[3,448,512]{2,1,0:T(8,128)(2,1)S(1)}, u32[]{:S(2)}) copy-start(bf16[3,448,512]{2,1,0:T(8,128)(2,1)S(1)} %collective-permute-done.11.a1) | copy-start | bytes 4128772
  94.3 5.5 %collective-permute-start.13 = (bf16[224,512]{1,0:T(8,128)(2,1)S(1)}, bf16[224,512]{1,0:T(8,128)(2,1)S(1)}, u32[]{:S(2)}, u32[]{:S(2)}) collective-permute-start(bf16[224,512]{1,0:T(8,128)(2,1)S(1)} %get-tuple-element.76), channel_id=1, source_target_pairs={{0,12},{1,13},{2,14},{3,15},{4,0},{5,1},{6,2},{7,3},{8,4},{9,5},{1... | collective-permute-start | bytes 688136 | tf_op jit(solution)/shard_map/ppermute | solution.py:54
  94.4 6.2 %collective-permute-start.12 = (bf16[224,512]{1,0:T(8,128)(2,1)S(1)}, bf16[224,512]{1,0:T(8,128)(2,1)S(1)}, u32[]{:S(2)}, u32[]{:S(2)}) collective-permute-start(bf16[224,512]{1,0:T(8,128)(2,1)S(1)} %get-tuple-element.77), channel_id=1, source_target_pairs={{0,4},{1,5},{2,6},{3,7},{4,8},{5,9},{6,10},{7,11},{8,12},{9,13},{1... | collective-permute-start | bytes 688136 | tf_op jit(solution)/shard_map/ppermute | solution.py:54
  99.8 0.8 copy-start.5
  99.8 0.9 copy-start.14
  100.5 0.7 copy-start.15
  101.2 0.9 copy-start.13
  101.2 3.0 %copy-start.12 = (bf16[224,512]{1,0:T(8,128)(2,1)S(1)}, bf16[224,512]{1,0:T(8,128)(2,1)}, u32[]{:S(2)}) copy-start(bf16[224,512]{1,0:T(8,128)(2,1)} %get-tuple-element.75.refs_5_) | copy-start | bytes 688132
  101.2 3.0 %copy-start.30 = (bf16[8192]{0:T(1024)(128)(2,1)S(1)}, bf16[8192]{0:T(1024)(128)(2,1)}, u32[]{:S(2)}) copy-start(bf16[8192]{0:T(1024)(128)(2,1)} %param.14) | copy-start | bytes 49156
  102.1 8.2 %collective-permute-start.17 = (bf16[224,512]{1,0:T(8,128)(2,1)S(1)}, bf16[224,512]{1,0:T(8,128)(2,1)S(1)}, u32[]{:S(2)}, u32[]{:S(2)}) collective-permute-start(bf16[224,512]{1,0:T(8,128)(2,1)S(1)} %copy-done.13), channel_id=1, source_target_pairs={{0,12},{1,13},{2,14},{3,15},{4,0},{5,1},{6,2},{7,3},{8,4},{9,5},{1... | collective-permute-start | bytes 688136 | tf_op jit(solution)/shard_map/ppermute | solution.py:54
  104.2 6.1 %collective-permute-start.16 = (bf16[224,512]{1,0:T(8,128)(2,1)S(1)}, bf16[224,512]{1,0:T(8,128)(2,1)S(1)}, u32[]{:S(2)}, u32[]{:S(2)}) collective-permute-start(bf16[224,512]{1,0:T(8,128)(2,1)S(1)} %copy-done.12), channel_id=1, source_target_pairs={{0,4},{1,5},{2,6},{3,7},{4,8},{5,9},{6,10},{7,11},{8,12},{9,13},{1... | collective-permute-start | bytes 688136 | tf_op jit(solution)/shard_map/ppermute | solution.py:54
  110.3 0.7 copy-start.28
  110.3 0.7 copy-start.29
  111.1 15.5 %copy-start.8 = (f32[512,128]{1,0:T(8,128)S(1)}, f32[512,128]{1,0:T(8,128)}, u32[]{:S(2)}) copy-start(f32[512,128]{1,0:T(8,128)} %momentum_ref.1) | copy-start | bytes 786436
  111.1 15.5 %copy-start.9 = (f32[512,128]{1,0:T(8,128)S(1)}, f32[512,128]{1,0:T(8,128)}, u32[]{:S(2)}) copy-start(f32[512,128]{1,0:T(8,128)} %anchor_ref.1) | copy-start | bytes 786436
  115.2 5.4 %collective-permute-start.18 = (f32[8,128]{1,0:T(8,128)}, f32[8,128]{1,0:T(8,128)S(1)}, u32[]{:S(2)}, u32[]{:S(2)}) collective-permute-start(f32[8,128]{1,0:T(8,128)} %get-tuple-element.60), channel_id=1, source_target_pairs={{0,1},{1,0},{2,3},{3,2},{4,5},{5,4},{6,7},{7,6},{8,9},{9,8},{10,11... | collective-permute-start | bytes 12296 | tf_op jit(solution)/shard_map/ppermute | solution.py:46
  121.2 2.9 %collective-permute-start.19 = (f32[8,128]{1,0:T(8,128)S(1)}, f32[8,128]{1,0:T(8,128)S(1)}, u32[]{:S(2)}, u32[]{:S(2)}) collective-permute-start(f32[8,128]{1,0:T(8,128)S(1)} %add.153), channel_id=1, source_target_pairs={{0,2},{1,3},{2,0},{3,1},{4,6},{5,7},{6,4},{7,5},{8,10},{9,11},{10,... | collective-permute-start | bytes 12296 | tf_op jit(solution)/shard_map/ppermute | solution.py:50
  124.2 4.8 %collective-permute-start.22 = (f32[8,128]{1,0:T(8,128)S(1)}, f32[8,128]{1,0:T(8,128)S(1)}, u32[]{:S(2)}, u32[]{:S(2)}) collective-permute-start(f32[8,128]{1,0:T(8,128)S(1)} %add.154), channel_id=1, source_target_pairs={{0,12},{1,13},{2,14},{3,15},{4,0},{5,1},{6,2},{7,3},{8,4},{9,5},{1... | collective-permute-start | bytes 12296 | tf_op jit(solution)/shard_map/ppermute | solution.py:54
  126.1 4.0 %collective-permute-start.21 = (f32[8,128]{1,0:T(8,128)S(1)}, f32[8,128]{1,0:T(8,128)S(1)}, u32[]{:S(2)}, u32[]{:S(2)}) collective-permute-start(f32[8,128]{1,0:T(8,128)S(1)} %add.154), channel_id=1, source_target_pairs={{0,8},{1,9},{2,10},{3,11},{4,12},{5,13},{6,14},{7,15},{8,0},{9,1},... | collective-permute-start | bytes 12296 | tf_op jit(solution)/shard_map/ppermute | solution.py:54
  126.2 3.9 %collective-permute-start.20 = (f32[8,128]{1,0:T(8,128)S(1)}, f32[8,128]{1,0:T(8,128)S(1)}, u32[]{:S(2)}, u32[]{:S(2)}) collective-permute-start(f32[8,128]{1,0:T(8,128)S(1)} %add.154), channel_id=1, source_target_pairs={{0,4},{1,5},{2,6},{3,7},{4,8},{5,9},{6,10},{7,11},{8,12},{9,13},{1... | collective-permute-start | bytes 12296 | tf_op jit(solution)/shard_map/ppermute | solution.py:54
  126.7 11.2 %copy-start.10 = (f32[512,128]{1,0:T(8,128)}, f32[512,128]{1,0:T(8,128)S(1)}, u32[]{:S(2)}) copy-start(f32[512,128]{1,0:T(8,128)S(1)} %multiply_subtract_fusion.kept_ref) | copy-start | bytes 786436
  126.7 16.0 %collective-permute-start.26 = (f32[512,128]{1,0:T(8,128)S(1)}, f32[512,128]{1,0:T(8,128)S(1)}, u32[]{:S(2)}, u32[]{:S(2)}) collective-permute-start(f32[512,128]{1,0:T(8,128)S(1)} %multiply_subtract_fusion.kept_ref), channel_id=1, source_target_pairs={{0,16},{16,0},{32,48},{48,32},{64,80},{80,64},{96,112},{112,96},{1... | collective-permute-start | bytes 786440 | tf_op jit(solution)/shard_map/ppermute | solution.py:58
  137.9 6.7 %collective-permute-start.23 = (bf16[2,512,128]{2,1,0:T(8,128)(2,1)}, bf16[2,512,128]{2,1,0:T(8,128)(2,1)S(1)}, u32[]{:S(2)}, u32[]{:S(2)}) collective-permute-start(bf16[2,512,128]{2,1,0:T(8,128)(2,1)} %get-tuple-element.65), channel_id=1, source_target_pairs={{0,32},{16,48},{32,64},{48,80},{64,96},{80,112},{96,0},{112,16},{1... | collective-permute-start | bytes 786440 | tf_op jit(solution)/shard_map/ppermute | solution.py:62
  139.1 11.5 %collective-permute-start.24 = (bf16[2,512,128]{2,1,0:T(8,128)(2,1)}, bf16[2,512,128]{2,1,0:T(8,128)(2,1)S(1)}, u32[]{:S(2)}, u32[]{:S(2)}) collective-permute-start(bf16[2,512,128]{2,1,0:T(8,128)(2,1)} %get-tuple-element.66), channel_id=1, source_target_pairs={{0,64},{16,80},{32,96},{48,112},{64,0},{80,16},{96,32},{112,48},{1... | collective-permute-start | bytes 786440 | tf_op jit(solution)/shard_map/ppermute | solution.py:62
  141.6 9.6 %collective-permute-start.25 = (bf16[2,512,128]{2,1,0:T(8,128)(2,1)}, bf16[2,512,128]{2,1,0:T(8,128)(2,1)S(1)}, u32[]{:S(2)}, u32[]{:S(2)}) collective-permute-start(bf16[2,512,128]{2,1,0:T(8,128)(2,1)} %get-tuple-element.67), channel_id=1, source_target_pairs={{0,96},{16,112},{32,0},{48,16},{64,32},{80,48},{96,64},{112,80},{1... | collective-permute-start | bytes 786440 | tf_op jit(solution)/shard_map/ppermute | solution.py:62
  142.7 8.4 %copy-start.11 = (f32[512,128]{1,0:T(8,128)}, f32[512,128]{1,0:T(8,128)S(1)}, u32[]{:S(2)}) copy-start(f32[512,128]{1,0:T(8,128)S(1)} %collective-permute-done.26.rest_0_.kept_theirs_ref) | copy-start | bytes 786436
  144.6 6.5 %copy-start.24 = (bf16[2,512,128]{2,1,0:T(8,128)(2,1)}, bf16[2,512,128]{2,1,0:T(8,128)(2,1)S(1)}, u32[]{:S(2)}) copy-start(bf16[2,512,128]{2,1,0:T(8,128)(2,1)S(1)} %collective-permute-done.23.b) | copy-start | bytes 786436
  150.6 0.7 copy-start.25
  151.1 0.7 copy-start.26
  154.0 14.3 %collective-permute-start.27 = (bf16[2,512,128]{2,1,0:T(8,128)(2,1)}, bf16[2,512,128]{2,1,0:T(8,128)(2,1)S(1)}, u32[]{:S(2)}, u32[]{:S(2)}) collective-permute-start(bf16[2,512,128]{2,1,0:T(8,128)(2,1)} %get-tuple-element.69), channel_id=1, source_target_pairs={{0,16},{16,0},{32,48},{48,32},{64,80},{80,64},{96,112},{112,96},{1... | collective-permute-start | bytes 786440 | tf_op jit(solution)/shard_map/ppermute | solution.py:58
  168.2 0.7 copy-start.27
  171.2 32.0 %collective-permute-start.30 = (bf16[2,512,128]{2,1,0:T(8,128)(2,1)}, bf16[2,512,128]{2,1,0:T(8,128)(2,1)S(1)}, u32[]{:S(2)}, u32[]{:S(2)}) collective-permute-start(bf16[2,512,128]{2,1,0:T(8,128)(2,1)} %get-tuple-element.70.refs_0_), channel_id=1, source_target_pairs={{0,32},{16,48},{32,64},{48,80},{64,96},{80,112},{96,0},{112,16},{1... | collective-permute-start | bytes 786440 | tf_op jit(solution)/shard_map/ppermute | solution.py:62
  175.6 27.7 %collective-permute-start.29 = (bf16[2,512,128]{2,1,0:T(8,128)(2,1)}, bf16[2,512,128]{2,1,0:T(8,128)(2,1)S(1)}, u32[]{:S(2)}, u32[]{:S(2)}) collective-permute-start(bf16[2,512,128]{2,1,0:T(8,128)(2,1)} %get-tuple-element.70.refs_0_), channel_id=1, source_target_pairs={{0,64},{16,80},{32,96},{48,112},{64,0},{80,16},{96,32},{112,48},{1... | collective-permute-start | bytes 786440 | tf_op jit(solution)/shard_map/ppermute | solution.py:62
  176.6 26.7 %collective-permute-start.28 = (bf16[2,512,128]{2,1,0:T(8,128)(2,1)}, bf16[2,512,128]{2,1,0:T(8,128)(2,1)S(1)}, u32[]{:S(2)}, u32[]{:S(2)}) collective-permute-start(bf16[2,512,128]{2,1,0:T(8,128)(2,1)} %get-tuple-element.70.refs_0_), channel_id=1, source_target_pairs={{0,96},{16,112},{32,0},{48,16},{64,32},{80,48},{96,64},{112,80},{1... | collective-permute-start | bytes 786440 | tf_op jit(solution)/shard_map/ppermute | solution.py:62
  203.2 0.7 copy-start.21
  203.3 0.8 copy-start.22
  203.3 0.9 copy-start.23
Sparse Core Ops, SparseCore 0:
  10.3 50.2 all-gather.5
  101.3 86.2 all-gather.3

commit v7 on v6

--- a/solution.py
+++ b/solution.py
@@ -217,11 +217,12 @@
     )(table, xk, xs, c, cs, *after)
 
 
-early_rows = 128
-
-
-def total_kernel(table_ref, a0, a1, ue, ul, de, dl, b0, b1, gain_ref, after_ref, grad_ref, sq_ref):
+early_rows = 256
+
+
+def total_kernel(table_ref, a0, a1, ue, ul, de, dl, b0, b1, gain_ref, w_ref, after_ref, grad_ref, sq_ref, late_ref):
     step = pl.program_id(0)
+    late_ref[...] = w_ref[early_rows:512, :]
     up = jnp.concatenate([ul[...], ue[...]], axis=0).astype(F32)
     down = jnp.concatenate([de[...], dl[...]], axis=0).astype(F32)
     top = (a0[...].astype(F32) + a1[...].astype(F32)) + (up + down)
@@ -239,7 +240,7 @@
         sq_ref[...] += square
 
 
-def total(table, parts, gain, after):
+def total(table, parts, gain, weight, after):
     specs, arrays = [], []
     for part in parts:
         if isinstance(part, tuple):
@@ -256,18 +257,20 @@
             in_specs=specs
             + [
                 pl.BlockSpec((1, 256), lambda t, tab: (0, 2 * tab[12] + t)),
+                pl.BlockSpec((None, 512, 512), lambda t, tab: (0, 0, t)),
                 pl.BlockSpec(memory_space=pl.ANY),
             ],
             out_specs=[
                 pl.BlockSpec((256, 1024), lambda t, tab: (t, 0)),
                 pl.BlockSpec((8, 128), lambda t, tab: (0, 0)),
-            ],
-        ),
-        out_shape=[sds((512, 1024), F32), sds((8, 128), F32)],
+                pl.BlockSpec((512 - early_rows, 512), lambda t, tab: (0, t)),
+            ],
+        ),
+        out_shape=[sds((512, 1024), F32), sds((8, 128), F32), sds((512 - early_rows, 1024), BF16)],
         compiler_params=params(60),
         cost_estimate=cost(5e6, 5e6),
         name="total",
-    )(table, *arrays, gain, after)
+    )(table, *arrays, gain, weight, after)
 
 
 def adam_kernel(table_ref, sq_ref, grad_ref, m_ref, v_ref, w_ref, first_ref, second_ref, *rest):
@@ -459,54 +462,6 @@
         cost_estimate=cost(5e9, 3e7),
         name="input_gradient",
     )(core, cp, inv, gain, xk, xs, q_early, m_early, late, late)
-
-
-def sum_kernel(a, b, c, d, *rest):
-    total_value = (a[...].astype(F32) + b[...].astype(F32)) + (c[...].astype(F32) + d[...].astype(F32))
-    total_value = total_value.astype(BF16)
-    sum_ref, flip_ref = rest[-2:]
-    sum_ref[...] = total_value
-    flip_ref[0] = total_value[1]
-    flip_ref[1] = total_value[0]
-
-
-def sum_over_y(parts, after):
-    block = pl.BlockSpec((2, 512, 128), lambda t: (0, 0, 0))
-    return pl.pallas_call(
-        sum_kernel,
-        grid=(1,),
-        in_specs=[block] * 4 + [anywhere] * len(after),
-        out_specs=[block] * 2,
-        out_shape=[sds((2, 512, 128), BF16)] * 2,
-        compiler_params=params(60),
-        cost_estimate=cost(1e6, 2e6),
-        name="sum_over_y",
-    )(*parts, *after)
-
-
-def outer_kernel(mine, theirs, kept_ref, kept_theirs_ref, anchor_ref, momentum_ref, sent_ref, new_momentum_ref, new_anchor_ref):
-    inner_total = mine[...].astype(F32) + theirs[...].astype(F32)
-    sent_ref[0] = (kept_ref[...] + (1.0 - outer_kept) / 8 * inner_total[0]).astype(BF16)
-    sent_ref[1] = (kept_theirs_ref[...] + (1.0 - outer_kept) / 8 * inner_total[1]).astype(BF16)
-    outer_grad = anchor_ref[...] - inner_total[0] / 8
-    new_momentum = outer_beta * momentum_ref[...] + outer_grad
-    new_momentum_ref[...] = new_momentum
-    new_anchor_ref[...] = anchor_ref[...] - outer_rate * (outer_grad + outer_beta * new_momentum)
-
-
-def outer_step(mine, theirs, kept, kept_theirs, anchor, momentum):
-    pair = pl.BlockSpec((2, 512, 128), lambda t: (0, 0, 0))
-    one = pl.BlockSpec((512, 128), lambda t: (0, 0))
-    return pl.pallas_call(
-        outer_kernel,
-        grid=(1,),
-        in_specs=[pair, pair, one, one, one, one],
-        out_specs=[pair, one, one],
-        out_shape=[sds((2, 512, 128), BF16), sds((512, 128), F32), sds((512, 128), F32)],
-        compiler_params=params(60),
-        cost_estimate=cost(1e6, 3e6),
-        name="outer_step",
-    )(mine, theirs, kept, kept_theirs, anchor, momentum)
 
 
 def add(*values):
@@ -571,20 +526,19 @@
     b_mine = add(b_00[0], l_up, e_down)
     b_theirs = add(b_01[0], e_up, l_down)
     r_b = over_x(b_theirs)
-    l_1 = add(a_own[0, :half], r_a[0, :half], p_up)
-    l_3 = add(a_own[1, half:], r_a[1, half:], p_down)
-    fl_up = over_z(l_1, 1)
-    fl_down = over_z(l_3, -1)
-    late = after(value_weight[0, early_rows:], b_mine, r_b, fe_up, fe_down, l_1, l_3)
-    late = lax.all_gather(late, "fsdp", axis=0, tiled=True)
+    fl_up = over_z(add(a_own[0, :half], r_a[0, :half], p_up), 1)
+    fl_down = over_z(add(a_own[1, half:], r_a[1, half:], p_down), -1)
 
     q_early, m_early = early_product(table, xk, xs, cp, gain, early)
-    grad, squares = total(
+    grad, squares, late = total(
         table,
         [(a_own, 2), (r_a, 2), fe_up, fl_up, fe_down, fl_down, b_mine, r_b],
         gain,
+        value_weight,
         m_early,
     )
+    late = lax.all_gather(late, "fsdp", axis=0, tiled=True)
+
     squares = squares + over_core(squares)
     squares = squares + over_x(squares)
     squares = squares + over_z(squares, 1) + over_z(squares, 2) + over_z(squares, 3)
@@ -599,10 +553,13 @@
     kept = outer_kept * anchor - (outer_rate * outer_beta * outer_beta) * outer_momentum
     kept = lax.optimization_barrier(kept)
     kept_theirs = over_x_hi(kept)
-    summed, flipped = sum_over_y([n_0, m_1, m_2, m_3], [kept_theirs])
-    sent, new_momentum, new_anchor = outer_step(
-        summed, over_x_hi(flipped), kept, kept_theirs, anchor, outer_momentum
-    )
+    kept = jnp.stack([kept, kept_theirs])
+    summed = add(after(n_0, kept_theirs), m_1, m_2, m_3)
+    inner_total = summed.astype(F32) + over_x_hi(summed[::-1]).astype(F32)
+    sent = (kept + (1.0 - outer_kept) / 8 * inner_total).astype(BF16)
+    outer_grad = anchor - inner_total[0] / 8
+    new_momentum = outer_beta * outer_momentum + outer_grad
+    new_anchor = anchor - outer_rate * (outer_grad + outer_beta * new_momentum)
     parts = [sent, over_y(sent, 3), over_y(sent, 2), over_y(sent, 1)]
     synced_weight = place_columns(table, parts, input_end)
     return (input_grad, first, second, synced_weight, new_momentum, new_anchor)

time: 215 us -> 214 us (level)
  waiting for transfers between devices: 70.1 us -> 82.2 us
  starting transfers between devices: 44.4 us -> 35.9 us
  Pallas kernels: 64.4 us -> 61.5 us
  local copies, waits for them, and re-layouts: 10.9 us -> 8.28 us
    ppermute x6, starting transfers between devices: 11.5 us -> 5.18 us  [over_y(): lax.ppermute(value, 'rep', [(i, (i + 2 * step) % 8) for i in range(8)])]
    ppermute x4, waiting for transfers between devices: 12.4 us -> 17.3 us  [over_x(): return lax.ppermute(value, 'fsdp', [(i, i ^ 2) for i in range(16)])]
    pallas_call x2 -> x0, Pallas kernels: 4.44 us -> none  [the longest x1 2.3 us: outer_step(): pl.pallas_call(outer_kernel, grid=(1,), in_specs=[pair, pair, one, one, o...]
    ppermute x6, waiting for transfers between devices: 8.43 us -> 12.3 us  [over_y(): lax.ppermute(value, 'rep', [(i, (i + 2 * step) % 8) for i in range(8)])]
    ppermute x15, waiting for transfers between devices: 23.9 us -> 27.3 us  [over_z(): lax.ppermute(value, 'fsdp', [(i, (i + 4 * step) % 16) for i in range(16)])]
    pallas_call x1, Pallas kernels: 5.45 us -> 7.96 us  [early_product(): pl.pallas_call(early_kernel, grid_spec=pltpu.PrefetchScalarGridSpec(num_s...]
    ppermute x4, starting transfers between devices: 6.33 us -> 4.01 us  [over_core(): return lax.ppermute(value, 'fsdp', [(i, i ^ 1) for i in range(16)])]
    unnamed x62 -> x54, local copies, waits for them, and re-layouts: 7.1 us -> 5.05 us
  transfers between devices with their start and end apart: 33 -> 33, of which waited for: 19 -> 15; matrix products, arithmetic and copies ran while one was open for 6% -> 6% of each run, Pallas kernels for 29% -> 25%
where the time goes in v7:
time: 214 us
  waiting for transfers between devices  82.2 us (38%)
  Pallas kernels  61.5 us (29%)
  starting transfers between devices  35.9 us (17%)
  between operations  14.5 us (7%)
  other arithmetic  11.3 us (5%)
  local copies, waits for them, and re-layouts  8.28 us (4%)
    ppermute x15, waiting for transfers between devices, over_z(): lax.ppermute(value, 'fsdp', [(i, (i + 4 * step) % 16) for i in range(16)])  27.3 us
    ppermute x4, waiting for transfers between devices, over_x(): return lax.ppermute(value, 'fsdp', [(i, i ^ 2) for i in range(16)])  17.3 us
    ppermute x15, starting transfers between devices, over_z(): lax.ppermute(value, 'fsdp', [(i, (i + 4 * step) % 16) for i in range(16)])  17.1 us
    pallas_call x2, Pallas kernels, grad_blocks(): pl.pallas_call(functools.partial(grad_kernel, outputs, len(after)), grid_...  16.5 us
    pallas_call x1, Pallas kernels, input_gradient(): pl.pallas_call(input_kernel, grid_spec=pltpu.PrefetchScalarGridSpec(num_s...  14.1 us
    ppermute x6, waiting for transfers between devices, over_y(): lax.ppermute(value, 'rep', [(i, (i + 2 * step) % 8) for i in range(8)])  12.3 us
    ppermute x2, waiting for transfers between devices, over_x_hi(): return lax.ppermute(value, 'rep', [(i, i ^ 1) for i in range(8)])  12 us
    all_gather x1, waiting for transfers between devices, on_device(): late = lax.all_gather(late, 'fsdp', axis=0, tiled=True)  9.41 us
  transfers between devices with their start and end apart: 33, of which 15 were waited for; matrix products, arithmetic and copies ran while one was open for 6% of the time, Pallas kernels for 25%

profile of v7, /device:TPU:1, one launch (start us, length us, event | category | flops | bytes accessed | tf_op | source)
XLA Modules:
  0.0 213.6 jit_solution(14784393873506679305)
XLA Ops:
  7.2 1.9 slice.42
  9.4 0.7 stack.64.core_ref.table_ref
  10.1 8.1 %prep.1 = (bf16[8,320,512]{2,1,0:T(8,128)(2,1)}, bf16[8,320,512]{2,1,0:T(8,128)(2,1)}, bf16[2,320,512]{2,1,0:T(8,128)(2,1)}, bf16[320,1024]{1,0:T(8,128)(2,1)}, f32[320,128]{1,0:T(8,128)}) custom-call(s32[13]{0:T(128)} %stack.64.core_ref.table_ref, s32[1,64]{1,0:T(1,128)} %index_ref.1, bf16[1,256,8192]{2,1,0:T(8,128)(2,1)} %h_ref.1, ...), custom_call_target="tpu_custom_call" | custom-call | flops 2000000000 | bytes 12000000 | tf_op jit(solution)/shard_map/prep/pallas_call | solution.py:111
  18.2 1.5 collective-permute-start
  19.8 1.8 collective-permute-done.refs_1_.xs_ref
  21.7 0.9 collective-permute-done.1.refs_2_.cs_ref
  22.6 0.8 copy-done.12
  23.5 0.4 collective-permute-start.2
  23.8 5.4 %grad_a.1 = (bf16[1,576,512]{2,1,0:T(8,128)(2,1)}, bf16[1,576,512]{2,1,0:T(8,128)(2,1)}, bf16[1,448,512]{2,1,0:T(8,128)(2,1)}, bf16[1,448,512]{2,1,0:T(8,128)(2,1)}) custom-call(s32[13]{0:T(128)} %stack.64.core_ref.table_ref, bf16[8,320,512]{2,1,0:T(8,128)(2,1)} %get-tuple-element.38.xk_ref, bf16[2,320,512]{2,1,0:T(8,128)(2,1)} %copy-done.13, ...), custom_call_target="tpu_custom_call" | custom-call | flops 1342177280 | bytes 3400000 | tf_op jit(solution)/shard_map/grad_a/pallas_call | solution.py:199
  29.3 1.3 collective-permute-start.3
  30.6 4.5 %collective-permute-start.13 = (bf16[576,512]{1,0:T(8,128)(2,1)}, bf16[576,512]{1,0:T(8,128)(2,1)S(1)}, u32[]{:S(2)}, u32[]{:S(2)}) collective-permute-start(bf16[576,512]{1,0:T(8,128)(2,1)} %bitcast.70), channel_id=1, source_target_pairs={{0,12},{1,13},{2,14},{3,15},{4,0},{5,1},{6,2},{7,3},{8,4},{9,5},{1... | collective-permute-start | bytes 1769480 | tf_op jit(solution)/shard_map/ppermute | solution.py:54
  35.1 11.1 %grad_b.1 = (bf16[1,576,512]{2,1,0:T(8,128)(2,1)}, bf16[1,576,512]{2,1,0:T(8,128)(2,1)}, bf16[1,576,512]{2,1,0:T(8,128)(2,1)}, bf16[1,576,512]{2,1,0:T(8,128)(2,...) custom-call(s32[13]{0:T(128)} %stack.64.core_ref.table_ref, ...), custom_call_target="tpu_custom_call" | custom-call | flops 4026531840 | bytes 10200000 | tf_op jit(solution)/shard_map/grad_b/pallas_call | solution.py:199
  46.2 5.5 %collective-permute-done.3.refs_1_ = bf16[448,512]{1,0:T(8,128)(2,1)S(1)} collective-permute-done((bf16[448,512]{1,0:T(8,128)(2,1)}, bf16[448,512]{1,0:T(8,128)(2,1)S(1)}, u32[]{:S(2)}, u32[]{:S(2)}) %collective-permute-start.3) | collective-permute-done | bytes 458784 | tf_op jit(solution)/shard_map/ppermute | solution.py:50
  51.7 0.8 copy-done.5
  52.5 1.3 collective-permute-start.4
  53.8 5.0 %collective-permute-done.13.refs_1_ = bf16[576,512]{1,0:T(8,128)(2,1)S(1)} collective-permute-done((bf16[576,512]{1,0:T(8,128)(2,1)}, bf16[576,512]{1,0:T(8,128)(2,1)S(1)}, u32[]{:S(2)}, u32[]{:S(2)}) %collective-permute-start.13) | collective-permute-done | bytes 589856 | tf_op jit(solution)/shard_map/ppermute | solution.py:54
  58.8 2.3 %fusion = bf16[576,512]{1,0:T(8,128)(2,1)} fusion(bf16[576,512]{1,0:T(8,128)(2,1)S(1)} %collective-permute-done.13.refs_1_, bf16[1,576,512]{2,1,0:T(8,128)(2,1)} %get-tuple-element.54), kind=kLoop, calls=%fused_computation.1 | loop fusion | flops 1179648 | bytes 1769472 | tf_op jit(solution)/shard_map/convert_element_type | solution.py:471
  61.1 2.3 %collective-permute-start.16 = (bf16[576,512]{1,0:T(8,128)(2,1)}, bf16[576,512]{1,0:T(8,128)(2,1)}, u32[]{:S(2)}, u32[]{:S(2)}) collective-permute-start(bf16[576,512]{1,0:T(8,128)(2,1)} %fusion), channel_id=1, source_target_pairs={{0,12},{1,13},{2,14},{3,15},{4,0},{5,1},{6,2},{7,3},{8,4},{9,5},{1... | collective-permute-start | bytes 1769480 | tf_op jit(solution)/shard_map/ppermute | solution.py:54
  63.4 0.8 copy-done.3
  64.2 0.6 broadcast_in_dim.3.gain_ref
  64.8 0.9 fusion.7
  65.7 2.7 %collective-permute-start.9 = (bf16[224,512]{1,0:T(8,128)(2,1)}, bf16[224,512]{1,0:T(8,128)(2,1)S(1)}, u32[]{:S(2)}, u32[]{:S(2)}) collective-permute-start(bf16[224,512]{1,0:T(8,128)(2,1)} %get-tuple-element.72), channel_id=1, source_target_pairs={{0,12},{1,13},{2,14},{3,15},{4,0},{5,1},{6,2},{7,3},{8,4},{9,5},{1... | collective-permute-start | bytes 688136 | tf_op jit(solution)/shard_map/ppermute | solution.py:54
  68.6 20.0 %collective-permute-done.16 = bf16[576,512]{1,0:T(8,128)(2,1)} collective-permute-done((bf16[576,512]{1,0:T(8,128)(2,1)}, bf16[576,512]{1,0:T(8,128)(2,1)}, u32[]{:S(2)}, u32[]{:S(2)}) %collective-permute-start.16) | collective-permute-done | bytes 589856 | tf_op jit(solution)/shard_map/ppermute | solution.py:54
  88.6 0.7 collective-permute-start.14
  89.3 1.0 collective-permute-start.12
  90.3 1.5 fusion.2
  91.7 10.7 %collective-permute-done.4.a1 = bf16[3,448,512]{2,1,0:T(8,128)(2,1)S(1)} collective-permute-done((bf16[3,448,512]{2,1,0:T(8,128)(2,1)}, bf16[3,448,512]{2,1,0:T(8,128)(2,1)S(1)}, u32[]{:S(2)}, u32[]{:S(2)}) %collective-permute-start.4) | collective-permute-done | bytes 1376288 | tf_op jit(solution)/shard_map/ppermute | solution.py:50
  102.5 0.9 fusion.14
  103.4 1.1 fusion.9
  104.6 1.5 collective-permute-done.14
  106.1 1.5 collective-permute-start.8
  107.6 1.5 collective-permute-start.10
  109.1 1.0 fusion.5.b0
  110.1 8.0 %early_product.1 = (bf16[2,8,320,256]{3,2,1,0:T(8,128)(2,1)}, f32[320,128]{1,0:T(8,128)}) custom-call(s32[13]{0:T(128)} %stack.64.core_ref.table_ref, bf16[320,1024]{1,0:T(8,128)(2,1)} %get-tuple-element.36.cp_ref.c_ref, bf16[1,8192]{1,0:T(2,128)(2,1)} %broadcast_in_dim.3.gain_ref, bf16[8,320,512]{2,1,0:T(8,128)(2,1)} %get-tuple-element.38.xk_ref, ...), custom_call_target="tpu_custom_call" | custom-call | flops 1400000000 | bytes 8000000 | tf_op jit(solution)/shard_map/early_product/pallas_call | solution.py:369
  118.2 0.8 copy-done.14
  119.2 4.5 %total.1 = (f32[512,1024]{1,0:T(8,128)}, f32[8,128]{1,0:T(8,128)}, bf16[256,1024]{1,0:T(8,128)(2,1)}) custom-call(s32[13]{0:T(128)} %stack.64.core_ref.table_ref, bf16[3,448,512]{2,1,0:T(8,128)(2,1)} %get-tuple-element.44.a0, bf16[3,448,512]{2,1,0:T(8,128)(2,1)} %copy-done.1, bf16[224,512]{1,0:T(8,128)(2,1)} %collective-permute-done.5.ue, ...), custom_call_target="tpu_custom_call" | custom-call | flops 5000000 | bytes 5000000 | tf_op jit(solution)/shard_map/total/pallas_call | solution.py:252
  123.7 2.0 collective-permute-start.18
  125.7 1.0 collective-permute-done.18
  126.7 0.7 add.174
  127.4 1.4 collective-permute-start.19
  128.8 1.1 collective-permute-done.19
  129.9 1.6 collective-permute-start.22
  131.5 1.3 collective-permute-start.21
  132.9 2.8 %collective-permute-start.23 = (f32[512,128]{1,0:T(8,128)S(1)}, f32[512,128]{1,0:T(8,128)S(1)}, u32[]{:S(2)}, u32[]{:S(2)}) collective-permute-start(f32[512,128]{1,0:T(8,128)S(1)} %multiply_subtract_fusion.1), channel_id=1, source_target_pairs={{0,16},{16,0},{32,48},{48,32},{64,80},{80,64},{96,112},{112,96},{1... | collective-permute-start | bytes 786440 | tf_op jit(solution)/shard_map/ppermute | solution.py:58
  135.7 0.8 collective-permute-done.20
  136.5 0.6 add_add_fusion.sq_ref
  137.1 7.3 %adam.1 = (f32[1,512,1024]{2,1,0:T(8,128)}, f32[1,512,1024]{2,1,0:T(8,128)}, bf16[2,512,128]{2,1,0:T(8,128)(2,1)}, bf16[2,512,128]{2,1,0:T(8,128)(2,1)}, bf16[2,...) custom-call(s32[13]{0:T(128)} %stack.64.core_ref.table_ref, f32[8,128]{1,0:T(8,128)} %add_add_fusion.sq_ref, ...), custom_call_target="tpu_custom_call" | custom-call | flops 20000000 | bytes 12000000 | tf_op jit(solution)/shard_map/adam/pallas_call | solution.py:299
  144.4 2.5 %collective-permute-start.26 = (bf16[2,512,128]{2,1,0:T(8,128)(2,1)}, bf16[2,512,128]{2,1,0:T(8,128)(2,1)S(1)}, u32[]{:S(2)}, u32[]{:S(2)}) collective-permute-start(bf16[2,512,128]{2,1,0:T(8,128)(2,1)} %get-tuple-element.64), channel_id=1, source_target_pairs={{0,96},{16,112},{32,0},{48,16},{64,32},{80,48},{96,64},{112,80},{1... | collective-permute-start | bytes 786440 | tf_op jit(solution)/shard_map/ppermute | solution.py:62
  146.8 0.6 collective-permute-start.25
  147.4 0.6 collective-permute-start.24
  148.0 0.7 copy-done.9
  148.7 4.6 %collective-permute-done.26 = bf16[2,512,128]{2,1,0:T(8,128)(2,1)S(1)} collective-permute-done((bf16[2,512,128]{2,1,0:T(8,128)(2,1)}, bf16[2,512,128]{2,1,0:T(8,128)(2,1)S(1)}, u32[]{:S(2)}, u32[]{:S(2)}) %collective-permute-start.26) | collective-permute-done | bytes 262176 | tf_op jit(solution)/shard_map/ppermute | solution.py:62
  153.3 0.6 collective-permute-done.25
  153.9 7.1 %collective-permute-done.24 = bf16[2,512,128]{2,1,0:T(8,128)(2,1)S(1)} collective-permute-done((bf16[2,512,128]{2,1,0:T(8,128)(2,1)}, bf16[2,512,128]{2,1,0:T(8,128)(2,1)S(1)}, u32[]{:S(2)}, u32[]{:S(2)}) %collective-permute-start.24) | collective-permute-done | bytes 262176 | tf_op jit(solution)/shard_map/ppermute | solution.py:62
  161.0 1.1 add_convert_fusion
  162.1 2.7 %collective-permute-start.27 = (bf16[2,512,128]{2,1,0:T(8,128)(2,1)S(1)}, bf16[2,512,128]{2,1,0:T(8,128)(2,1)S(1)}, u32[]{:S(2)}, u32[]{:S(2)}) collective-permute-start(bf16[2,512,128]{2,1,0:T(8,128)(2,1)S(1)} %rev.3), channel_id=1, source_target_pairs={{0,16},{16,0},{32,48},{48,32},{64,80},{80,64},{96,112},{112,96},{1... | collective-permute-start | bytes 786440 | tf_op jit(solution)/shard_map/ppermute | solution.py:58
  164.9 12.0 %collective-permute-done.27 = bf16[2,512,128]{2,1,0:T(8,128)(2,1)S(1)} collective-permute-done((bf16[2,512,128]{2,1,0:T(8,128)(2,1)S(1)}, bf16[2,512,128]{2,1,0:T(8,128)(2,1)S(1)}, u32[]{:S(2)}, u32[]{:S(2)}) %collective-permute-start.27) | collective-permute-done | bytes 262176 | tf_op jit(solution)/shard_map/ppermute | solution.py:58
  177.1 0.4 collective-permute-start.29
  177.4 1.1 collective-permute-start.30
  178.5 0.9 multiply_subtract_fusion
  179.4 9.4 %all-gather.4.cloned.1.call-done = bf16[4096,1024]{1,0:T(8,128)(2,1)} async-done(((bf16[256,1024]{1,0:T(8,128)(2,1)}), bf16[4096,1024]{1,0:T(8,128)(2,1)}) %all-gather.4.cloned.1.call-update) | async-done | bytes 8388624 | tf_op jit(solution)/shard_map/all_gather | solution.py:540
  188.8 14.1 %input_gradient.1 = (bf16[1,320,8192]{2,1,0:T(8,128)(2,1)}, f32[8,128]{1,0:T(8,128)}) custom-call(s32[13]{0:T(128)} %stack.64.core_ref.table_ref, bf16[320,1024]{1,0:T(8,128)(2,1)} %get-tuple-element.36.cp_ref.c_ref, f32[320,128]{1,0:T(8,128)} %get-tuple-element.37.inv_ref, bf16[1,8192]{1,0:T(2,128)(2,1)} %broadcast_in_dim.3.gain_ref, ...), custom_call_target="tpu_custom_call" | custom-call | flops 5000000000 | bytes 30000000 | tf_op jit(solution)/shard_map/input_gradient/pallas_call | solution.py:438
  203.0 0.7 copy-done.20
  203.9 2.9 %place.1 = bf16[512,1024]{1,0:T(8,128)(2,1)} custom-call(s32[13]{0:T(128)} %stack.64.core_ref.table_ref, bf16[2,512,128]{2,1,0:T(8,128)(2,1)} %copy-done.11, bf16[2,512,128]{2,1,0:T(8,128)(2,1)} %copy-done.20, bf16[2,512,128]{2,1,0:T(8,128)(2,1)} %copy-done.21, bf16[2,512,128]{2,1,0:T(8,128)(2,1)} %copy-done.22, f32[8,128]{1,0:T(8,128)} %get-tuple-element.65.refs_4_), custom_call_target="tpu_custom_call" | custom-call | flops 1000000 | bytes 2000000 | tf_op jit(solution)/shard_map/place/pallas_call | solution.py:323
  (89 shorter events, 1.3 us)
Async XLA Ops:
  7.2 103.0 %all-gather.6.cloned.1.call-start = ((), (), s32[]{:S(2)}) async-start(), calls=%async_computation.1 | async-start | bytes 8912896 | tf_op jit(solution)/shard_map/all_gather | solution.py:495
  9.1 179.7 %all-gather.4.cloned.1.call-start = ((), (), s32[]{:S(2)}) async-start(), calls=%async_computation | async-start | bytes 8912896 | tf_op jit(solution)/shard_map/all_gather | solution.py:540
  18.2 3.5 %collective-permute-start = (bf16[2,320,512]{2,1,0:T(8,128)(2,1)}, bf16[2,320,512]{2,1,0:T(8,128)(2,1)S(1)}, u32[]{:S(2)}, u32[]{:S(2)}) collective-permute-start(bf16[2,320,512]{2,1,0:T(8,128)(2,1)} %get-tuple-element.40), channel_id=1, source_target_pairs={{0,1},{1,0},{2,3},{3,2},{4,5},{5,4},{6,7},{7,6},{8,9},{9,8},{10,11... | collective-permute-start | bytes 1966088 | tf_op jit(solution)/shard_map/ppermute | solution.py:46
  19.7 2.9 %collective-permute-start.1 = (bf16[320,1024]{1,0:T(8,128)(2,1)}, bf16[320,1024]{1,0:T(8,128)(2,1)S(1)}, u32[]{:S(2)}, u32[]{:S(2)}) collective-permute-start(bf16[320,1024]{1,0:T(8,128)(2,1)} %get-tuple-element.36.cp_ref.c_ref), channel_id=1, source_target_pairs={{0,1},{1,0},{2,3},{3,2},{4,5},{5,4},{6,7},{7,6},{8,9},{9,8},{10,11... | collective-permute-start | bytes 1966088 | tf_op jit(solution)/shard_map/ppermute | solution.py:46
  21.7 0.9 copy-start.13
  22.6 0.8 copy-start.12
  23.5 11.7 %collective-permute-start.2 = (bf16[8,320,512]{2,1,0:T(8,128)(2,1)}, bf16[8,320,512]{2,1,0:T(8,128)(2,1)}, u32[]{:S(2)}, u32[]{:S(2)}) collective-permute-start(bf16[8,320,512]{2,1,0:T(8,128)(2,1)} %after.5.xs_ref), channel_id=1, source_target_pairs={{0,1},{1,0},{2,3},{3,2},{4,5},{5,4},{6,7},{7,6},{8,9},{9,8},{10,11... | collective-permute-start | bytes 7864328 | tf_op jit(solution)/shard_map/ppermute | solution.py:46
  29.3 22.5 %collective-permute-start.3 = (bf16[448,512]{1,0:T(8,128)(2,1)}, bf16[448,512]{1,0:T(8,128)(2,1)S(1)}, u32[]{:S(2)}, u32[]{:S(2)}) collective-permute-start(bf16[448,512]{1,0:T(8,128)(2,1)} %bitcast.71), channel_id=1, source_target_pairs={{0,2},{1,3},{2,0},{3,1},{4,6},{5,7},{6,4},{7,5},{8,10},{9,11},{10,... | collective-permute-start | bytes 1376264 | tf_op jit(solution)/shard_map/ppermute | solution.py:50
  30.6 28.2 %collective-permute-start.13 = (bf16[576,512]{1,0:T(8,128)(2,1)}, bf16[576,512]{1,0:T(8,128)(2,1)S(1)}, u32[]{:S(2)}, u32[]{:S(2)}) collective-permute-start(bf16[576,512]{1,0:T(8,128)(2,1)} %bitcast.70), channel_id=1, source_target_pairs={{0,12},{1,13},{2,14},{3,15},{4,0},{5,1},{6,2},{7,3},{8,4},{9,5},{1... | collective-permute-start | bytes 1769480 | tf_op jit(solution)/shard_map/ppermute | solution.py:54
  35.1 28.3 %collective-permute-start.11 = (bf16[576,512]{1,0:T(8,128)(2,1)}, bf16[576,512]{1,0:T(8,128)(2,1)S(1)}, u32[]{:S(2)}, u32[]{:S(2)}) collective-permute-start(bf16[576,512]{1,0:T(8,128)(2,1)} %bitcast.69), channel_id=1, source_target_pairs={{0,4},{1,5},{2,6},{3,7},{4,8},{5,9},{6,10},{7,11},{8,12},{9,13},{1... | collective-permute-start | bytes 1769480 | tf_op jit(solution)/shard_map/ppermute | solution.py:54
  51.7 0.8 copy-start.5
  52.5 50.0 %collective-permute-start.4 = (bf16[3,448,512]{2,1,0:T(8,128)(2,1)}, bf16[3,448,512]{2,1,0:T(8,128)(2,1)S(1)}, u32[]{:S(2)}, u32[]{:S(2)}) collective-permute-start(bf16[3,448,512]{2,1,0:T(8,128)(2,1)} %after.6), channel_id=1, source_target_pairs={{0,2},{1,3},{2,0},{3,1},{4,6},{5,7},{6,4},{7,5},{8,10},{9,11},{10,... | collective-permute-start | bytes 4128776 | tf_op jit(solution)/shard_map/ppermute | solution.py:50
  58.8 5.4 %copy-start.2 = (bf16[576,512]{1,0:T(8,128)(2,1)}, bf16[576,512]{1,0:T(8,128)(2,1)S(1)}, u32[]{:S(2)}) copy-start(bf16[576,512]{1,0:T(8,128)(2,1)S(1)} %collective-permute-done.13.refs_1_) | copy-start | bytes 1769476
  58.8 5.4 %copy-start.26 = (bf16[8192]{0:T(1024)(128)(2,1)S(1)}, bf16[8192]{0:T(1024)(128)(2,1)}, u32[]{:S(2)}) copy-start(bf16[8192]{0:T(1024)(128)(2,1)} %param.14) | copy-start | bytes 49156
  58.8 6.0 %copy-start.6 = (bf16[448,512]{1,0:T(8,128)(2,1)S(1)}, bf16[448,512]{1,0:T(8,128)(2,1)}, u32[]{:S(2)}) copy-start(bf16[448,512]{1,0:T(8,128)(2,1)} %copy-done.5) | copy-start | bytes 1376260
  58.8 6.0 %copy-start.19 = (bf16[1,448,512]{2,1,0:T(8,128)(2,1)S(1)}, bf16[1,448,512]{2,1,0:T(8,128)(2,1)}, u32[]{:S(2)}) copy-start(bf16[1,448,512]{2,1,0:T(8,128)(2,1)} %get-tuple-element.47) | copy-start | bytes 1376260
  61.1 27.5 %collective-permute-start.16 = (bf16[576,512]{1,0:T(8,128)(2,1)}, bf16[576,512]{1,0:T(8,128)(2,1)}, u32[]{:S(2)}, u32[]{:S(2)}) collective-permute-start(bf16[576,512]{1,0:T(8,128)(2,1)} %fusion), channel_id=1, source_target_pairs={{0,12},{1,13},{2,14},{3,15},{4,0},{5,1},{6,2},{7,3},{8,4},{9,5},{1... | collective-permute-start | bytes 1769480 | tf_op jit(solution)/shard_map/ppermute | solution.py:54
  63.4 0.8 copy-start.3
  64.2 25.1 %collective-permute-start.15 = (bf16[576,512]{1,0:T(8,128)(2,1)}, bf16[576,512]{1,0:T(8,128)(2,1)}, u32[]{:S(2)}, u32[]{:S(2)}) collective-permute-start(bf16[576,512]{1,0:T(8,128)(2,1)} %after.8), channel_id=1, source_target_pairs={{0,4},{1,5},{2,6},{3,7},{4,8},{5,9},{6,10},{7,11},{8,12},{9,13},{1... | collective-permute-start | bytes 1769480 | tf_op jit(solution)/shard_map/ppermute | solution.py:54
  64.8 3.6 %copy-start.4 = (bf16[576,512]{1,0:T(8,128)(2,1)S(1)}, bf16[576,512]{1,0:T(8,128)(2,1)}, u32[]{:S(2)}) copy-start(bf16[576,512]{1,0:T(8,128)(2,1)} %copy-done.3) | copy-start | bytes 1769476
  64.8 3.6 %copy-start.15 = (bf16[1,576,512]{2,1,0:T(8,128)(2,1)S(1)}, bf16[1,576,512]{2,1,0:T(8,128)(2,1)}, u32[]{:S(2)}) copy-start(bf16[1,576,512]{2,1,0:T(8,128)(2,1)} %get-tuple-element.49) | copy-start | bytes 1769476
  65.7 37.7 %collective-permute-start.9 = (bf16[224,512]{1,0:T(8,128)(2,1)}, bf16[224,512]{1,0:T(8,128)(2,1)S(1)}, u32[]{:S(2)}, u32[]{:S(2)}) collective-permute-start(bf16[224,512]{1,0:T(8,128)(2,1)} %get-tuple-element.72), channel_id=1, source_target_pairs={{0,12},{1,13},{2,14},{3,15},{4,0},{5,1},{6,2},{7,3},{8,4},{9,5},{1... | collective-permute-start | bytes 688136 | tf_op jit(solution)/shard_map/ppermute | solution.py:54
  68.4 35.0 %collective-permute-start.6 = (bf16[224,512]{1,0:T(8,128)(2,1)}, bf16[224,512]{1,0:T(8,128)(2,1)}, u32[]{:S(2)}, u32[]{:S(2)}) collective-permute-start(bf16[224,512]{1,0:T(8,128)(2,1)} %get-tuple-element.73), channel_id=1, source_target_pairs={{0,4},{1,5},{2,6},{3,7},{4,8},{5,9},{6,10},{7,11},{8,12},{9,13},{1... | collective-permute-start | bytes 688136 | tf_op jit(solution)/shard_map/ppermute | solution.py:54
  68.4 21.9 %copy-start.18 = (bf16[1,576,512]{2,1,0:T(8,128)(2,1)S(1)}, bf16[1,576,512]{2,1,0:T(8,128)(2,1)}, u32[]{:S(2)}) copy-start(bf16[1,576,512]{2,1,0:T(8,128)(2,1)} %get-tuple-element.52) | copy-start | bytes 1769476
  68.4 20.2 %copy-start.16 = (bf16[576,512]{1,0:T(8,128)(2,1)S(1)}, bf16[576,512]{1,0:T(8,128)(2,1)}, u32[]{:S(2)}) copy-start(bf16[576,512]{1,0:T(8,128)(2,1)} %after.7) | copy-start | bytes 1769476
  68.6 33.9 %copy-start = (bf16[3,448,512]{2,1,0:T(8,128)(2,1)S(1)}, bf16[3,448,512]{2,1,0:T(8,128)(2,1)}, u32[]{:S(2)}) copy-start(bf16[3,448,512]{2,1,0:T(8,128)(2,1)} %get-tuple-element.44.a0) | copy-start | bytes 4128772
  88.6 17.4 %collective-permute-start.14 = (bf16[576,512]{1,0:T(8,128)(2,1)S(1)}, bf16[576,512]{1,0:T(8,128)(2,1)S(1)}, u32[]{:S(2)}, u32[]{:S(2)}) collective-permute-start(bf16[576,512]{1,0:T(8,128)(2,1)S(1)} %copy-done.16), channel_id=1, source_target_pairs={{0,12},{1,13},{2,14},{3,15},{4,0},{5,1},{6,2},{7,3},{8,4},{9,5},{1... | collective-permute-start | bytes 1769480 | tf_op jit(solution)/shard_map/ppermute | solution.py:54
  89.3 18.3 %collective-permute-start.12 = (bf16[576,512]{1,0:T(8,128)(2,1)S(1)}, bf16[576,512]{1,0:T(8,128)(2,1)S(1)}, u32[]{:S(2)}, u32[]{:S(2)}) collective-permute-start(bf16[576,512]{1,0:T(8,128)(2,1)S(1)} %fusion.3), channel_id=1, source_target_pairs={{0,4},{1,5},{2,6},{3,7},{4,8},{5,9},{6,10},{7,11},{8,12},{9,13},{1... | collective-permute-start | bytes 1769480 | tf_op jit(solution)/shard_map/ppermute | solution.py:54
  102.5 2.1 copy-start.1
  102.5 15.6 %collective-permute-start.17 = (bf16[576,512]{1,0:T(8,128)(2,1)S(1)}, bf16[576,512]{1,0:T(8,128)(2,1)S(1)}, u32[]{:S(2)}, u32[]{:S(2)}) collective-permute-start(bf16[576,512]{1,0:T(8,128)(2,1)S(1)} %fusion.2), channel_id=1, source_target_pairs={{0,2},{1,3},{2,0},{3,1},{4,6},{5,7},{6,4},{7,5},{8,10},{9,11},{10,... | collective-permute-start | bytes 1769480 | tf_op jit(solution)/shard_map/ppermute | solution.py:50
  102.5 6.6 %copy-start.17 = (bf16[1,576,512]{2,1,0:T(8,128)(2,1)S(1)}, bf16[1,576,512]{2,1,0:T(8,128)(2,1)}, u32[]{:S(2)}) copy-start(bf16[1,576,512]{2,1,0:T(8,128)(2,1)} %get-tuple-element.48) | copy-start | bytes 1769476
  103.4 14.7 %collective-permute-start.5 = (bf16[224,512]{1,0:T(8,128)(2,1)}, bf16[224,512]{1,0:T(8,128)(2,1)}, u32[]{:S(2)}, u32[]{:S(2)}) collective-permute-start(bf16[224,512]{1,0:T(8,128)(2,1)} %get-tuple-element.71), channel_id=1, source_target_pairs={{0,4},{1,5},{2,6},{3,7},{4,8},{5,9},{6,10},{7,11},{8,12},{9,13},{1... | collective-permute-start | bytes 688136 | tf_op jit(solution)/shard_map/ppermute | solution.py:54
  104.5 13.6 %collective-permute-start.7 = (bf16[224,512]{1,0:T(8,128)(2,1)S(1)}, bf16[224,512]{1,0:T(8,128)(2,1)S(1)}, u32[]{:S(2)}, u32[]{:S(2)}) collective-permute-start(bf16[224,512]{1,0:T(8,128)(2,1)S(1)} %get-tuple-element.69), channel_id=1, source_target_pairs={{0,4},{1,5},{2,6},{3,7},{4,8},{5,9},{6,10},{7,11},{8,12},{9,13},{1... | collective-permute-start | bytes 688136 | tf_op jit(solution)/shard_map/ppermute | solution.py:54
  106.1 12.1 %collective-permute-start.8 = (bf16[224,512]{1,0:T(8,128)(2,1)}, bf16[224,512]{1,0:T(8,128)(2,1)S(1)}, u32[]{:S(2)}, u32[]{:S(2)}) collective-permute-start(bf16[224,512]{1,0:T(8,128)(2,1)} %get-tuple-element.70), channel_id=1, source_target_pairs={{0,12},{1,13},{2,14},{3,15},{4,0},{5,1},{6,2},{7,3},{8,4},{9,5},{1... | collective-permute-start | bytes 688136 | tf_op jit(solution)/shard_map/ppermute | solution.py:54
  107.6 10.5 %collective-permute-start.10 = (bf16[224,512]{1,0:T(8,128)(2,1)S(1)}, bf16[224,512]{1,0:T(8,128)(2,1)S(1)}, u32[]{:S(2)}, u32[]{:S(2)}) collective-permute-start(bf16[224,512]{1,0:T(8,128)(2,1)S(1)} %get-tuple-element.68), channel_id=1, source_target_pairs={{0,12},{1,13},{2,14},{3,15},{4,0},{5,1},{6,2},{7,3},{8,4},{9,5},{1... | collective-permute-start | bytes 688136 | tf_op jit(solution)/shard_map/ppermute | solution.py:54
  118.1 0.9 copy-start.14
  118.1 0.9 copy-start.23
  118.2 0.9 copy-start.24
  118.2 1.0 copy-start.25
  119.2 13.7 %copy-start.7 = (f32[512,128]{1,0:T(8,128)S(1)}, f32[512,128]{1,0:T(8,128)}, u32[]{:S(2)}) copy-start(f32[512,128]{1,0:T(8,128)} %param.19) | copy-start | bytes 786436
  119.2 13.7 %copy-start.8 = (f32[512,128]{1,0:T(8,128)S(1)}, f32[512,128]{1,0:T(8,128)}, u32[]{:S(2)}) copy-start(f32[512,128]{1,0:T(8,128)} %param.18) | copy-start | bytes 786436
  123.7 3.0 %collective-permute-start.18 = (f32[8,128]{1,0:T(8,128)}, f32[8,128]{1,0:T(8,128)S(1)}, u32[]{:S(2)}, u32[]{:S(2)}) collective-permute-start(f32[8,128]{1,0:T(8,128)} %get-tuple-element.57), channel_id=1, source_target_pairs={{0,1},{1,0},{2,3},{3,2},{4,5},{5,4},{6,7},{7,6},{8,9},{9,8},{10,11... | collective-permute-start | bytes 12296 | tf_op jit(solution)/shard_map/ppermute | solution.py:46
  127.4 2.5 %collective-permute-start.19 = (f32[8,128]{1,0:T(8,128)S(1)}, f32[8,128]{1,0:T(8,128)S(1)}, u32[]{:S(2)}, u32[]{:S(2)}) collective-permute-start(f32[8,128]{1,0:T(8,128)S(1)} %add.174), channel_id=1, source_target_pairs={{0,2},{1,3},{2,0},{3,1},{4,6},{5,7},{6,4},{7,5},{8,10},{9,11},{10,... | collective-permute-start | bytes 12296 | tf_op jit(solution)/shard_map/ppermute | solution.py:50
  129.9 5.8 %collective-permute-start.22 = (f32[8,128]{1,0:T(8,128)S(1)}, f32[8,128]{1,0:T(8,128)S(1)}, u32[]{:S(2)}, u32[]{:S(2)}) collective-permute-start(f32[8,128]{1,0:T(8,128)S(1)} %add.175), channel_id=1, source_target_pairs={{0,12},{1,13},{2,14},{3,15},{4,0},{5,1},{6,2},{7,3},{8,4},{9,5},{1... | collective-permute-start | bytes 12296 | tf_op jit(solution)/shard_map/ppermute | solution.py:54
  131.5 4.1 %collective-permute-start.21 = (f32[8,128]{1,0:T(8,128)S(1)}, f32[8,128]{1,0:T(8,128)S(1)}, u32[]{:S(2)}, u32[]{:S(2)}) collective-permute-start(f32[8,128]{1,0:T(8,128)S(1)} %add.175), channel_id=1, source_target_pairs={{0,8},{1,9},{2,10},{3,11},{4,12},{5,13},{6,14},{7,15},{8,0},{9,1},... | collective-permute-start | bytes 12296 | tf_op jit(solution)/shard_map/ppermute | solution.py:54
  132.8 3.7 %collective-permute-start.20 = (f32[8,128]{1,0:T(8,128)S(1)}, f32[8,128]{1,0:T(8,128)S(1)}, u32[]{:S(2)}, u32[]{:S(2)}) collective-permute-start(f32[8,128]{1,0:T(8,128)S(1)} %add.175), channel_id=1, source_target_pairs={{0,4},{1,5},{2,6},{3,7},{4,8},{5,9},{6,10},{7,11},{8,12},{9,13},{1... | collective-permute-start | bytes 12296 | tf_op jit(solution)/shard_map/ppermute | solution.py:54
  132.9 15.1 %collective-permute-start.23 = (f32[512,128]{1,0:T(8,128)S(1)}, f32[512,128]{1,0:T(8,128)S(1)}, u32[]{:S(2)}, u32[]{:S(2)}) collective-permute-start(f32[512,128]{1,0:T(8,128)S(1)} %multiply_subtract_fusion.1), channel_id=1, source_target_pairs={{0,16},{16,0},{32,48},{48,32},{64,80},{80,64},{96,112},{112,96},{1... | collective-permute-start | bytes 786440 | tf_op jit(solution)/shard_map/ppermute | solution.py:58
  144.4 8.9 %collective-permute-start.26 = (bf16[2,512,128]{2,1,0:T(8,128)(2,1)}, bf16[2,512,128]{2,1,0:T(8,128)(2,1)S(1)}, u32[]{:S(2)}, u32[]{:S(2)}) collective-permute-start(bf16[2,512,128]{2,1,0:T(8,128)(2,1)} %get-tuple-element.64), channel_id=1, source_target_pairs={{0,96},{16,112},{32,0},{48,16},{64,32},{80,48},{96,64},{112,80},{1... | collective-permute-start | bytes 786440 | tf_op jit(solution)/shard_map/ppermute | solution.py:62
  146.8 7.0 %collective-permute-start.25 = (bf16[2,512,128]{2,1,0:T(8,128)(2,1)}, bf16[2,512,128]{2,1,0:T(8,128)(2,1)S(1)}, u32[]{:S(2)}, u32[]{:S(2)}) collective-permute-start(bf16[2,512,128]{2,1,0:T(8,128)(2,1)} %get-tuple-element.63), channel_id=1, source_target_pairs={{0,64},{16,80},{32,96},{48,112},{64,0},{80,16},{96,32},{112,48},{1... | collective-permute-start | bytes 786440 | tf_op jit(solution)/shard_map/ppermute | solution.py:62
  147.4 13.6 %collective-permute-start.24 = (bf16[2,512,128]{2,1,0:T(8,128)(2,1)}, bf16[2,512,128]{2,1,0:T(8,128)(2,1)S(1)}, u32[]{:S(2)}, u32[]{:S(2)}) collective-permute-start(bf16[2,512,128]{2,1,0:T(8,128)(2,1)} %get-tuple-element.62), channel_id=1, source_target_pairs={{0,32},{16,48},{32,64},{48,80},{64,96},{80,112},{96,0},{112,16},{1... | collective-permute-start | bytes 786440 | tf_op jit(solution)/shard_map/ppermute | solution.py:62
  148.0 0.7 copy-start.9
  148.7 28.2 %copy-start.10 = (f32[512,128]{1,0:T(8,128)S(1)}, f32[512,128]{1,0:T(8,128)}, u32[]{:S(2)}) copy-start(f32[512,128]{1,0:T(8,128)} %copy-done.9) | copy-start | bytes 786436
  162.1 14.7 %collective-permute-start.27 = (bf16[2,512,128]{2,1,0:T(8,128)(2,1)S(1)}, bf16[2,512,128]{2,1,0:T(8,128)(2,1)S(1)}, u32[]{:S(2)}, u32[]{:S(2)}) collective-permute-start(bf16[2,512,128]{2,1,0:T(8,128)(2,1)S(1)} %rev.3), channel_id=1, source_target_pairs={{0,16},{16,0},{32,48},{48,32},{64,80},{80,64},{96,112},{112,96},{1... | collective-permute-start | bytes 786440 | tf_op jit(solution)/shard_map/ppermute | solution.py:58
  177.0 26.0 %copy-start.11 = (bf16[2,512,128]{2,1,0:T(8,128)(2,1)}, bf16[2,512,128]{2,1,0:T(8,128)(2,1)S(1)}, u32[]{:S(2)}) copy-start(bf16[2,512,128]{2,1,0:T(8,128)(2,1)S(1)} %get-tuple-element.75.refs_0_) | copy-start | bytes 786436
  177.0 26.0 %collective-permute-start.28 = (bf16[2,512,128]{2,1,0:T(8,128)(2,1)S(1)}, bf16[2,512,128]{2,1,0:T(8,128)(2,1)S(1)}, u32[]{:S(2)}, u32[]{:S(2)}) collective-permute-start(bf16[2,512,128]{2,1,0:T(8,128)(2,1)S(1)} %get-tuple-element.75.refs_0_), channel_id=1, source_target_pairs={{0,96},{16,112},{32,0},{48,16},{64,32},{80,48},{96,64},{112,80},{1... | collective-permute-start | bytes 786440 | tf_op jit(solution)/shard_map/ppermute | solution.py:62
  177.1 25.9 %collective-permute-start.29 = (bf16[2,512,128]{2,1,0:T(8,128)(2,1)S(1)}, bf16[2,512,128]{2,1,0:T(8,128)(2,1)S(1)}, u32[]{:S(2)}, u32[]{:S(2)}) collective-permute-start(bf16[2,512,128]{2,1,0:T(8,128)(2,1)S(1)} %get-tuple-element.75.refs_0_), channel_id=1, source_target_pairs={{0,64},{16,80},{32,96},{48,112},{64,0},{80,16},{96,32},{112,48},{1... | collective-permute-start | bytes 786440 | tf_op jit(solution)/shard_map/ppermute | solution.py:62
  177.4 25.5 %collective-permute-start.30 = (bf16[2,512,128]{2,1,0:T(8,128)(2,1)S(1)}, bf16[2,512,128]{2,1,0:T(8,128)(2,1)S(1)}, u32[]{:S(2)}, u32[]{:S(2)}) collective-permute-start(bf16[2,512,128]{2,1,0:T(8,128)(2,1)S(1)} %get-tuple-element.75.refs_0_), channel_id=1, source_target_pairs={{0,32},{16,48},{32,64},{48,80},{64,96},{80,112},{96,0},{112,16},{1... | collective-permute-start | bytes 786440 | tf_op jit(solution)/shard_map/ppermute | solution.py:62
  202.9 0.7 copy-start.20
  203.0 0.8 copy-start.21
  203.0 0.9 copy-start.22
Sparse Core Ops, SparseCore 0:
  9.7 83.2 all-gather.5
  123.8 64.9 all-gather.3
